TPU v7x, 256 devices: a whole 4x4x8 slice. The times are simulated.
256 devices in a mesh: samples: 4 (over y), channel: 32 (over z, x), spatial: 2 (over core).
Axes of the slice: x: 4, y: 4, z: 8, core: 2. Of those that a mesh axis runs over, the one named last changes fastest.
Arguments:
- features: bfloat16 [512, 4, 2, 1024], P('channel', 'samples', 'spatial'), may hold values from -6 to 6
- conv_one: bfloat16 [27, 512, 512], P(None, 'channel'), may hold values from -0.09375 to 0.09375
- conv_two: bfloat16 [27, 512, 512], P(None, 'channel'), may hold values from -0.09375 to 0.09375
- cotangent: bfloat16 [512, 4, 2, 1024], P('channel', 'samples', 'spatial'), may hold values from -6 to 6
Outputs:
- mixed_out: bfloat16 [512, 4, 2, 1024], P('channel', 'samples', 'spatial')
- input_grad: bfloat16 [512, 4, 2, 1024], P('channel', 'samples', 'spatial')
- grad_one: float32 [27, 512, 512], P(None, 'channel')
- grad_two: float32 [27, 512, 512], P(None, 'channel')
All inputs are finite; a program needn't handle non-finite values.
Results may differ from a plain program's by a relative error of at most 0.017.
Values may be sent and summed in bfloat16 or wider, within the bound.
No kernel may reach another device: no remote copies, remote signals or barrier semaphores. Data moves between devices by JAX's collectives and lax.ppermute only.
A program may use at most 64 MiB of HBM per device.

v0:
```python
import jax
import jax.numpy as jnp
from jax import lax
from jax.sharding import PartitionSpec as P

SIDE = 32


def with_halo(shard, sides, width):
    for axis, dim in sides:
        size, length = (lax.axis_size(axis), shard.shape[dim])
        up = [(i, (i + 1) % size) for i in range(size - 1)]
        down = [(j, i) for i, j in up]
        last = lax.slice_in_dim(shard, length - width, length, axis=dim)
        first = lax.slice_in_dim(shard, 0, width, axis=dim)
        before = lax.ppermute(last, axis, up)
        after = lax.ppermute(first, axis, down)
        shard = jnp.concatenate([before, shard, after], axis=dim)
    return shard


def to_grid(values):
    return values.reshape(values.shape[0], values.shape[1], values.shape[2], SIDE, SIDE)


def to_flat(values):
    return values.reshape(values.shape[0], values.shape[1], values.shape[2], SIDE * SIDE)


def as_taps(kernel):
    return kernel.reshape(3, 3, 3, kernel.shape[1], kernel.shape[2])


def forward_conv(source, kernel, rhs_spec):
    return lax.conv_general_dilated(
        source,
        as_taps(kernel),
        (1, 1, 1),
        [(0, 0), (1, 1), (1, 1)],
        dimension_numbers=("CNDHW", rhs_spec, "CNDHW"),
        preferred_element_type=jnp.float32,
    )


def data_grad(source, kernel, rhs_spec):
    flipped = as_taps(kernel)[::-1, ::-1, ::-1]
    return lax.conv_general_dilated(
        source,
        flipped,
        (1, 1, 1),
        [(0, 0), (1, 1), (1, 1)],
        dimension_numbers=("CNDHW", rhs_spec, "CNDHW"),
        preferred_element_type=jnp.float32,
    )


def weight_grad(padded, upstream, out_spec):
    result = lax.conv_general_dilated(
        padded,
        upstream,
        (1, 1, 1),
        [(0, 0), (0, 0), (0, 0)],
        dimension_numbers=("NCDHW", "OIDHW", out_spec),
        preferred_element_type=jnp.float32,
    )
    return result.reshape(27, result.shape[3], result.shape[4])


def pad_plane(values):
    return jnp.pad(values, ((0, 0), (0, 0), (0, 0), (1, 1), (1, 1)))


def body(features, conv_one, conv_two, cotangent):
    rims_x = with_halo(features, (("spatial", 2),), 1)
    whole_x = lax.all_gather(rims_x, "channel", axis=0, tiled=True)
    pre_act = forward_conv(to_grid(whole_x), conv_one, "DHWOI")
    hidden = jax.nn.silu(pre_act).astype(jnp.bfloat16)
    rims_h = with_halo(to_flat(hidden), (("spatial", 2),), 1)
    grid_h = to_grid(rims_h)
    weight_part = conv_two
    mixed_out = lax.psum_scatter(
        to_flat(forward_conv(grid_h, weight_part, "DHWIO")),
        "channel",
        scatter_dimension=0,
        tiled=True,
    ).astype(jnp.bfloat16)
    rims_c = with_halo(cotangent, (("spatial", 2),), 1)
    whole_c = to_grid(lax.all_gather(rims_c, "channel", axis=0, tiled=True))
    hidden_grad = data_grad(whole_c, conv_two, "DHWOI")
    sigmoid_v = jax.nn.sigmoid(pre_act)
    act_grad = (hidden_grad * sigmoid_v * (1.0 + pre_act * (1.0 - sigmoid_v))).astype(jnp.bfloat16)
    rims_g = with_halo(to_flat(act_grad), (("spatial", 2),), 1)
    grid_g = to_grid(rims_g)
    weight_part = conv_one
    input_grad = lax.psum_scatter(
        to_flat(data_grad(grid_g, weight_part, "DHWIO")).astype(jnp.bfloat16),
        "channel",
        scatter_dimension=0,
        tiled=True,
    )
    local_two = weight_grad(pad_plane(grid_h), whole_c[:, :, 1:-1], "DHWNC")
    local_one = weight_grad(pad_plane(to_grid(whole_x)), act_grad, "DHWCN")
    grad_one, grad_two = (
        lax.psum(local_one.astype(jnp.bfloat16), ("samples", "spatial")).astype(jnp.float32),
        lax.psum(local_two.astype(jnp.bfloat16), ("samples", "spatial")).astype(jnp.float32),
    )
    return (mixed_out, input_grad, grad_one, grad_two)


def solution(mesh):
    placed = (
        P("channel", "samples", "spatial", None),
        P(None, "channel", None),
        P(None, "channel", None),
        P("channel", "samples", "spatial", None),
    )
    return jax.shard_map(
        body,
        mesh=mesh,
        in_specs=placed,
        out_specs=(
            P("channel", "samples", "spatial", None),
            P("channel", "samples", "spatial", None),
            P(None, "channel", None),
            P(None, "channel", None),
        ),
        check_vma=False,
    )
```

profile of v0, /device:TPU:1, one launch (start us, length us, event | category | flops | bytes accessed | tf_op | source)
XLA Modules:
  0.0 702.3 jit_solution(16248663657768471116)
XLA Ops:
  7.2 1.4 collective-permute-start
  8.7 5.1 collective-permute-start.1
  13.8 1.0 collective-permute-done.1
  14.9 1.4 pad_maximum_fusion.1
  16.3 1.3 collective-permute-start.4
  17.6 3.0 collective-permute-start.5
  20.7 1.0 collective-permute-done.5
  21.7 1.4 pad_maximum_fusion.2
  23.2 1.3 dynamic-slice
  25.1 68.5 %all-gather.3.cloned.1.call-done = bf16[512,1,3,1024]{3,0,2,1:T(8,128)(2,1)} async-done(((bf16[16,1,3,1024]{3,0,2,1:T(8,128)(2,1)}), bf16[512,1,3,1024]{3,0,2,1:T(8,128)(2,1)}) %all-gather.3.cloned.1.call-update) | async-done | bytes 3145744 | tf_op jit(solution)/shard_map/all_gather | solution.py:75
  93.7 4.6 copy.133
  98.3 5.4 copy.180
  103.7 69.7 %all-gather.5.cloned.1.call-done = bf16[512,1,3,1024]{3,0,2,1:T(8,128)(2,1)} async-done(((bf16[16,1,3,1024]{3,0,2,1:T(8,128)(2,1)}), bf16[512,1,3,1024]{3,0,2,1:T(8,128)(2,1)}) %all-gather.5.cloned.1.call-update) | async-done | bytes 3145744 | tf_op jit(solution)/shard_map/all_gather | solution.py:88
  173.4 4.7 copy.149
  178.0 3.6 copy.183
  181.7 0.6 pad.8.clone
  182.2 2.2 copy.152
  184.5 0.4 slice.20
  184.9 1.5 copy-done.2
  186.4 2.6 fusion.83
  189.0 2.2 copy.136
  191.2 0.4 slice.16
  191.9 9.4 %multiply_convert_fusion = (bf16[1,32,8,5,16]{4,2,3,1,0:T(8,128)(2,1)S(1)}, f32[1,32,8,5,16]{4,2,3,1,0:T(8,128)S(1)}) fusion(bf16[3,3,3,16,512]{4,3,2,1,0:T(8,128)(2,1)S(1)} %bitcast.92, bf16[512,3,32,1,7,2]{0,4,5,2,1,3:T(8,128)(2,1)S(1)} %slice.16, bf16[512,3,32,1,8,5]{0,4,5,2,1,3:T(8,128)(2,1)S(1)} %copy.136, pred[8,5]{0,1:T(8,128)(4,1)S(1)} %copy-done.6), kind=kOutput, calls=%fused_computation.54 | convolution fusion | flops 571072512 | bytes 5873704 | tf_op jit(solution)/shard_map/conv_general_dilated | solution.py:35
  201.3 9.9 %fusion.58 = bf16[1,32,8,5,16]{4,2,3,1,0:T(8,128)(2,1)S(1)} fusion(bf16[3,3,3,16,512]{4,3,2,1,0:T(8,128)(2,1)S(1)} %bitcast.115, bf16[512,3,32,1,7,2]{0,4,5,2,1,3:T(8,128)(2,1)S(1)} %slice.20, bf16[512,3,32,1,8,5]{0,4,5,2,1,3:T(8,128)(2,1)S(1)} %copy.152, f32[1,32,8,5,16]{4,2,3,1,0:T(8,128)S(1)} %get-tuple-element.29, pred[8,5]{0,1:T(8,128)(4,1)S(1)} %copy-done.6), kind=kOutput, calls=%fused_computation.50 | convolution fusion | flops 571154432 | bytes 5873704 | tf_op jit(solution)/shard_map/conv_general_dilated | solution.py:47
  211.8 6.5 collective-permute-start.7
  218.3 1.3 collective-permute-start.6
  219.9 0.9 copy.174
  220.8 0.4 copy.139
  221.4 3.0 collective-permute-start.3
  224.4 1.5 collective-permute-start.2
  225.9 1.4 fusion.82
  227.3 3.6 fusion.81
  230.9 0.4 copy.175
  231.3 0.4 copy.178
  231.7 2.2 copy.168
  233.9 1.8 copy.176
  235.7 1.8 copy.177
  237.4 1.1 fusion.19
  238.5 6.3 fusion.43
  244.8 2.4 slice.28
  248.2 0.4 copy.141
  248.8 1.1 copy.140
  249.9 4.5 pad_maximum_fusion
  254.3 1.3 copy.142
  255.6 14.7 %fusion.40 = bf16[3,3,3,16,512]{4,3,2,1,0:T(8,128)(2,1)} fusion(bf16[16,1,3,32,32]{0,1,4,3,2:T(2,128)(2,1)S(1)} %pad_maximum_fusion, bf16[512,1,1,32,32]{0,4,3,2,1:T(8,128)(2,1)} %slice.28), kind=kOutput, calls=%fused_computation.44 | convolution fusion | flops 434528256 | bytes 1589248 | tf_op jit(solution)/shard_map/conv_general_dilated | solution.py:58
  270.3 0.3 copy.182
  270.8 0.8 copy.145
  271.6 0.9 slice.18
  272.4 0.6 copy.158
  273.2 1.7 select_convert_fusion
  274.9 0.4 copy.159
  275.3 3.2 convolution_select_fusion
  278.7 0.6 copy.160
  279.3 3.9 copy.161
  283.2 3.3 copy.146
  286.8 2.6 copy.147
  289.3 4.7 copy.148
  294.1 394.1 %all-reduce.10 = bf16[512,1,1,1024]{3,2,1,0:T(2,128)(2,1)} all-reduce(f32[512,1,1,1024]{3,2,1,0:T(1,128)S(1)} %copy.148), channel_id=2, replica_groups=mesh['samples'=4,'channel'=32,'spatial'=2] {'channel'}, use_global_device_ids=true, to_apply=%region_0.1.clone | all-reduce | flops 524288 | bytes 3145728
  688.2 0.9 dynamic-slice_convert_fusion
  689.1 0.6 copy.172
  689.7 2.0 convert_element_type.52
  691.8 2.0 convert_element_type.55
  693.8 0.9 constant_dynamic-slice_fusion
  694.7 0.6 copy.173
  (50 shorter events, 3.3 us)
Async XLA Ops:
  7.2 184.4 %copy-start = (bf16[27,16,512]{2,1,0:T(8,128)(2,1)S(1)}, bf16[27,16,512]{2,1,0:T(8,128)(2,1)}, u32[]{:S(2)}) copy-start(bf16[27,16,512]{2,1,0:T(8,128)(2,1)} %param.5) | copy-start | bytes 1327108
  7.2 86.5 %all-gather.3.cloned.1.call-start = ((), (), s32[]{:S(2)}) async-start(), calls=%async_computation | async-start | bytes 3244032 | tf_op jit(solution)/shard_map/all_gather | solution.py:75
  7.2 6.6 collective-permute-start
  8.7 6.2 collective-permute-start.1
  16.3 157.1 %all-gather.5.cloned.1.call-start = ((), (), s32[]{:S(2)}) async-start(), calls=%async_computation.1 | async-start | bytes 3244032 | tf_op jit(solution)/shard_map/all_gather | solution.py:88
  16.3 4.3 collective-permute-start.4
  17.6 4.1 collective-permute-start.5
  23.2 666.6 %all-reduce.9.cloned.1.call-start = ((), (), s32[]{:S(2)}) async-start(), calls=%async_computation.3 | async-start | bytes 1769472 | tf_op jit(solution)/shard_map/psum | solution.py:104
  184.5 1.9 copy-start.2
  191.2 0.7 copy-start.6
  191.9 9.4 %copy-start.4 = (bf16[27,16,512]{2,1,0:T(8,128)(2,1)S(1)}, bf16[27,16,512]{2,1,0:T(8,128)(2,1)}, u32[]{:S(2)}) copy-start(bf16[27,16,512]{2,1,0:T(8,128)(2,1)} %param.6) | copy-start | bytes 1327108
  211.8 35.6 %collective-permute-start.7 = (bf16[16,1,1,1024]{3,0,2,1:T(8,128)(2,1)S(1)}, bf16[16,1,1,1024]{3,0,2,1:T(8,128)(2,1)S(1)}, u32[]{:S(2)}, u32[]{:S(2)}) collective-permute-start(bf16[16,1,1,1024]{3,0,2,1:T(8,128)(2,1)S(1)} %reshape.66), channel_id=1, source_target_pairs={{1,0},{3,2},{5,4},{7,6},{9,8},{11,10},{13,12},{15,14},{17,16},{19,... | collective-permute-start | bytes 98312 | tf_op jit(solution)/shard_map/ppermute | solution.py:17
  218.3 28.8 %collective-permute-start.6 = (bf16[16,1,1,1024]{3,0,2,1:T(8,128)(2,1)S(1)}, bf16[16,1,1,1024]{3,0,2,1:T(8,128)(2,1)S(1)}, u32[]{:S(2)}, u32[]{:S(2)}) collective-permute-start(bf16[16,1,1,1024]{3,0,2,1:T(8,128)(2,1)S(1)} %reshape.66), channel_id=1, source_target_pairs={{0,1},{2,3},{4,5},{6,7},{8,9},{10,11},{12,13},{14,15},{16,17},{18,... | collective-permute-start | bytes 98312 | tf_op jit(solution)/shard_map/ppermute | solution.py:16
  221.4 26.7 %collective-permute-start.3 = (bf16[16,1,1,1024]{3,0,2,1:T(8,128)(2,1)S(1)}, bf16[16,1,1,1024]{3,0,2,1:T(8,128)(2,1)S(1)}, u32[]{:S(2)}, u32[]{:S(2)}) collective-permute-start(bf16[16,1,1,1024]{3,0,2,1:T(8,128)(2,1)S(1)} %reshape.62), channel_id=1, source_target_pairs={{1,0},{3,2},{5,4},{7,6},{9,8},{11,10},{13,12},{15,14},{17,16},{19,... | collective-permute-start | bytes 98312 | tf_op jit(solution)/shard_map/ppermute | solution.py:17
  224.4 24.2 %collective-permute-start.2 = (bf16[16,1,1,1024]{3,0,2,1:T(8,128)(2,1)S(1)}, bf16[16,1,1,1024]{3,0,2,1:T(8,128)(2,1)S(1)}, u32[]{:S(2)}, u32[]{:S(2)}) collective-permute-start(bf16[16,1,1,1024]{3,0,2,1:T(8,128)(2,1)S(1)} %reshape.62), channel_id=1, source_target_pairs={{0,1},{2,3},{4,5},{6,7},{8,9},{10,11},{12,13},{14,15},{16,17},{18,... | collective-permute-start | bytes 98312 | tf_op jit(solution)/shard_map/ppermute | solution.py:16
  227.3 4.4 copy-start.1
  270.3 2.8 copy-start.7
  273.1 2.1 copy-start.3
  273.1 2.1 copy-start.5
  278.5 415.3 %all-reduce.7.cloned.1.call-start = ((), (), s32[]{:S(2)}) async-start(), calls=%async_computation.2 | async-start | bytes 4194304
Sparse Core Ops, SparseCore 0:
  16.4 77.2 all-gather.2
  96.8 76.4 all-gather.4
  278.7 62.5 all-reduce.8
  345.1 272.6 all-reduce.6
where the time goes:
time: 716 us; the launch traced here: 702 us
  blocking collectives  394 us (55%)
  waiting for transfers between devices  140 us (20%)
  local copies, waits for them, and re-layouts  71.5 us (10%)
  matrix products  45.2 us (6%)
  starting transfers between devices  23.3 us (3%)
  between operations  15.4 us (2%)
  other arithmetic  12.5 us (2%)
    unnamed x1, blocking collectives  394 us
    all_gather x1, waiting for transfers between devices, body(): whole_c = to_grid(lax.all_gather(rims_c, 'channel', axis=0, tiled=True))  69.7 us
    all_gather x1, waiting for transfers between devices, body(): whole_x = lax.all_gather(rims_x, 'channel', axis=0, tiled=True)  68.5 us
    conv_general_dilated x2, matrix products, weight_grad(): lax.conv_general_dilated(padded, upstream, (1, 1, 1), [(0, 0), (0, 0), (0...  21 us
    unnamed x28, local copies, waits for them, and re-layouts  19.7 us
    ppermute x4, starting transfers between devices, with_halo(): after = lax.ppermute(first, axis, down)  17.7 us
  transfers between devices with their start and end apart: 12, of which 4 were waited for; matrix products, arithmetic and copies ran while one was open for 8% of the time, Pallas kernels for 0%

commit v1 on v0

v1 whole, which is shorter than its diff:
```python
import jax
import jax.numpy as jnp
from jax import lax
from jax.experimental import pallas as pl
from jax.experimental.pallas import tpu as pltpu
from jax.sharding import PartitionSpec as P

SIDE = 32
PLANE = SIDE * SIDE
TAPS9 = [(b, c) for b in range(3) for c in range(3)]
F32 = jnp.float32
BF16 = jnp.bfloat16
PARAMS = pltpu.CompilerParams(vmem_limit_bytes=48 * 1024 * 1024)


def masks(rows):
    cell = lax.broadcasted_iota(jnp.int32, (rows, PLANE), 1)
    column = cell & (SIDE - 1)
    row_ok = {-1: cell >= SIDE, 1: cell < PLANE - SIDE}
    col_ok = {-1: column > 0, 1: column < SIDE - 1}
    return row_ok, col_ok


def moved(values, step, ok):
    return jnp.where(ok, pltpu.roll(values, (-step) % PLANE, 1), 0.0)


def dot(lhs, rhs, dims):
    return lax.dot_general(lhs, rhs, (dims, ((), ())), preferred_element_type=F32)


def tap_sum(stack_ref, start, width, sign, ok):
    row_ok, col_ok = ok
    total = None
    for c in range(3):
        part = None
        for b in range(3):
            at = start + (3 * b + c) * width
            term = stack_ref[at : at + width, :]
            drow = sign * (b - 1)
            if drow:
                term = moved(term, SIDE * drow, row_ok[drow])
            part = term if part is None else part + term
        dcol = sign * (c - 1)
        if dcol:
            part = moved(part, dcol, col_ok[dcol])
        total = part if total is None else total + part
    return total


def first_kernel(core_ref, whole_ref, one_ref, two_ref, out_ref, near, far):
    blocks, _, width, _ = whole_ref.shape
    third = 9 * width
    ok = masks(width)

    def run(weights, sign):
        source = [whole_ref[:, d].reshape(blocks * width, PLANE) for d in range(2)]
        low, high = weights[0 : 2 * third, :], weights[third : 3 * third, :]
        left, right = (low, high) if sign > 0 else (high, low)
        near[...] = dot(left, source[0], ((1,), (0,)))
        far[...] = dot(right, source[1], ((1,), (0,)))
        near[...] = near[...] + far[...]
        for d in range(2):
            start = third * ((1 - d) if sign > 0 else d)
            out_ref[d] = tap_sum(near, start, width, sign, ok)

    @pl.when(core_ref[0] == 0)
    def _():
        run(one_ref, 1)

    @pl.when(core_ref[0] == 1)
    def _():
        run(two_ref, -1)


def spread(values, sign, col_ref, start, ok):
    row_ok, col_ok = ok
    width = values.shape[0]
    for c in range(3):
        dcol = sign * (c - 1)
        part = moved(values, dcol, col_ok[dcol]) if dcol else values
        for b in range(3):
            drow = sign * (b - 1)
            term = moved(part, SIDE * drow, row_ok[drow]) if drow else part
            at = start + (3 * b + c) * width
            col_ref[at : at + width, :] = term.astype(BF16)


def second_kernel(core_ref, own_ref, other_ref, whole_ref, one_ref, two_ref, out_ref, grad_ref, hid_col, act_col):
    blocks, _, width, _ = whole_ref.shape
    third = 9 * width
    channels = blocks * width
    ok = masks(width)
    first = core_ref[0] == 0
    for d in range(2):
        own, other = own_ref[d], other_ref[d]
        pre = jnp.where(first, own, other)
        upstream = jnp.where(first, other, own)
        gate = 1.0 / (1.0 + jnp.exp(-pre))
        hidden = (pre * gate).astype(BF16).astype(F32)
        act = (upstream * gate * (1.0 + pre * (1.0 - gate))).astype(BF16).astype(F32)
        spread(hidden, 1, hid_col, d * third, ok)
        spread(act, -1, act_col, (1 - d) * third, ok)

    def run(weights, out_col, grad_col, sign):
        for d in range(2):
            at = third * ((1 - d) if sign > 0 else d)
            part = dot(weights[at : at + 2 * third, :], out_col[...], ((0,), (0,)))
            out_ref[:, d] = part.astype(BF16).reshape(blocks, width, PLANE)
        source = [whole_ref[:, d].reshape(channels, PLANE) for d in range(2)]
        zero = dot(grad_col[...], source[0], ((1,), (1,)))
        last = dot(grad_col[...], source[1], ((1,), (1,)))
        low, high = (zero, last) if sign > 0 else (last, zero)
        grad_ref[0:third, :] = low[0:third].astype(BF16)
        grad_ref[third : 2 * third, :] = (low[third:] + high[0:third]).astype(BF16)
        grad_ref[2 * third :, :] = high[third:].astype(BF16)

    @pl.when(first)
    def _():
        run(two_ref, hid_col, act_col, 1)

    @pl.when(core_ref[0] == 1)
    def _():
        run(one_ref, act_col, hid_col, -1)


def vmem(count):
    return [pl.BlockSpec(memory_space=pltpu.VMEM)] * count


def smem():
    return [pl.BlockSpec(memory_space=pltpu.SMEM)]


def first_call(core, whole, one, two):
    width = whole.shape[2]
    return pl.pallas_call(
        first_kernel,
        out_shape=jax.ShapeDtypeStruct((2, width, PLANE), F32),
        in_specs=smem() + vmem(3),
        out_specs=vmem(1)[0],
        scratch_shapes=[pltpu.VMEM((18 * width, PLANE), F32)] * 2,
        compiler_params=PARAMS,
        name="conv_in",
    )(core, whole, one, two)


def second_call(core, own, other, whole, one, two):
    blocks, _, width, _ = whole.shape
    return pl.pallas_call(
        second_kernel,
        out_shape=(
            jax.ShapeDtypeStruct(whole.shape, BF16),
            jax.ShapeDtypeStruct((27 * width, blocks * width), BF16),
        ),
        in_specs=smem() + vmem(5),
        out_specs=tuple(vmem(2)),
        scratch_shapes=[pltpu.VMEM((18 * width, PLANE), BF16)] * 2,
        compiler_params=PARAMS,
        name="conv_out",
    )(core, own, other, whole, one, two)


def swap(values):
    return lax.ppermute(values, "spatial", [(0, 1), (1, 0)])


def around(values, axis, step):
    size = lax.axis_size(axis)
    return lax.ppermute(values, axis, [(i, (i + step) % size) for i in range(size)])


def body(features, conv_one, conv_two, cotangent):
    width, channels = conv_one.shape[1], conv_one.shape[2]
    count = lax.axis_size("channel")
    core = lax.axis_index("spatial")
    first = core == 0
    flag = core.astype(jnp.int32).reshape(1)
    one = conv_one.reshape(27 * width, channels)
    two = conv_two.reshape(27 * width, channels)
    features = features.reshape(width, PLANE)
    cotangent = cotangent.reshape(width, PLANE)

    came = swap(jnp.where(first, cotangent, features))
    kept = jnp.where(first, features, cotangent)
    block = jnp.where(first, jnp.stack([kept, came]), jnp.stack([came, kept]))
    whole = lax.all_to_all(
        jnp.broadcast_to(block, (count,) + block.shape), "channel", 0, 0, tiled=True
    )
    own = first_call(flag, whole, one, two)
    other = swap(own)
    parts, grad = second_call(flag, own, other, whole, one, two)

    grads = [grad] + [around(grad, "samples", k) for k in (1, 2, 3)]
    summed = sum(g.astype(F32) for g in grads).astype(BF16)
    summed_other = swap(summed)

    parts = lax.all_to_all(parts, "channel", 0, 0, tiled=True)
    result = jnp.sum(parts.astype(F32), axis=0).astype(BF16)
    mine = jnp.where(first, result[0], result[1])
    theirs = swap(jnp.where(first, result[1], result[0]))
    shape = (width, 1, 1, PLANE)
    mixed_out = jnp.where(first, mine, theirs).reshape(shape)
    input_grad = jnp.where(first, theirs, mine).reshape(shape)
    grad_one = jnp.where(first, summed, summed_other).astype(F32).reshape(27, width, channels)
    grad_two = jnp.where(first, summed_other, summed).astype(F32).reshape(27, width, channels)
    return mixed_out, input_grad, grad_one, grad_two


def solution(mesh):
    acts = P("channel", "samples", "spatial", None)
    kernels = P(None, "channel", None)
    return jax.shard_map(
        body,
        mesh=mesh,
        in_specs=(acts, kernels, kernels, acts),
        out_specs=(acts, acts, kernels, kernels),
        check_vma=False,
    )
```

time: 716 us -> 133 us (0.19); the launches traced: 702 us -> 132 us
  blocking collectives: 394 us -> 58.1 us
  waiting for transfers between devices: 140 us -> 45.6 us
  local copies, waits for them, and re-layouts: 71.5 us -> 0.26 us
  matrix products: 45.2 us -> 0 us
  between operations: 15.4 us -> 0.71 us
  other arithmetic: 12.5 us -> 4.14 us
    unnamed x1 -> x0, blocking collectives: 394 us -> none
    all_gather x2 -> x0, waiting for transfers between devices: 138 us -> none  [the longest x1 69.7 us: body(): whole_c = to_grid(lax.all_gather(rims_c, 'channel', axis=0, tiled=True))]
    all_to_all x0 -> x1, blocking collectives: none -> 58.1 us  [body(): lax.all_to_all(jnp.broadcast_to(block, (count,) + block.shape), 'channel'...]
    conv_general_dilated x6 -> x0, matrix products: 45.2 us -> none  [the longest x2 21 us: weight_grad(): lax.conv_general_dilated(padded, upstream, (1, 1, 1), [(0, 0), (0, 0), (0...]
    ppermute x8 -> x7, waiting for transfers between devices: 2.1 us -> 23.9 us  [the longest x3 22 us: around(): lax.ppermute(values, axis, [(i, (i + step) % size) for i in range(size)])]
    all_to_all x0 -> x1, waiting for transfers between devices: none -> 21.7 us  [body(): parts = lax.all_to_all(parts, 'channel', 0, 0, tiled=True)]
    unnamed x28 -> x4, local copies, waits for them, and re-layouts: 19.7 us -> 0.01 us
    reshape x8 -> x0, local copies, waits for them, and re-layouts: 15.4 us -> none  [the longest x5 10.3 us: to_grid(): values.reshape(values.shape[0], values.shape[1], values.shape[2], SIDE, S...]
  transfers between devices with their start and end apart: 12 -> 8, of which waited for: 4 -> 6; matrix products, arithmetic and copies ran while one was open for 8% -> 2% of each run, Pallas kernels for 0% -> 0%
where the time goes in v1:
time: 133 us; the launch traced here: 132 us
  blocking collectives  58.1 us (44%)
  waiting for transfers between devices  45.6 us (34%)
  starting transfers between devices  18.6 us (14%)
  Pallas kernels  4.96 us (4%)
  other arithmetic  4.14 us (3%)
    all_to_all x1, blocking collectives, body(): lax.all_to_all(jnp.broadcast_to(block, (count,) + block.shape), 'channel'...  58.1 us
    ppermute x3, waiting for transfers between devices, around(): lax.ppermute(values, axis, [(i, (i + step) % size) for i in range(size)])  22 us
    all_to_all x1, waiting for transfers between devices, body(): parts = lax.all_to_all(parts, 'channel', 0, 0, tiled=True)  21.7 us
    ppermute x4, starting transfers between devices, swap(): return lax.ppermute(values, 'spatial', [(0, 1), (1, 0)])  9.43 us
    all_to_all x1, starting transfers between devices, body(): parts = lax.all_to_all(parts, 'channel', 0, 0, tiled=True)  5.31 us
    pallas_call x1, Pallas kernels, second_call(): pl.pallas_call(second_kernel, out_shape=(jax.ShapeDtypeStruct(whole.shape...  3.97 us
    ppermute x3, starting transfers between devices, around(): lax.ppermute(values, axis, [(i, (i + step) % size) for i in range(size)])  3.85 us
  transfers between devices with their start and end apart: 8, of which 6 were waited for; matrix products, arithmetic and copies ran while one was open for 2% of the time, Pallas kernels for 0%

profile of v1, /device:TPU:1, one launch (start us, length us, event | category | flops | bytes accessed | tf_op | source)
XLA Modules:
  0.0 132.3 jit_solution(8978453691076209874)
XLA Ops:
  0.6 0.8 select_bitcast_fusion.2
  1.4 3.3 %collective-permute-start = (bf16[16,1024]{1,0:T(8,128)(2,1)S(1)}, bf16[16,1024]{1,0:T(8,128)(2,1)S(1)}, u32[]{:S(2)}, u32[]{:S(2)}) collective-permute-start(bf16[16,1024]{1,0:T(8,128)(2,1)S(1)} %get-tuple-element.13), channel_id=1, source_target_pairs={{0,1},{1,0},{2,3},{3,2},{4,5},{5,4},{6,7},{7,6},{8,9},{9,8},{10,11... | collective-permute-start | bytes 98312 | tf_op jit(solution)/shard_map/ppermute | solution.py:165
  4.7 0.9 collective-permute-done
  5.6 0.3 broadcast_in_dim.3
  5.9 0.0 copy-start
  5.9 0.0 copy-start.1
  5.9 58.1 %all_to_all.10.whole_ref = bf16[32,2,16,1024]{3,2,1,0:T(8,128)(2,1)S(1)} all-to-all(bf16[32,2,16,1024]{3,2,1,0:T(8,128)(2,1)S(1)} %broadcast_in_dim.3), channel_id=1, replica_groups=mesh['samples'=4,'channel'=32,'spatial'=2] {'channel'}, dimensions={0} | all-to-all | bytes 4194304 | tf_op jit(solution)/shard_map/all_to_all | solution.py:187
  64.0 0.0 copy-done
  64.0 0.0 copy-done.1
  64.0 1.0 conv_in.1.own_ref
  65.0 2.7 %collective-permute-start.1 = (f32[2,16,1024]{2,1,0:T(8,128)S(1)}, f32[2,16,1024]{2,1,0:T(8,128)S(1)}, u32[]{:S(2)}, u32[]{:S(2)}) collective-permute-start(f32[2,16,1024]{2,1,0:T(8,128)S(1)} %conv_in.1.own_ref), channel_id=1, source_target_pairs={{0,1},{1,0},{2,3},{3,2},{4,5},{5,4},{6,7},{7,6},{8,9},{9,8},{10,11... | collective-permute-start | bytes 393224 | tf_op jit(solution)/shard_map/ppermute | solution.py:165
  67.7 1.0 collective-permute-done.1.other_ref
  68.7 4.0 %conv_out.1 = (bf16[32,2,16,1024]{3,2,1,0:T(8,128)(2,1)}, bf16[432,512]{1,0:T(8,128)(2,1)S(1)}) custom-call(s32[1]{0:T(128)} %bitcast.core_ref, f32[2,16,1024]{2,1,0:T(8,128)S(1)} %conv_in.1.own_ref, f32[2,16,1024]{2,1,0:T(8,128)S(1)} %collective-permute-done.1.other_ref, bf16[32,2,16,1024]{3,2,1,0:T(8,128)(2,1)S(1)} %all_to_all.10.whole_ref, ...), custom_call_target="tpu_custom_call" | custom-call | tf_op jit(solution)/shard_map/conv_out/pallas_call | solution.py:150
  72.7 5.3 %all-to-all-start.1 = ((bf16[32,2,16,1024]{3,2,1,0:T(8,128)(2,1)}), bf16[32,2,16,1024]{3,2,1,0:T(8,128)(2,1)S(1)}, u32[]{:S(2)}, u32[]{:S(2)}) async-start(bf16[32,2,16,1024]{3,2,1,0:T(8,128)(2,1)} %get-tuple-element.6), calls=%async_computation.1 | async-start | bytes 4194304 | tf_op jit(solution)/shard_map/all_to_all | solution.py:198
  78.0 2.8 %collective-permute-start.5 = (bf16[432,512]{1,0:T(8,128)(2,1)S(1)}, bf16[432,512]{1,0:T(8,128)(2,1)S(1)}, u32[]{:S(2)}, u32[]{:S(2)}) collective-permute-start(bf16[432,512]{1,0:T(8,128)(2,1)S(1)} %get-tuple-element.7), channel_id=1, source_target_pairs={{0,192},{64,0},{128,64},{192,128},{1,193},{65,1},{129,65},{193,129... | collective-permute-start | bytes 1327112 | tf_op jit(solution)/shard_map/ppermute | solution.py:170
  80.8 0.3 collective-permute-start.4
  81.1 0.7 collective-permute-start.3
  81.8 8.8 %collective-permute-done.5 = bf16[432,512]{1,0:T(8,128)(2,1)S(1)} collective-permute-done((bf16[432,512]{1,0:T(8,128)(2,1)S(1)}, bf16[432,512]{1,0:T(8,128)(2,1)S(1)}, u32[]{:S(2)}, u32[]{:S(2)}) %collective-permute-start.5) | collective-permute-done | bytes 442400 | tf_op jit(solution)/shard_map/ppermute | solution.py:170
  90.6 2.4 %collective-permute-done.4 = bf16[432,512]{1,0:T(8,128)(2,1)S(1)} collective-permute-done((bf16[432,512]{1,0:T(8,128)(2,1)S(1)}, bf16[432,512]{1,0:T(8,128)(2,1)S(1)}, u32[]{:S(2)}, u32[]{:S(2)}) %collective-permute-start.4) | collective-permute-done | bytes 442400 | tf_op jit(solution)/shard_map/ppermute | solution.py:170
  93.1 10.8 %collective-permute-done.3 = bf16[432,512]{1,0:T(8,128)(2,1)S(1)} collective-permute-done((bf16[432,512]{1,0:T(8,128)(2,1)S(1)}, bf16[432,512]{1,0:T(8,128)(2,1)S(1)}, u32[]{:S(2)}, u32[]{:S(2)}) %collective-permute-start.3) | collective-permute-done | bytes 442400 | tf_op jit(solution)/shard_map/ppermute | solution.py:170
  103.9 0.2 add_convert_fusion
  104.1 0.6 collective-permute-start.6
  104.7 21.7 %all-to-all-done.1 = bf16[32,2,16,1024]{3,2,1,0:T(8,128)(2,1)S(1)} async-done(((bf16[32,2,16,1024]{3,2,1,0:T(8,128)(2,1)}), bf16[32,2,16,1024]{3,2,1,0:T(8,128)(2,1)S(1)}, u32[]{:S(2)}, u32[]{:S(2)}) %all-to-all-start.1) | async-done | bytes 2097184 | tf_op jit(solution)/shard_map/all_to_all | solution.py:198
  126.4 0.4 reduce_sum.12
  126.8 2.8 %collective-permute-start.2 = (bf16[16,1024]{1,0:T(8,128)(2,1)S(1)}, bf16[16,1024]{1,0:T(8,128)(2,1)S(1)}, u32[]{:S(2)}, u32[]{:S(2)}) collective-permute-start(bf16[16,1024]{1,0:T(8,128)(2,1)S(1)} %select_bitcast_fusion), channel_id=1, source_target_pairs={{0,1},{1,0},{2,3},{3,2},{4,5},{5,4},{6,7},{7,6},{8,9},{9,8},{10,11... | collective-permute-start | bytes 98312 | tf_op jit(solution)/shard_map/ppermute | solution.py:165
  129.6 0.0 collective-permute-done.6
  129.6 0.1 broadcast_select_fusion
  129.6 1.0 convert.3
  130.7 1.0 convert.4
  131.7 0.0 collective-permute-done.2
  131.7 0.6 fusion.1
  (2 shorter events, 0.0 us)
Async XLA Ops:
  1.4 4.2 %collective-permute-start = (bf16[16,1024]{1,0:T(8,128)(2,1)S(1)}, bf16[16,1024]{1,0:T(8,128)(2,1)S(1)}, u32[]{:S(2)}, u32[]{:S(2)}) collective-permute-start(bf16[16,1024]{1,0:T(8,128)(2,1)S(1)} %get-tuple-element.13), channel_id=1, source_target_pairs={{0,1},{1,0},{2,3},{3,2},{4,5},{5,4},{6,7},{7,6},{8,9},{9,8},{10,11... | collective-permute-start | bytes 98312 | tf_op jit(solution)/shard_map/ppermute | solution.py:165
  5.9 58.1 %copy-start = (bf16[27,16,512]{2,1,0:T(8,128)(2,1)S(1)}, bf16[27,16,512]{2,1,0:T(8,128)(2,1)}, u32[]{:S(2)}) copy-start(bf16[27,16,512]{2,1,0:T(8,128)(2,1)} %param.5) | copy-start | bytes 1327108
  5.9 58.1 %copy-start.1 = (bf16[27,16,512]{2,1,0:T(8,128)(2,1)S(1)}, bf16[27,16,512]{2,1,0:T(8,128)(2,1)}, u32[]{:S(2)}) copy-start(bf16[27,16,512]{2,1,0:T(8,128)(2,1)} %param.6) | copy-start | bytes 1327108
  65.0 3.7 %collective-permute-start.1 = (f32[2,16,1024]{2,1,0:T(8,128)S(1)}, f32[2,16,1024]{2,1,0:T(8,128)S(1)}, u32[]{:S(2)}, u32[]{:S(2)}) collective-permute-start(f32[2,16,1024]{2,1,0:T(8,128)S(1)} %conv_in.1.own_ref), channel_id=1, source_target_pairs={{0,1},{1,0},{2,3},{3,2},{4,5},{5,4},{6,7},{7,6},{8,9},{9,8},{10,11... | collective-permute-start | bytes 393224 | tf_op jit(solution)/shard_map/ppermute | solution.py:165
  72.7 53.7 %all-to-all-start.1 = ((bf16[32,2,16,1024]{3,2,1,0:T(8,128)(2,1)}), bf16[32,2,16,1024]{3,2,1,0:T(8,128)(2,1)S(1)}, u32[]{:S(2)}, u32[]{:S(2)}) async-start(bf16[32,2,16,1024]{3,2,1,0:T(8,128)(2,1)} %get-tuple-element.6), calls=%async_computation.1 | async-start | bytes 4194304 | tf_op jit(solution)/shard_map/all_to_all | solution.py:198
  78.0 12.7 %collective-permute-start.5 = (bf16[432,512]{1,0:T(8,128)(2,1)S(1)}, bf16[432,512]{1,0:T(8,128)(2,1)S(1)}, u32[]{:S(2)}, u32[]{:S(2)}) collective-permute-start(bf16[432,512]{1,0:T(8,128)(2,1)S(1)} %get-tuple-element.7), channel_id=1, source_target_pairs={{0,192},{64,0},{128,64},{192,128},{1,193},{65,1},{129,65},{193,129... | collective-permute-start | bytes 1327112 | tf_op jit(solution)/shard_map/ppermute | solution.py:170
  80.8 12.3 %collective-permute-start.4 = (bf16[432,512]{1,0:T(8,128)(2,1)S(1)}, bf16[432,512]{1,0:T(8,128)(2,1)S(1)}, u32[]{:S(2)}, u32[]{:S(2)}) collective-permute-start(bf16[432,512]{1,0:T(8,128)(2,1)S(1)} %get-tuple-element.7), channel_id=1, source_target_pairs={{0,128},{64,192},{128,0},{192,64},{1,129},{65,193},{129,1},{193,65... | collective-permute-start | bytes 1327112 | tf_op jit(solution)/shard_map/ppermute | solution.py:170
  81.1 22.7 %collective-permute-start.3 = (bf16[432,512]{1,0:T(8,128)(2,1)S(1)}, bf16[432,512]{1,0:T(8,128)(2,1)S(1)}, u32[]{:S(2)}, u32[]{:S(2)}) collective-permute-start(bf16[432,512]{1,0:T(8,128)(2,1)S(1)} %get-tuple-element.7), channel_id=1, source_target_pairs={{0,64},{64,128},{128,192},{192,0},{1,65},{65,129},{129,193},{193,1... | collective-permute-start | bytes 1327112 | tf_op jit(solution)/shard_map/ppermute | solution.py:170
  104.1 25.5 %collective-permute-start.6 = (bf16[432,512]{1,0:T(8,128)(2,1)S(1)}, bf16[432,512]{1,0:T(8,128)(2,1)S(1)}, u32[]{:S(2)}, u32[]{:S(2)}) collective-permute-start(bf16[432,512]{1,0:T(8,128)(2,1)S(1)} %add_convert_fusion), channel_id=1, source_target_pairs={{0,1},{1,0},{2,3},{3,2},{4,5},{5,4},{6,7},{7,6},{8,9},{9,8},{10,11... | collective-permute-start | bytes 1327112 | tf_op jit(solution)/shard_map/ppermute | solution.py:165
  126.8 4.9 %collective-permute-start.2 = (bf16[16,1024]{1,0:T(8,128)(2,1)S(1)}, bf16[16,1024]{1,0:T(8,128)(2,1)S(1)}, u32[]{:S(2)}, u32[]{:S(2)}) collective-permute-start(bf16[16,1024]{1,0:T(8,128)(2,1)S(1)} %select_bitcast_fusion), channel_id=1, source_target_pairs={{0,1},{1,0},{2,3},{3,2},{4,5},{5,4},{6,7},{7,6},{8,9},{9,8},{10,11... | collective-permute-start | bytes 98312 | tf_op jit(solution)/shard_map/ppermute | solution.py:165

commit v2 on v1

v2 whole, which is shorter than its diff:
```python
import jax
import jax.numpy as jnp
from jax import lax
from jax.experimental import pallas as pl
from jax.experimental.pallas import tpu as pltpu
from jax.sharding import Mesh, PartitionSpec as P

SIDE = 32
PLANE = SIDE * SIDE
F32 = jnp.float32
BF16 = jnp.bfloat16
PARAMS = pltpu.CompilerParams(vmem_limit_bytes=40 * 1024 * 1024)
NX = 4
NZ = 8


def masks(rows):
    cell = lax.broadcasted_iota(jnp.int32, (rows, PLANE), 1)
    column = cell & (SIDE - 1)
    row_ok = {-1: cell >= SIDE, 1: cell < PLANE - SIDE}
    col_ok = {-1: column > 0, 1: column < SIDE - 1}
    return row_ok, col_ok


def moved(values, step, ok):
    return jnp.where(ok, pltpu.roll(values, (-step) % PLANE, 1), 0.0)


def dot(lhs, rhs, dims):
    return lax.dot_general(lhs, rhs, (dims, ((), ())), preferred_element_type=F32)


def tap_sum(stack_ref, start, width, sign, ok):
    row_ok, col_ok = ok
    total = None
    for c in range(3):
        part = None
        for b in range(3):
            at = start + (3 * b + c) * width
            term = stack_ref[at : at + width, :]
            drow = sign * (b - 1)
            if drow:
                term = moved(term, SIDE * drow, row_ok[drow])
            part = term if part is None else part + term
        dcol = sign * (c - 1)
        if dcol:
            part = moved(part, dcol, col_ok[dcol])
        total = part if total is None else total + part
    return total


def spread(values, sign, col_ref, start, ok):
    row_ok, col_ok = ok
    width = values.shape[0]
    for c in range(3):
        dcol = sign * (c - 1)
        part = moved(values, dcol, col_ok[dcol]) if dcol else values
        for b in range(3):
            drow = sign * (b - 1)
            term = moved(part, SIDE * drow, row_ok[drow]) if drow else part
            at = start + (3 * b + c) * width
            col_ref[at : at + width, :] = term.astype(BF16)


def regroup_kernel(at_ref, one_ref, two_ref, out_ref):
    channels = one_ref.shape[1]
    width = channels // (NX * NZ)
    group = NZ * width
    old = lax.broadcasted_iota(jnp.int32, (channels, channels), 0)
    new = lax.broadcasted_iota(jnp.int32, (channels, channels), 1)
    home = ((new % group) // width) * (NX * width) + (new // group) * width + new % width
    order = (old == home).astype(F32).astype(BF16)

    def run(ref):
        for x in range(NX):
            out_ref[x] = dot(ref[...], order[:, x * group : (x + 1) * group], ((1,), (0,))).astype(BF16)

    @pl.when(at_ref[0] == 0)
    def _():
        run(two_ref)

    @pl.when(at_ref[0] == 1)
    def _():
        run(one_ref)


def first_kernel(at_ref, mine_ref, left_ref, right_ref, far0_ref, far1_ref, one_ref, two_ref, out_ref, whole_ref, near, far):
    width = mine_ref.shape[2]
    third = 9 * width
    ok = masks(width)
    x = at_ref[1]
    half = NZ // 2
    pieces = ((mine_ref, 0, 0, NZ), (left_ref, NX - 1, 0, NZ), (right_ref, 1, 0, NZ), (far0_ref, 2, 0, half), (far1_ref, 2, half, half))
    for ref, step, z0, count in pieces:
        source = lax.rem(x + step, NX)
        for z in range(count):
            rows = pl.ds(pl.multiple_of(((z0 + z) * NX + source) * width, 16), width)
            for d in range(2):
                whole_ref[d, rows, :] = ref[z, d]

    def run(weights, sign):
        low, high = weights[0 : 2 * third, :], weights[third : 3 * third, :]
        first, second = (low, high) if sign > 0 else (high, low)
        near[...] = dot(first, whole_ref[0], ((1,), (0,)))
        far[...] = dot(second, whole_ref[1], ((1,), (0,)))
        near[...] = near[...] + far[...]
        for d in range(2):
            start = third * ((1 - d) if sign > 0 else d)
            out_ref[d] = tap_sum(near, start, width, sign, ok)

    @pl.when(at_ref[0] == 0)
    def _():
        run(one_ref, 1)

    @pl.when(at_ref[0] == 1)
    def _():
        run(two_ref, -1)


def act_kernel(at_ref, own_ref, other_ref, send_ref, keep_ref):
    first = at_ref[0] == 0
    for d in range(2):
        own, other = own_ref[d], other_ref[d]
        pre = jnp.where(first, own, other)
        upstream = jnp.where(first, other, own)
        gate = 1.0 / (1.0 + jnp.exp(-pre))
        hidden = pre * gate
        act = upstream * gate * (1.0 + pre * (1.0 - gate))
        send_ref[d] = jnp.where(first, hidden, act).astype(BF16)
        keep_ref[d] = jnp.where(first, act, hidden).astype(BF16)


def grad_kernel(at_ref, keep_ref, whole_ref, grad_ref, col):
    width = keep_ref.shape[1]
    third = 9 * width
    ok = masks(width)

    def run(sign):
        for d in range(2):
            at = third * (d if sign > 0 else 1 - d)
            spread(keep_ref[d].astype(F32), sign, col, at, ok)
        zero = dot(col[...], whole_ref[0], ((1,), (1,)))
        last = dot(col[...], whole_ref[1], ((1,), (1,)))
        low, high = (last, zero) if sign > 0 else (zero, last)
        grad_ref[0:third, :] = low[0:third].astype(BF16)
        grad_ref[third : 2 * third, :] = (low[third:] + high[0:third]).astype(BF16)
        grad_ref[2 * third :, :] = high[third:].astype(BF16)

    @pl.when(at_ref[0] == 0)
    def _():
        run(-1)

    @pl.when(at_ref[0] == 1)
    def _():
        run(1)


def second_kernel(at_ref, *refs):
    acts, kernels, (out_ref, col, tall) = refs[:NX], refs[NX : 2 * NX], refs[2 * NX :]
    width = acts[0].shape[1]
    third = 9 * width
    ok = masks(width)

    def run(sign):
        for k in range(NX):
            for d in range(2):
                at = 2 * third * k + third * (d if sign > 0 else 1 - d)
                spread(acts[k][d].astype(F32), sign, col, at, ok)
        for d in range(2):
            at = third * ((1 - d) if sign > 0 else d)
            for k in range(NX):
                tall[2 * third * k : 2 * third * (k + 1), :] = kernels[k][at : at + 2 * third, :]
            part = dot(tall[...], col[...], ((0,), (0,)))
            out_ref[:, d] = part.astype(BF16).reshape(NZ, width, PLANE)

    @pl.when(at_ref[0] == 0)
    def _():
        run(1)

    @pl.when(at_ref[0] == 1)
    def _():
        run(-1)


def call(kernel, outs, scratch, name, cost, *args):
    vmem = pl.BlockSpec(memory_space=pltpu.VMEM)
    return pl.pallas_call(
        kernel,
        out_shape=tuple(jax.ShapeDtypeStruct(s, t) for s, t in outs),
        in_specs=[pl.BlockSpec(memory_space=pltpu.SMEM)] + [vmem] * (len(args) - 1),
        out_specs=tuple([vmem] * len(outs)),
        scratch_shapes=[pltpu.VMEM(s, t) for s, t in scratch],
        compiler_params=PARAMS,
        cost_estimate=pl.CostEstimate(flops=cost, bytes_accessed=0, transcendentals=0),
        name=name,
    )(*args)


def swap(values):
    return lax.ppermute(values, "spatial", [(0, 1), (1, 0)])


def around(values, axis, step):
    size = lax.axis_size(axis)
    return lax.ppermute(values, axis, [((i + step) % size, i) for i in range(size)])


def body(features, conv_one, conv_two, cotangent):
    width, channels = conv_one.shape[1], conv_one.shape[2]
    core = lax.axis_index("spatial")
    x = lax.axis_index("x")
    first = core == 0
    at = jnp.stack([core, x]).astype(jnp.int32)
    one = conv_one.reshape(27 * width, channels)
    two = conv_two.reshape(27 * width, channels)
    features = features.reshape(width, PLANE)
    cotangent = cotangent.reshape(width, PLANE)
    taps = 27 * width
    group = NZ * width

    came = swap(jnp.where(first, cotangent, features))
    kept = jnp.where(first, features, cotangent)
    block = jnp.where(first, jnp.stack([kept, came]), jnp.stack([came, kept]))
    mine = lax.all_to_all(jnp.broadcast_to(block, (NZ,) + block.shape), "z", 0, 0, tiled=True)

    (groups,) = call(regroup_kernel, [((NX, taps, group), BF16)], [], "regroup", 2 * taps * channels * channels, at, one, two)

    def group_for(step):
        return lax.dynamic_index_in_dim(groups, lax.rem(x + step, NX), 0, keepdims=False)

    kernels = [group_for(0)] + [around(group_for(NX - k), "x", k) for k in range(1, NX)]

    left = around(mine, "x", -1)
    right = around(mine, "x", 1)
    far0 = around(left[: NZ // 2], "x", -1)
    far1 = around(right[NZ // 2 :], "x", 1)

    plane = (2, width, PLANE)
    own, whole = call(
        first_kernel,
        [(plane, F32), ((2, channels, PLANE), BF16)],
        [((18 * width, PLANE), F32)] * 2,
        "conv_in",
        4 * 18 * width * channels * PLANE,
        at, mine, left, right, far0, far1, one, two,
    )
    other = swap(own)
    send, keep = call(act_kernel, [(plane, BF16)] * 2, [], "act", 0, at, own, other)
    acts = [send] + [around(send, "x", k) for k in range(1, NX)]
    (grad,) = call(
        grad_kernel,
        [((taps, channels), BF16)],
        [((18 * width, PLANE), BF16)],
        "grad",
        4 * 18 * width * channels * PLANE,
        at, keep, whole,
    )
    (parts,) = call(
        second_kernel,
        [((NZ,) + plane, BF16)],
        [((NX * 18 * width, PLANE), BF16), ((NX * 18 * width, group), BF16)],
        "conv_out",
        4 * 18 * width * channels * PLANE,
        at, *acts, *kernels,
    )
    parts = lax.all_to_all(parts, "z", 0, 0, tiled=True)

    grads = [grad] + [around(grad, "samples", k) for k in (1, 2, 3)]
    summed = sum(g.astype(F32) for g in grads).astype(BF16)
    summed_other = swap(summed)

    result = jnp.sum(parts.astype(F32), axis=0).astype(BF16)
    ours = jnp.where(first, result[0], result[1])
    theirs = swap(jnp.where(first, result[1], result[0]))
    shape = (width, 1, 1, PLANE)
    mixed_out = jnp.where(first, ours, theirs).reshape(shape)
    input_grad = jnp.where(first, theirs, ours).reshape(shape)
    grad_one = jnp.where(first, summed, summed_other).astype(F32).reshape(27, width, channels)
    grad_two = jnp.where(first, summed_other, summed).astype(F32).reshape(27, width, channels)
    return mixed_out, input_grad, grad_one, grad_two


def solution(mesh):
    fine = Mesh(
        mesh.devices.reshape(mesh.shape["samples"], NZ, NX, mesh.shape["spatial"]),
        ("samples", "z", "x", "spatial"),
    )
    acts = P(("z", "x"), "samples", "spatial", None)
    kernels = P(None, ("z", "x"), None)
    return jax.shard_map(
        body,
        mesh=fine,
        in_specs=(acts, kernels, kernels, acts),
        out_specs=(acts, acts, kernels, kernels),
        check_vma=False,
    )
```

time: 133 us -> 95.8 us (0.72)
  blocking collectives: 58.1 us -> 23 us
  waiting for transfers between devices: 45.6 us -> 28.5 us
  starting transfers between devices: 18.6 us -> 30.2 us
  Pallas kernels: 4.96 us -> 8.89 us
    all_to_all x1, blocking collectives: 58.1 us -> 23 us  [body(): lax.all_to_all(jnp.broadcast_to(block, (NZ,) + block.shape), 'z', 0, 0, t...]
    all_to_all x1, waiting for transfers between devices: 21.7 us -> 0.01 us  [body(): parts = lax.all_to_all(parts, 'z', 0, 0, tiled=True)]
    ppermute x3 -> x13, starting transfers between devices: 3.85 us -> 16.4 us  [around(): lax.ppermute(values, axis, [((i + step) % size, i) for i in range(size)])]
    ppermute x3 -> x13, waiting for transfers between devices: 22 us -> 27.6 us  [around(): lax.ppermute(values, axis, [((i + step) % size, i) for i in range(size)])]
    pallas_call x2 -> x5, Pallas kernels: 4.96 us -> 8.89 us  [call(): pl.pallas_call(kernel, out_shape=tuple((jax.ShapeDtypeStruct(s, t) for s,...]
    all_to_all x1, starting transfers between devices: 5.31 us -> 3.49 us  [body(): parts = lax.all_to_all(parts, 'z', 0, 0, tiled=True)]
  transfers between devices with their start and end apart: 8 -> 18, of which waited for: 6 -> 6; matrix products, arithmetic and copies ran while one was open for 2% -> 3% of each run, Pallas kernels for 0% -> 8%
where the time goes in v2:
time: 95.8 us; the launch traced here: 95.5 us
  starting transfers between devices  30.2 us (32%)
  waiting for transfers between devices  28.5 us (30%)
  blocking collectives  23 us (24%)
  Pallas kernels  8.89 us (9%)
  other arithmetic  3.99 us (4%)
    ppermute x13, waiting for transfers between devices, around(): lax.ppermute(values, axis, [((i + step) % size, i) for i in range(size)])  27.6 us
    all_to_all x1, blocking collectives, body(): lax.all_to_all(jnp.broadcast_to(block, (NZ,) + block.shape), 'z', 0, 0, t...  23 us
    ppermute x13, starting transfers between devices, around(): lax.ppermute(values, axis, [((i + step) % size, i) for i in range(size)])  16.4 us
    ppermute x4, starting transfers between devices, swap(): return lax.ppermute(values, 'spatial', [(0, 1), (1, 0)])  10.3 us
    pallas_call x5, Pallas kernels, call(): pl.pallas_call(kernel, out_shape=tuple((jax.ShapeDtypeStruct(s, t) for s,...  8.89 us
    all_to_all x1, starting transfers between devices, body(): parts = lax.all_to_all(parts, 'z', 0, 0, tiled=True)  3.49 us
  transfers between devices with their start and end apart: 18, of which 6 were waited for; matrix products, arithmetic and copies ran while one was open for 3% of the time, Pallas kernels for 8%

profile of v2, /device:TPU:1, one launch (start us, length us, event | category | flops | bytes accessed | tf_op | source)
XLA Modules:
  0.0 95.5 jit_solution(17033897198022365469)
XLA Ops:
  0.6 0.0 copy-start
  0.6 0.0 copy-start.1
  0.7 0.9 select_bitcast_fusion.2
  1.5 3.3 %collective-permute-start = (bf16[16,1024]{1,0:T(8,128)(2,1)S(1)}, bf16[16,1024]{1,0:T(8,128)(2,1)S(1)}, u32[]{:S(2)}, u32[]{:S(2)}) collective-permute-start(bf16[16,1024]{1,0:T(8,128)(2,1)S(1)} %get-tuple-element.21), channel_id=1, source_target_pairs={{0,1},{1,0},{2,3},{3,2},{4,5},{5,4},{6,7},{7,6},{8,9},{9,8},{10,11... | collective-permute-start | bytes 98312 | tf_op jit(solution)/shard_map/ppermute | solution.py:200
  4.8 0.9 collective-permute-done
  5.7 0.1 broadcast_in_dim.3
  5.8 23.0 %all_to_all.10.mine_ref = bf16[8,2,16,1024]{3,2,1,0:T(8,128)(2,1)S(1)} all-to-all(bf16[8,2,16,1024]{3,2,1,0:T(8,128)(2,1)S(1)} %broadcast_in_dim.3), channel_id=1, replica_groups=mesh['samples'=4,'z'=8,'x'=4,'spatial'=2] {'z'}, dimensions={0} | all-to-all | bytes 1048576 | tf_op jit(solution)/shard_map/all_to_all | solution.py:224
  28.8 1.2 %collective-permute-start.1 = (bf16[8,2,16,1024]{3,2,1,0:T(8,128)(2,1)S(1)}, bf16[8,2,16,1024]{3,2,1,0:T(8,128)(2,1)S(1)}, u32[]{:S(2)}, u32[]{:S(2)}) collective-permute-start(bf16[8,2,16,1024]{3,2,1,0:T(8,128)(2,1)S(1)} %all_to_all.10.mine_ref), channel_id=1, source_target_pairs={{6,0},{0,2},{2,4},{4,6},{7,1},{1,3},{3,5},{5,7},{14,8},{8,10},{10,... | collective-permute-start | bytes 1572872 | tf_op jit(solution)/shard_map/ppermute | solution.py:205
  30.0 1.5 %collective-permute-start.2 = (bf16[8,2,16,1024]{3,2,1,0:T(8,128)(2,1)S(1)}, bf16[8,2,16,1024]{3,2,1,0:T(8,128)(2,1)S(1)}, u32[]{:S(2)}, u32[]{:S(2)}) collective-permute-start(bf16[8,2,16,1024]{3,2,1,0:T(8,128)(2,1)S(1)} %all_to_all.10.mine_ref), channel_id=1, source_target_pairs={{2,0},{4,2},{6,4},{0,6},{3,1},{5,3},{7,5},{1,7},{10,8},{12,10},{14... | collective-permute-start | bytes 1572872 | tf_op jit(solution)/shard_map/ppermute | solution.py:205
  31.5 10.3 %collective-permute-done.1.left_ref = bf16[8,2,16,1024]{3,2,1,0:T(8,128)(2,1)S(1)} collective-permute-done((bf16[8,2,16,1024]{3,2,1,0:T(8,128)(2,1)S(1)}, bf16[8,2,16,1024]{3,2,1,0:T(8,128)(2,1)S(1)}, u32[]{:S(2)}, u32[]{:S(2)}) %collective-permute-start.1) | collective-permute-done | bytes 524320 | tf_op jit(solution)/shard_map/ppermute | solution.py:205
  41.8 0.1 collective-permute-start.3
  41.9 0.0 collective-permute-done.2.right_ref
  41.9 2.7 %collective-permute-start.4 = (bf16[4,2,16,1024]{3,2,1,0:T(8,128)(2,1)S(1)}, bf16[4,2,16,1024]{3,2,1,0:T(8,128)(2,1)S(1)}, u32[]{:S(2)}, u32[]{:S(2)}) collective-permute-start(bf16[4,2,16,1024]{3,2,1,0:T(8,128)(2,1)S(1)} %slice.19), channel_id=1, source_target_pairs={{2,0},{4,2},{6,4},{0,6},{3,1},{5,3},{7,5},{1,7},{10,8},{12,10},{14... | collective-permute-start | bytes 786440 | tf_op jit(solution)/shard_map/ppermute | solution.py:205
  44.7 0.1 pad_add_fusion.at_ref
  44.7 0.0 copy-done
  44.8 0.0 copy-done.1
  44.8 1.3 %regroup.1 = bf16[4,432,128]{2,1,0:T(8,128)(2,1)S(1)} custom-call(s32[2]{0:T(128)S(1)} %pad_add_fusion.at_ref, bf16[432,512]{1,0:T(8,128)(2,1)S(1)} %bitcast.34, bf16[432,512]{1,0:T(8,128)(2,1)S(1)} %bitcast.36), custom_call_target="tpu_custom_call" | custom-call | flops 226492416 | tf_op jit(solution)/shard_map/regroup/pallas_call | solution.py:187
  46.1 2.3 %collective-permute-done.3.far0_ref = bf16[4,2,16,1024]{3,2,1,0:T(8,128)(2,1)S(1)} collective-permute-done((bf16[4,2,16,1024]{3,2,1,0:T(8,128)(2,1)S(1)}, bf16[4,2,16,1024]{3,2,1,0:T(8,128)(2,1)S(1)}, u32[]{:S(2)}, u32[]{:S(2)}) %collective-permute-start.3) | collective-permute-done | bytes 262176 | tf_op jit(solution)/shard_map/ppermute | solution.py:205
  48.3 0.0 collective-permute-done.4.far1_ref
  48.3 1.7 %conv_in.1 = (f32[2,16,1024]{2,1,0:T(8,128)S(1)}, bf16[2,512,1024]{2,1,0:T(8,128)(2,1)S(1)}) custom-call(s32[2]{0:T(128)S(1)} %pad_add_fusion.at_ref, bf16[8,2,16,1024]{3,2,1,0:T(8,128)(2,1)S(1)} %all_to_all.10.mine_ref, bf16[8,2,16,1024]{3,2,1,0:T(8,128)(2,1)S(1)} %collective-permute-done.1.left_ref, ...), custom_call_target="tpu_custom_call" | custom-call | flops 603979776 | tf_op jit(solution)/shard_map/conv_in/pallas_call | solution.py:187
  50.0 3.8 %collective-permute-start.5 = (f32[2,16,1024]{2,1,0:T(8,128)S(1)}, f32[2,16,1024]{2,1,0:T(8,128)S(1)}, u32[]{:S(2)}, u32[]{:S(2)}) collective-permute-start(f32[2,16,1024]{2,1,0:T(8,128)S(1)} %get-tuple-element.8.own_ref), channel_id=1, source_target_pairs={{0,1},{1,0},{2,3},{3,2},{4,5},{5,4},{6,7},{7,6},{8,9},{9,8},{10,11... | collective-permute-start | bytes 393224 | tf_op jit(solution)/shard_map/ppermute | solution.py:200
  53.9 1.7 %collective-permute-start.10 = (bf16[432,128]{1,0:T(8,128)(2,1)S(1)}, bf16[432,128]{1,0:T(8,128)(2,1)S(1)}, u32[]{:S(2)}, u32[]{:S(2)}) collective-permute-start(bf16[432,128]{1,0:T(8,128)(2,1)S(1)} %get-tuple-element.15), channel_id=1, source_target_pairs={{4,0},{6,2},{0,4},{2,6},{5,1},{7,3},{1,5},{3,7},{12,8},{14,10},{8,... | collective-permute-start | bytes 331784 | tf_op jit(solution)/shard_map/ppermute | solution.py:205
  55.6 2.0 %collective-permute-start.11 = (bf16[432,128]{1,0:T(8,128)(2,1)S(1)}, bf16[432,128]{1,0:T(8,128)(2,1)S(1)}, u32[]{:S(2)}, u32[]{:S(2)}) collective-permute-start(bf16[432,128]{1,0:T(8,128)(2,1)S(1)} %get-tuple-element.14), channel_id=1, source_target_pairs={{6,0},{0,2},{2,4},{4,6},{7,1},{1,3},{3,5},{5,7},{14,8},{8,10},{10,... | collective-permute-start | bytes 331784 | tf_op jit(solution)/shard_map/ppermute | solution.py:205
  57.6 0.7 collective-permute-start.9
  58.3 0.0 collective-permute-done.5.other_ref
  58.3 0.6 act.1
  58.9 0.4 collective-permute-start.6
  59.3 2.3 %collective-permute-start.7 = (bf16[2,16,1024]{2,1,0:T(8,128)(2,1)S(1)}, bf16[2,16,1024]{2,1,0:T(8,128)(2,1)S(1)}, u32[]{:S(2)}, u32[]{:S(2)}) collective-permute-start(bf16[2,16,1024]{2,1,0:T(8,128)(2,1)S(1)} %get-tuple-element.9.refs_0_), channel_id=1, source_target_pairs={{4,0},{6,2},{0,4},{2,6},{5,1},{7,3},{1,5},{3,7},{12,8},{14,10},{8,... | collective-permute-start | bytes 196616 | tf_op jit(solution)/shard_map/ppermute | solution.py:205
  61.6 0.0 collective-permute-done.10.refs_6_
  61.6 0.0 collective-permute-start.8
  61.6 1.8 %grad.1 = bf16[432,512]{1,0:T(8,128)(2,1)S(1)} custom-call(s32[2]{0:T(128)S(1)} %pad_add_fusion.at_ref, bf16[2,16,1024]{2,1,0:T(8,128)(2,1)S(1)} %get-tuple-element.10.keep_ref, bf16[2,512,1024]{2,1,0:T(8,128)(2,1)S(1)} %get-tuple-element.11.whole_ref), custom_call_target="tpu_custom_call" | custom-call | flops 603979776 | tf_op jit(solution)/shard_map/grad/pallas_call | solution.py:187
  63.4 0.0 collective-permute-done.11.refs_7_
  63.4 2.8 %collective-permute-start.13 = (bf16[432,512]{1,0:T(8,128)(2,1)S(1)}, bf16[432,512]{1,0:T(8,128)(2,1)S(1)}, u32[]{:S(2)}, u32[]{:S(2)}) collective-permute-start(bf16[432,512]{1,0:T(8,128)(2,1)S(1)} %grad.1), channel_id=1, source_target_pairs={{64,0},{128,64},{192,128},{0,192},{65,1},{129,65},{193,129},{1,193... | collective-permute-start | bytes 1327112 | tf_op jit(solution)/shard_map/ppermute | solution.py:205
  66.2 0.0 collective-permute-done.9.refs_5_
  66.2 0.3 collective-permute-start.14
  66.6 0.0 collective-permute-done.6.refs_1_
  66.6 0.7 collective-permute-start.15
  67.3 0.0 collective-permute-done.7.refs_2_
  67.3 0.0 collective-permute-done.8.refs_3_
  67.3 3.5 %conv_out.1 = bf16[8,2,16,1024]{3,2,1,0:T(8,128)(2,1)} custom-call(s32[2]{0:T(128)S(1)} %pad_add_fusion.at_ref, bf16[2,16,1024]{2,1,0:T(8,128)(2,1)S(1)} %get-tuple-element.9.refs_0_, bf16[2,16,1024]{2,1,0:T(8,128)(2,1)S(1)} %collective-permute-done.6.refs_1_, bf16[2,16,1024]{2,1,0:T(8,128)(2,1)S(1)} %collective-permute-done.7.refs_2_, ...), custom_call_target="tpu_custom_call" | custom-call | flops 603979776 | tf_op jit(solution)/shard_map/conv_out/pallas_call | solution.py:187
  70.7 3.5 %all-to-all-start.1 = ((bf16[8,2,16,1024]{3,2,1,0:T(8,128)(2,1)}), bf16[8,2,16,1024]{3,2,1,0:T(8,128)(2,1)S(1)}, u32[]{:S(2)}, u32[]{:S(2)}) async-start(bf16[8,2,16,1024]{3,2,1,0:T(8,128)(2,1)} %conv_out.1), calls=%async_computation.1 | async-start | bytes 1048576 | tf_op jit(solution)/shard_map/all_to_all | solution.py:266
  74.2 1.0 %collective-permute-done.13 = bf16[432,512]{1,0:T(8,128)(2,1)S(1)} collective-permute-done((bf16[432,512]{1,0:T(8,128)(2,1)S(1)}, bf16[432,512]{1,0:T(8,128)(2,1)S(1)}, u32[]{:S(2)}, u32[]{:S(2)}) %collective-permute-start.13) | collective-permute-done | bytes 442400 | tf_op jit(solution)/shard_map/ppermute | solution.py:205
  75.2 2.4 %collective-permute-done.14 = bf16[432,512]{1,0:T(8,128)(2,1)S(1)} collective-permute-done((bf16[432,512]{1,0:T(8,128)(2,1)S(1)}, bf16[432,512]{1,0:T(8,128)(2,1)S(1)}, u32[]{:S(2)}, u32[]{:S(2)}) %collective-permute-start.14) | collective-permute-done | bytes 442400 | tf_op jit(solution)/shard_map/ppermute | solution.py:205
  77.7 11.6 %collective-permute-done.15 = bf16[432,512]{1,0:T(8,128)(2,1)S(1)} collective-permute-done((bf16[432,512]{1,0:T(8,128)(2,1)S(1)}, bf16[432,512]{1,0:T(8,128)(2,1)S(1)}, u32[]{:S(2)}, u32[]{:S(2)}) %collective-permute-start.15) | collective-permute-done | bytes 442400 | tf_op jit(solution)/shard_map/ppermute | solution.py:205
  89.3 0.2 add_convert_fusion
  89.5 0.6 collective-permute-start.16
  90.1 0.0 all-to-all-done.1
  90.1 0.1 reduce_sum.12
  90.2 2.6 %collective-permute-start.12 = (bf16[16,1024]{1,0:T(8,128)(2,1)S(1)}, bf16[16,1024]{1,0:T(8,128)(2,1)S(1)}, u32[]{:S(2)}, u32[]{:S(2)}) collective-permute-start(bf16[16,1024]{1,0:T(8,128)(2,1)S(1)} %select_bitcast_fusion), channel_id=1, source_target_pairs={{0,1},{1,0},{2,3},{3,2},{4,5},{5,4},{6,7},{7,6},{8,9},{9,8},{10,11... | collective-permute-start | bytes 98312 | tf_op jit(solution)/shard_map/ppermute | solution.py:200
  92.8 0.0 collective-permute-done.16
  92.8 0.1 broadcast_select_fusion
  92.9 1.0 %convert.3 = f32[27,16,512]{2,1,0:T(8,128)} convert(bf16[27,16,512]{2,1,0:T(8,128)(2,1)S(1)} %bitcast.39) | non-fusion elementwise | flops 221184 | bytes 1327104 | tf_op jit(solution)/shard_map/reshape | solution.py:278
  93.9 1.0 %convert.4 = f32[27,16,512]{2,1,0:T(8,128)} convert(bf16[27,16,512]{2,1,0:T(8,128)(2,1)S(1)} %bitcast.38) | non-fusion elementwise | flops 221184 | bytes 1327104 | tf_op jit(solution)/shard_map/reshape | solution.py:279
  94.9 0.0 collective-permute-done.12
  94.9 0.6 fusion.1
  (5 shorter events, 0.1 us)
Async XLA Ops:
  0.6 44.1 %copy-start = (bf16[27,16,512]{2,1,0:T(8,128)(2,1)S(1)}, bf16[27,16,512]{2,1,0:T(8,128)(2,1)}, u32[]{:S(2)}) copy-start(bf16[27,16,512]{2,1,0:T(8,128)(2,1)} %param.5) | copy-start | bytes 1327108
  0.6 44.1 %copy-start.1 = (bf16[27,16,512]{2,1,0:T(8,128)(2,1)S(1)}, bf16[27,16,512]{2,1,0:T(8,128)(2,1)}, u32[]{:S(2)}) copy-start(bf16[27,16,512]{2,1,0:T(8,128)(2,1)} %param.6) | copy-start | bytes 1327108
  1.5 4.2 %collective-permute-start = (bf16[16,1024]{1,0:T(8,128)(2,1)S(1)}, bf16[16,1024]{1,0:T(8,128)(2,1)S(1)}, u32[]{:S(2)}, u32[]{:S(2)}) collective-permute-start(bf16[16,1024]{1,0:T(8,128)(2,1)S(1)} %get-tuple-element.21), channel_id=1, source_target_pairs={{0,1},{1,0},{2,3},{3,2},{4,5},{5,4},{6,7},{7,6},{8,9},{9,8},{10,11... | collective-permute-start | bytes 98312 | tf_op jit(solution)/shard_map/ppermute | solution.py:200
  28.8 13.0 %collective-permute-start.1 = (bf16[8,2,16,1024]{3,2,1,0:T(8,128)(2,1)S(1)}, bf16[8,2,16,1024]{3,2,1,0:T(8,128)(2,1)S(1)}, u32[]{:S(2)}, u32[]{:S(2)}) collective-permute-start(bf16[8,2,16,1024]{3,2,1,0:T(8,128)(2,1)S(1)} %all_to_all.10.mine_ref), channel_id=1, source_target_pairs={{6,0},{0,2},{2,4},{4,6},{7,1},{1,3},{3,5},{5,7},{14,8},{8,10},{10,... | collective-permute-start | bytes 1572872 | tf_op jit(solution)/shard_map/ppermute | solution.py:205
  30.0 11.9 %collective-permute-start.2 = (bf16[8,2,16,1024]{3,2,1,0:T(8,128)(2,1)S(1)}, bf16[8,2,16,1024]{3,2,1,0:T(8,128)(2,1)S(1)}, u32[]{:S(2)}, u32[]{:S(2)}) collective-permute-start(bf16[8,2,16,1024]{3,2,1,0:T(8,128)(2,1)S(1)} %all_to_all.10.mine_ref), channel_id=1, source_target_pairs={{2,0},{4,2},{6,4},{0,6},{3,1},{5,3},{7,5},{1,7},{10,8},{12,10},{14... | collective-permute-start | bytes 1572872 | tf_op jit(solution)/shard_map/ppermute | solution.py:205
  41.8 6.5 %collective-permute-start.3 = (bf16[4,2,16,1024]{3,2,1,0:T(8,128)(2,1)S(1)}, bf16[4,2,16,1024]{3,2,1,0:T(8,128)(2,1)S(1)}, u32[]{:S(2)}, u32[]{:S(2)}) collective-permute-start(bf16[4,2,16,1024]{3,2,1,0:T(8,128)(2,1)S(1)} %slice.18), channel_id=1, source_target_pairs={{6,0},{0,2},{2,4},{4,6},{7,1},{1,3},{3,5},{5,7},{14,8},{8,10},{10,... | collective-permute-start | bytes 786440 | tf_op jit(solution)/shard_map/ppermute | solution.py:205
  41.9 6.4 %collective-permute-start.4 = (bf16[4,2,16,1024]{3,2,1,0:T(8,128)(2,1)S(1)}, bf16[4,2,16,1024]{3,2,1,0:T(8,128)(2,1)S(1)}, u32[]{:S(2)}, u32[]{:S(2)}) collective-permute-start(bf16[4,2,16,1024]{3,2,1,0:T(8,128)(2,1)S(1)} %slice.19), channel_id=1, source_target_pairs={{2,0},{4,2},{6,4},{0,6},{3,1},{5,3},{7,5},{1,7},{10,8},{12,10},{14... | collective-permute-start | bytes 786440 | tf_op jit(solution)/shard_map/ppermute | solution.py:205
  50.0 8.3 %collective-permute-start.5 = (f32[2,16,1024]{2,1,0:T(8,128)S(1)}, f32[2,16,1024]{2,1,0:T(8,128)S(1)}, u32[]{:S(2)}, u32[]{:S(2)}) collective-permute-start(f32[2,16,1024]{2,1,0:T(8,128)S(1)} %get-tuple-element.8.own_ref), channel_id=1, source_target_pairs={{0,1},{1,0},{2,3},{3,2},{4,5},{5,4},{6,7},{7,6},{8,9},{9,8},{10,11... | collective-permute-start | bytes 393224 | tf_op jit(solution)/shard_map/ppermute | solution.py:200
  53.9 7.7 %collective-permute-start.10 = (bf16[432,128]{1,0:T(8,128)(2,1)S(1)}, bf16[432,128]{1,0:T(8,128)(2,1)S(1)}, u32[]{:S(2)}, u32[]{:S(2)}) collective-permute-start(bf16[432,128]{1,0:T(8,128)(2,1)S(1)} %get-tuple-element.15), channel_id=1, source_target_pairs={{4,0},{6,2},{0,4},{2,6},{5,1},{7,3},{1,5},{3,7},{12,8},{14,10},{8,... | collective-permute-start | bytes 331784 | tf_op jit(solution)/shard_map/ppermute | solution.py:205
  55.6 7.8 %collective-permute-start.11 = (bf16[432,128]{1,0:T(8,128)(2,1)S(1)}, bf16[432,128]{1,0:T(8,128)(2,1)S(1)}, u32[]{:S(2)}, u32[]{:S(2)}) collective-permute-start(bf16[432,128]{1,0:T(8,128)(2,1)S(1)} %get-tuple-element.14), channel_id=1, source_target_pairs={{6,0},{0,2},{2,4},{4,6},{7,1},{1,3},{3,5},{5,7},{14,8},{8,10},{10,... | collective-permute-start | bytes 331784 | tf_op jit(solution)/shard_map/ppermute | solution.py:205
  57.6 8.6 %collective-permute-start.9 = (bf16[432,128]{1,0:T(8,128)(2,1)S(1)}, bf16[432,128]{1,0:T(8,128)(2,1)S(1)}, u32[]{:S(2)}, u32[]{:S(2)}) collective-permute-start(bf16[432,128]{1,0:T(8,128)(2,1)S(1)} %get-tuple-element.16), channel_id=1, source_target_pairs={{2,0},{4,2},{6,4},{0,6},{3,1},{5,3},{7,5},{1,7},{10,8},{12,10},{14... | collective-permute-start | bytes 331784 | tf_op jit(solution)/shard_map/ppermute | solution.py:205
  58.9 7.7 %collective-permute-start.6 = (bf16[2,16,1024]{2,1,0:T(8,128)(2,1)S(1)}, bf16[2,16,1024]{2,1,0:T(8,128)(2,1)S(1)}, u32[]{:S(2)}, u32[]{:S(2)}) collective-permute-start(bf16[2,16,1024]{2,1,0:T(8,128)(2,1)S(1)} %get-tuple-element.9.refs_0_), channel_id=1, source_target_pairs={{2,0},{4,2},{6,4},{0,6},{3,1},{5,3},{7,5},{1,7},{10,8},{12,10},{14... | collective-permute-start | bytes 196616 | tf_op jit(solution)/shard_map/ppermute | solution.py:205
  59.3 8.0 %collective-permute-start.7 = (bf16[2,16,1024]{2,1,0:T(8,128)(2,1)S(1)}, bf16[2,16,1024]{2,1,0:T(8,128)(2,1)S(1)}, u32[]{:S(2)}, u32[]{:S(2)}) collective-permute-start(bf16[2,16,1024]{2,1,0:T(8,128)(2,1)S(1)} %get-tuple-element.9.refs_0_), channel_id=1, source_target_pairs={{4,0},{6,2},{0,4},{2,6},{5,1},{7,3},{1,5},{3,7},{12,8},{14,10},{8,... | collective-permute-start | bytes 196616 | tf_op jit(solution)/shard_map/ppermute | solution.py:205
  61.6 5.7 %collective-permute-start.8 = (bf16[2,16,1024]{2,1,0:T(8,128)(2,1)S(1)}, bf16[2,16,1024]{2,1,0:T(8,128)(2,1)S(1)}, u32[]{:S(2)}, u32[]{:S(2)}) collective-permute-start(bf16[2,16,1024]{2,1,0:T(8,128)(2,1)S(1)} %get-tuple-element.9.refs_0_), channel_id=1, source_target_pairs={{6,0},{0,2},{2,4},{4,6},{7,1},{1,3},{3,5},{5,7},{14,8},{8,10},{10,... | collective-permute-start | bytes 196616 | tf_op jit(solution)/shard_map/ppermute | solution.py:205
  63.4 11.8 %collective-permute-start.13 = (bf16[432,512]{1,0:T(8,128)(2,1)S(1)}, bf16[432,512]{1,0:T(8,128)(2,1)S(1)}, u32[]{:S(2)}, u32[]{:S(2)}) collective-permute-start(bf16[432,512]{1,0:T(8,128)(2,1)S(1)} %grad.1), channel_id=1, source_target_pairs={{64,0},{128,64},{192,128},{0,192},{65,1},{129,65},{193,129},{1,193... | collective-permute-start | bytes 1327112 | tf_op jit(solution)/shard_map/ppermute | solution.py:205
  66.2 11.5 %collective-permute-start.14 = (bf16[432,512]{1,0:T(8,128)(2,1)S(1)}, bf16[432,512]{1,0:T(8,128)(2,1)S(1)}, u32[]{:S(2)}, u32[]{:S(2)}) collective-permute-start(bf16[432,512]{1,0:T(8,128)(2,1)S(1)} %grad.1), channel_id=1, source_target_pairs={{128,0},{192,64},{0,128},{64,192},{129,1},{193,65},{1,129},{65,193... | collective-permute-start | bytes 1327112 | tf_op jit(solution)/shard_map/ppermute | solution.py:205
  66.6 22.7 %collective-permute-start.15 = (bf16[432,512]{1,0:T(8,128)(2,1)S(1)}, bf16[432,512]{1,0:T(8,128)(2,1)S(1)}, u32[]{:S(2)}, u32[]{:S(2)}) collective-permute-start(bf16[432,512]{1,0:T(8,128)(2,1)S(1)} %grad.1), channel_id=1, source_target_pairs={{192,0},{0,64},{64,128},{128,192},{193,1},{1,65},{65,129},{129,193... | collective-permute-start | bytes 1327112 | tf_op jit(solution)/shard_map/ppermute | solution.py:205
  70.7 19.4 %all-to-all-start.1 = ((bf16[8,2,16,1024]{3,2,1,0:T(8,128)(2,1)}), bf16[8,2,16,1024]{3,2,1,0:T(8,128)(2,1)S(1)}, u32[]{:S(2)}, u32[]{:S(2)}) async-start(bf16[8,2,16,1024]{3,2,1,0:T(8,128)(2,1)} %conv_out.1), calls=%async_computation.1 | async-start | bytes 1048576 | tf_op jit(solution)/shard_map/all_to_all | solution.py:266
  89.5 3.3 %collective-permute-start.16 = (bf16[432,512]{1,0:T(8,128)(2,1)S(1)}, bf16[432,512]{1,0:T(8,128)(2,1)S(1)}, u32[]{:S(2)}, u32[]{:S(2)}) collective-permute-start(bf16[432,512]{1,0:T(8,128)(2,1)S(1)} %add_convert_fusion), channel_id=1, source_target_pairs={{0,1},{1,0},{2,3},{3,2},{4,5},{5,4},{6,7},{7,6},{8,9},{9,8},{10,11... | collective-permute-start | bytes 1327112 | tf_op jit(solution)/shard_map/ppermute | solution.py:200
  90.2 4.7 %collective-permute-start.12 = (bf16[16,1024]{1,0:T(8,128)(2,1)S(1)}, bf16[16,1024]{1,0:T(8,128)(2,1)S(1)}, u32[]{:S(2)}, u32[]{:S(2)}) collective-permute-start(bf16[16,1024]{1,0:T(8,128)(2,1)S(1)} %select_bitcast_fusion), channel_id=1, source_target_pairs={{0,1},{1,0},{2,3},{3,2},{4,5},{5,4},{6,7},{7,6},{8,9},{9,8},{10,11... | collective-permute-start | bytes 98312 | tf_op jit(solution)/shard_map/ppermute | solution.py:200

commit v3 on v2

v3 whole, which is shorter than its diff:
```python
import jax
import jax.numpy as jnp
from jax import lax
from jax.experimental import pallas as pl
from jax.experimental.pallas import tpu as pltpu
from jax.sharding import Mesh, PartitionSpec as P

SIDE = 32
PLANE = SIDE * SIDE
F32 = jnp.float32
BF16 = jnp.bfloat16
PARAMS = pltpu.CompilerParams(vmem_limit_bytes=40 * 1024 * 1024)
NX = 4
NZ = 8


def masks(rows):
    cell = lax.broadcasted_iota(jnp.int32, (rows, PLANE), 1)
    column = cell & (SIDE - 1)
    row_ok = {-1: cell >= SIDE, 1: cell < PLANE - SIDE}
    col_ok = {-1: column > 0, 1: column < SIDE - 1}
    return row_ok, col_ok


def moved(values, step, ok):
    return jnp.where(ok, pltpu.roll(values, (-step) % PLANE, 1), 0.0)


def dot(lhs, rhs, dims):
    return lax.dot_general(lhs, rhs, (dims, ((), ())), preferred_element_type=F32)


def tap_sum(stack_ref, start, width, sign, ok):
    row_ok, col_ok = ok
    total = None
    for c in range(3):
        part = None
        for b in range(3):
            at = start + (3 * b + c) * width
            term = stack_ref[at : at + width, :]
            drow = sign * (b - 1)
            if drow:
                term = moved(term, SIDE * drow, row_ok[drow])
            part = term if part is None else part + term
        dcol = sign * (c - 1)
        if dcol:
            part = moved(part, dcol, col_ok[dcol])
        total = part if total is None else total + part
    return total


def spread(values, sign, col_ref, start, ok):
    row_ok, col_ok = ok
    width = values.shape[0]
    for c in range(3):
        dcol = sign * (c - 1)
        part = moved(values, dcol, col_ok[dcol]) if dcol else values
        for b in range(3):
            drow = sign * (b - 1)
            term = moved(part, SIDE * drow, row_ok[drow]) if drow else part
            at = start + (3 * b + c) * width
            col_ref[at : at + width, :] = term.astype(BF16)


def regroup_kernel(at_ref, one_ref, two_ref, *out_refs):
    channels = one_ref.shape[1]
    width = channels // (NX * NZ)
    group = NZ * width
    old = lax.broadcasted_iota(jnp.int32, (channels, group), 0)
    new = lax.broadcasted_iota(jnp.int32, (channels, group), 1)

    def run(ref):
        for k in range(NX):
            x = lax.rem(at_ref[1] + k, NX)
            home = (new // width) * (NX * width) + x * width + new % width
            order = (old == home).astype(F32).astype(BF16)
            out_refs[k][...] = dot(ref[...], order, ((1,), (0,))).astype(BF16)

    @pl.when(at_ref[0] == 0)
    def _():
        run(one_ref)

    @pl.when(at_ref[0] == 1)
    def _():
        run(two_ref)


def first_kernel(at_ref, mine_ref, *refs):
    kernels, own_ref, out_refs = refs[:NX], refs[NX], refs[NX + 1 : 2 * NX]
    all_ref, lhs, rhs, stack = refs[2 * NX :]
    width = mine_ref.shape[2]
    group = NZ * width
    third = 9 * width
    ok = masks(width)
    for d in range(2):
        rhs[d * group : (d + 1) * group, :] = mine_ref[:, d].reshape(group, PLANE)
    for k in range(NX):
        all_ref[k] = kernels[k][...]

    def run(sign):
        for d in range(2):
            for k in range(NX):
                for e in range(2):
                    a = 1 + sign * (e - d)
                    lhs[k * third : (k + 1) * third, e * group : (e + 1) * group] = kernels[k][a * third : (a + 1) * third, :]
            stack[...] = dot(lhs[...], rhs[...], ((1,), (0,)))
            for k in range(NX):
                total = tap_sum(stack, k * third, width, sign, ok)
                if k:
                    out_refs[k - 1][d] = total.astype(BF16)
                else:
                    own_ref[d] = total

    @pl.when(at_ref[0] == 0)
    def _():
        run(1)

    @pl.when(at_ref[0] == 1)
    def _():
        run(-1)


def act_kernel(at_ref, own_ref, other_ref, send_ref, keep_ref):
    first = at_ref[0] == 0
    for d in range(2):
        own, other = own_ref[d], other_ref[d]
        pre = jnp.where(first, own, other)
        upstream = jnp.where(first, other, own)
        gate = 1.0 / (1.0 + jnp.exp(-pre))
        hidden = pre * gate
        act = upstream * gate * (1.0 + pre * (1.0 - gate))
        send_ref[d] = jnp.where(first, hidden, act).astype(BF16)
        keep_ref[d] = jnp.where(first, act, hidden).astype(BF16)


def grad_kernel(at_ref, keep_ref, mine_ref, left_ref, right_ref, far0_ref, far1_ref, *refs):
    out_refs, (whole, col, full) = refs[:4], refs[4:]
    width = keep_ref.shape[1]
    third = 9 * width
    ok = masks(width)
    x = at_ref[1]
    half = NZ // 2
    pieces = ((mine_ref, 0, 0, NZ), (left_ref, NX - 1, 0, NZ), (right_ref, 1, 0, NZ), (far0_ref, 2, 0, half), (far1_ref, 2, half, half))
    for ref, step, z0, count in pieces:
        source = lax.rem(x + step, NX)
        for z in range(count):
            rows = pl.ds(pl.multiple_of(((z0 + z) * NX + source) * width, 16), width)
            for d in range(2):
                whole[d, rows, :] = ref[z, d]

    def run(sign):
        for d in range(2):
            at = third * (d if sign > 0 else 1 - d)
            spread(keep_ref[d].astype(F32), sign, col, at, ok)
        zero = dot(col[...], whole[0], ((1,), (1,)))
        last = dot(col[...], whole[1], ((1,), (1,)))
        low, high = (last, zero) if sign > 0 else (zero, last)
        full[0:third, :] = low[0:third].astype(BF16)
        full[third : 2 * third, :] = (low[third:] + high[0:third]).astype(BF16)
        full[2 * third :, :] = high[third:].astype(BF16)

    @pl.when(at_ref[0] == 0)
    def _():
        run(-1)

    @pl.when(at_ref[0] == 1)
    def _():
        run(1)

    quarter = full.shape[1] // 4
    for k in range(4):
        columns = pl.ds(pl.multiple_of(lax.rem(at_ref[2] + k, 4) * quarter, quarter), quarter)
        out_refs[k][...] = full[:, columns]


def finish_kernel(at_ref, *refs):
    own_refs, other_ref, (one_ref, two_ref) = refs[:4], refs[4], refs[5:]
    quarter = other_ref.shape[2]

    def run(own_out, other_out):
        for k in range(4):
            columns = pl.ds(pl.multiple_of(lax.rem(at_ref[2] + k, 4) * quarter, quarter), quarter)
            own_out[:, columns] = own_refs[k][...].astype(F32)
            other_out[:, columns] = other_ref[k].astype(F32)

    @pl.when(at_ref[0] == 0)
    def _():
        run(one_ref, two_ref)

    @pl.when(at_ref[0] == 1)
    def _():
        run(two_ref, one_ref)


def second_kernel(at_ref, *refs):
    acts, kernels, (out_ref, col, tall) = refs[:NX], refs[NX], refs[NX + 1 :]
    width = acts[0].shape[1]
    third = 9 * width
    ok = masks(width)

    def run(sign):
        for k in range(NX):
            for d in range(2):
                at = 2 * third * k + third * (d if sign > 0 else 1 - d)
                spread(acts[k][d].astype(F32), sign, col, at, ok)
        for d in range(2):
            at = third * ((1 - d) if sign > 0 else d)
            for k in range(NX):
                tall[2 * third * k : 2 * third * (k + 1), :] = kernels[k, at : at + 2 * third, :]
            part = dot(tall[...], col[...], ((0,), (0,)))
            out_ref[:, d] = part.astype(BF16).reshape(NZ, width, PLANE)

    @pl.when(at_ref[0] == 0)
    def _():
        run(1)

    @pl.when(at_ref[0] == 1)
    def _():
        run(-1)


def call(kernel, outs, scratch, name, cost, *args):
    vmem = pl.BlockSpec(memory_space=pltpu.VMEM)
    return pl.pallas_call(
        kernel,
        out_shape=tuple(jax.ShapeDtypeStruct(s, t) for s, t in outs),
        in_specs=[pl.BlockSpec(memory_space=pltpu.SMEM)] + [vmem] * (len(args) - 1),
        out_specs=tuple([vmem] * len(outs)),
        scratch_shapes=[pltpu.VMEM(s, t) for s, t in scratch],
        compiler_params=PARAMS,
        cost_estimate=pl.CostEstimate(flops=cost, bytes_accessed=0, transcendentals=0),
        name=name,
    )(*args)


def swap(values):
    return lax.ppermute(values, "spatial", [(0, 1), (1, 0)])


def around(values, axis, step):
    size = lax.axis_size(axis)
    return lax.ppermute(values, axis, [((i + step) % size, i) for i in range(size)])


def body(features, conv_one, conv_two, cotangent):
    width, channels = conv_one.shape[1], conv_one.shape[2]
    core = lax.axis_index("spatial")
    first = core == 0
    at = jnp.stack([core, lax.axis_index("x"), lax.axis_index("samples")]).astype(jnp.int32)
    one = conv_one.reshape(27 * width, channels)
    two = conv_two.reshape(27 * width, channels)
    features = features.reshape(width, PLANE)
    cotangent = cotangent.reshape(width, PLANE)
    taps = 27 * width
    group = NZ * width
    quarter = channels // 4
    plane = (2, width, PLANE)
    work = 4 * 18 * width * channels * PLANE

    groups = call(regroup_kernel, [((taps, group), BF16)] * NX, [], "regroup", 2 * taps * channels * channels, at, one, two)
    kernels = [groups[0]] + [around(groups[NX - k], "x", k) for k in range(1, NX)]

    came = swap(jnp.where(first, cotangent, features))
    kept = jnp.where(first, features, cotangent)
    block = jnp.where(first, jnp.stack([kept, came]), jnp.stack([came, kept]))
    block, _ = lax.optimization_barrier((block, groups[0]))
    mine = lax.all_to_all(jnp.broadcast_to(block, (NZ,) + block.shape), "z", 0, 0, tiled=True)

    own, *sends, held = call(
        first_kernel,
        [(plane, F32)] + [(plane, BF16)] * (NX - 1) + [((NX, taps, group), BF16)],
        [((NX * 9 * width, 2 * group), BF16), ((2 * group, PLANE), BF16), ((NX * 9 * width, PLANE), F32)],
        "conv_in", work, at, mine, *kernels,
    )
    sends = [around(part, "x", NX - k) for k, part in enumerate(sends, 1)]
    own = own + sum(part.astype(F32) for part in sends)

    left = around(mine, "x", -1)
    right = around(mine, "x", 1)
    far0 = around(left[: NZ // 2], "x", -1)
    far1 = around(right[NZ // 2 :], "x", 1)
    held = swap(held)

    other = swap(own)
    send, keep = call(act_kernel, [(plane, BF16)] * 2, [], "act", 0, at, own, other)
    acts = [send] + [around(send, "x", k) for k in range(1, NX)]
    (parts,) = call(
        second_kernel,
        [((NZ,) + plane, BF16)],
        [((NX * 18 * width, PLANE), BF16), ((NX * 18 * width, group), BF16)],
        "conv_out", work, at, *acts, held,
    )
    parts = lax.all_to_all(parts, "z", 0, 0, tiled=True)

    grads = call(
        grad_kernel,
        [((taps, quarter), BF16)] * 4,
        [((2, channels, PLANE), BF16), ((18 * width, PLANE), BF16), ((taps, channels), BF16)],
        "grad", work, at, keep, mine, left, right, far0, far1,
    )
    pieces = [grads[0]] + [around(grads[4 - k], "samples", k) for k in (1, 2, 3)]
    summed = sum(g.astype(F32) for g in pieces).astype(BF16)
    pieces = [summed] + [around(summed, "samples", k) for k in (1, 2, 3)]
    others = swap(jnp.stack(pieces))
    grad_one, grad_two = call(
        finish_kernel, [((taps, channels), F32)] * 2, [], "finish", 0, at, *pieces, others
    )

    result = jnp.sum(parts.astype(F32), axis=0).astype(BF16)
    ours = jnp.where(first, result[0], result[1])
    theirs = swap(jnp.where(first, result[1], result[0]))
    shape = (width, 1, 1, PLANE)
    mixed_out = jnp.where(first, ours, theirs).reshape(shape)
    input_grad = jnp.where(first, theirs, ours).reshape(shape)
    weights = (27, width, channels)
    return mixed_out, input_grad, grad_one.reshape(weights), grad_two.reshape(weights)


def solution(mesh):
    fine = Mesh(
        mesh.devices.reshape(mesh.shape["samples"], NZ, NX, mesh.shape["spatial"]),
        ("samples", "z", "x", "spatial"),
    )
    acts = P(("z", "x"), "samples", "spatial", None)
    kernels = P(None, ("z", "x"), None)
    return jax.shard_map(
        body,
        mesh=fine,
        in_specs=(acts, kernels, kernels, acts),
        out_specs=(acts, acts, kernels, kernels),
        check_vma=False,
    )
```

time: 95.8 us -> 106 us (1.11)
  blocking collectives: 23 us -> 0 us
  waiting for transfers between devices: 28.5 us -> 44.3 us
  starting transfers between devices: 30.2 us -> 44.5 us
  local copies, waits for them, and re-layouts: 0.13 us -> 2.92 us
  Pallas kernels: 8.89 us -> 11.5 us
  other arithmetic: 3.99 us -> 1.74 us
    all_to_all x1 -> x0, blocking collectives: 23 us -> none  [body(): lax.all_to_all(jnp.broadcast_to(block, (NZ,) + block.shape), 'z', 0, 0, t...]
    ppermute x13 -> x19, waiting for transfers between devices: 27.6 us -> 35.4 us  [around(): lax.ppermute(values, axis, [((i + step) % size, i) for i in range(size)])]
    all_to_all x0 -> x1, waiting for transfers between devices: none -> 6.72 us  [body(): lax.all_to_all(jnp.broadcast_to(block, (NZ,) + block.shape), 'z', 0, 0, t...]
    all_to_all x0 -> x1, starting transfers between devices: none -> 6.45 us  [body(): lax.all_to_all(jnp.broadcast_to(block, (NZ,) + block.shape), 'z', 0, 0, t...]
    ppermute x13 -> x19, starting transfers between devices: 16.4 us -> 22.7 us  [around(): lax.ppermute(values, axis, [((i + step) % size, i) for i in range(size)])]
    pallas_call x5 -> x6, Pallas kernels: 8.89 us -> 11.5 us  [call(): pl.pallas_call(kernel, out_shape=tuple((jax.ShapeDtypeStruct(s, t) for s,...]
    reshape x2 -> x0, other arithmetic: 2.04 us -> none  [the longest x1 1.02 us: body(): jnp.where(first, summed, summed_other).astype(F32)]
    unnamed x4, local copies, waits for them, and re-layouts: 0.01 us -> 2.03 us
  transfers between devices with their start and end apart: 18 -> 26, of which waited for: 6 -> 15; matrix products, arithmetic and copies ran while one was open for 3% -> 1% of each run, Pallas kernels for 8% -> 7%
where the time goes in v3:
time: 106 us
  starting transfers between devices  44.5 us (42%)
  waiting for transfers between devices  44.3 us (42%)
  Pallas kernels  11.5 us (11%)
  local copies, waits for them, and re-layouts  2.92 us (3%)
  other arithmetic  1.74 us (2%)
    ppermute x19, waiting for transfers between devices, around(): lax.ppermute(values, axis, [((i + step) % size, i) for i in range(size)])  35.4 us
    ppermute x19, starting transfers between devices, around(): lax.ppermute(values, axis, [((i + step) % size, i) for i in range(size)])  22.7 us
    ppermute x5, starting transfers between devices, swap(): return lax.ppermute(values, 'spatial', [(0, 1), (1, 0)])  11.8 us
    pallas_call x6, Pallas kernels, call(): pl.pallas_call(kernel, out_shape=tuple((jax.ShapeDtypeStruct(s, t) for s,...  11.5 us
    all_to_all x1, waiting for transfers between devices, body(): lax.all_to_all(jnp.broadcast_to(block, (NZ,) + block.shape), 'z', 0, 0, t...  6.72 us
    all_to_all x1, starting transfers between devices, body(): lax.all_to_all(jnp.broadcast_to(block, (NZ,) + block.shape), 'z', 0, 0, t...  6.45 us
    all_to_all x1, starting transfers between devices, body(): parts = lax.all_to_all(parts, 'z', 0, 0, tiled=True)  3.49 us
    ppermute x5, waiting for transfers between devices, swap(): return lax.ppermute(values, 'spatial', [(0, 1), (1, 0)])  2.25 us
  transfers between devices with their start and end apart: 26, of which 15 were waited for; matrix products, arithmetic and copies ran while one was open for 1% of the time, Pallas kernels for 7%

profile of v3, /device:TPU:1, one launch (start us, length us, event | category | flops | bytes accessed | tf_op | source)
XLA Modules:
  0.0 105.8 jit_solution(9056773812384092122)
XLA Ops:
  0.6 0.8 select_bitcast_fusion.2
  1.4 3.3 %collective-permute-start = (bf16[16,1024]{1,0:T(8,128)(2,1)S(1)}, bf16[16,1024]{1,0:T(8,128)(2,1)S(1)}, u32[]{:S(2)}, u32[]{:S(2)}) collective-permute-start(bf16[16,1024]{1,0:T(8,128)(2,1)S(1)} %get-tuple-element.43), channel_id=1, source_target_pairs={{0,1},{1,0},{2,3},{3,2},{4,5},{5,4},{6,7},{7,6},{8,9},{9,8},{10,11... | collective-permute-start | bytes 98312 | tf_op jit(solution)/shard_map/ppermute | solution.py:237
  4.7 0.1 pad_add_fusion.at_ref
  4.8 1.0 copy-done
  5.8 1.0 copy-done.1
  6.8 1.2 %regroup.1 = (bf16[432,128]{1,0:T(8,128)(2,1)S(1)}, bf16[432,128]{1,0:T(8,128)(2,1)S(1)}, bf16[432,128]{1,0:T(8,128)(2,1)S(1)}, bf16[432,128]{1,0:T(8,128)(2,1)S(1)}) custom-call(s32[3]{0:T(128)S(1)} %pad_add_fusion.at_ref, bf16[432,512]{1,0:T(8,128)(2,1)S(1)} %bitcast.30, bf16[432,512]{1,0:T(8,128)(2,1)S(1)} %bitcast.31), custom_call_target="tpu_custom_call" | custom-call | flops 226492416 | tf_op jit(solution)/shard_map/regroup/pallas_call | solution.py:224
  8.0 0.0 collective-permute-done
  8.1 0.9 broadcast_in_dim.3
  8.9 6.5 %all-to-all-start = ((bf16[8,2,16,1024]{3,2,1,0:T(8,128)(2,1)}), bf16[8,2,16,1024]{3,2,1,0:T(8,128)(2,1)S(1)}, u32[]{:S(2)}, u32[]{:S(2)}) async-start(bf16[8,2,16,1024]{3,2,1,0:T(8,128)(2,1)} %broadcast_in_dim.3), calls=%async_computation | async-start | bytes 1048576 | tf_op jit(solution)/shard_map/all_to_all | solution.py:267
  15.4 2.5 %collective-permute-start.1 = (bf16[432,128]{1,0:T(8,128)(2,1)S(1)}, bf16[432,128]{1,0:T(8,128)(2,1)S(1)}, u32[]{:S(2)}, u32[]{:S(2)}) collective-permute-start(bf16[432,128]{1,0:T(8,128)(2,1)S(1)} %get-tuple-element.24), channel_id=1, source_target_pairs={{2,0},{4,2},{6,4},{0,6},{3,1},{5,3},{7,5},{1,7},{10,8},{12,10},{14... | collective-permute-start | bytes 331784 | tf_op jit(solution)/shard_map/ppermute | solution.py:242
  17.8 0.5 collective-permute-start.2
  18.4 0.6 collective-permute-start.3
  19.0 3.2 %collective-permute-done.1.refs_1_ = bf16[432,128]{1,0:T(8,128)(2,1)S(1)} collective-permute-done((bf16[432,128]{1,0:T(8,128)(2,1)S(1)}, bf16[432,128]{1,0:T(8,128)(2,1)S(1)}, u32[]{:S(2)}, u32[]{:S(2)}) %collective-permute-start.1) | collective-permute-done | bytes 110624 | tf_op jit(solution)/shard_map/ppermute | solution.py:242
  22.2 1.2 %collective-permute-done.2.refs_2_ = bf16[432,128]{1,0:T(8,128)(2,1)S(1)} collective-permute-done((bf16[432,128]{1,0:T(8,128)(2,1)S(1)}, bf16[432,128]{1,0:T(8,128)(2,1)S(1)}, u32[]{:S(2)}, u32[]{:S(2)}) %collective-permute-start.2) | collective-permute-done | bytes 110624 | tf_op jit(solution)/shard_map/ppermute | solution.py:242
  23.4 3.3 %collective-permute-done.3.refs_3_ = bf16[432,128]{1,0:T(8,128)(2,1)S(1)} collective-permute-done((bf16[432,128]{1,0:T(8,128)(2,1)S(1)}, bf16[432,128]{1,0:T(8,128)(2,1)S(1)}, u32[]{:S(2)}, u32[]{:S(2)}) %collective-permute-start.3) | collective-permute-done | bytes 110624 | tf_op jit(solution)/shard_map/ppermute | solution.py:242
  26.7 6.7 %all-to-all-done.mine_ref = bf16[8,2,16,1024]{3,2,1,0:T(8,128)(2,1)S(1)} async-done(((bf16[8,2,16,1024]{3,2,1,0:T(8,128)(2,1)}), bf16[8,2,16,1024]{3,2,1,0:T(8,128)(2,1)S(1)}, u32[]{:S(2)}, u32[]{:S(2)}) %all-to-all-start) | async-done | bytes 524320 | tf_op jit(solution)/shard_map/all_to_all | solution.py:267
  33.4 2.5 %conv_in.1 = (f32[2,16,1024]{2,1,0:T(8,128)S(1)}, bf16[2,16,1024]{2,1,0:T(8,128)(2,1)S(1)}, bf16[2,16,1024]{2,1,0:T(8,128)(2,1)S(1)}, bf16[2,16,1024]{2,1,0:T(8,128)(2,1)S(1)}, bf16[4,432,128]{2,1,0:T(8,128)(2,1)S(1)}) custom-call(s32[3]{0:T(128)S(1)} %pad_add_fusion.at_ref, bf16[8,2,16,1024]{3,2,1,0:T(8,128)(2,1)S(1)} %all-to-all-done.mine_ref, ...), custom_call_target="tpu_custom_call" | custom-call | flops 603979776 | tf_op jit(solution)/shard_map/conv_in/pallas_call | solution.py:224
  35.9 1.3 %collective-permute-start.4 = (bf16[2,16,1024]{2,1,0:T(8,128)(2,1)S(1)}, bf16[2,16,1024]{2,1,0:T(8,128)(2,1)S(1)}, u32[]{:S(2)}, u32[]{:S(2)}) collective-permute-start(bf16[2,16,1024]{2,1,0:T(8,128)(2,1)S(1)} %get-tuple-element.28), channel_id=1, source_target_pairs={{6,0},{0,2},{2,4},{4,6},{7,1},{1,3},{3,5},{5,7},{14,8},{8,10},{10,... | collective-permute-start | bytes 196616 | tf_op jit(solution)/shard_map/ppermute | solution.py:242
  37.2 2.5 %collective-permute-start.5 = (bf16[2,16,1024]{2,1,0:T(8,128)(2,1)S(1)}, bf16[2,16,1024]{2,1,0:T(8,128)(2,1)S(1)}, u32[]{:S(2)}, u32[]{:S(2)}) collective-permute-start(bf16[2,16,1024]{2,1,0:T(8,128)(2,1)S(1)} %get-tuple-element.29), channel_id=1, source_target_pairs={{4,0},{6,2},{0,4},{2,6},{5,1},{7,3},{1,5},{3,7},{12,8},{14,10},{8,... | collective-permute-start | bytes 196616 | tf_op jit(solution)/shard_map/ppermute | solution.py:242
  39.6 1.2 %collective-permute-start.6 = (bf16[2,16,1024]{2,1,0:T(8,128)(2,1)S(1)}, bf16[2,16,1024]{2,1,0:T(8,128)(2,1)S(1)}, u32[]{:S(2)}, u32[]{:S(2)}) collective-permute-start(bf16[2,16,1024]{2,1,0:T(8,128)(2,1)S(1)} %get-tuple-element.30), channel_id=1, source_target_pairs={{2,0},{4,2},{6,4},{0,6},{3,1},{5,3},{7,5},{1,7},{10,8},{12,10},{14... | collective-permute-start | bytes 196616 | tf_op jit(solution)/shard_map/ppermute | solution.py:242
  40.8 1.3 %collective-permute-start.11 = (bf16[4,432,128]{2,1,0:T(8,128)(2,1)S(1)}, bf16[4,432,128]{2,1,0:T(8,128)(2,1)S(1)}, u32[]{:S(2)}, u32[]{:S(2)}) collective-permute-start(bf16[4,432,128]{2,1,0:T(8,128)(2,1)S(1)} %get-tuple-element.32), channel_id=1, source_target_pairs={{0,1},{1,0},{2,3},{3,2},{4,5},{5,4},{6,7},{7,6},{8,9},{9,8},{10,11... | collective-permute-start | bytes 1327112 | tf_op jit(solution)/shard_map/ppermute | solution.py:237
  42.1 0.0 collective-permute-start.14
  42.1 0.0 collective-permute-done.4
  42.1 1.5 %collective-permute-start.13 = (bf16[8,2,16,1024]{3,2,1,0:T(8,128)(2,1)S(1)}, bf16[8,2,16,1024]{3,2,1,0:T(8,128)(2,1)S(1)}, u32[]{:S(2)}, u32[]{:S(2)}) collective-permute-start(bf16[8,2,16,1024]{3,2,1,0:T(8,128)(2,1)S(1)} %all-to-all-done.mine_ref), channel_id=1, source_target_pairs={{6,0},{0,2},{2,4},{4,6},{7,1},{1,3},{3,5},{5,7},{14,8},{8,10},{10,... | collective-permute-start | bytes 1572872 | tf_op jit(solution)/shard_map/ppermute | solution.py:242
  43.5 0.0 collective-permute-done.5
  43.6 1.4 %collective-permute-start.7 = (f32[2,16,1024]{2,1,0:T(8,128)S(1)}, f32[2,16,1024]{2,1,0:T(8,128)S(1)}, u32[]{:S(2)}, u32[]{:S(2)}) collective-permute-start(f32[2,16,1024]{2,1,0:T(8,128)S(1)} %add_add_fusion.own_ref), channel_id=1, source_target_pairs={{0,1},{1,0},{2,3},{3,2},{4,5},{5,4},{6,7},{7,6},{8,9},{9,8},{10,11... | collective-permute-start | bytes 393224 | tf_op jit(solution)/shard_map/ppermute | solution.py:237
  45.0 1.0 collective-permute-done.7.other_ref
  46.0 0.6 act.1
  46.6 0.8 collective-permute-start.10
  47.5 3.7 %collective-permute-start.9 = (bf16[2,16,1024]{2,1,0:T(8,128)(2,1)S(1)}, bf16[2,16,1024]{2,1,0:T(8,128)(2,1)S(1)}, u32[]{:S(2)}, u32[]{:S(2)}) collective-permute-start(bf16[2,16,1024]{2,1,0:T(8,128)(2,1)S(1)} %get-tuple-element.31.refs_0_), channel_id=1, source_target_pairs={{4,0},{6,2},{0,4},{2,6},{5,1},{7,3},{1,5},{3,7},{12,8},{14,10},{8,... | collective-permute-start | bytes 196616 | tf_op jit(solution)/shard_map/ppermute | solution.py:242
  51.1 8.4 %collective-permute-done.10.refs_3_ = bf16[2,16,1024]{2,1,0:T(8,128)(2,1)S(1)} collective-permute-done((bf16[2,16,1024]{2,1,0:T(8,128)(2,1)S(1)}, bf16[2,16,1024]{2,1,0:T(8,128)(2,1)S(1)}, u32[]{:S(2)}, u32[]{:S(2)}) %collective-permute-start.10) | collective-permute-done | bytes 65568 | tf_op jit(solution)/shard_map/ppermute | solution.py:242
  59.6 0.0 collective-permute-start.8
  59.6 0.0 collective-permute-done.9.refs_2_
  59.6 3.1 %collective-permute-done.8.refs_1_ = bf16[2,16,1024]{2,1,0:T(8,128)(2,1)S(1)} collective-permute-done((bf16[2,16,1024]{2,1,0:T(8,128)(2,1)S(1)}, bf16[2,16,1024]{2,1,0:T(8,128)(2,1)S(1)}, u32[]{:S(2)}, u32[]{:S(2)}) %collective-permute-start.8) | collective-permute-done | bytes 65568 | tf_op jit(solution)/shard_map/ppermute | solution.py:242
  62.7 0.0 collective-permute-done.11.refs_4_
  62.7 3.5 %conv_out.1 = bf16[8,2,16,1024]{3,2,1,0:T(8,128)(2,1)} custom-call(s32[3]{0:T(128)S(1)} %pad_add_fusion.at_ref, bf16[2,16,1024]{2,1,0:T(8,128)(2,1)S(1)} %get-tuple-element.31.refs_0_, bf16[2,16,1024]{2,1,0:T(8,128)(2,1)S(1)} %collective-permute-done.8.refs_1_, bf16[2,16,1024]{2,1,0:T(8,128)(2,1)S(1)} %collective-permute-done.9.refs_2_, ...), custom_call_target="tpu_custom_call" | custom-call | flops 603979776 | tf_op jit(solution)/shard_map/conv_out/pallas_call | solution.py:224
  66.2 3.5 %all-to-all-start.1 = ((bf16[8,2,16,1024]{3,2,1,0:T(8,128)(2,1)}), bf16[8,2,16,1024]{3,2,1,0:T(8,128)(2,1)S(1)}, u32[]{:S(2)}, u32[]{:S(2)}) async-start(bf16[8,2,16,1024]{3,2,1,0:T(8,128)(2,1)} %conv_out.1), calls=%async_computation.1 | async-start | bytes 1048576 | tf_op jit(solution)/shard_map/all_to_all | solution.py:293
  69.7 0.0 collective-permute-done.14.right_ref
  69.7 1.3 %collective-permute-start.16 = (bf16[4,2,16,1024]{3,2,1,0:T(8,128)(2,1)S(1)}, bf16[4,2,16,1024]{3,2,1,0:T(8,128)(2,1)S(1)}, u32[]{:S(2)}, u32[]{:S(2)}) collective-permute-start(bf16[4,2,16,1024]{3,2,1,0:T(8,128)(2,1)S(1)} %slice.21), channel_id=1, source_target_pairs={{2,0},{4,2},{6,4},{0,6},{3,1},{5,3},{7,5},{1,7},{10,8},{12,10},{14... | collective-permute-start | bytes 786440 | tf_op jit(solution)/shard_map/ppermute | solution.py:242
  71.0 0.0 collective-permute-done.13.left_ref
  71.0 0.3 collective-permute-start.15
  71.4 4.4 %collective-permute-done.16.far1_ref = bf16[4,2,16,1024]{3,2,1,0:T(8,128)(2,1)S(1)} collective-permute-done((bf16[4,2,16,1024]{3,2,1,0:T(8,128)(2,1)S(1)}, bf16[4,2,16,1024]{3,2,1,0:T(8,128)(2,1)S(1)}, u32[]{:S(2)}, u32[]{:S(2)}) %collective-permute-start.16) | collective-permute-done | bytes 262176 | tf_op jit(solution)/shard_map/ppermute | solution.py:242
  75.8 2.5 %collective-permute-done.15.far0_ref = bf16[4,2,16,1024]{3,2,1,0:T(8,128)(2,1)S(1)} collective-permute-done((bf16[4,2,16,1024]{3,2,1,0:T(8,128)(2,1)S(1)}, bf16[4,2,16,1024]{3,2,1,0:T(8,128)(2,1)S(1)}, u32[]{:S(2)}, u32[]{:S(2)}) %collective-permute-start.15) | collective-permute-done | bytes 262176 | tf_op jit(solution)/shard_map/ppermute | solution.py:242
  78.3 1.9 %grad.1 = (bf16[432,128]{1,0:T(8,128)(2,1)S(1)}, bf16[432,128]{1,0:T(8,128)(2,1)S(1)}, bf16[432,128]{1,0:T(8,128)(2,1)S(1)}, bf16[432,128]{1,0:T(8,128)(2,1)S(1)}) custom-call(s32[3]{0:T(128)S(1)} %pad_add_fusion.at_ref, bf16[2,16,1024]{2,1,0:T(8,128)(2,1)S(1)} %get-tuple-element.33.keep_ref, bf16[8,2,16,1024]{3,2,1,0:T(8,128)(2,1)S(1)} %all-to-all-done.mine_ref, ...), custom_call_target="tpu_custom_call" | custom-call | flops 603979776 | tf_op jit(solution)/shard_map/grad/pallas_call | solution.py:224
  80.2 2.8 %collective-permute-start.17 = (bf16[432,128]{1,0:T(8,128)(2,1)S(1)}, bf16[432,128]{1,0:T(8,128)(2,1)S(1)}, u32[]{:S(2)}, u32[]{:S(2)}) collective-permute-start(bf16[432,128]{1,0:T(8,128)(2,1)S(1)} %get-tuple-element.35), channel_id=1, source_target_pairs={{64,0},{128,64},{192,128},{0,192},{65,1},{129,65},{193,129},{1,193... | collective-permute-start | bytes 331784 | tf_op jit(solution)/shard_map/ppermute | solution.py:242
  83.0 0.3 collective-permute-start.18
  83.3 0.7 collective-permute-start.19
  84.0 1.9 %collective-permute-done.17 = bf16[432,128]{1,0:T(8,128)(2,1)S(1)} collective-permute-done((bf16[432,128]{1,0:T(8,128)(2,1)S(1)}, bf16[432,128]{1,0:T(8,128)(2,1)S(1)}, u32[]{:S(2)}, u32[]{:S(2)}) %collective-permute-start.17) | collective-permute-done | bytes 110624 | tf_op jit(solution)/shard_map/ppermute | solution.py:242
  85.9 2.3 %collective-permute-done.18 = bf16[432,128]{1,0:T(8,128)(2,1)S(1)} collective-permute-done((bf16[432,128]{1,0:T(8,128)(2,1)S(1)}, bf16[432,128]{1,0:T(8,128)(2,1)S(1)}, u32[]{:S(2)}, u32[]{:S(2)}) %collective-permute-start.18) | collective-permute-done | bytes 110624 | tf_op jit(solution)/shard_map/ppermute | solution.py:242
  88.2 1.1 %collective-permute-done.19 = bf16[432,128]{1,0:T(8,128)(2,1)S(1)} collective-permute-done((bf16[432,128]{1,0:T(8,128)(2,1)S(1)}, bf16[432,128]{1,0:T(8,128)(2,1)S(1)}, u32[]{:S(2)}, u32[]{:S(2)}) %collective-permute-start.19) | collective-permute-done | bytes 110624 | tf_op jit(solution)/shard_map/ppermute | solution.py:242
  89.3 0.1 add_convert_fusion.refs_0_
  89.4 0.1 collective-permute-start.22
  89.4 1.7 %collective-permute-start.21 = (bf16[432,128]{1,0:T(8,128)(2,1)S(1)}, bf16[432,128]{1,0:T(8,128)(2,1)S(1)}, u32[]{:S(2)}, u32[]{:S(2)}) collective-permute-start(bf16[432,128]{1,0:T(8,128)(2,1)S(1)} %add_convert_fusion.refs_0_), channel_id=1, source_target_pairs={{128,0},{192,64},{0,128},{64,192},{129,1},{193,65},{1,129},{65,193... | collective-permute-start | bytes 331784 | tf_op jit(solution)/shard_map/ppermute | solution.py:242
  91.2 0.9 collective-permute-start.20
  92.1 3.3 %collective-permute-done.22.refs_3_ = bf16[432,128]{1,0:T(8,128)(2,1)S(1)} collective-permute-done((bf16[432,128]{1,0:T(8,128)(2,1)S(1)}, bf16[432,128]{1,0:T(8,128)(2,1)S(1)}, u32[]{:S(2)}, u32[]{:S(2)}) %collective-permute-start.22) | collective-permute-done | bytes 110624 | tf_op jit(solution)/shard_map/ppermute | solution.py:242
  95.4 0.6 collective-permute-done.20.refs_1_
  96.1 0.1 pad_maximum_fusion
  96.1 5.7 %collective-permute-start.23 = (bf16[4,432,128]{2,1,0:T(8,128)(2,1)S(1)}, bf16[4,432,128]{2,1,0:T(8,128)(2,1)S(1)}, u32[]{:S(2)}, u32[]{:S(2)}) collective-permute-start(bf16[4,432,128]{2,1,0:T(8,128)(2,1)S(1)} %pad_maximum_fusion), channel_id=1, source_target_pairs={{0,1},{1,0},{2,3},{3,2},{4,5},{5,4},{6,7},{7,6},{8,9},{9,8},{10,11... | collective-permute-start | bytes 1327112 | tf_op jit(solution)/shard_map/ppermute | solution.py:237
  101.8 0.0 all-to-all-done.1
  101.8 0.1 reduce_sum.12
  101.9 0.1 collective-permute-start.12
  102.0 1.3 %collective-permute-done.12 = bf16[16,1024]{1,0:T(8,128)(2,1)S(1)} collective-permute-done((bf16[16,1024]{1,0:T(8,128)(2,1)S(1)}, bf16[16,1024]{1,0:T(8,128)(2,1)S(1)}, u32[]{:S(2)}, u32[]{:S(2)}) %collective-permute-start.12) | collective-permute-done | bytes 32800 | tf_op jit(solution)/shard_map/ppermute | solution.py:237
  103.3 0.6 fusion.1
  103.9 1.9 %finish.1 = (f32[432,512]{1,0:T(8,128)}, f32[432,512]{1,0:T(8,128)}) custom-call(s32[3]{0:T(128)S(1)} %pad_add_fusion.at_ref, bf16[432,128]{1,0:T(8,128)(2,1)S(1)} %add_convert_fusion.refs_0_, bf16[432,128]{1,0:T(8,128)(2,1)S(1)} %collective-permute-done.20.refs_1_, bf16[432,128]{1,0:T(8,128)(2,1)S(1)} %collective-permute-done.21.refs_2_, ...), custom_call_target="tpu_custom_call" | custom-call | tf_op jit(solution)/shard_map/finish/pallas_call | solution.py:224
  (10 shorter events, 0.1 us)
Async XLA Ops:
  1.4 6.6 %collective-permute-start = (bf16[16,1024]{1,0:T(8,128)(2,1)S(1)}, bf16[16,1024]{1,0:T(8,128)(2,1)S(1)}, u32[]{:S(2)}, u32[]{:S(2)}) collective-permute-start(bf16[16,1024]{1,0:T(8,128)(2,1)S(1)} %get-tuple-element.43), channel_id=1, source_target_pairs={{0,1},{1,0},{2,3},{3,2},{4,5},{5,4},{6,7},{7,6},{8,9},{9,8},{10,11... | collective-permute-start | bytes 98312 | tf_op jit(solution)/shard_map/ppermute | solution.py:237
  4.8 1.0 copy-start
  5.8 1.0 copy-start.1
  8.9 24.5 %all-to-all-start = ((bf16[8,2,16,1024]{3,2,1,0:T(8,128)(2,1)}), bf16[8,2,16,1024]{3,2,1,0:T(8,128)(2,1)S(1)}, u32[]{:S(2)}, u32[]{:S(2)}) async-start(bf16[8,2,16,1024]{3,2,1,0:T(8,128)(2,1)} %broadcast_in_dim.3), calls=%async_computation | async-start | bytes 1048576 | tf_op jit(solution)/shard_map/all_to_all | solution.py:267
  15.4 6.8 %collective-permute-start.1 = (bf16[432,128]{1,0:T(8,128)(2,1)S(1)}, bf16[432,128]{1,0:T(8,128)(2,1)S(1)}, u32[]{:S(2)}, u32[]{:S(2)}) collective-permute-start(bf16[432,128]{1,0:T(8,128)(2,1)S(1)} %get-tuple-element.24), channel_id=1, source_target_pairs={{2,0},{4,2},{6,4},{0,6},{3,1},{5,3},{7,5},{1,7},{10,8},{12,10},{14... | collective-permute-start | bytes 331784 | tf_op jit(solution)/shard_map/ppermute | solution.py:242
  17.8 5.5 %collective-permute-start.2 = (bf16[432,128]{1,0:T(8,128)(2,1)S(1)}, bf16[432,128]{1,0:T(8,128)(2,1)S(1)}, u32[]{:S(2)}, u32[]{:S(2)}) collective-permute-start(bf16[432,128]{1,0:T(8,128)(2,1)S(1)} %get-tuple-element.25), channel_id=1, source_target_pairs={{4,0},{6,2},{0,4},{2,6},{5,1},{7,3},{1,5},{3,7},{12,8},{14,10},{8,... | collective-permute-start | bytes 331784 | tf_op jit(solution)/shard_map/ppermute | solution.py:242
  18.4 8.3 %collective-permute-start.3 = (bf16[432,128]{1,0:T(8,128)(2,1)S(1)}, bf16[432,128]{1,0:T(8,128)(2,1)S(1)}, u32[]{:S(2)}, u32[]{:S(2)}) collective-permute-start(bf16[432,128]{1,0:T(8,128)(2,1)S(1)} %get-tuple-element.26), channel_id=1, source_target_pairs={{6,0},{0,2},{2,4},{4,6},{7,1},{1,3},{3,5},{5,7},{14,8},{8,10},{10,... | collective-permute-start | bytes 331784 | tf_op jit(solution)/shard_map/ppermute | solution.py:242
  35.9 6.2 %collective-permute-start.4 = (bf16[2,16,1024]{2,1,0:T(8,128)(2,1)S(1)}, bf16[2,16,1024]{2,1,0:T(8,128)(2,1)S(1)}, u32[]{:S(2)}, u32[]{:S(2)}) collective-permute-start(bf16[2,16,1024]{2,1,0:T(8,128)(2,1)S(1)} %get-tuple-element.28), channel_id=1, source_target_pairs={{6,0},{0,2},{2,4},{4,6},{7,1},{1,3},{3,5},{5,7},{14,8},{8,10},{10,... | collective-permute-start | bytes 196616 | tf_op jit(solution)/shard_map/ppermute | solution.py:242
  37.2 6.4 %collective-permute-start.5 = (bf16[2,16,1024]{2,1,0:T(8,128)(2,1)S(1)}, bf16[2,16,1024]{2,1,0:T(8,128)(2,1)S(1)}, u32[]{:S(2)}, u32[]{:S(2)}) collective-permute-start(bf16[2,16,1024]{2,1,0:T(8,128)(2,1)S(1)} %get-tuple-element.29), channel_id=1, source_target_pairs={{4,0},{6,2},{0,4},{2,6},{5,1},{7,3},{1,5},{3,7},{12,8},{14,10},{8,... | collective-permute-start | bytes 196616 | tf_op jit(solution)/shard_map/ppermute | solution.py:242
  39.6 3.9 %collective-permute-start.6 = (bf16[2,16,1024]{2,1,0:T(8,128)(2,1)S(1)}, bf16[2,16,1024]{2,1,0:T(8,128)(2,1)S(1)}, u32[]{:S(2)}, u32[]{:S(2)}) collective-permute-start(bf16[2,16,1024]{2,1,0:T(8,128)(2,1)S(1)} %get-tuple-element.30), channel_id=1, source_target_pairs={{2,0},{4,2},{6,4},{0,6},{3,1},{5,3},{7,5},{1,7},{10,8},{12,10},{14... | collective-permute-start | bytes 196616 | tf_op jit(solution)/shard_map/ppermute | solution.py:242
  40.8 21.9 %collective-permute-start.11 = (bf16[4,432,128]{2,1,0:T(8,128)(2,1)S(1)}, bf16[4,432,128]{2,1,0:T(8,128)(2,1)S(1)}, u32[]{:S(2)}, u32[]{:S(2)}) collective-permute-start(bf16[4,432,128]{2,1,0:T(8,128)(2,1)S(1)} %get-tuple-element.32), channel_id=1, source_target_pairs={{0,1},{1,0},{2,3},{3,2},{4,5},{5,4},{6,7},{7,6},{8,9},{9,8},{10,11... | collective-permute-start | bytes 1327112 | tf_op jit(solution)/shard_map/ppermute | solution.py:237
  42.1 27.6 %collective-permute-start.14 = (bf16[8,2,16,1024]{3,2,1,0:T(8,128)(2,1)S(1)}, bf16[8,2,16,1024]{3,2,1,0:T(8,128)(2,1)S(1)}, u32[]{:S(2)}, u32[]{:S(2)}) collective-permute-start(bf16[8,2,16,1024]{3,2,1,0:T(8,128)(2,1)S(1)} %all-to-all-done.mine_ref), channel_id=1, source_target_pairs={{2,0},{4,2},{6,4},{0,6},{3,1},{5,3},{7,5},{1,7},{10,8},{12,10},{14... | collective-permute-start | bytes 1572872 | tf_op jit(solution)/shard_map/ppermute | solution.py:242
  42.1 28.9 %collective-permute-start.13 = (bf16[8,2,16,1024]{3,2,1,0:T(8,128)(2,1)S(1)}, bf16[8,2,16,1024]{3,2,1,0:T(8,128)(2,1)S(1)}, u32[]{:S(2)}, u32[]{:S(2)}) collective-permute-start(bf16[8,2,16,1024]{3,2,1,0:T(8,128)(2,1)S(1)} %all-to-all-done.mine_ref), channel_id=1, source_target_pairs={{6,0},{0,2},{2,4},{4,6},{7,1},{1,3},{3,5},{5,7},{14,8},{8,10},{10,... | collective-permute-start | bytes 1572872 | tf_op jit(solution)/shard_map/ppermute | solution.py:242
  43.6 2.4 %collective-permute-start.7 = (f32[2,16,1024]{2,1,0:T(8,128)S(1)}, f32[2,16,1024]{2,1,0:T(8,128)S(1)}, u32[]{:S(2)}, u32[]{:S(2)}) collective-permute-start(f32[2,16,1024]{2,1,0:T(8,128)S(1)} %add_add_fusion.own_ref), channel_id=1, source_target_pairs={{0,1},{1,0},{2,3},{3,2},{4,5},{5,4},{6,7},{7,6},{8,9},{9,8},{10,11... | collective-permute-start | bytes 393224 | tf_op jit(solution)/shard_map/ppermute | solution.py:237
  46.6 12.9 %collective-permute-start.10 = (bf16[2,16,1024]{2,1,0:T(8,128)(2,1)S(1)}, bf16[2,16,1024]{2,1,0:T(8,128)(2,1)S(1)}, u32[]{:S(2)}, u32[]{:S(2)}) collective-permute-start(bf16[2,16,1024]{2,1,0:T(8,128)(2,1)S(1)} %get-tuple-element.31.refs_0_), channel_id=1, source_target_pairs={{6,0},{0,2},{2,4},{4,6},{7,1},{1,3},{3,5},{5,7},{14,8},{8,10},{10,... | collective-permute-start | bytes 196616 | tf_op jit(solution)/shard_map/ppermute | solution.py:242
  47.5 12.1 %collective-permute-start.9 = (bf16[2,16,1024]{2,1,0:T(8,128)(2,1)S(1)}, bf16[2,16,1024]{2,1,0:T(8,128)(2,1)S(1)}, u32[]{:S(2)}, u32[]{:S(2)}) collective-permute-start(bf16[2,16,1024]{2,1,0:T(8,128)(2,1)S(1)} %get-tuple-element.31.refs_0_), channel_id=1, source_target_pairs={{4,0},{6,2},{0,4},{2,6},{5,1},{7,3},{1,5},{3,7},{12,8},{14,10},{8,... | collective-permute-start | bytes 196616 | tf_op jit(solution)/shard_map/ppermute | solution.py:242
  59.6 3.1 %collective-permute-start.8 = (bf16[2,16,1024]{2,1,0:T(8,128)(2,1)S(1)}, bf16[2,16,1024]{2,1,0:T(8,128)(2,1)S(1)}, u32[]{:S(2)}, u32[]{:S(2)}) collective-permute-start(bf16[2,16,1024]{2,1,0:T(8,128)(2,1)S(1)} %get-tuple-element.31.refs_0_), channel_id=1, source_target_pairs={{2,0},{4,2},{6,4},{0,6},{3,1},{5,3},{7,5},{1,7},{10,8},{12,10},{14... | collective-permute-start | bytes 196616 | tf_op jit(solution)/shard_map/ppermute | solution.py:242
  66.2 35.6 %all-to-all-start.1 = ((bf16[8,2,16,1024]{3,2,1,0:T(8,128)(2,1)}), bf16[8,2,16,1024]{3,2,1,0:T(8,128)(2,1)S(1)}, u32[]{:S(2)}, u32[]{:S(2)}) async-start(bf16[8,2,16,1024]{3,2,1,0:T(8,128)(2,1)} %conv_out.1), calls=%async_computation.1 | async-start | bytes 1048576 | tf_op jit(solution)/shard_map/all_to_all | solution.py:293
  69.7 6.1 %collective-permute-start.16 = (bf16[4,2,16,1024]{3,2,1,0:T(8,128)(2,1)S(1)}, bf16[4,2,16,1024]{3,2,1,0:T(8,128)(2,1)S(1)}, u32[]{:S(2)}, u32[]{:S(2)}) collective-permute-start(bf16[4,2,16,1024]{3,2,1,0:T(8,128)(2,1)S(1)} %slice.21), channel_id=1, source_target_pairs={{2,0},{4,2},{6,4},{0,6},{3,1},{5,3},{7,5},{1,7},{10,8},{12,10},{14... | collective-permute-start | bytes 786440 | tf_op jit(solution)/shard_map/ppermute | solution.py:242
  71.0 7.3 %collective-permute-start.15 = (bf16[4,2,16,1024]{3,2,1,0:T(8,128)(2,1)S(1)}, bf16[4,2,16,1024]{3,2,1,0:T(8,128)(2,1)S(1)}, u32[]{:S(2)}, u32[]{:S(2)}) collective-permute-start(bf16[4,2,16,1024]{3,2,1,0:T(8,128)(2,1)S(1)} %slice.20), channel_id=1, source_target_pairs={{6,0},{0,2},{2,4},{4,6},{7,1},{1,3},{3,5},{5,7},{14,8},{8,10},{10,... | collective-permute-start | bytes 786440 | tf_op jit(solution)/shard_map/ppermute | solution.py:242
  80.2 5.7 %collective-permute-start.17 = (bf16[432,128]{1,0:T(8,128)(2,1)S(1)}, bf16[432,128]{1,0:T(8,128)(2,1)S(1)}, u32[]{:S(2)}, u32[]{:S(2)}) collective-permute-start(bf16[432,128]{1,0:T(8,128)(2,1)S(1)} %get-tuple-element.35), channel_id=1, source_target_pairs={{64,0},{128,64},{192,128},{0,192},{65,1},{129,65},{193,129},{1,193... | collective-permute-start | bytes 331784 | tf_op jit(solution)/shard_map/ppermute | solution.py:242
  83.0 5.2 %collective-permute-start.18 = (bf16[432,128]{1,0:T(8,128)(2,1)S(1)}, bf16[432,128]{1,0:T(8,128)(2,1)S(1)}, u32[]{:S(2)}, u32[]{:S(2)}) collective-permute-start(bf16[432,128]{1,0:T(8,128)(2,1)S(1)} %get-tuple-element.36), channel_id=1, source_target_pairs={{128,0},{192,64},{0,128},{64,192},{129,1},{193,65},{1,129},{65,193... | collective-permute-start | bytes 331784 | tf_op jit(solution)/shard_map/ppermute | solution.py:242
  83.3 5.9 %collective-permute-start.19 = (bf16[432,128]{1,0:T(8,128)(2,1)S(1)}, bf16[432,128]{1,0:T(8,128)(2,1)S(1)}, u32[]{:S(2)}, u32[]{:S(2)}) collective-permute-start(bf16[432,128]{1,0:T(8,128)(2,1)S(1)} %get-tuple-element.37), channel_id=1, source_target_pairs={{192,0},{0,64},{64,128},{128,192},{193,1},{1,65},{65,129},{129,193... | collective-permute-start | bytes 331784 | tf_op jit(solution)/shard_map/ppermute | solution.py:242
  89.4 6.1 %collective-permute-start.22 = (bf16[432,128]{1,0:T(8,128)(2,1)S(1)}, bf16[432,128]{1,0:T(8,128)(2,1)S(1)}, u32[]{:S(2)}, u32[]{:S(2)}) collective-permute-start(bf16[432,128]{1,0:T(8,128)(2,1)S(1)} %add_convert_fusion.refs_0_), channel_id=1, source_target_pairs={{192,0},{0,64},{64,128},{128,192},{193,1},{1,65},{65,129},{129,193... | collective-permute-start | bytes 331784 | tf_op jit(solution)/shard_map/ppermute | solution.py:242
  89.4 6.0 %collective-permute-start.21 = (bf16[432,128]{1,0:T(8,128)(2,1)S(1)}, bf16[432,128]{1,0:T(8,128)(2,1)S(1)}, u32[]{:S(2)}, u32[]{:S(2)}) collective-permute-start(bf16[432,128]{1,0:T(8,128)(2,1)S(1)} %add_convert_fusion.refs_0_), channel_id=1, source_target_pairs={{128,0},{192,64},{0,128},{64,192},{129,1},{193,65},{1,129},{65,193... | collective-permute-start | bytes 331784 | tf_op jit(solution)/shard_map/ppermute | solution.py:242
  91.2 4.9 %collective-permute-start.20 = (bf16[432,128]{1,0:T(8,128)(2,1)S(1)}, bf16[432,128]{1,0:T(8,128)(2,1)S(1)}, u32[]{:S(2)}, u32[]{:S(2)}) collective-permute-start(bf16[432,128]{1,0:T(8,128)(2,1)S(1)} %add_convert_fusion.refs_0_), channel_id=1, source_target_pairs={{64,0},{128,64},{192,128},{0,192},{65,1},{129,65},{193,129},{1,193... | collective-permute-start | bytes 331784 | tf_op jit(solution)/shard_map/ppermute | solution.py:242
  96.1 7.8 %collective-permute-start.23 = (bf16[4,432,128]{2,1,0:T(8,128)(2,1)S(1)}, bf16[4,432,128]{2,1,0:T(8,128)(2,1)S(1)}, u32[]{:S(2)}, u32[]{:S(2)}) collective-permute-start(bf16[4,432,128]{2,1,0:T(8,128)(2,1)S(1)} %pad_maximum_fusion), channel_id=1, source_target_pairs={{0,1},{1,0},{2,3},{3,2},{4,5},{5,4},{6,7},{7,6},{8,9},{9,8},{10,11... | collective-permute-start | bytes 1327112 | tf_op jit(solution)/shard_map/ppermute | solution.py:237
  101.9 1.4 %collective-permute-start.12 = (bf16[16,1024]{1,0:T(8,128)(2,1)S(1)}, bf16[16,1024]{1,0:T(8,128)(2,1)S(1)}, u32[]{:S(2)}, u32[]{:S(2)}) collective-permute-start(bf16[16,1024]{1,0:T(8,128)(2,1)S(1)} %select_bitcast_fusion), channel_id=1, source_target_pairs={{0,1},{1,0},{2,3},{3,2},{4,5},{5,4},{6,7},{7,6},{8,9},{9,8},{10,11... | collective-permute-start | bytes 98312 | tf_op jit(solution)/shard_map/ppermute | solution.py:237

commit v4 on v2

--- a/solution.py
+++ b/solution.py
@@ -62,18 +62,19 @@
             col_ref[at : at + width, :] = term.astype(BF16)
 
 
-def regroup_kernel(at_ref, one_ref, two_ref, out_ref):
+def regroup_kernel(at_ref, one_ref, two_ref, *out_refs):
     channels = one_ref.shape[1]
     width = channels // (NX * NZ)
     group = NZ * width
-    old = lax.broadcasted_iota(jnp.int32, (channels, channels), 0)
-    new = lax.broadcasted_iota(jnp.int32, (channels, channels), 1)
-    home = ((new % group) // width) * (NX * width) + (new // group) * width + new % width
-    order = (old == home).astype(F32).astype(BF16)
+    old = lax.broadcasted_iota(jnp.int32, (channels, group), 0)
+    new = lax.broadcasted_iota(jnp.int32, (channels, group), 1)
 
     def run(ref):
-        for x in range(NX):
-            out_ref[x] = dot(ref[...], order[:, x * group : (x + 1) * group], ((1,), (0,))).astype(BF16)
+        for k in range(NX):
+            x = lax.rem(at_ref[1] + k, NX)
+            home = (new // width) * (NX * width) + x * width + new % width
+            order = (old == home).astype(F32).astype(BF16)
+            out_refs[k][...] = dot(ref[...], order, ((1,), (0,))).astype(BF16)
 
     @pl.when(at_ref[0] == 0)
     def _():
@@ -130,7 +131,8 @@
         keep_ref[d] = jnp.where(first, act, hidden).astype(BF16)
 
 
-def grad_kernel(at_ref, keep_ref, whole_ref, grad_ref, col):
+def grad_kernel(at_ref, keep_ref, whole_ref, *refs):
+    out_refs, (col, full) = refs[:4], refs[4:]
     width = keep_ref.shape[1]
     third = 9 * width
     ok = masks(width)
@@ -142,9 +144,9 @@
         zero = dot(col[...], whole_ref[0], ((1,), (1,)))
         last = dot(col[...], whole_ref[1], ((1,), (1,)))
         low, high = (last, zero) if sign > 0 else (zero, last)
-        grad_ref[0:third, :] = low[0:third].astype(BF16)
-        grad_ref[third : 2 * third, :] = (low[third:] + high[0:third]).astype(BF16)
-        grad_ref[2 * third :, :] = high[third:].astype(BF16)
+        full[0:third, :] = low[0:third].astype(BF16)
+        full[third : 2 * third, :] = (low[third:] + high[0:third]).astype(BF16)
+        full[2 * third :, :] = high[third:].astype(BF16)
 
     @pl.when(at_ref[0] == 0)
     def _():
@@ -153,6 +155,30 @@
     @pl.when(at_ref[0] == 1)
     def _():
         run(1)
+
+    quarter = full.shape[1] // 4
+    for k in range(4):
+        columns = pl.ds(pl.multiple_of(lax.rem(at_ref[2] + k, 4) * quarter, quarter), quarter)
+        out_refs[k][...] = full[:, columns]
+
+
+def finish_kernel(at_ref, *refs):
+    own_refs, other_ref, (one_ref, two_ref) = refs[:4], refs[4], refs[5:]
+    quarter = other_ref.shape[2]
+
+    def run(own_out, other_out):
+        for k in range(4):
+            columns = pl.ds(pl.multiple_of(lax.rem(at_ref[2] + k, 4) * quarter, quarter), quarter)
+            own_out[:, columns] = own_refs[k][...].astype(F32)
+            other_out[:, columns] = other_ref[k].astype(F32)
+
+    @pl.when(at_ref[0] == 0)
+    def _():
+        run(one_ref, two_ref)
+
+    @pl.when(at_ref[0] == 1)
+    def _():
+        run(two_ref, one_ref)
 
 
 def second_kernel(at_ref, *refs):
@@ -207,77 +233,65 @@
 
 def body(features, conv_one, conv_two, cotangent):
     width, channels = conv_one.shape[1], conv_one.shape[2]
-    core = lax.axis_index("spatial")
-    x = lax.axis_index("x")
-    first = core == 0
-    at = jnp.stack([core, x]).astype(jnp.int32)
+    at = jnp.stack([lax.axis_index(a) for a in ("spatial", "x", "samples")]).astype(jnp.int32)
     one = conv_one.reshape(27 * width, channels)
     two = conv_two.reshape(27 * width, channels)
-    features = features.reshape(width, PLANE)
-    cotangent = cotangent.reshape(width, PLANE)
     taps = 27 * width
     group = NZ * width
-
-    came = swap(jnp.where(first, cotangent, features))
-    kept = jnp.where(first, features, cotangent)
-    block = jnp.where(first, jnp.stack([kept, came]), jnp.stack([came, kept]))
-    mine = lax.all_to_all(jnp.broadcast_to(block, (NZ,) + block.shape), "z", 0, 0, tiled=True)
-
-    (groups,) = call(regroup_kernel, [((NX, taps, group), BF16)], [], "regroup", 2 * taps * channels * channels, at, one, two)
-
-    def group_for(step):
-        return lax.dynamic_index_in_dim(groups, lax.rem(x + step, NX), 0, keepdims=False)
-
-    kernels = [group_for(0)] + [around(group_for(NX - k), "x", k) for k in range(1, NX)]
+    quarter = channels // 4
+    plane = (2, width, PLANE)
+    everyone = (2 * NZ, width, PLANE)
+    work = 4 * 18 * width * channels * PLANE
+
+    pair = jnp.stack([features.reshape(width, PLANE), cotangent.reshape(width, PLANE)])
+    pair = jnp.broadcast_to(pair, (NZ,) + plane).reshape(everyone)
+    mine = lax.all_to_all(pair, ("z", "spatial"), 0, 0, tiled=True).reshape((NZ,) + plane)
+
+    groups = call(regroup_kernel, [((taps, group), BF16)] * NX, [], "regroup", 2 * taps * channels * channels, at, one, two)
+    kernels = [groups[0]] + [around(groups[NX - k], "x", k) for k in range(1, NX)]
+    mine, kernels = lax.optimization_barrier((mine, kernels))
 
     left = around(mine, "x", -1)
     right = around(mine, "x", 1)
     far0 = around(left[: NZ // 2], "x", -1)
     far1 = around(right[NZ // 2 :], "x", 1)
 
-    plane = (2, width, PLANE)
     own, whole = call(
         first_kernel,
         [(plane, F32), ((2, channels, PLANE), BF16)],
         [((18 * width, PLANE), F32)] * 2,
-        "conv_in",
-        4 * 18 * width * channels * PLANE,
-        at, mine, left, right, far0, far1, one, two,
+        "conv_in", work, at, mine, left, right, far0, far1, one, two,
     )
     other = swap(own)
     send, keep = call(act_kernel, [(plane, BF16)] * 2, [], "act", 0, at, own, other)
     acts = [send] + [around(send, "x", k) for k in range(1, NX)]
-    (grad,) = call(
+    grads = call(
         grad_kernel,
-        [((taps, channels), BF16)],
-        [((18 * width, PLANE), BF16)],
-        "grad",
-        4 * 18 * width * channels * PLANE,
-        at, keep, whole,
+        [((taps, quarter), BF16)] * 4,
+        [((18 * width, PLANE), BF16), ((taps, channels), BF16)],
+        "grad", work, at, keep, whole,
     )
     (parts,) = call(
         second_kernel,
         [((NZ,) + plane, BF16)],
         [((NX * 18 * width, PLANE), BF16), ((NX * 18 * width, group), BF16)],
-        "conv_out",
-        4 * 18 * width * channels * PLANE,
-        at, *acts, *kernels,
-    )
-    parts = lax.all_to_all(parts, "z", 0, 0, tiled=True)
-
-    grads = [grad] + [around(grad, "samples", k) for k in (1, 2, 3)]
-    summed = sum(g.astype(F32) for g in grads).astype(BF16)
-    summed_other = swap(summed)
-
-    result = jnp.sum(parts.astype(F32), axis=0).astype(BF16)
-    ours = jnp.where(first, result[0], result[1])
-    theirs = swap(jnp.where(first, result[1], result[0]))
+        "conv_out", work, at, *acts, *kernels,
+    )
+    parts = lax.all_to_all(parts.reshape(everyone), ("z", "spatial"), 0, 0, tiled=True)
+
+    pieces = [grads[0]] + [around(grads[4 - k], "samples", k) for k in (1, 2, 3)]
+    summed = sum(g.astype(F32) for g in pieces).astype(BF16)
+    pieces = [summed] + [around(summed, "samples", k) for k in (1, 2, 3)]
+    others = swap(jnp.stack(pieces))
+    grad_one, grad_two = call(
+        finish_kernel, [((taps, channels), F32)] * 2, [], "finish", 0, at, *pieces, others
+    )
+    parts, grad_one, grad_two = lax.optimization_barrier((parts, grad_one, grad_two))
+
+    result = jnp.sum(parts.reshape((NZ,) + plane).astype(F32), axis=0).astype(BF16)
     shape = (width, 1, 1, PLANE)
-    mixed_out = jnp.where(first, ours, theirs).reshape(shape)
-    input_grad = jnp.where(first, theirs, ours).reshape(shape)
-    grad_one = jnp.where(first, summed, summed_other).astype(F32).reshape(27, width, channels)
-    grad_two = jnp.where(first, summed_other, summed).astype(F32).reshape(27, width, channels)
-    return mixed_out, input_grad, grad_one, grad_two
+    weights = (27, width, channels)
+    return result[0].reshape(shape), result[1].reshape(shape), grad_one.reshape(weights), grad_two.reshape(weights)
 
 
 def solution(mesh):

time: 95.8 us -> 95.5 us (level)
  blocking collectives: 23 us -> 0 us
  waiting for transfers between devices: 28.5 us -> 41.2 us
  starting transfers between devices: 30.2 us -> 37.6 us
  local copies, waits for them, and re-layouts: 0.13 us -> 3.56 us
  other arithmetic: 3.99 us -> 1.13 us
  Pallas kernels: 8.89 us -> 10.8 us
    all_to_all x1 -> x0, blocking collectives: 23 us -> none  [body(): lax.all_to_all(jnp.broadcast_to(block, (NZ,) + block.shape), 'z', 0, 0, t...]
    all_to_all x1 -> x2, starting transfers between devices: 3.49 us -> 15 us  [the longest x1 9.98 us: body(): lax.all_to_all(pair, ('z', 'spatial'), 0, 0, tiled=True)]
    ppermute x4 -> x2, starting transfers between devices: 10.3 us -> 2.46 us  [swap(): return lax.ppermute(values, 'spatial', [(0, 1), (1, 0)])]
    all_to_all x1 -> x2, waiting for transfers between devices: 0.01 us -> 6.69 us  [the longest x1 4.07 us: body(): lax.all_to_all(parts.reshape(everyone), ('z', 'spatial'), 0, 0, tiled=True)]
    ppermute x13 -> x16, waiting for transfers between devices: 27.6 us -> 32.1 us  [around(): lax.ppermute(values, axis, [((i + step) % size, i) for i in range(size)])]
    ppermute x13 -> x16, starting transfers between devices: 16.4 us -> 20.2 us  [around(): lax.ppermute(values, axis, [((i + step) % size, i) for i in range(size)])]
    reshape x3 -> x0, other arithmetic: 2.67 us -> none  [the longest x1 1.02 us: body(): jnp.where(first, summed, summed_other).astype(F32)]
    unnamed x4 -> x8, local copies, waits for them, and re-layouts: 0.01 us -> 2.04 us
  transfers between devices with their start and end apart: 18 -> 20, of which waited for: 6 -> 13; matrix products, arithmetic and copies ran while one was open for 3% -> 0% of each run, Pallas kernels for 8% -> 9%
where the time goes in v4:
time: 95.5 us; the launch traced here: 95.1 us
  waiting for transfers between devices  41.2 us (43%)
  starting transfers between devices  37.6 us (39%)
  Pallas kernels  10.8 us (11%)
  local copies, waits for them, and re-layouts  3.56 us (4%)
  other arithmetic  1.13 us (1%)
    ppermute x16, waiting for transfers between devices, around(): lax.ppermute(values, axis, [((i + step) % size, i) for i in range(size)])  32.1 us
    ppermute x16, starting transfers between devices, around(): lax.ppermute(values, axis, [((i + step) % size, i) for i in range(size)])  20.2 us
    pallas_call x6, Pallas kernels, call(): pl.pallas_call(kernel, out_shape=tuple((jax.ShapeDtypeStruct(s, t) for s,...  10.8 us
    all_to_all x1, starting transfers between devices, body(): lax.all_to_all(pair, ('z', 'spatial'), 0, 0, tiled=True)  9.98 us
    all_to_all x1, starting transfers between devices, body(): lax.all_to_all(parts.reshape(everyone), ('z', 'spatial'), 0, 0, tiled=True)  4.99 us
    all_to_all x1, waiting for transfers between devices, body(): lax.all_to_all(parts.reshape(everyone), ('z', 'spatial'), 0, 0, tiled=True)  4.07 us
    all_to_all x1, waiting for transfers between devices, body(): lax.all_to_all(pair, ('z', 'spatial'), 0, 0, tiled=True)  2.62 us
    ppermute x2, starting transfers between devices, swap(): return lax.ppermute(values, 'spatial', [(0, 1), (1, 0)])  2.46 us
  transfers between devices with their start and end apart: 20, of which 13 were waited for; matrix products, arithmetic and copies ran while one was open for 0% of the time, Pallas kernels for 9%

profile of v4, /device:TPU:1, one launch (start us, length us, event | category | flops | bytes accessed | tf_op | source)
XLA Modules:
  0.0 95.1 jit_solution(10824993936470814410)
XLA Ops:
  0.6 0.0 copy-start.3
  0.6 0.0 copy-start.1
  0.7 0.9 pad_maximum_fusion.1
  1.5 0.9 broadcast_in_dim.3
  2.4 10.0 %all-to-all-start = ((bf16[16,16,1024]{2,1,0:T(8,128)(2,1)}), bf16[16,16,1024]{2,1,0:T(8,128)(2,1)S(1)}, u32[]{:S(2)}, u32[]{:S(2)}) async-start(bf16[16,16,1024]{2,1,0:T(8,128)(2,1)} %bitcast.5), calls=%async_computation | async-start | bytes 1048576 | tf_op jit(solution)/shard_map/all_to_all | solution.py:248
  12.3 0.1 pad_add_fusion.at_ref
  12.4 0.0 copy-start
  12.4 1.0 %copy-done = bf16[27,16,512]{2,1,0:T(8,128)(2,1)S(1)} copy-done((bf16[27,16,512]{2,1,0:T(8,128)(2,1)S(1)}, bf16[27,16,512]{2,1,0:T(8,128)(2,1)}, u32[]{:S(2)}) %copy-start) | copy-done | bytes 442392
  13.4 0.0 copy-start.2
  13.4 1.0 %copy-done.2 = bf16[27,16,512]{2,1,0:T(8,128)(2,1)S(1)} copy-done((bf16[27,16,512]{2,1,0:T(8,128)(2,1)S(1)}, bf16[27,16,512]{2,1,0:T(8,128)(2,1)}, u32[]{:S(2)}) %copy-start.2) | copy-done | bytes 442392
  14.5 1.2 %regroup.1 = (bf16[432,128]{1,0:T(8,128)(2,1)S(1)}, bf16[432,128]{1,0:T(8,128)(2,1)S(1)}, bf16[432,128]{1,0:T(8,128)(2,1)S(1)}, bf16[432,128]{1,0:T(8,128)(2,1)S(1)}) custom-call(s32[3]{0:T(128)S(1)} %pad_add_fusion.at_ref, bf16[432,512]{1,0:T(8,128)(2,1)S(1)} %bitcast.24, bf16[432,512]{1,0:T(8,128)(2,1)S(1)} %bitcast.26), custom_call_target="tpu_custom_call" | custom-call | flops 226492416 | tf_op jit(solution)/shard_map/regroup/pallas_call | solution.py:213
  15.6 2.6 %collective-permute-start = (bf16[432,128]{1,0:T(8,128)(2,1)S(1)}, bf16[432,128]{1,0:T(8,128)(2,1)S(1)}, u32[]{:S(2)}, u32[]{:S(2)}) collective-permute-start(bf16[432,128]{1,0:T(8,128)(2,1)S(1)} %get-tuple-element.27), channel_id=1, source_target_pairs={{2,0},{4,2},{6,4},{0,6},{3,1},{5,3},{7,5},{1,7},{10,8},{12,10},{14... | collective-permute-start | bytes 331784 | tf_op jit(solution)/shard_map/ppermute | solution.py:231
  18.2 0.5 collective-permute-start.1
  18.7 0.6 collective-permute-start.2
  19.3 3.4 %collective-permute-done.refs_5_ = bf16[432,128]{1,0:T(8,128)(2,1)S(1)} collective-permute-done((bf16[432,128]{1,0:T(8,128)(2,1)S(1)}, bf16[432,128]{1,0:T(8,128)(2,1)S(1)}, u32[]{:S(2)}, u32[]{:S(2)}) %collective-permute-start) | collective-permute-done | bytes 110624 | tf_op jit(solution)/shard_map/ppermute | solution.py:231
  22.7 1.2 %collective-permute-done.1.refs_6_ = bf16[432,128]{1,0:T(8,128)(2,1)S(1)} collective-permute-done((bf16[432,128]{1,0:T(8,128)(2,1)S(1)}, bf16[432,128]{1,0:T(8,128)(2,1)S(1)}, u32[]{:S(2)}, u32[]{:S(2)}) %collective-permute-start.1) | collective-permute-done | bytes 110624 | tf_op jit(solution)/shard_map/ppermute | solution.py:231
  23.9 3.1 %collective-permute-done.2.refs_7_ = bf16[432,128]{1,0:T(8,128)(2,1)S(1)} collective-permute-done((bf16[432,128]{1,0:T(8,128)(2,1)S(1)}, bf16[432,128]{1,0:T(8,128)(2,1)S(1)}, u32[]{:S(2)}, u32[]{:S(2)}) %collective-permute-start.2) | collective-permute-done | bytes 110624 | tf_op jit(solution)/shard_map/ppermute | solution.py:231
  27.0 2.6 %all-to-all-done = bf16[16,16,1024]{2,1,0:T(8,128)(2,1)S(1)} async-done(((bf16[16,16,1024]{2,1,0:T(8,128)(2,1)}), bf16[16,16,1024]{2,1,0:T(8,128)(2,1)S(1)}, u32[]{:S(2)}, u32[]{:S(2)}) %all-to-all-start) | async-done | bytes 524320 | tf_op jit(solution)/shard_map/all_to_all | solution.py:248
  29.7 2.5 %collective-permute-start.4 = (bf16[8,2,16,1024]{3,2,1,0:T(8,128)(2,1)S(1)}, bf16[8,2,16,1024]{3,2,1,0:T(8,128)(2,1)S(1)}, u32[]{:S(2)}, u32[]{:S(2)}) collective-permute-start(bf16[8,2,16,1024]{3,2,1,0:T(8,128)(2,1)S(1)} %bitcast.21), channel_id=1, source_target_pairs={{2,0},{4,2},{6,4},{0,6},{3,1},{5,3},{7,5},{1,7},{10,8},{12,10},{14... | collective-permute-start | bytes 1572872 | tf_op jit(solution)/shard_map/ppermute | solution.py:231
  32.1 0.0 collective-permute-start.3
  32.2 11.0 %collective-permute-done.4.right_ref = bf16[8,2,16,1024]{3,2,1,0:T(8,128)(2,1)S(1)} collective-permute-done((bf16[8,2,16,1024]{3,2,1,0:T(8,128)(2,1)S(1)}, bf16[8,2,16,1024]{3,2,1,0:T(8,128)(2,1)S(1)}, u32[]{:S(2)}, u32[]{:S(2)}) %collective-permute-start.4) | collective-permute-done | bytes 524320 | tf_op jit(solution)/shard_map/ppermute | solution.py:231
  43.2 3.2 %collective-permute-start.6 = (bf16[4,2,16,1024]{3,2,1,0:T(8,128)(2,1)S(1)}, bf16[4,2,16,1024]{3,2,1,0:T(8,128)(2,1)S(1)}, u32[]{:S(2)}, u32[]{:S(2)}) collective-permute-start(bf16[4,2,16,1024]{3,2,1,0:T(8,128)(2,1)S(1)} %slice.17), channel_id=1, source_target_pairs={{2,0},{4,2},{6,4},{0,6},{3,1},{5,3},{7,5},{1,7},{10,8},{12,10},{14... | collective-permute-start | bytes 786440 | tf_op jit(solution)/shard_map/ppermute | solution.py:231
  46.4 0.2 collective-permute-done.3.left_ref
  46.6 0.1 collective-permute-start.5
  46.7 5.5 %collective-permute-done.6.far1_ref = bf16[4,2,16,1024]{3,2,1,0:T(8,128)(2,1)S(1)} collective-permute-done((bf16[4,2,16,1024]{3,2,1,0:T(8,128)(2,1)S(1)}, bf16[4,2,16,1024]{3,2,1,0:T(8,128)(2,1)S(1)}, u32[]{:S(2)}, u32[]{:S(2)}) %collective-permute-start.6) | collective-permute-done | bytes 262176 | tf_op jit(solution)/shard_map/ppermute | solution.py:231
  52.1 3.3 %collective-permute-done.5.far0_ref = bf16[4,2,16,1024]{3,2,1,0:T(8,128)(2,1)S(1)} collective-permute-done((bf16[4,2,16,1024]{3,2,1,0:T(8,128)(2,1)S(1)}, bf16[4,2,16,1024]{3,2,1,0:T(8,128)(2,1)S(1)}, u32[]{:S(2)}, u32[]{:S(2)}) %collective-permute-start.5) | collective-permute-done | bytes 262176 | tf_op jit(solution)/shard_map/ppermute | solution.py:231
  55.4 0.0 copy-done.3
  55.5 0.0 copy-done.1
  55.5 1.7 %conv_in.1 = (f32[2,16,1024]{2,1,0:T(8,128)S(1)}, bf16[2,512,1024]{2,1,0:T(8,128)(2,1)S(1)}) custom-call(s32[3]{0:T(128)S(1)} %pad_add_fusion.at_ref, bf16[8,2,16,1024]{3,2,1,0:T(8,128)(2,1)S(1)} %bitcast.23, bf16[8,2,16,1024]{3,2,1,0:T(8,128)(2,1)S(1)} %collective-permute-done.3.left_ref, bf16[8,2,16,1024]{3,2,1,0:T(8,128)(2,1)S(1)} %collective-permute-done.4.right_ref, ...), custom_call_target="tpu_custom_call" | custom-call | flops 603979776 | tf_op jit(solution)/shard_map/conv_in/pallas_call | solution.py:213
  57.1 1.2 %collective-permute-start.7 = (f32[2,16,1024]{2,1,0:T(8,128)S(1)}, f32[2,16,1024]{2,1,0:T(8,128)S(1)}, u32[]{:S(2)}, u32[]{:S(2)}) collective-permute-start(f32[2,16,1024]{2,1,0:T(8,128)S(1)} %get-tuple-element.31.own_ref), channel_id=1, source_target_pairs={{0,1},{1,0},{2,3},{3,2},{4,5},{5,4},{6,7},{7,6},{8,9},{9,8},{10,11... | collective-permute-start | bytes 393224 | tf_op jit(solution)/shard_map/ppermute | solution.py:226
  58.4 1.0 %collective-permute-done.7.other_ref = f32[2,16,1024]{2,1,0:T(8,128)S(1)} collective-permute-done((f32[2,16,1024]{2,1,0:T(8,128)S(1)}, f32[2,16,1024]{2,1,0:T(8,128)S(1)}, u32[]{:S(2)}, u32[]{:S(2)}) %collective-permute-start.7) | collective-permute-done | bytes 131104 | tf_op jit(solution)/shard_map/ppermute | solution.py:226
  59.4 0.6 act.1
  60.0 0.1 collective-permute-start.10
  60.1 0.9 collective-permute-start.9
  61.0 1.8 %collective-permute-start.8 = (bf16[2,16,1024]{2,1,0:T(8,128)(2,1)S(1)}, bf16[2,16,1024]{2,1,0:T(8,128)(2,1)S(1)}, u32[]{:S(2)}, u32[]{:S(2)}) collective-permute-start(bf16[2,16,1024]{2,1,0:T(8,128)(2,1)S(1)} %get-tuple-element.32.refs_0_), channel_id=1, source_target_pairs={{2,0},{4,2},{6,4},{0,6},{3,1},{5,3},{7,5},{1,7},{10,8},{12,10},{14... | collective-permute-start | bytes 196616 | tf_op jit(solution)/shard_map/ppermute | solution.py:231
  62.8 1.9 %grad.1 = (bf16[432,128]{1,0:T(8,128)(2,1)S(1)}, bf16[432,128]{1,0:T(8,128)(2,1)S(1)}, bf16[432,128]{1,0:T(8,128)(2,1)S(1)}, bf16[432,128]{1,0:T(8,128)(2,1)S(1)}) custom-call(s32[3]{0:T(128)S(1)} %pad_add_fusion.at_ref, bf16[2,16,1024]{2,1,0:T(8,128)(2,1)S(1)} %get-tuple-element.37.keep_ref, bf16[2,512,1024]{2,1,0:T(8,128)(2,1)S(1)} %get-tuple-element.38.whole_ref), custom_call_target="tpu_custom_call" | custom-call | flops 603979776 | tf_op jit(solution)/shard_map/grad/pallas_call | solution.py:213
  64.7 2.8 %collective-permute-start.11 = (bf16[432,128]{1,0:T(8,128)(2,1)S(1)}, bf16[432,128]{1,0:T(8,128)(2,1)S(1)}, u32[]{:S(2)}, u32[]{:S(2)}) collective-permute-start(bf16[432,128]{1,0:T(8,128)(2,1)S(1)} %get-tuple-element.40), channel_id=1, source_target_pairs={{64,0},{128,64},{192,128},{0,192},{65,1},{129,65},{193,129},{1,193... | collective-permute-start | bytes 331784 | tf_op jit(solution)/shard_map/ppermute | solution.py:231
  67.5 0.3 collective-permute-start.12
  67.8 0.0 collective-permute-done.10.refs_3_
  67.8 0.7 collective-permute-start.13
  68.5 0.0 collective-permute-done.9.refs_2_
  68.5 0.0 collective-permute-done.8.refs_1_
  68.5 3.5 %conv_out.1 = bf16[8,2,16,1024]{3,2,1,0:T(8,128)(2,1)} custom-call(s32[3]{0:T(128)S(1)} %pad_add_fusion.at_ref, bf16[2,16,1024]{2,1,0:T(8,128)(2,1)S(1)} %get-tuple-element.32.refs_0_, bf16[2,16,1024]{2,1,0:T(8,128)(2,1)S(1)} %collective-permute-done.8.refs_1_, bf16[2,16,1024]{2,1,0:T(8,128)(2,1)S(1)} %collective-permute-done.9.refs_2_, ...), custom_call_target="tpu_custom_call" | custom-call | flops 603979776 | tf_op jit(solution)/shard_map/conv_out/pallas_call | solution.py:213
  72.0 5.0 %all-to-all-start.1 = ((bf16[16,16,1024]{2,1,0:T(8,128)(2,1)}), bf16[16,16,1024]{2,1,0:T(8,128)(2,1)S(1)}, u32[]{:S(2)}, u32[]{:S(2)}) async-start(bf16[16,16,1024]{2,1,0:T(8,128)(2,1)} %bitcast.9), calls=%async_computation.1 | async-start | bytes 1048576 | tf_op jit(solution)/shard_map/all_to_all | solution.py:280
  77.0 0.0 collective-permute-done.11
  77.0 0.0 collective-permute-done.12
  77.0 0.0 collective-permute-done.13
  77.0 0.1 add_convert_fusion.refs_0_
  77.1 1.7 %collective-permute-start.16 = (bf16[432,128]{1,0:T(8,128)(2,1)S(1)}, bf16[432,128]{1,0:T(8,128)(2,1)S(1)}, u32[]{:S(2)}, u32[]{:S(2)}) collective-permute-start(bf16[432,128]{1,0:T(8,128)(2,1)S(1)} %add_convert_fusion.refs_0_), channel_id=1, source_target_pairs={{192,0},{0,64},{64,128},{128,192},{193,1},{1,65},{65,129},{129,193... | collective-permute-start | bytes 331784 | tf_op jit(solution)/shard_map/ppermute | solution.py:231
  78.8 1.5 %collective-permute-start.15 = (bf16[432,128]{1,0:T(8,128)(2,1)S(1)}, bf16[432,128]{1,0:T(8,128)(2,1)S(1)}, u32[]{:S(2)}, u32[]{:S(2)}) collective-permute-start(bf16[432,128]{1,0:T(8,128)(2,1)S(1)} %add_convert_fusion.refs_0_), channel_id=1, source_target_pairs={{128,0},{192,64},{0,128},{64,192},{129,1},{193,65},{1,129},{65,193... | collective-permute-start | bytes 331784 | tf_op jit(solution)/shard_map/ppermute | solution.py:231
  80.3 0.9 collective-permute-start.14
  81.3 1.5 %collective-permute-done.16.refs_3_ = bf16[432,128]{1,0:T(8,128)(2,1)S(1)} collective-permute-done((bf16[432,128]{1,0:T(8,128)(2,1)S(1)}, bf16[432,128]{1,0:T(8,128)(2,1)S(1)}, u32[]{:S(2)}, u32[]{:S(2)}) %collective-permute-start.16) | collective-permute-done | bytes 110624 | tf_op jit(solution)/shard_map/ppermute | solution.py:231
  82.8 2.9 %collective-permute-done.15.refs_2_ = bf16[432,128]{1,0:T(8,128)(2,1)S(1)} collective-permute-done((bf16[432,128]{1,0:T(8,128)(2,1)S(1)}, bf16[432,128]{1,0:T(8,128)(2,1)S(1)}, u32[]{:S(2)}, u32[]{:S(2)}) %collective-permute-start.15) | collective-permute-done | bytes 110624 | tf_op jit(solution)/shard_map/ppermute | solution.py:231
  85.7 0.0 collective-permute-done.14.refs_1_
  85.7 0.1 pad_maximum_fusion
  85.7 1.2 %collective-permute-start.17 = (bf16[4,432,128]{2,1,0:T(8,128)(2,1)S(1)}, bf16[4,432,128]{2,1,0:T(8,128)(2,1)S(1)}, u32[]{:S(2)}, u32[]{:S(2)}) collective-permute-start(bf16[4,432,128]{2,1,0:T(8,128)(2,1)S(1)} %pad_maximum_fusion), channel_id=1, source_target_pairs={{0,1},{1,0},{2,3},{3,2},{4,5},{5,4},{6,7},{7,6},{8,9},{9,8},{10,11... | collective-permute-start | bytes 1327112 | tf_op jit(solution)/shard_map/ppermute | solution.py:226
  87.0 1.4 %collective-permute-done.17.refs_4_ = bf16[4,432,128]{2,1,0:T(8,128)(2,1)S(1)} collective-permute-done((bf16[4,432,128]{2,1,0:T(8,128)(2,1)S(1)}, bf16[4,432,128]{2,1,0:T(8,128)(2,1)S(1)}, u32[]{:S(2)}, u32[]{:S(2)}) %collective-permute-start.17) | collective-permute-done | bytes 442400 | tf_op jit(solution)/shard_map/ppermute | solution.py:226
  88.4 1.9 %finish.1 = (f32[432,512]{1,0:T(8,128)}, f32[432,512]{1,0:T(8,128)}) custom-call(s32[3]{0:T(128)S(1)} %pad_add_fusion.at_ref, bf16[432,128]{1,0:T(8,128)(2,1)S(1)} %add_convert_fusion.refs_0_, bf16[432,128]{1,0:T(8,128)(2,1)S(1)} %collective-permute-done.14.refs_1_, bf16[432,128]{1,0:T(8,128)(2,1)S(1)} %collective-permute-done.15.refs_2_, ...), custom_call_target="tpu_custom_call" | custom-call | tf_op jit(solution)/shard_map/finish/pallas_call | solution.py:213
  90.3 4.1 %all-to-all-done.1 = bf16[16,16,1024]{2,1,0:T(8,128)(2,1)S(1)} async-done(((bf16[16,16,1024]{2,1,0:T(8,128)(2,1)}), bf16[16,16,1024]{2,1,0:T(8,128)(2,1)S(1)}, u32[]{:S(2)}, u32[]{:S(2)}) %all-to-all-start.1) | async-done | bytes 524320 | tf_op jit(solution)/shard_map/all_to_all | solution.py:280
  94.4 0.1 reduce_sum.12
  94.4 0.6 slice_bitcast_fusion
  (2 shorter events, 0.0 us)
Async XLA Ops:
  0.6 54.8 %copy-start.3 = (bf16[27,16,512]{2,1,0:T(8,128)(2,1)S(1)}, bf16[27,16,512]{2,1,0:T(8,128)(2,1)}, u32[]{:S(2)}) copy-start(bf16[27,16,512]{2,1,0:T(8,128)(2,1)} %param.6) | copy-start | bytes 1327108
  0.6 54.8 %copy-start.1 = (bf16[27,16,512]{2,1,0:T(8,128)(2,1)S(1)}, bf16[27,16,512]{2,1,0:T(8,128)(2,1)}, u32[]{:S(2)}) copy-start(bf16[27,16,512]{2,1,0:T(8,128)(2,1)} %param.5) | copy-start | bytes 1327108
  2.4 27.3 %all-to-all-start = ((bf16[16,16,1024]{2,1,0:T(8,128)(2,1)}), bf16[16,16,1024]{2,1,0:T(8,128)(2,1)S(1)}, u32[]{:S(2)}, u32[]{:S(2)}) async-start(bf16[16,16,1024]{2,1,0:T(8,128)(2,1)} %bitcast.5), calls=%async_computation | async-start | bytes 1048576 | tf_op jit(solution)/shard_map/all_to_all | solution.py:248
  12.4 1.0 %copy-start = (bf16[27,16,512]{2,1,0:T(8,128)(2,1)S(1)}, bf16[27,16,512]{2,1,0:T(8,128)(2,1)}, u32[]{:S(2)}) copy-start(bf16[27,16,512]{2,1,0:T(8,128)(2,1)} %param.5) | copy-start | bytes 1327108
  13.4 1.0 %copy-start.2 = (bf16[27,16,512]{2,1,0:T(8,128)(2,1)S(1)}, bf16[27,16,512]{2,1,0:T(8,128)(2,1)}, u32[]{:S(2)}) copy-start(bf16[27,16,512]{2,1,0:T(8,128)(2,1)} %param.6) | copy-start | bytes 1327108
  15.6 7.1 %collective-permute-start = (bf16[432,128]{1,0:T(8,128)(2,1)S(1)}, bf16[432,128]{1,0:T(8,128)(2,1)S(1)}, u32[]{:S(2)}, u32[]{:S(2)}) collective-permute-start(bf16[432,128]{1,0:T(8,128)(2,1)S(1)} %get-tuple-element.27), channel_id=1, source_target_pairs={{2,0},{4,2},{6,4},{0,6},{3,1},{5,3},{7,5},{1,7},{10,8},{12,10},{14... | collective-permute-start | bytes 331784 | tf_op jit(solution)/shard_map/ppermute | solution.py:231
  18.2 5.7 %collective-permute-start.1 = (bf16[432,128]{1,0:T(8,128)(2,1)S(1)}, bf16[432,128]{1,0:T(8,128)(2,1)S(1)}, u32[]{:S(2)}, u32[]{:S(2)}) collective-permute-start(bf16[432,128]{1,0:T(8,128)(2,1)S(1)} %get-tuple-element.28), channel_id=1, source_target_pairs={{4,0},{6,2},{0,4},{2,6},{5,1},{7,3},{1,5},{3,7},{12,8},{14,10},{8,... | collective-permute-start | bytes 331784 | tf_op jit(solution)/shard_map/ppermute | solution.py:231
  18.7 8.3 %collective-permute-start.2 = (bf16[432,128]{1,0:T(8,128)(2,1)S(1)}, bf16[432,128]{1,0:T(8,128)(2,1)S(1)}, u32[]{:S(2)}, u32[]{:S(2)}) collective-permute-start(bf16[432,128]{1,0:T(8,128)(2,1)S(1)} %get-tuple-element.29), channel_id=1, source_target_pairs={{6,0},{0,2},{2,4},{4,6},{7,1},{1,3},{3,5},{5,7},{14,8},{8,10},{10,... | collective-permute-start | bytes 331784 | tf_op jit(solution)/shard_map/ppermute | solution.py:231
  29.7 13.5 %collective-permute-start.4 = (bf16[8,2,16,1024]{3,2,1,0:T(8,128)(2,1)S(1)}, bf16[8,2,16,1024]{3,2,1,0:T(8,128)(2,1)S(1)}, u32[]{:S(2)}, u32[]{:S(2)}) collective-permute-start(bf16[8,2,16,1024]{3,2,1,0:T(8,128)(2,1)S(1)} %bitcast.21), channel_id=1, source_target_pairs={{2,0},{4,2},{6,4},{0,6},{3,1},{5,3},{7,5},{1,7},{10,8},{12,10},{14... | collective-permute-start | bytes 1572872 | tf_op jit(solution)/shard_map/ppermute | solution.py:231
  32.1 14.4 %collective-permute-start.3 = (bf16[8,2,16,1024]{3,2,1,0:T(8,128)(2,1)S(1)}, bf16[8,2,16,1024]{3,2,1,0:T(8,128)(2,1)S(1)}, u32[]{:S(2)}, u32[]{:S(2)}) collective-permute-start(bf16[8,2,16,1024]{3,2,1,0:T(8,128)(2,1)S(1)} %bitcast.22), channel_id=1, source_target_pairs={{6,0},{0,2},{2,4},{4,6},{7,1},{1,3},{3,5},{5,7},{14,8},{8,10},{10,... | collective-permute-start | bytes 1572872 | tf_op jit(solution)/shard_map/ppermute | solution.py:231
  43.2 8.9 %collective-permute-start.6 = (bf16[4,2,16,1024]{3,2,1,0:T(8,128)(2,1)S(1)}, bf16[4,2,16,1024]{3,2,1,0:T(8,128)(2,1)S(1)}, u32[]{:S(2)}, u32[]{:S(2)}) collective-permute-start(bf16[4,2,16,1024]{3,2,1,0:T(8,128)(2,1)S(1)} %slice.17), channel_id=1, source_target_pairs={{2,0},{4,2},{6,4},{0,6},{3,1},{5,3},{7,5},{1,7},{10,8},{12,10},{14... | collective-permute-start | bytes 786440 | tf_op jit(solution)/shard_map/ppermute | solution.py:231
  46.6 8.9 %collective-permute-start.5 = (bf16[4,2,16,1024]{3,2,1,0:T(8,128)(2,1)S(1)}, bf16[4,2,16,1024]{3,2,1,0:T(8,128)(2,1)S(1)}, u32[]{:S(2)}, u32[]{:S(2)}) collective-permute-start(bf16[4,2,16,1024]{3,2,1,0:T(8,128)(2,1)S(1)} %slice.16), channel_id=1, source_target_pairs={{6,0},{0,2},{2,4},{4,6},{7,1},{1,3},{3,5},{5,7},{14,8},{8,10},{10,... | collective-permute-start | bytes 786440 | tf_op jit(solution)/shard_map/ppermute | solution.py:231
  57.1 2.2 %collective-permute-start.7 = (f32[2,16,1024]{2,1,0:T(8,128)S(1)}, f32[2,16,1024]{2,1,0:T(8,128)S(1)}, u32[]{:S(2)}, u32[]{:S(2)}) collective-permute-start(f32[2,16,1024]{2,1,0:T(8,128)S(1)} %get-tuple-element.31.own_ref), channel_id=1, source_target_pairs={{0,1},{1,0},{2,3},{3,2},{4,5},{5,4},{6,7},{7,6},{8,9},{9,8},{10,11... | collective-permute-start | bytes 393224 | tf_op jit(solution)/shard_map/ppermute | solution.py:226
  60.0 7.8 %collective-permute-start.10 = (bf16[2,16,1024]{2,1,0:T(8,128)(2,1)S(1)}, bf16[2,16,1024]{2,1,0:T(8,128)(2,1)S(1)}, u32[]{:S(2)}, u32[]{:S(2)}) collective-permute-start(bf16[2,16,1024]{2,1,0:T(8,128)(2,1)S(1)} %get-tuple-element.32.refs_0_), channel_id=1, source_target_pairs={{6,0},{0,2},{2,4},{4,6},{7,1},{1,3},{3,5},{5,7},{14,8},{8,10},{10,... | collective-permute-start | bytes 196616 | tf_op jit(solution)/shard_map/ppermute | solution.py:231
  60.1 8.4 %collective-permute-start.9 = (bf16[2,16,1024]{2,1,0:T(8,128)(2,1)S(1)}, bf16[2,16,1024]{2,1,0:T(8,128)(2,1)S(1)}, u32[]{:S(2)}, u32[]{:S(2)}) collective-permute-start(bf16[2,16,1024]{2,1,0:T(8,128)(2,1)S(1)} %get-tuple-element.32.refs_0_), channel_id=1, source_target_pairs={{4,0},{6,2},{0,4},{2,6},{5,1},{7,3},{1,5},{3,7},{12,8},{14,10},{8,... | collective-permute-start | bytes 196616 | tf_op jit(solution)/shard_map/ppermute | solution.py:231
  61.0 7.5 %collective-permute-start.8 = (bf16[2,16,1024]{2,1,0:T(8,128)(2,1)S(1)}, bf16[2,16,1024]{2,1,0:T(8,128)(2,1)S(1)}, u32[]{:S(2)}, u32[]{:S(2)}) collective-permute-start(bf16[2,16,1024]{2,1,0:T(8,128)(2,1)S(1)} %get-tuple-element.32.refs_0_), channel_id=1, source_target_pairs={{2,0},{4,2},{6,4},{0,6},{3,1},{5,3},{7,5},{1,7},{10,8},{12,10},{14... | collective-permute-start | bytes 196616 | tf_op jit(solution)/shard_map/ppermute | solution.py:231
  64.7 12.3 %collective-permute-start.11 = (bf16[432,128]{1,0:T(8,128)(2,1)S(1)}, bf16[432,128]{1,0:T(8,128)(2,1)S(1)}, u32[]{:S(2)}, u32[]{:S(2)}) collective-permute-start(bf16[432,128]{1,0:T(8,128)(2,1)S(1)} %get-tuple-element.40), channel_id=1, source_target_pairs={{64,0},{128,64},{192,128},{0,192},{65,1},{129,65},{193,129},{1,193... | collective-permute-start | bytes 331784 | tf_op jit(solution)/shard_map/ppermute | solution.py:231
  67.5 9.5 %collective-permute-start.12 = (bf16[432,128]{1,0:T(8,128)(2,1)S(1)}, bf16[432,128]{1,0:T(8,128)(2,1)S(1)}, u32[]{:S(2)}, u32[]{:S(2)}) collective-permute-start(bf16[432,128]{1,0:T(8,128)(2,1)S(1)} %get-tuple-element.41), channel_id=1, source_target_pairs={{128,0},{192,64},{0,128},{64,192},{129,1},{193,65},{1,129},{65,193... | collective-permute-start | bytes 331784 | tf_op jit(solution)/shard_map/ppermute | solution.py:231
  67.8 9.2 %collective-permute-start.13 = (bf16[432,128]{1,0:T(8,128)(2,1)S(1)}, bf16[432,128]{1,0:T(8,128)(2,1)S(1)}, u32[]{:S(2)}, u32[]{:S(2)}) collective-permute-start(bf16[432,128]{1,0:T(8,128)(2,1)S(1)} %get-tuple-element.42), channel_id=1, source_target_pairs={{192,0},{0,64},{64,128},{128,192},{193,1},{1,65},{65,129},{129,193... | collective-permute-start | bytes 331784 | tf_op jit(solution)/shard_map/ppermute | solution.py:231
  72.0 22.3 %all-to-all-start.1 = ((bf16[16,16,1024]{2,1,0:T(8,128)(2,1)}), bf16[16,16,1024]{2,1,0:T(8,128)(2,1)S(1)}, u32[]{:S(2)}, u32[]{:S(2)}) async-start(bf16[16,16,1024]{2,1,0:T(8,128)(2,1)} %bitcast.9), calls=%async_computation.1 | async-start | bytes 1048576 | tf_op jit(solution)/shard_map/all_to_all | solution.py:280
  77.1 5.7 %collective-permute-start.16 = (bf16[432,128]{1,0:T(8,128)(2,1)S(1)}, bf16[432,128]{1,0:T(8,128)(2,1)S(1)}, u32[]{:S(2)}, u32[]{:S(2)}) collective-permute-start(bf16[432,128]{1,0:T(8,128)(2,1)S(1)} %add_convert_fusion.refs_0_), channel_id=1, source_target_pairs={{192,0},{0,64},{64,128},{128,192},{193,1},{1,65},{65,129},{129,193... | collective-permute-start | bytes 331784 | tf_op jit(solution)/shard_map/ppermute | solution.py:231
  78.8 6.9 %collective-permute-start.15 = (bf16[432,128]{1,0:T(8,128)(2,1)S(1)}, bf16[432,128]{1,0:T(8,128)(2,1)S(1)}, u32[]{:S(2)}, u32[]{:S(2)}) collective-permute-start(bf16[432,128]{1,0:T(8,128)(2,1)S(1)} %add_convert_fusion.refs_0_), channel_id=1, source_target_pairs={{128,0},{192,64},{0,128},{64,192},{129,1},{193,65},{1,129},{65,193... | collective-permute-start | bytes 331784 | tf_op jit(solution)/shard_map/ppermute | solution.py:231
  80.3 5.3 %collective-permute-start.14 = (bf16[432,128]{1,0:T(8,128)(2,1)S(1)}, bf16[432,128]{1,0:T(8,128)(2,1)S(1)}, u32[]{:S(2)}, u32[]{:S(2)}) collective-permute-start(bf16[432,128]{1,0:T(8,128)(2,1)S(1)} %add_convert_fusion.refs_0_), channel_id=1, source_target_pairs={{64,0},{128,64},{192,128},{0,192},{65,1},{129,65},{193,129},{1,193... | collective-permute-start | bytes 331784 | tf_op jit(solution)/shard_map/ppermute | solution.py:231
  85.7 2.6 %collective-permute-start.17 = (bf16[4,432,128]{2,1,0:T(8,128)(2,1)S(1)}, bf16[4,432,128]{2,1,0:T(8,128)(2,1)S(1)}, u32[]{:S(2)}, u32[]{:S(2)}) collective-permute-start(bf16[4,432,128]{2,1,0:T(8,128)(2,1)S(1)} %pad_maximum_fusion), channel_id=1, source_target_pairs={{0,1},{1,0},{2,3},{3,2},{4,5},{5,4},{6,7},{7,6},{8,9},{9,8},{10,11... | collective-permute-start | bytes 1327112 | tf_op jit(solution)/shard_map/ppermute | solution.py:226

commit v5 on v3

--- a/solution.py
+++ b/solution.py
@@ -120,7 +120,7 @@
         run(-1)
 
 
-def act_kernel(at_ref, own_ref, other_ref, send_ref, keep_ref):
+def act_kernel(at_ref, own_ref, other_ref, send_ref):
     first = at_ref[0] == 0
     for d in range(2):
         own, other = own_ref[d], other_ref[d]
@@ -130,72 +130,13 @@
         hidden = pre * gate
         act = upstream * gate * (1.0 + pre * (1.0 - gate))
         send_ref[d] = jnp.where(first, hidden, act).astype(BF16)
-        keep_ref[d] = jnp.where(first, act, hidden).astype(BF16)
-
-
-def grad_kernel(at_ref, keep_ref, mine_ref, left_ref, right_ref, far0_ref, far1_ref, *refs):
-    out_refs, (whole, col, full) = refs[:4], refs[4:]
-    width = keep_ref.shape[1]
+
+
+def second_kernel(at_ref, *refs):
+    acts, held, across, (out_ref, grad_ref, col, tall, both) = refs[:NX], refs[NX], refs[NX + 1], refs[NX + 2 :]
+    width = held.shape[1] // 27
     third = 9 * width
-    ok = masks(width)
-    x = at_ref[1]
-    half = NZ // 2
-    pieces = ((mine_ref, 0, 0, NZ), (left_ref, NX - 1, 0, NZ), (right_ref, 1, 0, NZ), (far0_ref, 2, 0, half), (far1_ref, 2, half, half))
-    for ref, step, z0, count in pieces:
-        source = lax.rem(x + step, NX)
-        for z in range(count):
-            rows = pl.ds(pl.multiple_of(((z0 + z) * NX + source) * width, 16), width)
-            for d in range(2):
-                whole[d, rows, :] = ref[z, d]
-
-    def run(sign):
-        for d in range(2):
-            at = third * (d if sign > 0 else 1 - d)
-            spread(keep_ref[d].astype(F32), sign, col, at, ok)
-        zero = dot(col[...], whole[0], ((1,), (1,)))
-        last = dot(col[...], whole[1], ((1,), (1,)))
-        low, high = (last, zero) if sign > 0 else (zero, last)
-        full[0:third, :] = low[0:third].astype(BF16)
-        full[third : 2 * third, :] = (low[third:] + high[0:third]).astype(BF16)
-        full[2 * third :, :] = high[third:].astype(BF16)
-
-    @pl.when(at_ref[0] == 0)
-    def _():
-        run(-1)
-
-    @pl.when(at_ref[0] == 1)
-    def _():
-        run(1)
-
-    quarter = full.shape[1] // 4
-    for k in range(4):
-        columns = pl.ds(pl.multiple_of(lax.rem(at_ref[2] + k, 4) * quarter, quarter), quarter)
-        out_refs[k][...] = full[:, columns]
-
-
-def finish_kernel(at_ref, *refs):
-    own_refs, other_ref, (one_ref, two_ref) = refs[:4], refs[4], refs[5:]
-    quarter = other_ref.shape[2]
-
-    def run(own_out, other_out):
-        for k in range(4):
-            columns = pl.ds(pl.multiple_of(lax.rem(at_ref[2] + k, 4) * quarter, quarter), quarter)
-            own_out[:, columns] = own_refs[k][...].astype(F32)
-            other_out[:, columns] = other_ref[k].astype(F32)
-
-    @pl.when(at_ref[0] == 0)
-    def _():
-        run(one_ref, two_ref)
-
-    @pl.when(at_ref[0] == 1)
-    def _():
-        run(two_ref, one_ref)
-
-
-def second_kernel(at_ref, *refs):
-    acts, kernels, (out_ref, col, tall) = refs[:NX], refs[NX], refs[NX + 1 :]
-    width = acts[0].shape[1]
-    third = 9 * width
+    group = NZ * width
     ok = masks(width)
 
     def run(sign):
@@ -204,9 +145,24 @@
                 at = 2 * third * k + third * (d if sign > 0 else 1 - d)
                 spread(acts[k][d].astype(F32), sign, col, at, ok)
         for d in range(2):
+            both[d * group : (d + 1) * group, :] = across[:, d].reshape(group, PLANE)
+        grad = dot(col[...], both[...], ((1,), (1,)))
+        zero, last = grad[:, 0:group], grad[:, group:]
+        low, high = (last, zero) if sign > 0 else (zero, last)
+        for k in range(NX):
+            at, mid, end = (2 * k + 0) * third, (2 * k + 1) * third, (2 * k + 2) * third
+            taps = jnp.concatenate([low[at:mid], low[mid:end] + high[at:mid], high[mid:end]], axis=0).astype(BF16)
+            x = lax.rem(at_ref[1] + k, NX)
+            size = grad_ref.shape[1]
+            for y in range(4):
+                rows = taps[y * size : min((y + 1) * size, 3 * third)]
+                grad_ref[y * NX + x, 0 : rows.shape[0], :] = rows
+                if rows.shape[0] < size:
+                    grad_ref[y * NX + x, rows.shape[0] :, :] = jnp.zeros((size - rows.shape[0], group), BF16)
+        for d in range(2):
             at = third * ((1 - d) if sign > 0 else d)
             for k in range(NX):
-                tall[2 * third * k : 2 * third * (k + 1), :] = kernels[k, at : at + 2 * third, :]
+                tall[2 * third * k : 2 * third * (k + 1), :] = held[k, at : at + 2 * third, :]
             part = dot(tall[...], col[...], ((0,), (0,)))
             out_ref[:, d] = part.astype(BF16).reshape(NZ, width, PLANE)
 
@@ -217,6 +173,36 @@
     @pl.when(at_ref[0] == 1)
     def _():
         run(-1)
+
+
+def finish_kernel(at_ref, *refs):
+    own_refs, other_ref, (one_ref, two_ref, near, far) = refs[:4], refs[4], refs[5:]
+    taps, channels = one_ref.shape
+    _, _, size, group = other_ref.shape
+    width = group // NZ
+    old = lax.broadcasted_iota(jnp.int32, (channels, channels), 0)
+    new = lax.broadcasted_iota(jnp.int32, (channels, channels), 1)
+    place = (new // width) % NX * group + new // (NX * width) * width + new % width
+    order = (old == place).astype(F32).astype(BF16)
+
+    def put(piece, full, out_ref):
+        for k in range(4):
+            rows = pl.ds(pl.multiple_of(lax.rem(at_ref[2] + k, 4) * size, 16), size)
+            for x in range(NX):
+                full[rows, x * group : (x + 1) * group] = piece(k, x)
+        out_ref[...] = dot(full[0:taps, :], order, ((1,), (0,)))
+
+    def run(own_out, other_out):
+        put(lambda k, x: own_refs[k][x], near, own_out)
+        put(lambda k, x: other_ref[k, x], far, other_out)
+
+    @pl.when(at_ref[0] == 0)
+    def _():
+        run(two_ref, one_ref)
+
+    @pl.when(at_ref[0] == 1)
+    def _():
+        run(one_ref, two_ref)
 
 
 def call(kernel, outs, scratch, name, cost, *args):
@@ -244,27 +230,22 @@
 
 def body(features, conv_one, conv_two, cotangent):
     width, channels = conv_one.shape[1], conv_one.shape[2]
-    core = lax.axis_index("spatial")
-    first = core == 0
-    at = jnp.stack([core, lax.axis_index("x"), lax.axis_index("samples")]).astype(jnp.int32)
+    at = jnp.stack([lax.axis_index(a) for a in ("spatial", "x", "samples")]).astype(jnp.int32)
     one = conv_one.reshape(27 * width, channels)
     two = conv_two.reshape(27 * width, channels)
-    features = features.reshape(width, PLANE)
-    cotangent = cotangent.reshape(width, PLANE)
     taps = 27 * width
     group = NZ * width
-    quarter = channels // 4
     plane = (2, width, PLANE)
+    everyone = (2 * NZ, width, PLANE)
+    piece = (7 * width, group)
     work = 4 * 18 * width * channels * PLANE
+
+    pair = jnp.stack([features.reshape(width, PLANE), cotangent.reshape(width, PLANE)])
+    pair = jnp.broadcast_to(pair, (NZ,) + plane).reshape(everyone)
+    mine = lax.all_to_all(pair, ("z", "spatial"), 0, 0, tiled=True).reshape((NZ,) + plane)
 
     groups = call(regroup_kernel, [((taps, group), BF16)] * NX, [], "regroup", 2 * taps * channels * channels, at, one, two)
     kernels = [groups[0]] + [around(groups[NX - k], "x", k) for k in range(1, NX)]
-
-    came = swap(jnp.where(first, cotangent, features))
-    kept = jnp.where(first, features, cotangent)
-    block = jnp.where(first, jnp.stack([kept, came]), jnp.stack([came, kept]))
-    block, _ = lax.optimization_barrier((block, groups[0]))
-    mine = lax.all_to_all(jnp.broadcast_to(block, (NZ,) + block.shape), "z", 0, 0, tiled=True)
 
     own, *sends, held = call(
         first_kernel,
@@ -274,46 +255,31 @@
     )
     sends = [around(part, "x", NX - k) for k, part in enumerate(sends, 1)]
     own = own + sum(part.astype(F32) for part in sends)
-
-    left = around(mine, "x", -1)
-    right = around(mine, "x", 1)
-    far0 = around(left[: NZ // 2], "x", -1)
-    far1 = around(right[NZ // 2 :], "x", 1)
-    held = swap(held)
-
-    other = swap(own)
-    send, keep = call(act_kernel, [(plane, BF16)] * 2, [], "act", 0, at, own, other)
+    held, across = swap(held), swap(mine)
+
+    (send,) = call(act_kernel, [(plane, BF16)], [], "act", 0, at, own, swap(own))
     acts = [send] + [around(send, "x", k) for k in range(1, NX)]
-    (parts,) = call(
+    parts, grads = call(
         second_kernel,
-        [((NZ,) + plane, BF16)],
-        [((NX * 18 * width, PLANE), BF16), ((NX * 18 * width, group), BF16)],
-        "conv_out", work, at, *acts, held,
-    )
-    parts = lax.all_to_all(parts, "z", 0, 0, tiled=True)
-
-    grads = call(
-        grad_kernel,
-        [((taps, quarter), BF16)] * 4,
-        [((2, channels, PLANE), BF16), ((18 * width, PLANE), BF16), ((taps, channels), BF16)],
-        "grad", work, at, keep, mine, left, right, far0, far1,
-    )
-    pieces = [grads[0]] + [around(grads[4 - k], "samples", k) for k in (1, 2, 3)]
-    summed = sum(g.astype(F32) for g in pieces).astype(BF16)
+        [((NZ,) + plane, BF16), ((4 * NX,) + piece, BF16)],
+        [((NX * 18 * width, PLANE), BF16), ((NX * 18 * width, group), BF16), ((2 * group, PLANE), BF16)],
+        "conv_out", 2 * work, at, *acts, held, across,
+    )
+    grads = lax.all_to_all(grads, ("samples", "x"), 0, 0, tiled=True)
+    parts = lax.all_to_all(parts.reshape(everyone), ("z", "spatial"), 0, 0, tiled=True)
+
+    summed = jnp.sum(grads.reshape((4, NX) + piece).astype(F32), axis=0).astype(BF16)
     pieces = [summed] + [around(summed, "samples", k) for k in (1, 2, 3)]
     others = swap(jnp.stack(pieces))
     grad_one, grad_two = call(
-        finish_kernel, [((taps, channels), F32)] * 2, [], "finish", 0, at, *pieces, others
-    )
-
-    result = jnp.sum(parts.astype(F32), axis=0).astype(BF16)
-    ours = jnp.where(first, result[0], result[1])
-    theirs = swap(jnp.where(first, result[1], result[0]))
+        finish_kernel, [((taps, channels), F32)] * 2, [((28 * width, channels), BF16)] * 2, "finish", 0, at, *pieces, others
+    )
+    parts, grad_one, grad_two = lax.optimization_barrier((parts, grad_one, grad_two))
+
+    result = jnp.sum(parts.reshape((NZ,) + plane).astype(F32), axis=0).astype(BF16)
     shape = (width, 1, 1, PLANE)
-    mixed_out = jnp.where(first, ours, theirs).reshape(shape)
-    input_grad = jnp.where(first, theirs, ours).reshape(shape)
     weights = (27, width, channels)
-    return mixed_out, input_grad, grad_one.reshape(weights), grad_two.reshape(weights)
+    return result[0].reshape(shape), result[1].reshape(shape), grad_one.reshape(weights), grad_two.reshape(weights)
 
 
 def solution(mesh):

time: 106 us -> 93.2 us (0.88)
  waiting for transfers between devices: 44.3 us -> 28.2 us
  blocking collectives: 0 us -> 15.5 us
  starting transfers between devices: 44.5 us -> 35.3 us
  local copies, waits for them, and re-layouts: 2.92 us -> 1.49 us
    ppermute x19 -> x12, waiting for transfers between devices: 35.4 us -> 10.3 us  [around(): lax.ppermute(values, axis, [((i + step) % size, i) for i in range(size)])]
    all_to_all x0 -> x1, blocking collectives: none -> 15.5 us  [body(): grads = lax.all_to_all(grads, ('samples', 'x'), 0, 0, tiled=True)]
    all_to_all x2, waiting for transfers between devices: 6.72 us -> 15.5 us  [the longest x1 12.3 us: body(): lax.all_to_all(pair, ('z', 'spatial'), 0, 0, tiled=True)]
    ppermute x19 -> x12, starting transfers between devices: 22.7 us -> 15 us  [around(): lax.ppermute(values, axis, [((i + step) % size, i) for i in range(size)])]
    ppermute x5 -> x4, starting transfers between devices: 11.8 us -> 4.7 us  [swap(): return lax.ppermute(values, 'spatial', [(0, 1), (1, 0)])]
    all_to_all x2, starting transfers between devices: 9.95 us -> 15.6 us  [the longest x1 10.1 us: body(): lax.all_to_all(pair, ('z', 'spatial'), 0, 0, tiled=True)]
    unnamed x4, local copies, waits for them, and re-layouts: 2.03 us -> 0.01 us
    pallas_call x6 -> x5, Pallas kernels: 11.5 us -> 10.6 us  [call(): pl.pallas_call(kernel, out_shape=tuple((jax.ShapeDtypeStruct(s, t) for s,...]
  transfers between devices with their start and end apart: 26 -> 18, of which waited for: 15 -> 11; matrix products, arithmetic and copies ran while one was open for 1% -> 0% of each run, Pallas kernels for 7% -> 7%
where the time goes in v5:
time: 93.2 us; the launch traced here: 92.8 us
  starting transfers between devices  35.3 us (38%)
  waiting for transfers between devices  28.2 us (30%)
  blocking collectives  15.5 us (17%)
  Pallas kernels  10.6 us (11%)
  local copies, waits for them, and re-layouts  1.49 us (2%)
  other arithmetic  1.1 us (1%)
    all_to_all x1, blocking collectives, body(): grads = lax.all_to_all(grads, ('samples', 'x'), 0, 0, tiled=True)  15.5 us
    ppermute x12, starting transfers between devices, around(): lax.ppermute(values, axis, [((i + step) % size, i) for i in range(size)])  15 us
    all_to_all x1, waiting for transfers between devices, body(): lax.all_to_all(pair, ('z', 'spatial'), 0, 0, tiled=True)  12.3 us
    pallas_call x5, Pallas kernels, call(): pl.pallas_call(kernel, out_shape=tuple((jax.ShapeDtypeStruct(s, t) for s,...  10.6 us
    ppermute x12, waiting for transfers between devices, around(): lax.ppermute(values, axis, [((i + step) % size, i) for i in range(size)])  10.3 us
    all_to_all x1, starting transfers between devices, body(): lax.all_to_all(pair, ('z', 'spatial'), 0, 0, tiled=True)  10.1 us
    all_to_all x1, starting transfers between devices, body(): lax.all_to_all(parts.reshape(everyone), ('z', 'spatial'), 0, 0, tiled=True)  5.48 us
    ppermute x4, starting transfers between devices, swap(): return lax.ppermute(values, 'spatial', [(0, 1), (1, 0)])  4.7 us
  transfers between devices with their start and end apart: 18, of which 11 were waited for; matrix products, arithmetic and copies ran while one was open for 0% of the time, Pallas kernels for 7%

profile of v5, /device:TPU:1, one launch (start us, length us, event | category | flops | bytes accessed | tf_op | source)
XLA Modules:
  0.0 92.8 jit_solution(5386308857282447973)
XLA Ops:
  0.6 0.8 pad_maximum_fusion.1
  1.4 0.9 broadcast_in_dim.3
  2.3 0.0 copy-start
  2.3 0.0 copy-start.1
  2.3 10.1 %all-to-all-start = ((bf16[16,16,1024]{2,1,0:T(8,128)(2,1)}), bf16[16,16,1024]{2,1,0:T(8,128)(2,1)S(1)}, u32[]{:S(2)}, u32[]{:S(2)}) async-start(bf16[16,16,1024]{2,1,0:T(8,128)(2,1)} %bitcast.5), calls=%async_computation | async-start | bytes 1048576 | tf_op jit(solution)/shard_map/all_to_all | solution.py:245
  12.4 0.1 pad_add_fusion.at_ref
  12.5 0.0 copy-done
  12.5 0.0 copy-done.1
  12.5 1.2 %regroup.1 = (bf16[432,128]{1,0:T(8,128)(2,1)S(1)}, bf16[432,128]{1,0:T(8,128)(2,1)S(1)}, bf16[432,128]{1,0:T(8,128)(2,1)S(1)}, bf16[432,128]{1,0:T(8,128)(2,1)S(1)}) custom-call(s32[3]{0:T(128)S(1)} %pad_add_fusion.at_ref, bf16[432,512]{1,0:T(8,128)(2,1)S(1)} %bitcast.28, bf16[432,512]{1,0:T(8,128)(2,1)S(1)} %bitcast.29), custom_call_target="tpu_custom_call" | custom-call | flops 226492416 | tf_op jit(solution)/shard_map/regroup/pallas_call | solution.py:210
  13.7 2.6 %collective-permute-start = (bf16[432,128]{1,0:T(8,128)(2,1)S(1)}, bf16[432,128]{1,0:T(8,128)(2,1)S(1)}, u32[]{:S(2)}, u32[]{:S(2)}) collective-permute-start(bf16[432,128]{1,0:T(8,128)(2,1)S(1)} %get-tuple-element.21), channel_id=1, source_target_pairs={{2,0},{4,2},{6,4},{0,6},{3,1},{5,3},{7,5},{1,7},{10,8},{12,10},{14... | collective-permute-start | bytes 331784 | tf_op jit(solution)/shard_map/ppermute | solution.py:228
  16.2 0.5 collective-permute-start.1
  16.7 0.6 collective-permute-start.2
  17.4 12.3 %all-to-all-done = bf16[16,16,1024]{2,1,0:T(8,128)(2,1)S(1)} async-done(((bf16[16,16,1024]{2,1,0:T(8,128)(2,1)}), bf16[16,16,1024]{2,1,0:T(8,128)(2,1)S(1)}, u32[]{:S(2)}, u32[]{:S(2)}) %all-to-all-start) | async-done | bytes 524320 | tf_op jit(solution)/shard_map/all_to_all | solution.py:245
  29.7 0.0 collective-permute-start.11
  29.7 0.0 collective-permute-done.refs_1_
  29.7 0.0 collective-permute-done.1.refs_2_
  29.7 0.0 collective-permute-done.2.refs_3_
  29.7 2.5 %conv_in.1 = (f32[2,16,1024]{2,1,0:T(8,128)S(1)}, bf16[2,16,1024]{2,1,0:T(8,128)(2,1)S(1)}, bf16[2,16,1024]{2,1,0:T(8,128)(2,1)S(1)}, bf16[2,16,1024]{2,1,0:T(8,128)(2,1)S(1)}, bf16[4,432,128]{2,1,0:T(8,128)(2,1)S(1)}) custom-call(s32[3]{0:T(128)S(1)} %pad_add_fusion.at_ref, bf16[8,2,16,1024]{3,2,1,0:T(8,128)(2,1)S(1)} %bitcast.24, ...), custom_call_target="tpu_custom_call" | custom-call | flops 603979776 | tf_op jit(solution)/shard_map/conv_in/pallas_call | solution.py:210
  32.2 1.3 %collective-permute-start.3 = (bf16[2,16,1024]{2,1,0:T(8,128)(2,1)S(1)}, bf16[2,16,1024]{2,1,0:T(8,128)(2,1)S(1)}, u32[]{:S(2)}, u32[]{:S(2)}) collective-permute-start(bf16[2,16,1024]{2,1,0:T(8,128)(2,1)S(1)} %get-tuple-element.25), channel_id=1, source_target_pairs={{6,0},{0,2},{2,4},{4,6},{7,1},{1,3},{3,5},{5,7},{14,8},{8,10},{10,... | collective-permute-start | bytes 196616 | tf_op jit(solution)/shard_map/ppermute | solution.py:228
  33.5 2.4 %collective-permute-start.4 = (bf16[2,16,1024]{2,1,0:T(8,128)(2,1)S(1)}, bf16[2,16,1024]{2,1,0:T(8,128)(2,1)S(1)}, u32[]{:S(2)}, u32[]{:S(2)}) collective-permute-start(bf16[2,16,1024]{2,1,0:T(8,128)(2,1)S(1)} %get-tuple-element.26), channel_id=1, source_target_pairs={{4,0},{6,2},{0,4},{2,6},{5,1},{7,3},{1,5},{3,7},{12,8},{14,10},{8,... | collective-permute-start | bytes 196616 | tf_op jit(solution)/shard_map/ppermute | solution.py:228
  36.0 1.1 %collective-permute-start.5 = (bf16[2,16,1024]{2,1,0:T(8,128)(2,1)S(1)}, bf16[2,16,1024]{2,1,0:T(8,128)(2,1)S(1)}, u32[]{:S(2)}, u32[]{:S(2)}) collective-permute-start(bf16[2,16,1024]{2,1,0:T(8,128)(2,1)S(1)} %get-tuple-element.27), channel_id=1, source_target_pairs={{2,0},{4,2},{6,4},{0,6},{3,1},{5,3},{7,5},{1,7},{10,8},{12,10},{14... | collective-permute-start | bytes 196616 | tf_op jit(solution)/shard_map/ppermute | solution.py:228
  37.1 1.3 %collective-permute-start.10 = (bf16[4,432,128]{2,1,0:T(8,128)(2,1)S(1)}, bf16[4,432,128]{2,1,0:T(8,128)(2,1)S(1)}, u32[]{:S(2)}, u32[]{:S(2)}) collective-permute-start(bf16[4,432,128]{2,1,0:T(8,128)(2,1)S(1)} %get-tuple-element.28), channel_id=1, source_target_pairs={{0,1},{1,0},{2,3},{3,2},{4,5},{5,4},{6,7},{7,6},{8,9},{9,8},{10,11... | collective-permute-start | bytes 1327112 | tf_op jit(solution)/shard_map/ppermute | solution.py:223
  38.4 0.0 collective-permute-done.3
  38.4 0.4 collective-permute-done.4
  38.8 0.6 collective-permute-done.5
  39.5 1.9 %collective-permute-start.6 = (f32[2,16,1024]{2,1,0:T(8,128)S(1)}, f32[2,16,1024]{2,1,0:T(8,128)S(1)}, u32[]{:S(2)}, u32[]{:S(2)}) collective-permute-start(f32[2,16,1024]{2,1,0:T(8,128)S(1)} %add_add_fusion.own_ref), channel_id=1, source_target_pairs={{0,1},{1,0},{2,3},{3,2},{4,5},{5,4},{6,7},{7,6},{8,9},{9,8},{10,11... | collective-permute-start | bytes 393224 | tf_op jit(solution)/shard_map/ppermute | solution.py:223
  41.4 1.0 %collective-permute-done.6.other_ref = f32[2,16,1024]{2,1,0:T(8,128)S(1)} collective-permute-done((f32[2,16,1024]{2,1,0:T(8,128)S(1)}, f32[2,16,1024]{2,1,0:T(8,128)S(1)}, u32[]{:S(2)}, u32[]{:S(2)}) %collective-permute-start.6) | collective-permute-done | bytes 131104 | tf_op jit(solution)/shard_map/ppermute | solution.py:223
  42.4 0.6 act.1.refs_0_
  43.0 0.4 collective-permute-start.9
  43.4 3.3 %collective-permute-start.8 = (bf16[2,16,1024]{2,1,0:T(8,128)(2,1)S(1)}, bf16[2,16,1024]{2,1,0:T(8,128)(2,1)S(1)}, u32[]{:S(2)}, u32[]{:S(2)}) collective-permute-start(bf16[2,16,1024]{2,1,0:T(8,128)(2,1)S(1)} %act.1.refs_0_), channel_id=1, source_target_pairs={{4,0},{6,2},{0,4},{2,6},{5,1},{7,3},{1,5},{3,7},{12,8},{14,10},{8,... | collective-permute-start | bytes 196616 | tf_op jit(solution)/shard_map/ppermute | solution.py:228
  46.6 0.0 collective-permute-start.7
  46.6 0.8 collective-permute-done.9.refs_3_
  47.4 2.2 %collective-permute-done.8.refs_2_ = bf16[2,16,1024]{2,1,0:T(8,128)(2,1)S(1)} collective-permute-done((bf16[2,16,1024]{2,1,0:T(8,128)(2,1)S(1)}, bf16[2,16,1024]{2,1,0:T(8,128)(2,1)S(1)}, u32[]{:S(2)}, u32[]{:S(2)}) %collective-permute-start.8) | collective-permute-done | bytes 65568 | tf_op jit(solution)/shard_map/ppermute | solution.py:228
  49.6 0.5 collective-permute-done.7.refs_1_
  50.1 0.0 collective-permute-done.10.refs_4_
  50.1 0.0 collective-permute-done.11.refs_5_
  50.1 3.7 %conv_out.1 = (bf16[8,2,16,1024]{3,2,1,0:T(8,128)(2,1)}, bf16[16,112,128]{2,1,0:T(8,128)(2,1)S(1)}) custom-call(s32[3]{0:T(128)S(1)} %pad_add_fusion.at_ref, bf16[2,16,1024]{2,1,0:T(8,128)(2,1)S(1)} %act.1.refs_0_, bf16[2,16,1024]{2,1,0:T(8,128)(2,1)S(1)} %collective-permute-done.7.refs_1_, bf16[2,16,1024]{2,1,0:T(8,128)(2,1)S(1)} %collective-permute-done.8.refs_2_, ...), custom_call_target="tpu_custom_call" | custom-call | flops 1207959552 | tf_op jit(solution)/shard_map/conv_out/pallas_call | solution.py:210
  53.8 15.5 %all_to_all.15 = bf16[16,112,128]{2,1,0:T(8,128)(2,1)S(1)} all-to-all(bf16[16,112,128]{2,1,0:T(8,128)(2,1)S(1)} %get-tuple-element.30), channel_id=1, replica_groups=mesh['samples'=4,'z'=8,'x'=4,'spatial'=2] {'samples','x'}, dimensions={0} | all-to-all | bytes 917504 | tf_op jit(solution)/shard_map/all_to_all | solution.py:268
  69.3 5.5 %all-to-all-start.1 = ((bf16[16,16,1024]{2,1,0:T(8,128)(2,1)}), bf16[16,16,1024]{2,1,0:T(8,128)(2,1)S(1)}, u32[]{:S(2)}, u32[]{:S(2)}) async-start(bf16[16,16,1024]{2,1,0:T(8,128)(2,1)} %bitcast.9), calls=%async_computation.1 | async-start | bytes 1048576 | tf_op jit(solution)/shard_map/all_to_all | solution.py:269
  74.8 0.1 reduce_sum.24.refs_0_
  74.8 0.1 collective-permute-start.14
  74.9 1.7 %collective-permute-start.13 = (bf16[4,112,128]{2,1,0:T(8,128)(2,1)S(1)}, bf16[4,112,128]{2,1,0:T(8,128)(2,1)S(1)}, u32[]{:S(2)}, u32[]{:S(2)}) collective-permute-start(bf16[4,112,128]{2,1,0:T(8,128)(2,1)S(1)} %reduce_sum.24.refs_0_), channel_id=1, source_target_pairs={{128,0},{192,64},{0,128},{64,192},{129,1},{193,65},{1,129},{65,193... | collective-permute-start | bytes 344072 | tf_op jit(solution)/shard_map/ppermute | solution.py:228
  76.7 0.9 collective-permute-start.12
  77.6 5.5 %collective-permute-done.14.refs_3_ = bf16[4,112,128]{2,1,0:T(8,128)(2,1)S(1)} collective-permute-done((bf16[4,112,128]{2,1,0:T(8,128)(2,1)S(1)}, bf16[4,112,128]{2,1,0:T(8,128)(2,1)S(1)}, u32[]{:S(2)}, u32[]{:S(2)}) %collective-permute-start.14) | collective-permute-done | bytes 114720 | tf_op jit(solution)/shard_map/ppermute | solution.py:228
  83.1 0.0 collective-permute-done.13.refs_2_
  83.1 0.3 collective-permute-done.12.refs_1_
  83.4 0.1 pad_maximum_fusion
  83.5 1.4 %collective-permute-start.15 = (bf16[4,4,112,128]{3,2,1,0:T(8,128)(2,1)S(1)}, bf16[4,4,112,128]{3,2,1,0:T(8,128)(2,1)S(1)}, u32[]{:S(2)}, u32[]{:S(2)}) collective-permute-start(bf16[4,4,112,128]{3,2,1,0:T(8,128)(2,1)S(1)} %pad_maximum_fusion), channel_id=1, source_target_pairs={{0,1},{1,0},{2,3},{3,2},{4,5},{5,4},{6,7},{7,6},{8,9},{9,8},{10,11... | collective-permute-start | bytes 1376264 | tf_op jit(solution)/shard_map/ppermute | solution.py:223
  84.9 1.4 %collective-permute-done.15.refs_4_ = bf16[4,4,112,128]{3,2,1,0:T(8,128)(2,1)S(1)} collective-permute-done((bf16[4,4,112,128]{3,2,1,0:T(8,128)(2,1)S(1)}, bf16[4,4,112,128]{3,2,1,0:T(8,128)(2,1)S(1)}, u32[]{:S(2)}, u32[]{:S(2)}) %collective-permute-start.15) | collective-permute-done | bytes 458784 | tf_op jit(solution)/shard_map/ppermute | solution.py:223
  86.3 2.6 %finish.1 = (f32[432,512]{1,0:T(8,128)}, f32[432,512]{1,0:T(8,128)}) custom-call(s32[3]{0:T(128)S(1)} %pad_add_fusion.at_ref, bf16[4,112,128]{2,1,0:T(8,128)(2,1)S(1)} %reduce_sum.24.refs_0_, bf16[4,112,128]{2,1,0:T(8,128)(2,1)S(1)} %collective-permute-done.12.refs_1_, bf16[4,112,128]{2,1,0:T(8,128)(2,1)S(1)} %collective-permute-done.13.refs_2_, ...), custom_call_target="tpu_custom_call" | custom-call | tf_op jit(solution)/shard_map/finish/pallas_call | solution.py:210
  88.9 3.2 %all-to-all-done.1 = bf16[16,16,1024]{2,1,0:T(8,128)(2,1)S(1)} async-done(((bf16[16,16,1024]{2,1,0:T(8,128)(2,1)}), bf16[16,16,1024]{2,1,0:T(8,128)(2,1)S(1)}, u32[]{:S(2)}, u32[]{:S(2)}) %all-to-all-start.1) | async-done | bytes 524320 | tf_op jit(solution)/shard_map/all_to_all | solution.py:269
  92.1 0.1 reduce_sum.25
  92.2 0.6 slice_bitcast_fusion
  (1 shorter events, 0.0 us)
Async XLA Ops:
  2.3 10.2 %copy-start = (bf16[27,16,512]{2,1,0:T(8,128)(2,1)S(1)}, bf16[27,16,512]{2,1,0:T(8,128)(2,1)}, u32[]{:S(2)}) copy-start(bf16[27,16,512]{2,1,0:T(8,128)(2,1)} %param.5) | copy-start | bytes 1327108
  2.3 10.2 %copy-start.1 = (bf16[27,16,512]{2,1,0:T(8,128)(2,1)S(1)}, bf16[27,16,512]{2,1,0:T(8,128)(2,1)}, u32[]{:S(2)}) copy-start(bf16[27,16,512]{2,1,0:T(8,128)(2,1)} %param.6) | copy-start | bytes 1327108
  2.3 27.4 %all-to-all-start = ((bf16[16,16,1024]{2,1,0:T(8,128)(2,1)}), bf16[16,16,1024]{2,1,0:T(8,128)(2,1)S(1)}, u32[]{:S(2)}, u32[]{:S(2)}) async-start(bf16[16,16,1024]{2,1,0:T(8,128)(2,1)} %bitcast.5), calls=%async_computation | async-start | bytes 1048576 | tf_op jit(solution)/shard_map/all_to_all | solution.py:245
  13.7 16.1 %collective-permute-start = (bf16[432,128]{1,0:T(8,128)(2,1)S(1)}, bf16[432,128]{1,0:T(8,128)(2,1)S(1)}, u32[]{:S(2)}, u32[]{:S(2)}) collective-permute-start(bf16[432,128]{1,0:T(8,128)(2,1)S(1)} %get-tuple-element.21), channel_id=1, source_target_pairs={{2,0},{4,2},{6,4},{0,6},{3,1},{5,3},{7,5},{1,7},{10,8},{12,10},{14... | collective-permute-start | bytes 331784 | tf_op jit(solution)/shard_map/ppermute | solution.py:228
  16.2 13.5 %collective-permute-start.1 = (bf16[432,128]{1,0:T(8,128)(2,1)S(1)}, bf16[432,128]{1,0:T(8,128)(2,1)S(1)}, u32[]{:S(2)}, u32[]{:S(2)}) collective-permute-start(bf16[432,128]{1,0:T(8,128)(2,1)S(1)} %get-tuple-element.22), channel_id=1, source_target_pairs={{4,0},{6,2},{0,4},{2,6},{5,1},{7,3},{1,5},{3,7},{12,8},{14,10},{8,... | collective-permute-start | bytes 331784 | tf_op jit(solution)/shard_map/ppermute | solution.py:228
  16.7 13.0 %collective-permute-start.2 = (bf16[432,128]{1,0:T(8,128)(2,1)S(1)}, bf16[432,128]{1,0:T(8,128)(2,1)S(1)}, u32[]{:S(2)}, u32[]{:S(2)}) collective-permute-start(bf16[432,128]{1,0:T(8,128)(2,1)S(1)} %get-tuple-element.23), channel_id=1, source_target_pairs={{6,0},{0,2},{2,4},{4,6},{7,1},{1,3},{3,5},{5,7},{14,8},{8,10},{10,... | collective-permute-start | bytes 331784 | tf_op jit(solution)/shard_map/ppermute | solution.py:228
  29.7 20.4 %collective-permute-start.11 = (bf16[8,2,16,1024]{3,2,1,0:T(8,128)(2,1)S(1)}, bf16[8,2,16,1024]{3,2,1,0:T(8,128)(2,1)S(1)}, u32[]{:S(2)}, u32[]{:S(2)}) collective-permute-start(bf16[8,2,16,1024]{3,2,1,0:T(8,128)(2,1)S(1)} %bitcast.23), channel_id=1, source_target_pairs={{0,1},{1,0},{2,3},{3,2},{4,5},{5,4},{6,7},{7,6},{8,9},{9,8},{10,11... | collective-permute-start | bytes 1572872 | tf_op jit(solution)/shard_map/ppermute | solution.py:223
  32.2 6.2 %collective-permute-start.3 = (bf16[2,16,1024]{2,1,0:T(8,128)(2,1)S(1)}, bf16[2,16,1024]{2,1,0:T(8,128)(2,1)S(1)}, u32[]{:S(2)}, u32[]{:S(2)}) collective-permute-start(bf16[2,16,1024]{2,1,0:T(8,128)(2,1)S(1)} %get-tuple-element.25), channel_id=1, source_target_pairs={{6,0},{0,2},{2,4},{4,6},{7,1},{1,3},{3,5},{5,7},{14,8},{8,10},{10,... | collective-permute-start | bytes 196616 | tf_op jit(solution)/shard_map/ppermute | solution.py:228
  33.5 5.3 %collective-permute-start.4 = (bf16[2,16,1024]{2,1,0:T(8,128)(2,1)S(1)}, bf16[2,16,1024]{2,1,0:T(8,128)(2,1)S(1)}, u32[]{:S(2)}, u32[]{:S(2)}) collective-permute-start(bf16[2,16,1024]{2,1,0:T(8,128)(2,1)S(1)} %get-tuple-element.26), channel_id=1, source_target_pairs={{4,0},{6,2},{0,4},{2,6},{5,1},{7,3},{1,5},{3,7},{12,8},{14,10},{8,... | collective-permute-start | bytes 196616 | tf_op jit(solution)/shard_map/ppermute | solution.py:228
  36.0 3.5 %collective-permute-start.5 = (bf16[2,16,1024]{2,1,0:T(8,128)(2,1)S(1)}, bf16[2,16,1024]{2,1,0:T(8,128)(2,1)S(1)}, u32[]{:S(2)}, u32[]{:S(2)}) collective-permute-start(bf16[2,16,1024]{2,1,0:T(8,128)(2,1)S(1)} %get-tuple-element.27), channel_id=1, source_target_pairs={{2,0},{4,2},{6,4},{0,6},{3,1},{5,3},{7,5},{1,7},{10,8},{12,10},{14... | collective-permute-start | bytes 196616 | tf_op jit(solution)/shard_map/ppermute | solution.py:228
  37.1 13.0 %collective-permute-start.10 = (bf16[4,432,128]{2,1,0:T(8,128)(2,1)S(1)}, bf16[4,432,128]{2,1,0:T(8,128)(2,1)S(1)}, u32[]{:S(2)}, u32[]{:S(2)}) collective-permute-start(bf16[4,432,128]{2,1,0:T(8,128)(2,1)S(1)} %get-tuple-element.28), channel_id=1, source_target_pairs={{0,1},{1,0},{2,3},{3,2},{4,5},{5,4},{6,7},{7,6},{8,9},{9,8},{10,11... | collective-permute-start | bytes 1327112 | tf_op jit(solution)/shard_map/ppermute | solution.py:223
  39.5 2.9 %collective-permute-start.6 = (f32[2,16,1024]{2,1,0:T(8,128)S(1)}, f32[2,16,1024]{2,1,0:T(8,128)S(1)}, u32[]{:S(2)}, u32[]{:S(2)}) collective-permute-start(f32[2,16,1024]{2,1,0:T(8,128)S(1)} %add_add_fusion.own_ref), channel_id=1, source_target_pairs={{0,1},{1,0},{2,3},{3,2},{4,5},{5,4},{6,7},{7,6},{8,9},{9,8},{10,11... | collective-permute-start | bytes 393224 | tf_op jit(solution)/shard_map/ppermute | solution.py:223
  43.0 4.4 %collective-permute-start.9 = (bf16[2,16,1024]{2,1,0:T(8,128)(2,1)S(1)}, bf16[2,16,1024]{2,1,0:T(8,128)(2,1)S(1)}, u32[]{:S(2)}, u32[]{:S(2)}) collective-permute-start(bf16[2,16,1024]{2,1,0:T(8,128)(2,1)S(1)} %act.1.refs_0_), channel_id=1, source_target_pairs={{6,0},{0,2},{2,4},{4,6},{7,1},{1,3},{3,5},{5,7},{14,8},{8,10},{10,... | collective-permute-start | bytes 196616 | tf_op jit(solution)/shard_map/ppermute | solution.py:228
  43.4 6.2 %collective-permute-start.8 = (bf16[2,16,1024]{2,1,0:T(8,128)(2,1)S(1)}, bf16[2,16,1024]{2,1,0:T(8,128)(2,1)S(1)}, u32[]{:S(2)}, u32[]{:S(2)}) collective-permute-start(bf16[2,16,1024]{2,1,0:T(8,128)(2,1)S(1)} %act.1.refs_0_), channel_id=1, source_target_pairs={{4,0},{6,2},{0,4},{2,6},{5,1},{7,3},{1,5},{3,7},{12,8},{14,10},{8,... | collective-permute-start | bytes 196616 | tf_op jit(solution)/shard_map/ppermute | solution.py:228
  46.6 3.5 %collective-permute-start.7 = (bf16[2,16,1024]{2,1,0:T(8,128)(2,1)S(1)}, bf16[2,16,1024]{2,1,0:T(8,128)(2,1)S(1)}, u32[]{:S(2)}, u32[]{:S(2)}) collective-permute-start(bf16[2,16,1024]{2,1,0:T(8,128)(2,1)S(1)} %act.1.refs_0_), channel_id=1, source_target_pairs={{2,0},{4,2},{6,4},{0,6},{3,1},{5,3},{7,5},{1,7},{10,8},{12,10},{14... | collective-permute-start | bytes 196616 | tf_op jit(solution)/shard_map/ppermute | solution.py:228
  69.3 22.8 %all-to-all-start.1 = ((bf16[16,16,1024]{2,1,0:T(8,128)(2,1)}), bf16[16,16,1024]{2,1,0:T(8,128)(2,1)S(1)}, u32[]{:S(2)}, u32[]{:S(2)}) async-start(bf16[16,16,1024]{2,1,0:T(8,128)(2,1)} %bitcast.9), calls=%async_computation.1 | async-start | bytes 1048576 | tf_op jit(solution)/shard_map/all_to_all | solution.py:269
  74.8 8.3 %collective-permute-start.14 = (bf16[4,112,128]{2,1,0:T(8,128)(2,1)S(1)}, bf16[4,112,128]{2,1,0:T(8,128)(2,1)S(1)}, u32[]{:S(2)}, u32[]{:S(2)}) collective-permute-start(bf16[4,112,128]{2,1,0:T(8,128)(2,1)S(1)} %reduce_sum.24.refs_0_), channel_id=1, source_target_pairs={{192,0},{0,64},{64,128},{128,192},{193,1},{1,65},{65,129},{129,193... | collective-permute-start | bytes 344072 | tf_op jit(solution)/shard_map/ppermute | solution.py:228
  74.9 8.2 %collective-permute-start.13 = (bf16[4,112,128]{2,1,0:T(8,128)(2,1)S(1)}, bf16[4,112,128]{2,1,0:T(8,128)(2,1)S(1)}, u32[]{:S(2)}, u32[]{:S(2)}) collective-permute-start(bf16[4,112,128]{2,1,0:T(8,128)(2,1)S(1)} %reduce_sum.24.refs_0_), channel_id=1, source_target_pairs={{128,0},{192,64},{0,128},{64,192},{129,1},{193,65},{1,129},{65,193... | collective-permute-start | bytes 344072 | tf_op jit(solution)/shard_map/ppermute | solution.py:228
  76.7 6.7 %collective-permute-start.12 = (bf16[4,112,128]{2,1,0:T(8,128)(2,1)S(1)}, bf16[4,112,128]{2,1,0:T(8,128)(2,1)S(1)}, u32[]{:S(2)}, u32[]{:S(2)}) collective-permute-start(bf16[4,112,128]{2,1,0:T(8,128)(2,1)S(1)} %reduce_sum.24.refs_0_), channel_id=1, source_target_pairs={{64,0},{128,64},{192,128},{0,192},{65,1},{129,65},{193,129},{1,193... | collective-permute-start | bytes 344072 | tf_op jit(solution)/shard_map/ppermute | solution.py:228
  83.5 2.9 %collective-permute-start.15 = (bf16[4,4,112,128]{3,2,1,0:T(8,128)(2,1)S(1)}, bf16[4,4,112,128]{3,2,1,0:T(8,128)(2,1)S(1)}, u32[]{:S(2)}, u32[]{:S(2)}) collective-permute-start(bf16[4,4,112,128]{3,2,1,0:T(8,128)(2,1)S(1)} %pad_maximum_fusion), channel_id=1, source_target_pairs={{0,1},{1,0},{2,3},{3,2},{4,5},{5,4},{6,7},{7,6},{8,9},{9,8},{10,11... | collective-permute-start | bytes 1376264 | tf_op jit(solution)/shard_map/ppermute | solution.py:223

commit v6 on v5

--- a/solution.py
+++ b/solution.py
@@ -132,9 +132,9 @@
         send_ref[d] = jnp.where(first, hidden, act).astype(BF16)
 
 
-def second_kernel(at_ref, *refs):
-    acts, held, across, (out_ref, grad_ref, col, tall, both) = refs[:NX], refs[NX], refs[NX + 1], refs[NX + 2 :]
-    width = held.shape[1] // 27
+def grad_kernel(at_ref, *refs):
+    acts, across, (grad_ref, col, both) = refs[:NX], refs[NX], refs[NX + 1 :]
+    width = acts[0].shape[1]
     third = 9 * width
     group = NZ * width
     ok = masks(width)
@@ -159,12 +159,6 @@
                 grad_ref[y * NX + x, 0 : rows.shape[0], :] = rows
                 if rows.shape[0] < size:
                     grad_ref[y * NX + x, rows.shape[0] :, :] = jnp.zeros((size - rows.shape[0], group), BF16)
-        for d in range(2):
-            at = third * ((1 - d) if sign > 0 else d)
-            for k in range(NX):
-                tall[2 * third * k : 2 * third * (k + 1), :] = held[k, at : at + 2 * third, :]
-            part = dot(tall[...], col[...], ((0,), (0,)))
-            out_ref[:, d] = part.astype(BF16).reshape(NZ, width, PLANE)
 
     @pl.when(at_ref[0] == 0)
     def _():
@@ -173,6 +167,31 @@
     @pl.when(at_ref[0] == 1)
     def _():
         run(-1)
+
+
+def second_kernel(at_ref, col, held, out_ref, tall):
+    width = held.shape[1] // 27
+    third = 9 * width
+    for d in range(2):
+        at = pl.multiple_of(third * jnp.where(at_ref[0] == 0, 1 - d, d), 16)
+        for k in range(NX):
+            tall[d, 2 * third * k : 2 * third * (k + 1), :] = held[k, pl.ds(at, 2 * third), :]
+        part = dot(tall[d], col[...], ((0,), (0,)))
+        out_ref[:, d] = part.astype(BF16).reshape(NZ, width, PLANE)
+
+
+def pack_kernel(at_ref, features_ref, cotangent_ref, out_ref):
+    for z in range(NZ):
+        out_ref[z, 0] = features_ref[...]
+        out_ref[z, 1] = cotangent_ref[...]
+
+
+def sum_kernel(at_ref, parts_ref, mixed_ref, input_ref):
+    for d, out_ref in enumerate((mixed_ref, input_ref)):
+        total = parts_ref[0, d].astype(F32)
+        for z in range(1, NZ):
+            total = total + parts_ref[z, d].astype(F32)
+        out_ref[...] = total.astype(BF16)
 
 
 def finish_kernel(at_ref, *refs):
@@ -240,9 +259,11 @@
     piece = (7 * width, group)
     work = 4 * 18 * width * channels * PLANE
 
-    pair = jnp.stack([features.reshape(width, PLANE), cotangent.reshape(width, PLANE)])
-    pair = jnp.broadcast_to(pair, (NZ,) + plane).reshape(everyone)
-    mine = lax.all_to_all(pair, ("z", "spatial"), 0, 0, tiled=True).reshape((NZ,) + plane)
+    (pair,) = call(
+        pack_kernel, [((NZ,) + plane, BF16)], [], "pack", 0,
+        at, features.reshape(width, PLANE), cotangent.reshape(width, PLANE),
+    )
+    mine = lax.all_to_all(pair.reshape(everyone), ("z", "spatial"), 0, 0, tiled=True).reshape((NZ,) + plane)
 
     groups = call(regroup_kernel, [((taps, group), BF16)] * NX, [], "regroup", 2 * taps * channels * channels, at, one, two)
     kernels = [groups[0]] + [around(groups[NX - k], "x", k) for k in range(1, NX)]
@@ -259,13 +280,20 @@
 
     (send,) = call(act_kernel, [(plane, BF16)], [], "act", 0, at, own, swap(own))
     acts = [send] + [around(send, "x", k) for k in range(1, NX)]
-    parts, grads = call(
+    grads, col = call(
+        grad_kernel,
+        [((4 * NX,) + piece, BF16), ((NX * 18 * width, PLANE), BF16)],
+        [((2 * group, PLANE), BF16)],
+        "grad", work, at, *acts, across,
+    )
+    grads = lax.all_to_all(grads, ("samples", "x"), 0, 0, tiled=True)
+    (parts,) = call(
         second_kernel,
-        [((NZ,) + plane, BF16), ((4 * NX,) + piece, BF16)],
-        [((NX * 18 * width, PLANE), BF16), ((NX * 18 * width, group), BF16), ((2 * group, PLANE), BF16)],
-        "conv_out", 2 * work, at, *acts, held, across,
-    )
-    grads = lax.all_to_all(grads, ("samples", "x"), 0, 0, tiled=True)
+        [((NZ,) + plane, BF16)],
+        [((2, NX * 18 * width, group), BF16)],
+        "conv_out", work, at, col, held,
+    )
+    parts, grads = lax.optimization_barrier((parts, grads))
     parts = lax.all_to_all(parts.reshape(everyone), ("z", "spatial"), 0, 0, tiled=True)
 
     summed = jnp.sum(grads.reshape((4, NX) + piece).astype(F32), axis=0).astype(BF16)
@@ -276,10 +304,12 @@
     )
     parts, grad_one, grad_two = lax.optimization_barrier((parts, grad_one, grad_two))
 
-    result = jnp.sum(parts.reshape((NZ,) + plane).astype(F32), axis=0).astype(BF16)
+    mixed_out, input_grad = call(
+        sum_kernel, [((width, PLANE), BF16)] * 2, [], "sum", 0, at, parts.reshape((NZ,) + plane)
+    )
     shape = (width, 1, 1, PLANE)
     weights = (27, width, channels)
-    return result[0].reshape(shape), result[1].reshape(shape), grad_one.reshape(weights), grad_two.reshape(weights)
+    return mixed_out.reshape(shape), input_grad.reshape(shape), grad_one.reshape(weights), grad_two.reshape(weights)
 
 
 def solution(mesh):

time: 93.2 us -> 94.7 us (1.016)
  blocking collectives: 15.5 us -> 0 us
  starting transfers between devices: 35.3 us -> 41.3 us
  waiting for transfers between devices: 28.2 us -> 32.6 us
  Pallas kernels: 10.6 us -> 14.7 us
  local copies, waits for them, and re-layouts: 1.49 us -> 3.54 us
    all_to_all x1 -> x0, blocking collectives: 15.5 us -> none  [body(): grads = lax.all_to_all(grads, ('samples', 'x'), 0, 0, tiled=True)]
    all_to_all x1 -> x2, starting transfers between devices: 10.1 us -> 16.1 us  [the longest x1 9.98 us: body(): lax.all_to_all(pair.reshape(everyone), ('z', 'spatial'), 0, 0, tiled=True)]
    all_to_all x1 -> x2, waiting for transfers between devices: 12.3 us -> 17.7 us  [the longest x1 10.4 us: body(): lax.all_to_all(pair.reshape(everyone), ('z', 'spatial'), 0, 0, tiled=True)]
    pallas_call x5 -> x8, Pallas kernels: 10.6 us -> 14.7 us  [call(): pl.pallas_call(kernel, out_shape=tuple((jax.ShapeDtypeStruct(s, t) for s,...]
    unnamed x4 -> x8, local copies, waits for them, and re-layouts: 0.01 us -> 3.54 us
    all_to_all x1, waiting for transfers between devices: 3.16 us -> 2.14 us  [body(): lax.all_to_all(parts.reshape(everyone), ('z', 'spatial'), 0, 0, tiled=True)]
    reduce_sum x1, other arithmetic: 0.07 us -> 1.09 us  [body(): jnp.sum(grads.reshape((4, NX) + piece).astype(F32), axis=0).astype(BF16)]
  transfers between devices with their start and end apart: 18 -> 19, of which waited for: 11 -> 11; matrix products, arithmetic and copies ran while one was open for 0% -> 1% of each run, Pallas kernels for 7% -> 13%
where the time goes in v6:
time: 94.7 us; the launch traced here: 94.1 us
  starting transfers between devices  41.3 us (44%)
  waiting for transfers between devices  32.6 us (34%)
  Pallas kernels  14.7 us (16%)
  local copies, waits for them, and re-layouts  3.54 us (4%)
  other arithmetic  1.26 us (1%)
    ppermute x12, starting transfers between devices, around(): lax.ppermute(values, axis, [((i + step) % size, i) for i in range(size)])  15 us
    pallas_call x8, Pallas kernels, call(): pl.pallas_call(kernel, out_shape=tuple((jax.ShapeDtypeStruct(s, t) for s,...  14.7 us
    all_to_all x1, waiting for transfers between devices, body(): lax.all_to_all(pair.reshape(everyone), ('z', 'spatial'), 0, 0, tiled=True)  10.4 us
    ppermute x12, waiting for transfers between devices, around(): lax.ppermute(values, axis, [((i + step) % size, i) for i in range(size)])  10.4 us
    all_to_all x1, starting transfers between devices, body(): lax.all_to_all(pair.reshape(everyone), ('z', 'spatial'), 0, 0, tiled=True)  9.98 us
    all_to_all x1, waiting for transfers between devices, body(): grads = lax.all_to_all(grads, ('samples', 'x'), 0, 0, tiled=True)  7.29 us
    all_to_all x1, starting transfers between devices, body(): grads = lax.all_to_all(grads, ('samples', 'x'), 0, 0, tiled=True)  6.15 us
    all_to_all x1, starting transfers between devices, body(): lax.all_to_all(parts.reshape(everyone), ('z', 'spatial'), 0, 0, tiled=True)  5.57 us
  transfers between devices with their start and end apart: 19, of which 11 were waited for; matrix products, arithmetic and copies ran while one was open for 1% of the time, Pallas kernels for 13%

profile of v6, /device:TPU:1, one launch (start us, length us, event | category | flops | bytes accessed | tf_op | source)
XLA Modules:
  0.0 94.1 jit_solution(3899639367140219513)
XLA Ops:
  0.6 0.1 pad_add_fusion.at_ref
  0.7 0.0 copy-start.2
  0.7 0.8 copy-done.2
  1.5 0.0 copy-start.3
  1.5 0.8 copy-done.3
  2.2 1.4 %pack.1 = bf16[8,2,16,1024]{3,2,1,0:T(8,128)(2,1)} custom-call(s32[3]{0:T(128)S(1)} %pad_add_fusion.at_ref, bf16[16,1024]{1,0:T(8,128)(2,1)S(1)} %bitcast.29, bf16[16,1024]{1,0:T(8,128)(2,1)S(1)} %bitcast.30), custom_call_target="tpu_custom_call" | custom-call | tf_op jit(solution)/shard_map/pack/pallas_call | solution.py:229
  3.6 10.0 %all-to-all-start = ((bf16[16,16,1024]{2,1,0:T(8,128)(2,1)}), bf16[16,16,1024]{2,1,0:T(8,128)(2,1)S(1)}, u32[]{:S(2)}, u32[]{:S(2)}) async-start(bf16[16,16,1024]{2,1,0:T(8,128)(2,1)} %bitcast.5), calls=%async_computation | async-start | bytes 1048576 | tf_op jit(solution)/shard_map/all_to_all | solution.py:266
  13.6 0.0 copy-start
  13.6 1.0 %copy-done = bf16[27,16,512]{2,1,0:T(8,128)(2,1)S(1)} copy-done((bf16[27,16,512]{2,1,0:T(8,128)(2,1)S(1)}, bf16[27,16,512]{2,1,0:T(8,128)(2,1)}, u32[]{:S(2)}) %copy-start) | copy-done | bytes 442392
  14.6 0.0 copy-start.1
  14.6 1.0 %copy-done.1 = bf16[27,16,512]{2,1,0:T(8,128)(2,1)S(1)} copy-done((bf16[27,16,512]{2,1,0:T(8,128)(2,1)S(1)}, bf16[27,16,512]{2,1,0:T(8,128)(2,1)}, u32[]{:S(2)}) %copy-start.1) | copy-done | bytes 442392
  15.6 1.2 %regroup.1 = (bf16[432,128]{1,0:T(8,128)(2,1)S(1)}, bf16[432,128]{1,0:T(8,128)(2,1)S(1)}, bf16[432,128]{1,0:T(8,128)(2,1)S(1)}, bf16[432,128]{1,0:T(8,128)(2,1)S(1)}) custom-call(s32[3]{0:T(128)S(1)} %pad_add_fusion.at_ref, bf16[432,512]{1,0:T(8,128)(2,1)S(1)} %bitcast.27, bf16[432,512]{1,0:T(8,128)(2,1)S(1)} %bitcast.28), custom_call_target="tpu_custom_call" | custom-call | flops 226492416 | tf_op jit(solution)/shard_map/regroup/pallas_call | solution.py:229
  16.8 2.6 %collective-permute-start = (bf16[432,128]{1,0:T(8,128)(2,1)S(1)}, bf16[432,128]{1,0:T(8,128)(2,1)S(1)}, u32[]{:S(2)}, u32[]{:S(2)}) collective-permute-start(bf16[432,128]{1,0:T(8,128)(2,1)S(1)} %get-tuple-element.25), channel_id=1, source_target_pairs={{2,0},{4,2},{6,4},{0,6},{3,1},{5,3},{7,5},{1,7},{10,8},{12,10},{14... | collective-permute-start | bytes 331784 | tf_op jit(solution)/shard_map/ppermute | solution.py:247
  19.4 0.5 collective-permute-start.1
  19.9 0.6 collective-permute-start.2
  20.5 10.4 %all-to-all-done = bf16[16,16,1024]{2,1,0:T(8,128)(2,1)S(1)} async-done(((bf16[16,16,1024]{2,1,0:T(8,128)(2,1)}), bf16[16,16,1024]{2,1,0:T(8,128)(2,1)S(1)}, u32[]{:S(2)}, u32[]{:S(2)}) %all-to-all-start) | async-done | bytes 524320 | tf_op jit(solution)/shard_map/all_to_all | solution.py:266
  30.9 0.0 collective-permute-start.10
  30.9 0.0 collective-permute-done.refs_1_
  30.9 0.0 collective-permute-done.1.refs_2_
  30.9 0.0 collective-permute-done.2.refs_3_
  30.9 2.5 %conv_in.1 = (f32[2,16,1024]{2,1,0:T(8,128)S(1)}, bf16[2,16,1024]{2,1,0:T(8,128)(2,1)S(1)}, bf16[2,16,1024]{2,1,0:T(8,128)(2,1)S(1)}, bf16[2,16,1024]{2,1,0:T(8,128)(2,1)S(1)}, bf16[4,432,128]{2,1,0:T(8,128)(2,1)S(1)}) custom-call(s32[3]{0:T(128)S(1)} %pad_add_fusion.at_ref, bf16[8,2,16,1024]{3,2,1,0:T(8,128)(2,1)S(1)} %bitcast.23, ...), custom_call_target="tpu_custom_call" | custom-call | flops 603979776 | tf_op jit(solution)/shard_map/conv_in/pallas_call | solution.py:229
  33.4 1.3 %collective-permute-start.3 = (bf16[2,16,1024]{2,1,0:T(8,128)(2,1)S(1)}, bf16[2,16,1024]{2,1,0:T(8,128)(2,1)S(1)}, u32[]{:S(2)}, u32[]{:S(2)}) collective-permute-start(bf16[2,16,1024]{2,1,0:T(8,128)(2,1)S(1)} %get-tuple-element.29), channel_id=1, source_target_pairs={{6,0},{0,2},{2,4},{4,6},{7,1},{1,3},{3,5},{5,7},{14,8},{8,10},{10,... | collective-permute-start | bytes 196616 | tf_op jit(solution)/shard_map/ppermute | solution.py:247
  34.7 2.4 %collective-permute-start.4 = (bf16[2,16,1024]{2,1,0:T(8,128)(2,1)S(1)}, bf16[2,16,1024]{2,1,0:T(8,128)(2,1)S(1)}, u32[]{:S(2)}, u32[]{:S(2)}) collective-permute-start(bf16[2,16,1024]{2,1,0:T(8,128)(2,1)S(1)} %get-tuple-element.30), channel_id=1, source_target_pairs={{4,0},{6,2},{0,4},{2,6},{5,1},{7,3},{1,5},{3,7},{12,8},{14,10},{8,... | collective-permute-start | bytes 196616 | tf_op jit(solution)/shard_map/ppermute | solution.py:247
  37.2 1.2 %collective-permute-start.5 = (bf16[2,16,1024]{2,1,0:T(8,128)(2,1)S(1)}, bf16[2,16,1024]{2,1,0:T(8,128)(2,1)S(1)}, u32[]{:S(2)}, u32[]{:S(2)}) collective-permute-start(bf16[2,16,1024]{2,1,0:T(8,128)(2,1)S(1)} %get-tuple-element.31), channel_id=1, source_target_pairs={{2,0},{4,2},{6,4},{0,6},{3,1},{5,3},{7,5},{1,7},{10,8},{12,10},{14... | collective-permute-start | bytes 196616 | tf_op jit(solution)/shard_map/ppermute | solution.py:247
  38.3 0.0 collective-permute-done.3
  38.3 1.7 %collective-permute-done.4 = bf16[2,16,1024]{2,1,0:T(8,128)(2,1)S(1)} collective-permute-done((bf16[2,16,1024]{2,1,0:T(8,128)(2,1)S(1)}, bf16[2,16,1024]{2,1,0:T(8,128)(2,1)S(1)}, u32[]{:S(2)}, u32[]{:S(2)}) %collective-permute-start.4) | collective-permute-done | bytes 65568 | tf_op jit(solution)/shard_map/ppermute | solution.py:247
  40.0 0.6 collective-permute-done.5
  40.7 1.9 %collective-permute-start.6 = (f32[2,16,1024]{2,1,0:T(8,128)S(1)}, f32[2,16,1024]{2,1,0:T(8,128)S(1)}, u32[]{:S(2)}, u32[]{:S(2)}) collective-permute-start(f32[2,16,1024]{2,1,0:T(8,128)S(1)} %add_add_fusion.own_ref), channel_id=1, source_target_pairs={{0,1},{1,0},{2,3},{3,2},{4,5},{5,4},{6,7},{7,6},{8,9},{9,8},{10,11... | collective-permute-start | bytes 393224 | tf_op jit(solution)/shard_map/ppermute | solution.py:242
  42.6 1.0 %collective-permute-done.6.other_ref = f32[2,16,1024]{2,1,0:T(8,128)S(1)} collective-permute-done((f32[2,16,1024]{2,1,0:T(8,128)S(1)}, f32[2,16,1024]{2,1,0:T(8,128)S(1)}, u32[]{:S(2)}, u32[]{:S(2)}) %collective-permute-start.6) | collective-permute-done | bytes 131104 | tf_op jit(solution)/shard_map/ppermute | solution.py:242
  43.6 0.6 act.1.refs_0_
  44.2 0.4 collective-permute-start.9
  44.6 3.3 %collective-permute-start.8 = (bf16[2,16,1024]{2,1,0:T(8,128)(2,1)S(1)}, bf16[2,16,1024]{2,1,0:T(8,128)(2,1)S(1)}, u32[]{:S(2)}, u32[]{:S(2)}) collective-permute-start(bf16[2,16,1024]{2,1,0:T(8,128)(2,1)S(1)} %act.1.refs_0_), channel_id=1, source_target_pairs={{4,0},{6,2},{0,4},{2,6},{5,1},{7,3},{1,5},{3,7},{12,8},{14,10},{8,... | collective-permute-start | bytes 196616 | tf_op jit(solution)/shard_map/ppermute | solution.py:247
  47.8 0.0 collective-permute-start.7
  47.8 1.2 %collective-permute-start.11 = (bf16[4,432,128]{2,1,0:T(8,128)(2,1)S(1)}, bf16[4,432,128]{2,1,0:T(8,128)(2,1)S(1)}, u32[]{:S(2)}, u32[]{:S(2)}) collective-permute-start(bf16[4,432,128]{2,1,0:T(8,128)(2,1)S(1)} %get-tuple-element.33), channel_id=1, source_target_pairs={{0,1},{1,0},{2,3},{3,2},{4,5},{5,4},{6,7},{7,6},{8,9},{9,8},{10,11... | collective-permute-start | bytes 1327112 | tf_op jit(solution)/shard_map/ppermute | solution.py:242
  49.0 0.0 collective-permute-done.9.refs_3_
  49.0 1.7 %collective-permute-done.8.refs_2_ = bf16[2,16,1024]{2,1,0:T(8,128)(2,1)S(1)} collective-permute-done((bf16[2,16,1024]{2,1,0:T(8,128)(2,1)S(1)}, bf16[2,16,1024]{2,1,0:T(8,128)(2,1)S(1)}, u32[]{:S(2)}, u32[]{:S(2)}) %collective-permute-start.8) | collective-permute-done | bytes 65568 | tf_op jit(solution)/shard_map/ppermute | solution.py:247
  50.8 0.5 collective-permute-done.7.refs_1_
  51.3 0.0 collective-permute-done.10.refs_4_
  51.3 2.9 %grad.1 = (bf16[16,112,128]{2,1,0:T(8,128)(2,1)}, bf16[1152,1024]{1,0:T(8,128)(2,1)S(1)}) custom-call(s32[3]{0:T(128)S(1)} %pad_add_fusion.at_ref, bf16[2,16,1024]{2,1,0:T(8,128)(2,1)S(1)} %act.1.refs_0_, bf16[2,16,1024]{2,1,0:T(8,128)(2,1)S(1)} %collective-permute-done.7.refs_1_, bf16[2,16,1024]{2,1,0:T(8,128)(2,1)S(1)} %collective-permute-done.8.refs_2_, ...), custom_call_target="tpu_custom_call" | custom-call | flops 603979776 | tf_op jit(solution)/shard_map/grad/pallas_call | solution.py:229
  54.2 6.1 %all-to-all-start.1 = ((bf16[16,112,128]{2,1,0:T(8,128)(2,1)}), bf16[16,112,128]{2,1,0:T(8,128)(2,1)}, u32[]{:S(2)}, u32[]{:S(2)}) async-start(bf16[16,112,128]{2,1,0:T(8,128)(2,1)} %get-tuple-element.34), calls=%async_computation.1 | async-start | bytes 917504 | tf_op jit(solution)/shard_map/all_to_all | solution.py:289
  60.4 0.0 collective-permute-done.11.held
  60.4 2.3 %conv_out.1 = bf16[8,2,16,1024]{3,2,1,0:T(8,128)(2,1)} custom-call(s32[3]{0:T(128)S(1)} %pad_add_fusion.at_ref, bf16[1152,1024]{1,0:T(8,128)(2,1)S(1)} %get-tuple-element.32.col, bf16[4,432,128]{2,1,0:T(8,128)(2,1)S(1)} %collective-permute-done.11.held), custom_call_target="tpu_custom_call" | custom-call | flops 603979776 | tf_op jit(solution)/shard_map/conv_out/pallas_call | solution.py:229
  62.7 7.3 %all-to-all-done.1 = bf16[16,112,128]{2,1,0:T(8,128)(2,1)} async-done(((bf16[16,112,128]{2,1,0:T(8,128)(2,1)}), bf16[16,112,128]{2,1,0:T(8,128)(2,1)}, u32[]{:S(2)}, u32[]{:S(2)}) %all-to-all-start.1) | async-done | bytes 458784 | tf_op jit(solution)/shard_map/all_to_all | solution.py:289
  69.9 5.6 %all-to-all-start.2 = ((bf16[16,16,1024]{2,1,0:T(8,128)(2,1)}), bf16[16,16,1024]{2,1,0:T(8,128)(2,1)S(1)}, u32[]{:S(2)}, u32[]{:S(2)}) async-start(bf16[16,16,1024]{2,1,0:T(8,128)(2,1)} %bitcast.9), calls=%async_computation.2 | async-start | bytes 1048576 | tf_op jit(solution)/shard_map/all_to_all | solution.py:297
  75.5 1.1 %reduce_sum.12.refs_0_ = bf16[4,112,128]{2,1,0:T(8,128)(2,1)S(1)} reduce(bf16[4,4,112,128]{3,2,1,0:T(8,128)(2,1)} %bitcast.10, bf16[]{:T(256)} %constant.14.clone.1), dimensions={0}, to_apply=%region_0.0 | reduce | flops 172032 | bytes 573442 | tf_op jit(solution)/shard_map/reduce_sum | solution.py:299
  76.6 0.1 collective-permute-start.14
  76.7 1.7 %collective-permute-start.13 = (bf16[4,112,128]{2,1,0:T(8,128)(2,1)S(1)}, bf16[4,112,128]{2,1,0:T(8,128)(2,1)S(1)}, u32[]{:S(2)}, u32[]{:S(2)}) collective-permute-start(bf16[4,112,128]{2,1,0:T(8,128)(2,1)S(1)} %reduce_sum.12.refs_0_), channel_id=1, source_target_pairs={{128,0},{192,64},{0,128},{64,192},{129,1},{193,65},{1,129},{65,193... | collective-permute-start | bytes 344072 | tf_op jit(solution)/shard_map/ppermute | solution.py:247
  78.4 0.9 collective-permute-start.12
  79.4 5.5 %collective-permute-done.14.refs_3_ = bf16[4,112,128]{2,1,0:T(8,128)(2,1)S(1)} collective-permute-done((bf16[4,112,128]{2,1,0:T(8,128)(2,1)S(1)}, bf16[4,112,128]{2,1,0:T(8,128)(2,1)S(1)}, u32[]{:S(2)}, u32[]{:S(2)}) %collective-permute-start.14) | collective-permute-done | bytes 114720 | tf_op jit(solution)/shard_map/ppermute | solution.py:247
  84.9 0.0 collective-permute-done.13.refs_2_
  84.9 0.3 collective-permute-done.12.refs_1_
  85.2 0.1 pad_maximum_fusion
  85.2 1.4 %collective-permute-start.15 = (bf16[4,4,112,128]{3,2,1,0:T(8,128)(2,1)S(1)}, bf16[4,4,112,128]{3,2,1,0:T(8,128)(2,1)S(1)}, u32[]{:S(2)}, u32[]{:S(2)}) collective-permute-start(bf16[4,4,112,128]{3,2,1,0:T(8,128)(2,1)S(1)} %pad_maximum_fusion), channel_id=1, source_target_pairs={{0,1},{1,0},{2,3},{3,2},{4,5},{5,4},{6,7},{7,6},{8,9},{9,8},{10,11... | collective-permute-start | bytes 1376264 | tf_op jit(solution)/shard_map/ppermute | solution.py:242
  86.7 1.4 %collective-permute-done.15.refs_4_ = bf16[4,4,112,128]{3,2,1,0:T(8,128)(2,1)S(1)} collective-permute-done((bf16[4,4,112,128]{3,2,1,0:T(8,128)(2,1)S(1)}, bf16[4,4,112,128]{3,2,1,0:T(8,128)(2,1)S(1)}, u32[]{:S(2)}, u32[]{:S(2)}) %collective-permute-start.15) | collective-permute-done | bytes 458784 | tf_op jit(solution)/shard_map/ppermute | solution.py:242
  88.1 2.6 %finish.1 = (f32[432,512]{1,0:T(8,128)}, f32[432,512]{1,0:T(8,128)}) custom-call(s32[3]{0:T(128)S(1)} %pad_add_fusion.at_ref, bf16[4,112,128]{2,1,0:T(8,128)(2,1)S(1)} %reduce_sum.12.refs_0_, bf16[4,112,128]{2,1,0:T(8,128)(2,1)S(1)} %collective-permute-done.12.refs_1_, bf16[4,112,128]{2,1,0:T(8,128)(2,1)S(1)} %collective-permute-done.13.refs_2_, ...), custom_call_target="tpu_custom_call" | custom-call | tf_op jit(solution)/shard_map/finish/pallas_call | solution.py:229
  90.7 2.1 %all-to-all-done.2 = bf16[16,16,1024]{2,1,0:T(8,128)(2,1)S(1)} async-done(((bf16[16,16,1024]{2,1,0:T(8,128)(2,1)}), bf16[16,16,1024]{2,1,0:T(8,128)(2,1)S(1)}, u32[]{:S(2)}, u32[]{:S(2)}) %all-to-all-start.2) | async-done | bytes 524320 | tf_op jit(solution)/shard_map/all_to_all | solution.py:297
  92.9 1.2 %sum.1 = (bf16[16,1024]{1,0:T(8,128)(2,1)}, bf16[16,1024]{1,0:T(8,128)(2,1)}) custom-call(s32[3]{0:T(128)S(1)} %pad_add_fusion.at_ref, bf16[8,2,16,1024]{3,2,1,0:T(8,128)(2,1)S(1)} %bitcast.20), custom_call_target="tpu_custom_call" | custom-call | tf_op jit(solution)/shard_map/sum/pallas_call | solution.py:229
  (1 shorter events, 0.0 us)
Async XLA Ops:
  0.7 0.8 copy-start.2
  1.5 0.8 copy-start.3
  3.6 27.3 %all-to-all-start = ((bf16[16,16,1024]{2,1,0:T(8,128)(2,1)}), bf16[16,16,1024]{2,1,0:T(8,128)(2,1)S(1)}, u32[]{:S(2)}, u32[]{:S(2)}) async-start(bf16[16,16,1024]{2,1,0:T(8,128)(2,1)} %bitcast.5), calls=%async_computation | async-start | bytes 1048576 | tf_op jit(solution)/shard_map/all_to_all | solution.py:266
  13.6 1.0 %copy-start = (bf16[27,16,512]{2,1,0:T(8,128)(2,1)S(1)}, bf16[27,16,512]{2,1,0:T(8,128)(2,1)}, u32[]{:S(2)}) copy-start(bf16[27,16,512]{2,1,0:T(8,128)(2,1)} %param.5) | copy-start | bytes 1327108
  14.6 1.0 %copy-start.1 = (bf16[27,16,512]{2,1,0:T(8,128)(2,1)S(1)}, bf16[27,16,512]{2,1,0:T(8,128)(2,1)}, u32[]{:S(2)}) copy-start(bf16[27,16,512]{2,1,0:T(8,128)(2,1)} %param.6) | copy-start | bytes 1327108
  16.8 14.1 %collective-permute-start = (bf16[432,128]{1,0:T(8,128)(2,1)S(1)}, bf16[432,128]{1,0:T(8,128)(2,1)S(1)}, u32[]{:S(2)}, u32[]{:S(2)}) collective-permute-start(bf16[432,128]{1,0:T(8,128)(2,1)S(1)} %get-tuple-element.25), channel_id=1, source_target_pairs={{2,0},{4,2},{6,4},{0,6},{3,1},{5,3},{7,5},{1,7},{10,8},{12,10},{14... | collective-permute-start | bytes 331784 | tf_op jit(solution)/shard_map/ppermute | solution.py:247
  19.4 11.5 %collective-permute-start.1 = (bf16[432,128]{1,0:T(8,128)(2,1)S(1)}, bf16[432,128]{1,0:T(8,128)(2,1)S(1)}, u32[]{:S(2)}, u32[]{:S(2)}) collective-permute-start(bf16[432,128]{1,0:T(8,128)(2,1)S(1)} %get-tuple-element.26), channel_id=1, source_target_pairs={{4,0},{6,2},{0,4},{2,6},{5,1},{7,3},{1,5},{3,7},{12,8},{14,10},{8,... | collective-permute-start | bytes 331784 | tf_op jit(solution)/shard_map/ppermute | solution.py:247
  19.9 11.0 %collective-permute-start.2 = (bf16[432,128]{1,0:T(8,128)(2,1)S(1)}, bf16[432,128]{1,0:T(8,128)(2,1)S(1)}, u32[]{:S(2)}, u32[]{:S(2)}) collective-permute-start(bf16[432,128]{1,0:T(8,128)(2,1)S(1)} %get-tuple-element.27), channel_id=1, source_target_pairs={{6,0},{0,2},{2,4},{4,6},{7,1},{1,3},{3,5},{5,7},{14,8},{8,10},{10,... | collective-permute-start | bytes 331784 | tf_op jit(solution)/shard_map/ppermute | solution.py:247
  30.9 20.4 %collective-permute-start.10 = (bf16[8,2,16,1024]{3,2,1,0:T(8,128)(2,1)S(1)}, bf16[8,2,16,1024]{3,2,1,0:T(8,128)(2,1)S(1)}, u32[]{:S(2)}, u32[]{:S(2)}) collective-permute-start(bf16[8,2,16,1024]{3,2,1,0:T(8,128)(2,1)S(1)} %bitcast.22), channel_id=1, source_target_pairs={{0,1},{1,0},{2,3},{3,2},{4,5},{5,4},{6,7},{7,6},{8,9},{9,8},{10,11... | collective-permute-start | bytes 1572872 | tf_op jit(solution)/shard_map/ppermute | solution.py:242
  33.4 4.9 %collective-permute-start.3 = (bf16[2,16,1024]{2,1,0:T(8,128)(2,1)S(1)}, bf16[2,16,1024]{2,1,0:T(8,128)(2,1)S(1)}, u32[]{:S(2)}, u32[]{:S(2)}) collective-permute-start(bf16[2,16,1024]{2,1,0:T(8,128)(2,1)S(1)} %get-tuple-element.29), channel_id=1, source_target_pairs={{6,0},{0,2},{2,4},{4,6},{7,1},{1,3},{3,5},{5,7},{14,8},{8,10},{10,... | collective-permute-start | bytes 196616 | tf_op jit(solution)/shard_map/ppermute | solution.py:247
  34.7 5.3 %collective-permute-start.4 = (bf16[2,16,1024]{2,1,0:T(8,128)(2,1)S(1)}, bf16[2,16,1024]{2,1,0:T(8,128)(2,1)S(1)}, u32[]{:S(2)}, u32[]{:S(2)}) collective-permute-start(bf16[2,16,1024]{2,1,0:T(8,128)(2,1)S(1)} %get-tuple-element.30), channel_id=1, source_target_pairs={{4,0},{6,2},{0,4},{2,6},{5,1},{7,3},{1,5},{3,7},{12,8},{14,10},{8,... | collective-permute-start | bytes 196616 | tf_op jit(solution)/shard_map/ppermute | solution.py:247
  37.2 3.5 %collective-permute-start.5 = (bf16[2,16,1024]{2,1,0:T(8,128)(2,1)S(1)}, bf16[2,16,1024]{2,1,0:T(8,128)(2,1)S(1)}, u32[]{:S(2)}, u32[]{:S(2)}) collective-permute-start(bf16[2,16,1024]{2,1,0:T(8,128)(2,1)S(1)} %get-tuple-element.31), channel_id=1, source_target_pairs={{2,0},{4,2},{6,4},{0,6},{3,1},{5,3},{7,5},{1,7},{10,8},{12,10},{14... | collective-permute-start | bytes 196616 | tf_op jit(solution)/shard_map/ppermute | solution.py:247
  40.7 2.9 %collective-permute-start.6 = (f32[2,16,1024]{2,1,0:T(8,128)S(1)}, f32[2,16,1024]{2,1,0:T(8,128)S(1)}, u32[]{:S(2)}, u32[]{:S(2)}) collective-permute-start(f32[2,16,1024]{2,1,0:T(8,128)S(1)} %add_add_fusion.own_ref), channel_id=1, source_target_pairs={{0,1},{1,0},{2,3},{3,2},{4,5},{5,4},{6,7},{7,6},{8,9},{9,8},{10,11... | collective-permute-start | bytes 393224 | tf_op jit(solution)/shard_map/ppermute | solution.py:242
  44.2 4.8 %collective-permute-start.9 = (bf16[2,16,1024]{2,1,0:T(8,128)(2,1)S(1)}, bf16[2,16,1024]{2,1,0:T(8,128)(2,1)S(1)}, u32[]{:S(2)}, u32[]{:S(2)}) collective-permute-start(bf16[2,16,1024]{2,1,0:T(8,128)(2,1)S(1)} %act.1.refs_0_), channel_id=1, source_target_pairs={{6,0},{0,2},{2,4},{4,6},{7,1},{1,3},{3,5},{5,7},{14,8},{8,10},{10,... | collective-permute-start | bytes 196616 | tf_op jit(solution)/shard_map/ppermute | solution.py:247
  44.6 6.2 %collective-permute-start.8 = (bf16[2,16,1024]{2,1,0:T(8,128)(2,1)S(1)}, bf16[2,16,1024]{2,1,0:T(8,128)(2,1)S(1)}, u32[]{:S(2)}, u32[]{:S(2)}) collective-permute-start(bf16[2,16,1024]{2,1,0:T(8,128)(2,1)S(1)} %act.1.refs_0_), channel_id=1, source_target_pairs={{4,0},{6,2},{0,4},{2,6},{5,1},{7,3},{1,5},{3,7},{12,8},{14,10},{8,... | collective-permute-start | bytes 196616 | tf_op jit(solution)/shard_map/ppermute | solution.py:247
  47.8 3.5 %collective-permute-start.7 = (bf16[2,16,1024]{2,1,0:T(8,128)(2,1)S(1)}, bf16[2,16,1024]{2,1,0:T(8,128)(2,1)S(1)}, u32[]{:S(2)}, u32[]{:S(2)}) collective-permute-start(bf16[2,16,1024]{2,1,0:T(8,128)(2,1)S(1)} %act.1.refs_0_), channel_id=1, source_target_pairs={{2,0},{4,2},{6,4},{0,6},{3,1},{5,3},{7,5},{1,7},{10,8},{12,10},{14... | collective-permute-start | bytes 196616 | tf_op jit(solution)/shard_map/ppermute | solution.py:247
  47.8 12.5 %collective-permute-start.11 = (bf16[4,432,128]{2,1,0:T(8,128)(2,1)S(1)}, bf16[4,432,128]{2,1,0:T(8,128)(2,1)S(1)}, u32[]{:S(2)}, u32[]{:S(2)}) collective-permute-start(bf16[4,432,128]{2,1,0:T(8,128)(2,1)S(1)} %get-tuple-element.33), channel_id=1, source_target_pairs={{0,1},{1,0},{2,3},{3,2},{4,5},{5,4},{6,7},{7,6},{8,9},{9,8},{10,11... | collective-permute-start | bytes 1327112 | tf_op jit(solution)/shard_map/ppermute | solution.py:242
  54.2 15.7 %all-to-all-start.1 = ((bf16[16,112,128]{2,1,0:T(8,128)(2,1)}), bf16[16,112,128]{2,1,0:T(8,128)(2,1)}, u32[]{:S(2)}, u32[]{:S(2)}) async-start(bf16[16,112,128]{2,1,0:T(8,128)(2,1)} %get-tuple-element.34), calls=%async_computation.1 | async-start | bytes 917504 | tf_op jit(solution)/shard_map/all_to_all | solution.py:289
  69.9 22.9 %all-to-all-start.2 = ((bf16[16,16,1024]{2,1,0:T(8,128)(2,1)}), bf16[16,16,1024]{2,1,0:T(8,128)(2,1)S(1)}, u32[]{:S(2)}, u32[]{:S(2)}) async-start(bf16[16,16,1024]{2,1,0:T(8,128)(2,1)} %bitcast.9), calls=%async_computation.2 | async-start | bytes 1048576 | tf_op jit(solution)/shard_map/all_to_all | solution.py:297
  76.6 8.3 %collective-permute-start.14 = (bf16[4,112,128]{2,1,0:T(8,128)(2,1)S(1)}, bf16[4,112,128]{2,1,0:T(8,128)(2,1)S(1)}, u32[]{:S(2)}, u32[]{:S(2)}) collective-permute-start(bf16[4,112,128]{2,1,0:T(8,128)(2,1)S(1)} %reduce_sum.12.refs_0_), channel_id=1, source_target_pairs={{192,0},{0,64},{64,128},{128,192},{193,1},{1,65},{65,129},{129,193... | collective-permute-start | bytes 344072 | tf_op jit(solution)/shard_map/ppermute | solution.py:247
  76.7 8.2 %collective-permute-start.13 = (bf16[4,112,128]{2,1,0:T(8,128)(2,1)S(1)}, bf16[4,112,128]{2,1,0:T(8,128)(2,1)S(1)}, u32[]{:S(2)}, u32[]{:S(2)}) collective-permute-start(bf16[4,112,128]{2,1,0:T(8,128)(2,1)S(1)} %reduce_sum.12.refs_0_), channel_id=1, source_target_pairs={{128,0},{192,64},{0,128},{64,192},{129,1},{193,65},{1,129},{65,193... | collective-permute-start | bytes 344072 | tf_op jit(solution)/shard_map/ppermute | solution.py:247
  78.4 6.7 %collective-permute-start.12 = (bf16[4,112,128]{2,1,0:T(8,128)(2,1)S(1)}, bf16[4,112,128]{2,1,0:T(8,128)(2,1)S(1)}, u32[]{:S(2)}, u32[]{:S(2)}) collective-permute-start(bf16[4,112,128]{2,1,0:T(8,128)(2,1)S(1)} %reduce_sum.12.refs_0_), channel_id=1, source_target_pairs={{64,0},{128,64},{192,128},{0,192},{65,1},{129,65},{193,129},{1,193... | collective-permute-start | bytes 344072 | tf_op jit(solution)/shard_map/ppermute | solution.py:247
  85.2 2.9 %collective-permute-start.15 = (bf16[4,4,112,128]{3,2,1,0:T(8,128)(2,1)S(1)}, bf16[4,4,112,128]{3,2,1,0:T(8,128)(2,1)S(1)}, u32[]{:S(2)}, u32[]{:S(2)}) collective-permute-start(bf16[4,4,112,128]{3,2,1,0:T(8,128)(2,1)S(1)} %pad_maximum_fusion), channel_id=1, source_target_pairs={{0,1},{1,0},{2,3},{3,2},{4,5},{5,4},{6,7},{7,6},{8,9},{9,8},{10,11... | collective-permute-start | bytes 1376264 | tf_op jit(solution)/shard_map/ppermute | solution.py:242

commit v7 on v5

--- a/solution.py
+++ b/solution.py
@@ -133,7 +133,8 @@
 
 
 def second_kernel(at_ref, *refs):
-    acts, held, across, (out_ref, grad_ref, col, tall, both) = refs[:NX], refs[NX], refs[NX + 1], refs[NX + 2 :]
+    acts, held, across, refs = refs[:NX], refs[NX], refs[NX + 1], refs[NX + 2 :]
+    out_refs, (grad_ref, col, tall, both, parts) = refs[:NZ], refs[NZ:]
     width = held.shape[1] // 27
     third = 9 * width
     group = NZ * width
@@ -164,7 +165,9 @@
             for k in range(NX):
                 tall[2 * third * k : 2 * third * (k + 1), :] = held[k, at : at + 2 * third, :]
             part = dot(tall[...], col[...], ((0,), (0,)))
-            out_ref[:, d] = part.astype(BF16).reshape(NZ, width, PLANE)
+            parts[:, d] = part.astype(BF16).reshape(NZ, width, PLANE)
+        for k in range(NZ):
+            out_refs[k][...] = parts[lax.rem(at_ref[3] + k, NZ)]
 
     @pl.when(at_ref[0] == 0)
     def _():
@@ -230,7 +233,7 @@
 
 def body(features, conv_one, conv_two, cotangent):
     width, channels = conv_one.shape[1], conv_one.shape[2]
-    at = jnp.stack([lax.axis_index(a) for a in ("spatial", "x", "samples")]).astype(jnp.int32)
+    at = jnp.stack([lax.axis_index(a) for a in ("spatial", "x", "samples", "z")]).astype(jnp.int32)
     one = conv_one.reshape(27 * width, channels)
     two = conv_two.reshape(27 * width, channels)
     taps = 27 * width
@@ -259,14 +262,18 @@
 
     (send,) = call(act_kernel, [(plane, BF16)], [], "act", 0, at, own, swap(own))
     acts = [send] + [around(send, "x", k) for k in range(1, NX)]
-    parts, grads = call(
+    *parts, grads = call(
         second_kernel,
-        [((NZ,) + plane, BF16), ((4 * NX,) + piece, BF16)],
-        [((NX * 18 * width, PLANE), BF16), ((NX * 18 * width, group), BF16), ((2 * group, PLANE), BF16)],
+        [(plane, BF16)] * NZ + [((4 * NX,) + piece, BF16)],
+        [((NX * 18 * width, PLANE), BF16), ((NX * 18 * width, group), BF16), ((2 * group, PLANE), BF16), ((NZ,) + plane, BF16)],
         "conv_out", 2 * work, at, *acts, held, across,
     )
     grads = lax.all_to_all(grads, ("samples", "x"), 0, 0, tiled=True)
-    parts = lax.all_to_all(parts.reshape(everyone), ("z", "spatial"), 0, 0, tiled=True)
+    parts = [parts[0]] + [around(parts[k], "z", NZ - k) for k in (4, 3, 5, 2, 6, 1, 7)]
+    result = sum(part.astype(F32) for part in parts).astype(BF16)
+    first = lax.axis_index("spatial") == 0
+    ours = jnp.where(first, result[0], result[1])
+    theirs = swap(jnp.where(first, result[1], result[0]))
 
     summed = jnp.sum(grads.reshape((4, NX) + piece).astype(F32), axis=0).astype(BF16)
     pieces = [summed] + [around(summed, "samples", k) for k in (1, 2, 3)]
@@ -274,12 +281,11 @@
     grad_one, grad_two = call(
         finish_kernel, [((taps, channels), F32)] * 2, [((28 * width, channels), BF16)] * 2, "finish", 0, at, *pieces, others
     )
-    parts, grad_one, grad_two = lax.optimization_barrier((parts, grad_one, grad_two))
-
-    result = jnp.sum(parts.reshape((NZ,) + plane).astype(F32), axis=0).astype(BF16)
     shape = (width, 1, 1, PLANE)
+    mixed_out = jnp.where(first, ours, theirs).reshape(shape)
+    input_grad = jnp.where(first, theirs, ours).reshape(shape)
     weights = (27, width, channels)
-    return result[0].reshape(shape), result[1].reshape(shape), grad_one.reshape(weights), grad_two.reshape(weights)
+    return mixed_out, input_grad, grad_one.reshape(weights), grad_two.reshape(weights)
 
 
 def solution(mesh):

time: 93.2 us -> 90.5 us (0.971)
  starting transfers between devices: 35.3 us -> 52.4 us
  blocking collectives: 15.5 us -> 0 us
  waiting for transfers between devices: 28.2 us -> 23.8 us
    all_to_all x1 -> x0, blocking collectives: 15.5 us -> none  [body(): grads = lax.all_to_all(grads, ('samples', 'x'), 0, 0, tiled=True)]
    ppermute x12 -> x19, starting transfers between devices: 15 us -> 27.2 us  [around(): lax.ppermute(values, axis, [((i + step) % size, i) for i in range(size)])]
    ppermute x4 -> x5, starting transfers between devices: 4.7 us -> 9.05 us  [swap(): return lax.ppermute(values, 'spatial', [(0, 1), (1, 0)])]
    all_to_all x1, waiting for transfers between devices: 3.16 us -> 0.01 us  [body(): grads = lax.all_to_all(grads, ('samples', 'x'), 0, 0, tiled=True)]
    ppermute x12 -> x19, waiting for transfers between devices: 10.3 us -> 9.13 us  [around(): lax.ppermute(values, axis, [((i + step) % size, i) for i in range(size)])]
    ppermute x4 -> x5, waiting for transfers between devices: 2.43 us -> 2.37 us  [swap(): return lax.ppermute(values, 'spatial', [(0, 1), (1, 0)])]
  transfers between devices with their start and end apart: 18 -> 26, of which waited for: 11 -> 12; matrix products, arithmetic and copies ran while one was open for 0% -> 1% of each run, Pallas kernels for 7% -> 5%
where the time goes in v7:
time: 90.5 us; the launch traced here: 90.2 us
  starting transfers between devices  52.4 us (58%)
  waiting for transfers between devices  23.8 us (26%)
  Pallas kernels  10.6 us (12%)
  other arithmetic  1.74 us (2%)
    ppermute x19, starting transfers between devices, around(): lax.ppermute(values, axis, [((i + step) % size, i) for i in range(size)])  27.2 us
    all_to_all x1, waiting for transfers between devices, body(): lax.all_to_all(pair, ('z', 'spatial'), 0, 0, tiled=True)  12.3 us
    pallas_call x5, Pallas kernels, call(): pl.pallas_call(kernel, out_shape=tuple((jax.ShapeDtypeStruct(s, t) for s,...  10.6 us
    all_to_all x1, starting transfers between devices, body(): lax.all_to_all(pair, ('z', 'spatial'), 0, 0, tiled=True)  10.1 us
    ppermute x19, waiting for transfers between devices, around(): lax.ppermute(values, axis, [((i + step) % size, i) for i in range(size)])  9.13 us
    ppermute x5, starting transfers between devices, swap(): return lax.ppermute(values, 'spatial', [(0, 1), (1, 0)])  9.05 us
    all_to_all x1, starting transfers between devices, body(): grads = lax.all_to_all(grads, ('samples', 'x'), 0, 0, tiled=True)  6.1 us
    ppermute x5, waiting for transfers between devices, swap(): return lax.ppermute(values, 'spatial', [(0, 1), (1, 0)])  2.37 us
  transfers between devices with their start and end apart: 26, of which 12 were waited for; matrix products, arithmetic and copies ran while one was open for 1% of the time, Pallas kernels for 5%

profile of v7, /device:TPU:1, one launch (start us, length us, event | category | flops | bytes accessed | tf_op | source)
XLA Modules:
  0.0 90.2 jit_solution(4413136144212591125)
XLA Ops:
  0.6 0.8 pad_maximum_fusion.1
  1.4 0.9 broadcast_in_dim.3
  2.3 10.1 %all-to-all-start = ((bf16[16,16,1024]{2,1,0:T(8,128)(2,1)}), bf16[16,16,1024]{2,1,0:T(8,128)(2,1)S(1)}, u32[]{:S(2)}, u32[]{:S(2)}) async-start(bf16[16,16,1024]{2,1,0:T(8,128)(2,1)} %bitcast.6), calls=%async_computation | async-start | bytes 1048576 | tf_op jit(solution)/shard_map/all_to_all | solution.py:248
  12.4 0.1 pad_add_fusion.at_ref
  12.5 1.2 %regroup.1 = (bf16[432,128]{1,0:T(8,128)(2,1)S(1)}, bf16[432,128]{1,0:T(8,128)(2,1)S(1)}, bf16[432,128]{1,0:T(8,128)(2,1)S(1)}, bf16[432,128]{1,0:T(8,128)(2,1)S(1)}) custom-call(s32[4]{0:T(128)S(1)} %pad_add_fusion.at_ref, bf16[432,512]{1,0:T(8,128)(2,1)S(1)} %bitcast.36, bf16[432,512]{1,0:T(8,128)(2,1)S(1)} %bitcast.37), custom_call_target="tpu_custom_call" | custom-call | flops 226492416 | tf_op jit(solution)/shard_map/regroup/pallas_call | solution.py:213
  13.7 2.6 %collective-permute-start = (bf16[432,128]{1,0:T(8,128)(2,1)S(1)}, bf16[432,128]{1,0:T(8,128)(2,1)S(1)}, u32[]{:S(2)}, u32[]{:S(2)}) collective-permute-start(bf16[432,128]{1,0:T(8,128)(2,1)S(1)} %get-tuple-element.25), channel_id=1, source_target_pairs={{2,0},{4,2},{6,4},{0,6},{3,1},{5,3},{7,5},{1,7},{10,8},{12,10},{14... | collective-permute-start | bytes 331784 | tf_op jit(solution)/shard_map/ppermute | solution.py:231
  16.2 0.5 collective-permute-start.1
  16.7 0.6 collective-permute-start.2
  17.4 12.3 %all-to-all-done = bf16[16,16,1024]{2,1,0:T(8,128)(2,1)S(1)} async-done(((bf16[16,16,1024]{2,1,0:T(8,128)(2,1)}), bf16[16,16,1024]{2,1,0:T(8,128)(2,1)S(1)}, u32[]{:S(2)}, u32[]{:S(2)}) %all-to-all-start) | async-done | bytes 524320 | tf_op jit(solution)/shard_map/all_to_all | solution.py:248
  29.7 0.0 collective-permute-start.11
  29.7 0.0 collective-permute-done.refs_1_
  29.7 0.0 collective-permute-done.1.refs_2_
  29.7 0.0 collective-permute-done.2.refs_3_
  29.7 2.5 %conv_in.1 = (f32[2,16,1024]{2,1,0:T(8,128)S(1)}, bf16[2,16,1024]{2,1,0:T(8,128)(2,1)S(1)}, bf16[2,16,1024]{2,1,0:T(8,128)(2,1)S(1)}, bf16[2,16,1024]{2,1,0:T(8,128)(2,1)S(1)}, bf16[4,432,128]{2,1,0:T(8,128)(2,1)S(1)}) custom-call(s32[4]{0:T(128)S(1)} %pad_add_fusion.at_ref, bf16[8,2,16,1024]{3,2,1,0:T(8,128)(2,1)S(1)} %bitcast.32, ...), custom_call_target="tpu_custom_call" | custom-call | flops 603979776 | tf_op jit(solution)/shard_map/conv_in/pallas_call | solution.py:213
  32.2 1.3 %collective-permute-start.3 = (bf16[2,16,1024]{2,1,0:T(8,128)(2,1)S(1)}, bf16[2,16,1024]{2,1,0:T(8,128)(2,1)S(1)}, u32[]{:S(2)}, u32[]{:S(2)}) collective-permute-start(bf16[2,16,1024]{2,1,0:T(8,128)(2,1)S(1)} %get-tuple-element.29), channel_id=1, source_target_pairs={{6,0},{0,2},{2,4},{4,6},{7,1},{1,3},{3,5},{5,7},{14,8},{8,10},{10,... | collective-permute-start | bytes 196616 | tf_op jit(solution)/shard_map/ppermute | solution.py:231
  33.5 2.4 %collective-permute-start.4 = (bf16[2,16,1024]{2,1,0:T(8,128)(2,1)S(1)}, bf16[2,16,1024]{2,1,0:T(8,128)(2,1)S(1)}, u32[]{:S(2)}, u32[]{:S(2)}) collective-permute-start(bf16[2,16,1024]{2,1,0:T(8,128)(2,1)S(1)} %get-tuple-element.30), channel_id=1, source_target_pairs={{4,0},{6,2},{0,4},{2,6},{5,1},{7,3},{1,5},{3,7},{12,8},{14,10},{8,... | collective-permute-start | bytes 196616 | tf_op jit(solution)/shard_map/ppermute | solution.py:231
  36.0 1.1 %collective-permute-start.5 = (bf16[2,16,1024]{2,1,0:T(8,128)(2,1)S(1)}, bf16[2,16,1024]{2,1,0:T(8,128)(2,1)S(1)}, u32[]{:S(2)}, u32[]{:S(2)}) collective-permute-start(bf16[2,16,1024]{2,1,0:T(8,128)(2,1)S(1)} %get-tuple-element.31), channel_id=1, source_target_pairs={{2,0},{4,2},{6,4},{0,6},{3,1},{5,3},{7,5},{1,7},{10,8},{12,10},{14... | collective-permute-start | bytes 196616 | tf_op jit(solution)/shard_map/ppermute | solution.py:231
  37.1 1.3 %collective-permute-start.10 = (bf16[4,432,128]{2,1,0:T(8,128)(2,1)S(1)}, bf16[4,432,128]{2,1,0:T(8,128)(2,1)S(1)}, u32[]{:S(2)}, u32[]{:S(2)}) collective-permute-start(bf16[4,432,128]{2,1,0:T(8,128)(2,1)S(1)} %get-tuple-element.32), channel_id=1, source_target_pairs={{0,1},{1,0},{2,3},{3,2},{4,5},{5,4},{6,7},{7,6},{8,9},{9,8},{10,11... | collective-permute-start | bytes 1327112 | tf_op jit(solution)/shard_map/ppermute | solution.py:226
  38.4 0.0 collective-permute-done.3
  38.4 0.4 collective-permute-done.4
  38.8 0.6 collective-permute-done.5
  39.5 1.9 %collective-permute-start.6 = (f32[2,16,1024]{2,1,0:T(8,128)S(1)}, f32[2,16,1024]{2,1,0:T(8,128)S(1)}, u32[]{:S(2)}, u32[]{:S(2)}) collective-permute-start(f32[2,16,1024]{2,1,0:T(8,128)S(1)} %add_add_fusion.own_ref), channel_id=1, source_target_pairs={{0,1},{1,0},{2,3},{3,2},{4,5},{5,4},{6,7},{7,6},{8,9},{9,8},{10,11... | collective-permute-start | bytes 393224 | tf_op jit(solution)/shard_map/ppermute | solution.py:226
  41.4 1.0 %collective-permute-done.6.other_ref = f32[2,16,1024]{2,1,0:T(8,128)S(1)} collective-permute-done((f32[2,16,1024]{2,1,0:T(8,128)S(1)}, f32[2,16,1024]{2,1,0:T(8,128)S(1)}, u32[]{:S(2)}, u32[]{:S(2)}) %collective-permute-start.6) | collective-permute-done | bytes 131104 | tf_op jit(solution)/shard_map/ppermute | solution.py:226
  42.4 0.6 act.1.refs_0_
  43.0 0.4 collective-permute-start.9
  43.4 3.3 %collective-permute-start.8 = (bf16[2,16,1024]{2,1,0:T(8,128)(2,1)S(1)}, bf16[2,16,1024]{2,1,0:T(8,128)(2,1)S(1)}, u32[]{:S(2)}, u32[]{:S(2)}) collective-permute-start(bf16[2,16,1024]{2,1,0:T(8,128)(2,1)S(1)} %act.1.refs_0_), channel_id=1, source_target_pairs={{4,0},{6,2},{0,4},{2,6},{5,1},{7,3},{1,5},{3,7},{12,8},{14,10},{8,... | collective-permute-start | bytes 196616 | tf_op jit(solution)/shard_map/ppermute | solution.py:231
  46.6 0.0 collective-permute-start.7
  46.6 0.8 collective-permute-done.9.refs_3_
  47.4 2.2 %collective-permute-done.8.refs_2_ = bf16[2,16,1024]{2,1,0:T(8,128)(2,1)S(1)} collective-permute-done((bf16[2,16,1024]{2,1,0:T(8,128)(2,1)S(1)}, bf16[2,16,1024]{2,1,0:T(8,128)(2,1)S(1)}, u32[]{:S(2)}, u32[]{:S(2)}) %collective-permute-start.8) | collective-permute-done | bytes 65568 | tf_op jit(solution)/shard_map/ppermute | solution.py:231
  49.6 0.5 collective-permute-done.7.refs_1_
  50.1 0.0 collective-permute-done.10.refs_4_
  50.1 0.0 collective-permute-done.11.refs_5_
  50.1 3.7 %conv_out.1 = (bf16[2,16,1024]{2,1,0:T(8,128)(2,1)S(1)}, bf16[2,16,1024]{2,1,0:T(8,128)(2,1)S(1)}, bf16[2,16,1024]{2,1,0:T(8,128)(2,1)S(1)}, bf16[2,16,1024]{2,1...) custom-call(s32[4]{0:T(128)S(1)} %pad_add_fusion.at_ref, ...), custom_call_target="tpu_custom_call" | custom-call | flops 1207959552 | tf_op jit(solution)/shard_map/conv_out/pallas_call | solution.py:213
  53.8 6.1 %all-to-all-start.1 = ((bf16[16,112,128]{2,1,0:T(8,128)(2,1)}), bf16[16,112,128]{2,1,0:T(8,128)(2,1)S(1)}, u32[]{:S(2)}, u32[]{:S(2)}) async-start(bf16[16,112,128]{2,1,0:T(8,128)(2,1)} %get-tuple-element.41), calls=%async_computation.1 | async-start | bytes 917504 | tf_op jit(solution)/shard_map/all_to_all | solution.py:271
  59.9 0.9 %collective-permute-start.12 = (bf16[2,16,1024]{2,1,0:T(8,128)(2,1)S(1)}, bf16[2,16,1024]{2,1,0:T(8,128)(2,1)S(1)}, u32[]{:S(2)}, u32[]{:S(2)}) collective-permute-start(bf16[2,16,1024]{2,1,0:T(8,128)(2,1)S(1)} %get-tuple-element.34), channel_id=1, source_target_pairs={{32,0},{40,8},{48,16},{56,24},{0,32},{8,40},{16,48},{24,56},{33,1}... | collective-permute-start | bytes 196616 | tf_op jit(solution)/shard_map/ppermute | solution.py:231
  60.8 0.9 %collective-permute-start.13 = (bf16[2,16,1024]{2,1,0:T(8,128)(2,1)S(1)}, bf16[2,16,1024]{2,1,0:T(8,128)(2,1)S(1)}, u32[]{:S(2)}, u32[]{:S(2)}) collective-permute-start(bf16[2,16,1024]{2,1,0:T(8,128)(2,1)S(1)} %get-tuple-element.35), channel_id=1, source_target_pairs={{40,0},{48,8},{56,16},{0,24},{8,32},{16,40},{24,48},{32,56},{41,1}... | collective-permute-start | bytes 196616 | tf_op jit(solution)/shard_map/ppermute | solution.py:231
  61.7 3.6 %collective-permute-start.14 = (bf16[2,16,1024]{2,1,0:T(8,128)(2,1)S(1)}, bf16[2,16,1024]{2,1,0:T(8,128)(2,1)S(1)}, u32[]{:S(2)}, u32[]{:S(2)}) collective-permute-start(bf16[2,16,1024]{2,1,0:T(8,128)(2,1)S(1)} %get-tuple-element.36), channel_id=1, source_target_pairs={{24,0},{32,8},{40,16},{48,24},{56,32},{0,40},{8,48},{16,56},{25,1}... | collective-permute-start | bytes 196616 | tf_op jit(solution)/shard_map/ppermute | solution.py:231
  65.3 1.5 %collective-permute-start.15 = (bf16[2,16,1024]{2,1,0:T(8,128)(2,1)S(1)}, bf16[2,16,1024]{2,1,0:T(8,128)(2,1)S(1)}, u32[]{:S(2)}, u32[]{:S(2)}) collective-permute-start(bf16[2,16,1024]{2,1,0:T(8,128)(2,1)S(1)} %get-tuple-element.37), channel_id=1, source_target_pairs={{48,0},{56,8},{0,16},{8,24},{16,32},{24,40},{32,48},{40,56},{49,1}... | collective-permute-start | bytes 196616 | tf_op jit(solution)/shard_map/ppermute | solution.py:231
  66.8 2.1 %collective-permute-start.16 = (bf16[2,16,1024]{2,1,0:T(8,128)(2,1)S(1)}, bf16[2,16,1024]{2,1,0:T(8,128)(2,1)S(1)}, u32[]{:S(2)}, u32[]{:S(2)}) collective-permute-start(bf16[2,16,1024]{2,1,0:T(8,128)(2,1)S(1)} %get-tuple-element.38), channel_id=1, source_target_pairs={{16,0},{24,8},{32,16},{40,24},{48,32},{56,40},{0,48},{8,56},{17,1}... | collective-permute-start | bytes 196616 | tf_op jit(solution)/shard_map/ppermute | solution.py:231
  68.8 0.0 collective-permute-done.12
  68.8 1.2 %collective-permute-start.17 = (bf16[2,16,1024]{2,1,0:T(8,128)(2,1)S(1)}, bf16[2,16,1024]{2,1,0:T(8,128)(2,1)S(1)}, u32[]{:S(2)}, u32[]{:S(2)}) collective-permute-start(bf16[2,16,1024]{2,1,0:T(8,128)(2,1)S(1)} %get-tuple-element.39), channel_id=1, source_target_pairs={{56,0},{0,8},{8,16},{16,24},{24,32},{32,40},{40,48},{48,56},{57,1}... | collective-permute-start | bytes 196616 | tf_op jit(solution)/shard_map/ppermute | solution.py:231
  70.0 1.8 %collective-permute-done.13 = bf16[2,16,1024]{2,1,0:T(8,128)(2,1)S(1)} collective-permute-done((bf16[2,16,1024]{2,1,0:T(8,128)(2,1)S(1)}, bf16[2,16,1024]{2,1,0:T(8,128)(2,1)S(1)}, u32[]{:S(2)}, u32[]{:S(2)}) %collective-permute-start.13) | collective-permute-done | bytes 65568 | tf_op jit(solution)/shard_map/ppermute | solution.py:231
  71.8 0.0 collective-permute-start.18
  71.8 0.0 all-to-all-done.1
  71.8 0.1 reduce_sum.12.refs_0_
  71.8 0.0 collective-permute-done.14
  71.9 1.1 %collective-permute-start.22 = (bf16[4,112,128]{2,1,0:T(8,128)(2,1)S(1)}, bf16[4,112,128]{2,1,0:T(8,128)(2,1)S(1)}, u32[]{:S(2)}, u32[]{:S(2)}) collective-permute-start(bf16[4,112,128]{2,1,0:T(8,128)(2,1)S(1)} %reduce_sum.12.refs_0_), channel_id=1, source_target_pairs={{192,0},{0,64},{64,128},{128,192},{193,1},{1,65},{65,129},{129,193... | collective-permute-start | bytes 344072 | tf_op jit(solution)/shard_map/ppermute | solution.py:231
  73.0 0.2 collective-permute-done.15
  73.2 2.8 %collective-permute-start.21 = (bf16[4,112,128]{2,1,0:T(8,128)(2,1)S(1)}, bf16[4,112,128]{2,1,0:T(8,128)(2,1)S(1)}, u32[]{:S(2)}, u32[]{:S(2)}) collective-permute-start(bf16[4,112,128]{2,1,0:T(8,128)(2,1)S(1)} %reduce_sum.12.refs_0_), channel_id=1, source_target_pairs={{128,0},{192,64},{0,128},{64,192},{129,1},{193,65},{1,129},{65,193... | collective-permute-start | bytes 344072 | tf_op jit(solution)/shard_map/ppermute | solution.py:231
  76.0 0.0 collective-permute-done.16
  76.0 0.9 collective-permute-start.20
  76.9 0.0 collective-permute-done.17
  76.9 0.0 collective-permute-done.18
  76.9 0.1 add_convert_fusion
  77.0 0.0 collective-permute-done.22.refs_3_
  77.0 1.8 %collective-permute-done.21.refs_2_ = bf16[4,112,128]{2,1,0:T(8,128)(2,1)S(1)} collective-permute-done((bf16[4,112,128]{2,1,0:T(8,128)(2,1)S(1)}, bf16[4,112,128]{2,1,0:T(8,128)(2,1)S(1)}, u32[]{:S(2)}, u32[]{:S(2)}) %collective-permute-start.21) | collective-permute-done | bytes 114720 | tf_op jit(solution)/shard_map/ppermute | solution.py:231
  78.8 0.9 %collective-permute-done.20.refs_1_ = bf16[4,112,128]{2,1,0:T(8,128)(2,1)S(1)} collective-permute-done((bf16[4,112,128]{2,1,0:T(8,128)(2,1)S(1)}, bf16[4,112,128]{2,1,0:T(8,128)(2,1)S(1)}, u32[]{:S(2)}, u32[]{:S(2)}) %collective-permute-start.20) | collective-permute-done | bytes 114720 | tf_op jit(solution)/shard_map/ppermute | solution.py:231
  79.7 0.1 pad_maximum_fusion
  79.7 5.7 %collective-permute-start.23 = (bf16[4,4,112,128]{3,2,1,0:T(8,128)(2,1)S(1)}, bf16[4,4,112,128]{3,2,1,0:T(8,128)(2,1)S(1)}, u32[]{:S(2)}, u32[]{:S(2)}) collective-permute-start(bf16[4,4,112,128]{3,2,1,0:T(8,128)(2,1)S(1)} %pad_maximum_fusion), channel_id=1, source_target_pairs={{0,1},{1,0},{2,3},{3,2},{4,5},{5,4},{6,7},{7,6},{8,9},{9,8},{10,11... | collective-permute-start | bytes 1376264 | tf_op jit(solution)/shard_map/ppermute | solution.py:226
  85.4 0.1 collective-permute-start.19
  85.5 1.4 %collective-permute-done.19 = bf16[16,1024]{1,0:T(8,128)(2,1)S(1)} collective-permute-done((bf16[16,1024]{1,0:T(8,128)(2,1)S(1)}, bf16[16,1024]{1,0:T(8,128)(2,1)S(1)}, u32[]{:S(2)}, u32[]{:S(2)}) %collective-permute-start.19) | collective-permute-done | bytes 32800 | tf_op jit(solution)/shard_map/ppermute | solution.py:226
  86.9 0.6 fusion.1
  87.6 0.0 collective-permute-done.23.refs_4_
  87.6 2.6 %finish.1 = (f32[432,512]{1,0:T(8,128)}, f32[432,512]{1,0:T(8,128)}) custom-call(s32[4]{0:T(128)S(1)} %pad_add_fusion.at_ref, bf16[4,112,128]{2,1,0:T(8,128)(2,1)S(1)} %reduce_sum.12.refs_0_, bf16[4,112,128]{2,1,0:T(8,128)(2,1)S(1)} %collective-permute-done.20.refs_1_, bf16[4,112,128]{2,1,0:T(8,128)(2,1)S(1)} %collective-permute-done.21.refs_2_, ...), custom_call_target="tpu_custom_call" | custom-call | tf_op jit(solution)/shard_map/finish/pallas_call | solution.py:213
  (6 shorter events, 0.0 us)
Async XLA Ops:
  2.3 10.2 %copy-start = (bf16[27,16,512]{2,1,0:T(8,128)(2,1)S(1)}, bf16[27,16,512]{2,1,0:T(8,128)(2,1)}, u32[]{:S(2)}) copy-start(bf16[27,16,512]{2,1,0:T(8,128)(2,1)} %param.5) | copy-start | bytes 1327108
  2.3 10.2 %copy-start.1 = (bf16[27,16,512]{2,1,0:T(8,128)(2,1)S(1)}, bf16[27,16,512]{2,1,0:T(8,128)(2,1)}, u32[]{:S(2)}) copy-start(bf16[27,16,512]{2,1,0:T(8,128)(2,1)} %param.6) | copy-start | bytes 1327108
  2.3 27.4 %all-to-all-start = ((bf16[16,16,1024]{2,1,0:T(8,128)(2,1)}), bf16[16,16,1024]{2,1,0:T(8,128)(2,1)S(1)}, u32[]{:S(2)}, u32[]{:S(2)}) async-start(bf16[16,16,1024]{2,1,0:T(8,128)(2,1)} %bitcast.6), calls=%async_computation | async-start | bytes 1048576 | tf_op jit(solution)/shard_map/all_to_all | solution.py:248
  13.7 16.1 %collective-permute-start = (bf16[432,128]{1,0:T(8,128)(2,1)S(1)}, bf16[432,128]{1,0:T(8,128)(2,1)S(1)}, u32[]{:S(2)}, u32[]{:S(2)}) collective-permute-start(bf16[432,128]{1,0:T(8,128)(2,1)S(1)} %get-tuple-element.25), channel_id=1, source_target_pairs={{2,0},{4,2},{6,4},{0,6},{3,1},{5,3},{7,5},{1,7},{10,8},{12,10},{14... | collective-permute-start | bytes 331784 | tf_op jit(solution)/shard_map/ppermute | solution.py:231
  16.2 13.5 %collective-permute-start.1 = (bf16[432,128]{1,0:T(8,128)(2,1)S(1)}, bf16[432,128]{1,0:T(8,128)(2,1)S(1)}, u32[]{:S(2)}, u32[]{:S(2)}) collective-permute-start(bf16[432,128]{1,0:T(8,128)(2,1)S(1)} %get-tuple-element.26), channel_id=1, source_target_pairs={{4,0},{6,2},{0,4},{2,6},{5,1},{7,3},{1,5},{3,7},{12,8},{14,10},{8,... | collective-permute-start | bytes 331784 | tf_op jit(solution)/shard_map/ppermute | solution.py:231
  16.7 13.0 %collective-permute-start.2 = (bf16[432,128]{1,0:T(8,128)(2,1)S(1)}, bf16[432,128]{1,0:T(8,128)(2,1)S(1)}, u32[]{:S(2)}, u32[]{:S(2)}) collective-permute-start(bf16[432,128]{1,0:T(8,128)(2,1)S(1)} %get-tuple-element.27), channel_id=1, source_target_pairs={{6,0},{0,2},{2,4},{4,6},{7,1},{1,3},{3,5},{5,7},{14,8},{8,10},{10,... | collective-permute-start | bytes 331784 | tf_op jit(solution)/shard_map/ppermute | solution.py:231
  29.7 20.4 %collective-permute-start.11 = (bf16[8,2,16,1024]{3,2,1,0:T(8,128)(2,1)S(1)}, bf16[8,2,16,1024]{3,2,1,0:T(8,128)(2,1)S(1)}, u32[]{:S(2)}, u32[]{:S(2)}) collective-permute-start(bf16[8,2,16,1024]{3,2,1,0:T(8,128)(2,1)S(1)} %bitcast.31), channel_id=1, source_target_pairs={{0,1},{1,0},{2,3},{3,2},{4,5},{5,4},{6,7},{7,6},{8,9},{9,8},{10,11... | collective-permute-start | bytes 1572872 | tf_op jit(solution)/shard_map/ppermute | solution.py:226
  32.2 6.2 %collective-permute-start.3 = (bf16[2,16,1024]{2,1,0:T(8,128)(2,1)S(1)}, bf16[2,16,1024]{2,1,0:T(8,128)(2,1)S(1)}, u32[]{:S(2)}, u32[]{:S(2)}) collective-permute-start(bf16[2,16,1024]{2,1,0:T(8,128)(2,1)S(1)} %get-tuple-element.29), channel_id=1, source_target_pairs={{6,0},{0,2},{2,4},{4,6},{7,1},{1,3},{3,5},{5,7},{14,8},{8,10},{10,... | collective-permute-start | bytes 196616 | tf_op jit(solution)/shard_map/ppermute | solution.py:231
  33.5 5.3 %collective-permute-start.4 = (bf16[2,16,1024]{2,1,0:T(8,128)(2,1)S(1)}, bf16[2,16,1024]{2,1,0:T(8,128)(2,1)S(1)}, u32[]{:S(2)}, u32[]{:S(2)}) collective-permute-start(bf16[2,16,1024]{2,1,0:T(8,128)(2,1)S(1)} %get-tuple-element.30), channel_id=1, source_target_pairs={{4,0},{6,2},{0,4},{2,6},{5,1},{7,3},{1,5},{3,7},{12,8},{14,10},{8,... | collective-permute-start | bytes 196616 | tf_op jit(solution)/shard_map/ppermute | solution.py:231
  36.0 3.5 %collective-permute-start.5 = (bf16[2,16,1024]{2,1,0:T(8,128)(2,1)S(1)}, bf16[2,16,1024]{2,1,0:T(8,128)(2,1)S(1)}, u32[]{:S(2)}, u32[]{:S(2)}) collective-permute-start(bf16[2,16,1024]{2,1,0:T(8,128)(2,1)S(1)} %get-tuple-element.31), channel_id=1, source_target_pairs={{2,0},{4,2},{6,4},{0,6},{3,1},{5,3},{7,5},{1,7},{10,8},{12,10},{14... | collective-permute-start | bytes 196616 | tf_op jit(solution)/shard_map/ppermute | solution.py:231
  37.1 13.0 %collective-permute-start.10 = (bf16[4,432,128]{2,1,0:T(8,128)(2,1)S(1)}, bf16[4,432,128]{2,1,0:T(8,128)(2,1)S(1)}, u32[]{:S(2)}, u32[]{:S(2)}) collective-permute-start(bf16[4,432,128]{2,1,0:T(8,128)(2,1)S(1)} %get-tuple-element.32), channel_id=1, source_target_pairs={{0,1},{1,0},{2,3},{3,2},{4,5},{5,4},{6,7},{7,6},{8,9},{9,8},{10,11... | collective-permute-start | bytes 1327112 | tf_op jit(solution)/shard_map/ppermute | solution.py:226
  39.5 2.9 %collective-permute-start.6 = (f32[2,16,1024]{2,1,0:T(8,128)S(1)}, f32[2,16,1024]{2,1,0:T(8,128)S(1)}, u32[]{:S(2)}, u32[]{:S(2)}) collective-permute-start(f32[2,16,1024]{2,1,0:T(8,128)S(1)} %add_add_fusion.own_ref), channel_id=1, source_target_pairs={{0,1},{1,0},{2,3},{3,2},{4,5},{5,4},{6,7},{7,6},{8,9},{9,8},{10,11... | collective-permute-start | bytes 393224 | tf_op jit(solution)/shard_map/ppermute | solution.py:226
  43.0 4.4 %collective-permute-start.9 = (bf16[2,16,1024]{2,1,0:T(8,128)(2,1)S(1)}, bf16[2,16,1024]{2,1,0:T(8,128)(2,1)S(1)}, u32[]{:S(2)}, u32[]{:S(2)}) collective-permute-start(bf16[2,16,1024]{2,1,0:T(8,128)(2,1)S(1)} %act.1.refs_0_), channel_id=1, source_target_pairs={{6,0},{0,2},{2,4},{4,6},{7,1},{1,3},{3,5},{5,7},{14,8},{8,10},{10,... | collective-permute-start | bytes 196616 | tf_op jit(solution)/shard_map/ppermute | solution.py:231
  43.4 6.2 %collective-permute-start.8 = (bf16[2,16,1024]{2,1,0:T(8,128)(2,1)S(1)}, bf16[2,16,1024]{2,1,0:T(8,128)(2,1)S(1)}, u32[]{:S(2)}, u32[]{:S(2)}) collective-permute-start(bf16[2,16,1024]{2,1,0:T(8,128)(2,1)S(1)} %act.1.refs_0_), channel_id=1, source_target_pairs={{4,0},{6,2},{0,4},{2,6},{5,1},{7,3},{1,5},{3,7},{12,8},{14,10},{8,... | collective-permute-start | bytes 196616 | tf_op jit(solution)/shard_map/ppermute | solution.py:231
  46.6 3.5 %collective-permute-start.7 = (bf16[2,16,1024]{2,1,0:T(8,128)(2,1)S(1)}, bf16[2,16,1024]{2,1,0:T(8,128)(2,1)S(1)}, u32[]{:S(2)}, u32[]{:S(2)}) collective-permute-start(bf16[2,16,1024]{2,1,0:T(8,128)(2,1)S(1)} %act.1.refs_0_), channel_id=1, source_target_pairs={{2,0},{4,2},{6,4},{0,6},{3,1},{5,3},{7,5},{1,7},{10,8},{12,10},{14... | collective-permute-start | bytes 196616 | tf_op jit(solution)/shard_map/ppermute | solution.py:231
  53.8 18.0 %all-to-all-start.1 = ((bf16[16,112,128]{2,1,0:T(8,128)(2,1)}), bf16[16,112,128]{2,1,0:T(8,128)(2,1)S(1)}, u32[]{:S(2)}, u32[]{:S(2)}) async-start(bf16[16,112,128]{2,1,0:T(8,128)(2,1)} %get-tuple-element.41), calls=%async_computation.1 | async-start | bytes 917504 | tf_op jit(solution)/shard_map/all_to_all | solution.py:271
  59.9 9.0 %collective-permute-start.12 = (bf16[2,16,1024]{2,1,0:T(8,128)(2,1)S(1)}, bf16[2,16,1024]{2,1,0:T(8,128)(2,1)S(1)}, u32[]{:S(2)}, u32[]{:S(2)}) collective-permute-start(bf16[2,16,1024]{2,1,0:T(8,128)(2,1)S(1)} %get-tuple-element.34), channel_id=1, source_target_pairs={{32,0},{40,8},{48,16},{56,24},{0,32},{8,40},{16,48},{24,56},{33,1}... | collective-permute-start | bytes 196616 | tf_op jit(solution)/shard_map/ppermute | solution.py:231
  60.8 11.0 %collective-permute-start.13 = (bf16[2,16,1024]{2,1,0:T(8,128)(2,1)S(1)}, bf16[2,16,1024]{2,1,0:T(8,128)(2,1)S(1)}, u32[]{:S(2)}, u32[]{:S(2)}) collective-permute-start(bf16[2,16,1024]{2,1,0:T(8,128)(2,1)S(1)} %get-tuple-element.35), channel_id=1, source_target_pairs={{40,0},{48,8},{56,16},{0,24},{8,32},{16,40},{24,48},{32,56},{41,1}... | collective-permute-start | bytes 196616 | tf_op jit(solution)/shard_map/ppermute | solution.py:231
  61.7 10.1 %collective-permute-start.14 = (bf16[2,16,1024]{2,1,0:T(8,128)(2,1)S(1)}, bf16[2,16,1024]{2,1,0:T(8,128)(2,1)S(1)}, u32[]{:S(2)}, u32[]{:S(2)}) collective-permute-start(bf16[2,16,1024]{2,1,0:T(8,128)(2,1)S(1)} %get-tuple-element.36), channel_id=1, source_target_pairs={{24,0},{32,8},{40,16},{48,24},{56,32},{0,40},{8,48},{16,56},{25,1}... | collective-permute-start | bytes 196616 | tf_op jit(solution)/shard_map/ppermute | solution.py:231
  65.3 7.9 %collective-permute-start.15 = (bf16[2,16,1024]{2,1,0:T(8,128)(2,1)S(1)}, bf16[2,16,1024]{2,1,0:T(8,128)(2,1)S(1)}, u32[]{:S(2)}, u32[]{:S(2)}) collective-permute-start(bf16[2,16,1024]{2,1,0:T(8,128)(2,1)S(1)} %get-tuple-element.37), channel_id=1, source_target_pairs={{48,0},{56,8},{0,16},{8,24},{16,32},{24,40},{32,48},{40,56},{49,1}... | collective-permute-start | bytes 196616 | tf_op jit(solution)/shard_map/ppermute | solution.py:231
  66.8 9.2 %collective-permute-start.16 = (bf16[2,16,1024]{2,1,0:T(8,128)(2,1)S(1)}, bf16[2,16,1024]{2,1,0:T(8,128)(2,1)S(1)}, u32[]{:S(2)}, u32[]{:S(2)}) collective-permute-start(bf16[2,16,1024]{2,1,0:T(8,128)(2,1)S(1)} %get-tuple-element.38), channel_id=1, source_target_pairs={{16,0},{24,8},{32,16},{40,24},{48,32},{56,40},{0,48},{8,56},{17,1}... | collective-permute-start | bytes 196616 | tf_op jit(solution)/shard_map/ppermute | solution.py:231
  68.8 8.0 %collective-permute-start.17 = (bf16[2,16,1024]{2,1,0:T(8,128)(2,1)S(1)}, bf16[2,16,1024]{2,1,0:T(8,128)(2,1)S(1)}, u32[]{:S(2)}, u32[]{:S(2)}) collective-permute-start(bf16[2,16,1024]{2,1,0:T(8,128)(2,1)S(1)} %get-tuple-element.39), channel_id=1, source_target_pairs={{56,0},{0,8},{8,16},{16,24},{24,32},{32,40},{40,48},{48,56},{57,1}... | collective-permute-start | bytes 196616 | tf_op jit(solution)/shard_map/ppermute | solution.py:231
  71.8 5.1 %collective-permute-start.18 = (bf16[2,16,1024]{2,1,0:T(8,128)(2,1)S(1)}, bf16[2,16,1024]{2,1,0:T(8,128)(2,1)S(1)}, u32[]{:S(2)}, u32[]{:S(2)}) collective-permute-start(bf16[2,16,1024]{2,1,0:T(8,128)(2,1)S(1)} %get-tuple-element.40), channel_id=1, source_target_pairs={{8,0},{16,8},{24,16},{32,24},{40,32},{48,40},{56,48},{0,56},{9,1},... | collective-permute-start | bytes 196616 | tf_op jit(solution)/shard_map/ppermute | solution.py:231
  71.9 5.1 %collective-permute-start.22 = (bf16[4,112,128]{2,1,0:T(8,128)(2,1)S(1)}, bf16[4,112,128]{2,1,0:T(8,128)(2,1)S(1)}, u32[]{:S(2)}, u32[]{:S(2)}) collective-permute-start(bf16[4,112,128]{2,1,0:T(8,128)(2,1)S(1)} %reduce_sum.12.refs_0_), channel_id=1, source_target_pairs={{192,0},{0,64},{64,128},{128,192},{193,1},{1,65},{65,129},{129,193... | collective-permute-start | bytes 344072 | tf_op jit(solution)/shard_map/ppermute | solution.py:231
  73.2 5.6 %collective-permute-start.21 = (bf16[4,112,128]{2,1,0:T(8,128)(2,1)S(1)}, bf16[4,112,128]{2,1,0:T(8,128)(2,1)S(1)}, u32[]{:S(2)}, u32[]{:S(2)}) collective-permute-start(bf16[4,112,128]{2,1,0:T(8,128)(2,1)S(1)} %reduce_sum.12.refs_0_), channel_id=1, source_target_pairs={{128,0},{192,64},{0,128},{64,192},{129,1},{193,65},{1,129},{65,193... | collective-permute-start | bytes 344072 | tf_op jit(solution)/shard_map/ppermute | solution.py:231
  76.0 3.7 %collective-permute-start.20 = (bf16[4,112,128]{2,1,0:T(8,128)(2,1)S(1)}, bf16[4,112,128]{2,1,0:T(8,128)(2,1)S(1)}, u32[]{:S(2)}, u32[]{:S(2)}) collective-permute-start(bf16[4,112,128]{2,1,0:T(8,128)(2,1)S(1)} %reduce_sum.12.refs_0_), channel_id=1, source_target_pairs={{64,0},{128,64},{192,128},{0,192},{65,1},{129,65},{193,129},{1,193... | collective-permute-start | bytes 344072 | tf_op jit(solution)/shard_map/ppermute | solution.py:231
  79.7 7.8 %collective-permute-start.23 = (bf16[4,4,112,128]{3,2,1,0:T(8,128)(2,1)S(1)}, bf16[4,4,112,128]{3,2,1,0:T(8,128)(2,1)S(1)}, u32[]{:S(2)}, u32[]{:S(2)}) collective-permute-start(bf16[4,4,112,128]{3,2,1,0:T(8,128)(2,1)S(1)} %pad_maximum_fusion), channel_id=1, source_target_pairs={{0,1},{1,0},{2,3},{3,2},{4,5},{5,4},{6,7},{7,6},{8,9},{9,8},{10,11... | collective-permute-start | bytes 1376264 | tf_op jit(solution)/shard_map/ppermute | solution.py:226
  85.4 1.5 %collective-permute-start.19 = (bf16[16,1024]{1,0:T(8,128)(2,1)S(1)}, bf16[16,1024]{1,0:T(8,128)(2,1)S(1)}, u32[]{:S(2)}, u32[]{:S(2)}) collective-permute-start(bf16[16,1024]{1,0:T(8,128)(2,1)S(1)} %select_bitcast_fusion), channel_id=1, source_target_pairs={{0,1},{1,0},{2,3},{3,2},{4,5},{5,4},{6,7},{7,6},{8,9},{9,8},{10,11... | collective-permute-start | bytes 98312 | tf_op jit(solution)/shard_map/ppermute | solution.py:226

commit v8 on v7

--- a/solution.py
+++ b/solution.py
@@ -134,7 +134,7 @@
 
 def second_kernel(at_ref, *refs):
     acts, held, across, refs = refs[:NX], refs[NX], refs[NX + 1], refs[NX + 2 :]
-    out_refs, (grad_ref, col, tall, both, parts) = refs[:NZ], refs[NZ:]
+    zero_ref, hold_ref, half_ref, give_ref, grad_ref, col, tall, both, parts = refs
     width = held.shape[1] // 27
     third = 9 * width
     group = NZ * width
@@ -166,8 +166,13 @@
                 tall[2 * third * k : 2 * third * (k + 1), :] = held[k, at : at + 2 * third, :]
             part = dot(tall[...], col[...], ((0,), (0,)))
             parts[:, d] = part.astype(BF16).reshape(NZ, width, PLANE)
-        for k in range(NZ):
-            out_refs[k][...] = parts[lax.rem(at_ref[3] + k, NZ)]
+        core = 0 if sign > 0 else 1
+        zero_ref[...] = parts[at_ref[3]]
+        for j in range(1, NZ // 2):
+            hold_ref[j - 1] = parts[lax.rem(at_ref[3] + (j if sign > 0 else NZ - j), NZ)]
+            give_ref[2 * j - 2 : 2 * j] = parts[lax.rem(at_ref[3] + (NZ - j if sign > 0 else j), NZ)]
+        half_ref[...] = parts[lax.rem(at_ref[3] + NZ // 2, NZ), core]
+        give_ref[NZ - 2] = parts[lax.rem(at_ref[3] + NZ // 2, NZ), 1 - core]
 
     @pl.when(at_ref[0] == 0)
     def _():
@@ -176,6 +181,31 @@
     @pl.when(at_ref[0] == 1)
     def _():
         run(-1)
+
+
+def sum_kernel(at_ref, *refs):
+    near_refs, (far_ref, zero_ref, keep_ref, give_ref) = refs[: NZ // 2 - 1], refs[NZ // 2 - 1 :]
+
+    def run(mine, other):
+        for array in range(2):
+            kept, given = far_ref[array].astype(F32), None
+            for ref in near_refs:
+                kept = kept + ref[array, mine].astype(F32)
+                term = ref[array, other].astype(F32)
+                given = term if given is None else given + term
+            if array == 0:
+                kept = kept + zero_ref[mine].astype(F32)
+                given = given + zero_ref[other].astype(F32)
+            keep_ref[array] = kept
+            give_ref[array] = given.astype(BF16)
+
+    @pl.when(at_ref[0] == 0)
+    def _():
+        run(0, 1)
+
+    @pl.when(at_ref[0] == 1)
+    def _():
+        run(1, 0)
 
 
 def finish_kernel(at_ref, *refs):
@@ -231,6 +261,12 @@
     return lax.ppermute(values, axis, [((i + step) % size, i) for i in range(size)])
 
 
+def apart(values, step):
+    pairs = [(2 * z, 2 * ((z + step) % NZ)) for z in range(NZ)]
+    pairs += [(2 * z + 1, 2 * ((z - step) % NZ) + 1) for z in range(NZ)]
+    return lax.ppermute(values, ("z", "spatial"), pairs)
+
+
 def body(features, conv_one, conv_two, cotangent):
     width, channels = conv_one.shape[1], conv_one.shape[2]
     at = jnp.stack([lax.axis_index(a) for a in ("spatial", "x", "samples", "z")]).astype(jnp.int32)
@@ -262,22 +298,31 @@
 
     (send,) = call(act_kernel, [(plane, BF16)], [], "act", 0, at, own, swap(own))
     acts = [send] + [around(send, "x", k) for k in range(1, NX)]
-    *parts, grads = call(
+    far = NZ // 2
+    zero, hold, half, give, grads = call(
         second_kernel,
-        [(plane, BF16)] * NZ + [((4 * NX,) + piece, BF16)],
+        [(plane, BF16), ((far - 1,) + plane, BF16), (plane[1:], BF16), ((NZ - 1,) + plane[1:], BF16), ((4 * NX,) + piece, BF16)],
         [((NX * 18 * width, PLANE), BF16), ((NX * 18 * width, group), BF16), ((2 * group, PLANE), BF16), ((NZ,) + plane, BF16)],
         "conv_out", 2 * work, at, *acts, held, across,
     )
     grads = lax.all_to_all(grads, ("samples", "x"), 0, 0, tiled=True)
-    parts = [parts[0]] + [around(parts[k], "z", NZ - k) for k in (4, 3, 5, 2, 6, 1, 7)]
-    result = sum(part.astype(F32) for part in parts).astype(BF16)
+    got = swap(give)
+    sends = [jnp.stack([hold[j - 1], got[2 * j - 2 : 2 * j]]) for j in range(1, far)] + [jnp.stack([half, got[NZ - 2]])]
+    came = {j: apart(sends[j - 1], j) for j in range(far, 0, -1)}
+    summed = jnp.sum(grads.reshape((4, NX) + piece).astype(F32), axis=0).astype(BF16)
+    summed, came[far] = lax.optimization_barrier((summed, came[far]))
+    pieces = [summed] + [around(summed, "samples", k) for k in (1, 2, 3)]
+    pieces, came = lax.optimization_barrier((pieces, came))
+    others = swap(jnp.stack(pieces))
+    keep, give = call(
+        sum_kernel, [(plane, F32), (plane, BF16)], [], "sum", 0,
+        at, *[came[j] for j in range(1, far)], came[far], zero,
+    )
+    got = swap(give)
     first = lax.axis_index("spatial") == 0
-    ours = jnp.where(first, result[0], result[1])
-    theirs = swap(jnp.where(first, result[1], result[0]))
-
-    summed = jnp.sum(grads.reshape((4, NX) + piece).astype(F32), axis=0).astype(BF16)
-    pieces = [summed] + [around(summed, "samples", k) for k in (1, 2, 3)]
-    others = swap(jnp.stack(pieces))
+    ours = (keep[0] + got[1].astype(F32)).astype(BF16)
+    theirs = (keep[1] + got[0].astype(F32)).astype(BF16)
+
     grad_one, grad_two = call(
         finish_kernel, [((taps, channels), F32)] * 2, [((28 * width, channels), BF16)] * 2, "finish", 0, at, *pieces, others
     )

time: 90.5 us -> 87.4 us (0.966)
  starting transfers between devices: 52.4 us -> 46.2 us
  waiting for transfers between devices: 23.8 us -> 26.4 us
    ppermute x19 -> x12, starting transfers between devices: 27.2 us -> 17.4 us  [around(): lax.ppermute(values, axis, [((i + step) % size, i) for i in range(size)])]
    ppermute x0 -> x4, starting transfers between devices: none -> 6.26 us  [apart(): return lax.ppermute(values, ('z', 'spatial'), pairs)]
    ppermute x5 -> x6, starting transfers between devices: 9.05 us -> 6.31 us  [swap(): return lax.ppermute(values, 'spatial', [(0, 1), (1, 0)])]
    ppermute x0 -> x4, waiting for transfers between devices: none -> 1.64 us  [apart(): return lax.ppermute(values, ('z', 'spatial'), pairs)]
    ppermute x5 -> x6, waiting for transfers between devices: 2.37 us -> 3.33 us  [swap(): return lax.ppermute(values, 'spatial', [(0, 1), (1, 0)])]
    ppermute x19 -> x12, waiting for transfers between devices: 9.13 us -> 8.23 us  [around(): lax.ppermute(values, axis, [((i + step) % size, i) for i in range(size)])]
    pallas_call x5 -> x6, Pallas kernels: 10.6 us -> 11.2 us  [call(): pl.pallas_call(kernel, out_shape=tuple((jax.ShapeDtypeStruct(s, t) for s,...]
  transfers between devices with their start and end apart: 26 -> 24, of which waited for: 12 -> 13; matrix products, arithmetic and copies ran while one was open for 1% -> 1% of each run, Pallas kernels for 5% -> 6%
where the time goes in v8:
time: 87.4 us; the launch traced here: 87.1 us
  starting transfers between devices  46.2 us (53%)
  waiting for transfers between devices  26.4 us (30%)
  Pallas kernels  11.2 us (13%)
  other arithmetic  1.72 us (2%)
  local copies, waits for them, and re-layouts  0.89 us (1%)
    ppermute x12, starting transfers between devices, around(): lax.ppermute(values, axis, [((i + step) % size, i) for i in range(size)])  17.4 us
    all_to_all x1, waiting for transfers between devices, body(): lax.all_to_all(pair, ('z', 'spatial'), 0, 0, tiled=True)  12.3 us
    pallas_call x6, Pallas kernels, call(): pl.pallas_call(kernel, out_shape=tuple((jax.ShapeDtypeStruct(s, t) for s,...  11.2 us
    all_to_all x1, starting transfers between devices, body(): lax.all_to_all(pair, ('z', 'spatial'), 0, 0, tiled=True)  10.1 us
    ppermute x12, waiting for transfers between devices, around(): lax.ppermute(values, axis, [((i + step) % size, i) for i in range(size)])  8.23 us
    ppermute x6, starting transfers between devices, swap(): return lax.ppermute(values, 'spatial', [(0, 1), (1, 0)])  6.31 us
    ppermute x4, starting transfers between devices, apart(): return lax.ppermute(values, ('z', 'spatial'), pairs)  6.26 us
    all_to_all x1, starting transfers between devices, body(): grads = lax.all_to_all(grads, ('samples', 'x'), 0, 0, tiled=True)  6.1 us
  transfers between devices with their start and end apart: 24, of which 13 were waited for; matrix products, arithmetic and copies ran while one was open for 1% of the time, Pallas kernels for 6%

profile of v8, /device:TPU:1, one launch (start us, length us, event | category | flops | bytes accessed | tf_op | source)
XLA Modules:
  0.0 87.1 jit_solution(11719461173611336178)
XLA Ops:
  0.6 0.8 pad_maximum_fusion.4
  1.4 0.9 broadcast_in_dim.3
  2.3 0.0 copy-start
  2.3 0.0 copy-start.1
  2.3 10.1 %all-to-all-start = ((bf16[16,16,1024]{2,1,0:T(8,128)(2,1)}), bf16[16,16,1024]{2,1,0:T(8,128)(2,1)S(1)}, u32[]{:S(2)}, u32[]{:S(2)}) async-start(bf16[16,16,1024]{2,1,0:T(8,128)(2,1)} %bitcast.6), calls=%async_computation | async-start | bytes 1048576 | tf_op jit(solution)/shard_map/all_to_all | solution.py:284
  12.4 0.1 pad_add_fusion.at_ref
  12.5 0.0 copy-done
  12.5 0.0 copy-done.1
  12.5 1.2 %regroup.1 = (bf16[432,128]{1,0:T(8,128)(2,1)S(1)}, bf16[432,128]{1,0:T(8,128)(2,1)S(1)}, bf16[432,128]{1,0:T(8,128)(2,1)S(1)}, bf16[432,128]{1,0:T(8,128)(2,1)S(1)}) custom-call(s32[4]{0:T(128)S(1)} %pad_add_fusion.at_ref, bf16[432,512]{1,0:T(8,128)(2,1)S(1)} %bitcast.34, bf16[432,512]{1,0:T(8,128)(2,1)S(1)} %bitcast.35), custom_call_target="tpu_custom_call" | custom-call | flops 226492416 | tf_op jit(solution)/shard_map/regroup/pallas_call | solution.py:243
  13.7 2.6 %collective-permute-start = (bf16[432,128]{1,0:T(8,128)(2,1)S(1)}, bf16[432,128]{1,0:T(8,128)(2,1)S(1)}, u32[]{:S(2)}, u32[]{:S(2)}) collective-permute-start(bf16[432,128]{1,0:T(8,128)(2,1)S(1)} %get-tuple-element.33), channel_id=1, source_target_pairs={{2,0},{4,2},{6,4},{0,6},{3,1},{5,3},{7,5},{1,7},{10,8},{12,10},{14... | collective-permute-start | bytes 331784 | tf_op jit(solution)/shard_map/ppermute | solution.py:261
  16.2 0.5 collective-permute-start.1
  16.7 0.6 collective-permute-start.2
  17.4 12.3 %all-to-all-done = bf16[16,16,1024]{2,1,0:T(8,128)(2,1)S(1)} async-done(((bf16[16,16,1024]{2,1,0:T(8,128)(2,1)}), bf16[16,16,1024]{2,1,0:T(8,128)(2,1)S(1)}, u32[]{:S(2)}, u32[]{:S(2)}) %all-to-all-start) | async-done | bytes 524320 | tf_op jit(solution)/shard_map/all_to_all | solution.py:284
  29.7 0.0 collective-permute-start.11
  29.7 0.0 collective-permute-done.refs_1_
  29.7 0.0 collective-permute-done.1.refs_2_
  29.7 0.0 collective-permute-done.2.refs_3_
  29.7 2.5 %conv_in.1 = (f32[2,16,1024]{2,1,0:T(8,128)S(1)}, bf16[2,16,1024]{2,1,0:T(8,128)(2,1)S(1)}, bf16[2,16,1024]{2,1,0:T(8,128)(2,1)S(1)}, bf16[2,16,1024]{2,1,0:T(8,128)(2,1)S(1)}, bf16[4,432,128]{2,1,0:T(8,128)(2,1)S(1)}) custom-call(s32[4]{0:T(128)S(1)} %pad_add_fusion.at_ref, bf16[8,2,16,1024]{3,2,1,0:T(8,128)(2,1)S(1)} %bitcast.30, ...), custom_call_target="tpu_custom_call" | custom-call | flops 603979776 | tf_op jit(solution)/shard_map/conv_in/pallas_call | solution.py:243
  32.2 1.3 %collective-permute-start.3 = (bf16[2,16,1024]{2,1,0:T(8,128)(2,1)S(1)}, bf16[2,16,1024]{2,1,0:T(8,128)(2,1)S(1)}, u32[]{:S(2)}, u32[]{:S(2)}) collective-permute-start(bf16[2,16,1024]{2,1,0:T(8,128)(2,1)S(1)} %get-tuple-element.37), channel_id=1, source_target_pairs={{6,0},{0,2},{2,4},{4,6},{7,1},{1,3},{3,5},{5,7},{14,8},{8,10},{10,... | collective-permute-start | bytes 196616 | tf_op jit(solution)/shard_map/ppermute | solution.py:261
  33.5 2.5 %collective-permute-start.4 = (bf16[2,16,1024]{2,1,0:T(8,128)(2,1)S(1)}, bf16[2,16,1024]{2,1,0:T(8,128)(2,1)S(1)}, u32[]{:S(2)}, u32[]{:S(2)}) collective-permute-start(bf16[2,16,1024]{2,1,0:T(8,128)(2,1)S(1)} %get-tuple-element.38), channel_id=1, source_target_pairs={{4,0},{6,2},{0,4},{2,6},{5,1},{7,3},{1,5},{3,7},{12,8},{14,10},{8,... | collective-permute-start | bytes 196616 | tf_op jit(solution)/shard_map/ppermute | solution.py:261
  36.0 1.1 %collective-permute-start.5 = (bf16[2,16,1024]{2,1,0:T(8,128)(2,1)S(1)}, bf16[2,16,1024]{2,1,0:T(8,128)(2,1)S(1)}, u32[]{:S(2)}, u32[]{:S(2)}) collective-permute-start(bf16[2,16,1024]{2,1,0:T(8,128)(2,1)S(1)} %get-tuple-element.39), channel_id=1, source_target_pairs={{2,0},{4,2},{6,4},{0,6},{3,1},{5,3},{7,5},{1,7},{10,8},{12,10},{14... | collective-permute-start | bytes 196616 | tf_op jit(solution)/shard_map/ppermute | solution.py:261
  37.1 1.3 %collective-permute-start.10 = (bf16[4,432,128]{2,1,0:T(8,128)(2,1)S(1)}, bf16[4,432,128]{2,1,0:T(8,128)(2,1)S(1)}, u32[]{:S(2)}, u32[]{:S(2)}) collective-permute-start(bf16[4,432,128]{2,1,0:T(8,128)(2,1)S(1)} %get-tuple-element.40), channel_id=1, source_target_pairs={{0,1},{1,0},{2,3},{3,2},{4,5},{5,4},{6,7},{7,6},{8,9},{9,8},{10,11... | collective-permute-start | bytes 1327112 | tf_op jit(solution)/shard_map/ppermute | solution.py:256
  38.4 0.0 collective-permute-done.3
  38.4 0.4 collective-permute-done.4
  38.8 0.6 collective-permute-done.5
  39.5 1.9 %collective-permute-start.6 = (f32[2,16,1024]{2,1,0:T(8,128)S(1)}, f32[2,16,1024]{2,1,0:T(8,128)S(1)}, u32[]{:S(2)}, u32[]{:S(2)}) collective-permute-start(f32[2,16,1024]{2,1,0:T(8,128)S(1)} %add_add_fusion.own_ref), channel_id=1, source_target_pairs={{0,1},{1,0},{2,3},{3,2},{4,5},{5,4},{6,7},{7,6},{8,9},{9,8},{10,11... | collective-permute-start | bytes 393224 | tf_op jit(solution)/shard_map/ppermute | solution.py:256
  41.4 1.0 %collective-permute-done.6.other_ref = f32[2,16,1024]{2,1,0:T(8,128)S(1)} collective-permute-done((f32[2,16,1024]{2,1,0:T(8,128)S(1)}, f32[2,16,1024]{2,1,0:T(8,128)S(1)}, u32[]{:S(2)}, u32[]{:S(2)}) %collective-permute-start.6) | collective-permute-done | bytes 131104 | tf_op jit(solution)/shard_map/ppermute | solution.py:256
  42.4 0.6 act.1.refs_0_
  43.0 0.4 collective-permute-start.9
  43.4 3.3 %collective-permute-start.8 = (bf16[2,16,1024]{2,1,0:T(8,128)(2,1)S(1)}, bf16[2,16,1024]{2,1,0:T(8,128)(2,1)S(1)}, u32[]{:S(2)}, u32[]{:S(2)}) collective-permute-start(bf16[2,16,1024]{2,1,0:T(8,128)(2,1)S(1)} %act.1.refs_0_), channel_id=1, source_target_pairs={{4,0},{6,2},{0,4},{2,6},{5,1},{7,3},{1,5},{3,7},{12,8},{14,10},{8,... | collective-permute-start | bytes 196616 | tf_op jit(solution)/shard_map/ppermute | solution.py:261
  46.6 0.0 collective-permute-start.7
  46.6 0.8 collective-permute-done.9.refs_3_
  47.4 2.2 %collective-permute-done.8.refs_2_ = bf16[2,16,1024]{2,1,0:T(8,128)(2,1)S(1)} collective-permute-done((bf16[2,16,1024]{2,1,0:T(8,128)(2,1)S(1)}, bf16[2,16,1024]{2,1,0:T(8,128)(2,1)S(1)}, u32[]{:S(2)}, u32[]{:S(2)}) %collective-permute-start.8) | collective-permute-done | bytes 65568 | tf_op jit(solution)/shard_map/ppermute | solution.py:261
  49.6 0.5 collective-permute-done.7.refs_1_
  50.1 0.0 collective-permute-done.10.refs_4_
  50.1 0.0 collective-permute-done.11.refs_5_
  50.1 3.7 %conv_out.1 = (bf16[2,16,1024]{2,1,0:T(8,128)(2,1)S(1)}, bf16[3,2,16,1024]{3,2,1,0:T(8,128)(2,1)S(1)}, bf16[16,1024]{1,0:T(8,128)(2,1)S(1)}, bf16[7,16,1024]{2,1,0:T(8,128)(2,1)S(1)}, bf16[16,112,128]{2,1,0:T(8,128)(2,1)}) custom-call(s32[4]{0:T(128)S(1)} %pad_add_fusion.at_ref, bf16[2,16,1024]{2,1,0:T(8,128)(2,1)S(1)} %act.1.refs_0_, ...), custom_call_target="tpu_custom_call" | custom-call | flops 1207959552 | tf_op jit(solution)/shard_map/conv_out/pallas_call | solution.py:243
  53.8 6.1 %all-to-all-start.1 = ((bf16[16,112,128]{2,1,0:T(8,128)(2,1)}), bf16[16,112,128]{2,1,0:T(8,128)(2,1)S(1)}, u32[]{:S(2)}, u32[]{:S(2)}) async-start(bf16[16,112,128]{2,1,0:T(8,128)(2,1)} %get-tuple-element.41), calls=%async_computation.1 | async-start | bytes 917504 | tf_op jit(solution)/shard_map/all_to_all | solution.py:308
  59.9 1.3 %collective-permute-start.12 = (bf16[7,16,1024]{2,1,0:T(8,128)(2,1)S(1)}, bf16[7,16,1024]{2,1,0:T(8,128)(2,1)S(1)}, u32[]{:S(2)}, u32[]{:S(2)}) collective-permute-start(bf16[7,16,1024]{2,1,0:T(8,128)(2,1)S(1)} %get-tuple-element.43), channel_id=1, source_target_pairs={{0,1},{1,0},{2,3},{3,2},{4,5},{5,4},{6,7},{7,6},{8,9},{9,8},{10,11... | collective-permute-start | bytes 688136 | tf_op jit(solution)/shard_map/ppermute | solution.py:256
  61.2 1.1 %collective-permute-done.12 = bf16[7,16,1024]{2,1,0:T(8,128)(2,1)S(1)} collective-permute-done((bf16[7,16,1024]{2,1,0:T(8,128)(2,1)S(1)}, bf16[7,16,1024]{2,1,0:T(8,128)(2,1)S(1)}, u32[]{:S(2)}, u32[]{:S(2)}) %collective-permute-start.12) | collective-permute-done | bytes 229408 | tf_op jit(solution)/shard_map/ppermute | solution.py:256
  62.3 1.3 %collective-permute-start.13 = (bf16[2,16,1024]{2,1,0:T(8,128)(2,1)S(1)}, bf16[2,16,1024]{2,1,0:T(8,128)(2,1)S(1)}, u32[]{:S(2)}, u32[]{:S(2)}) collective-permute-start(bf16[2,16,1024]{2,1,0:T(8,128)(2,1)S(1)} %pad_maximum_fusion.5), channel_id=1, source_target_pairs={{0,32},{8,40},{16,48},{24,56},{32,0},{40,8},{48,16},{56,24},{1,33}... | collective-permute-start | bytes 196616 | tf_op jit(solution)/shard_map/ppermute | solution.py:267
  63.6 2.4 %collective-permute-start.17 = (bf16[2,2,16,1024]{3,2,1,0:T(8,128)(2,1)S(1)}, bf16[2,2,16,1024]{3,2,1,0:T(8,128)(2,1)S(1)}, u32[]{:S(2)}, u32[]{:S(2)}) collective-permute-start(bf16[2,2,16,1024]{3,2,1,0:T(8,128)(2,1)S(1)} %pad_maximum_fusion.1), channel_id=1, source_target_pairs={{0,8},{8,16},{16,24},{24,32},{32,40},{40,48},{48,56},{56,0},{1,57}... | collective-permute-start | bytes 393224 | tf_op jit(solution)/shard_map/ppermute | solution.py:267
  66.0 0.1 collective-permute-start.18
  66.1 2.5 %collective-permute-start.19 = (bf16[2,2,16,1024]{3,2,1,0:T(8,128)(2,1)S(1)}, bf16[2,2,16,1024]{3,2,1,0:T(8,128)(2,1)S(1)}, u32[]{:S(2)}, u32[]{:S(2)}) collective-permute-start(bf16[2,2,16,1024]{3,2,1,0:T(8,128)(2,1)S(1)} %pad_maximum_fusion.3), channel_id=1, source_target_pairs={{0,24},{8,32},{16,40},{24,48},{32,56},{40,0},{48,8},{56,16},{1,41}... | collective-permute-start | bytes 393224 | tf_op jit(solution)/shard_map/ppermute | solution.py:267
  68.6 0.8 all-to-all-done.1
  69.5 0.1 reduce_sum.12.refs_0_
  69.6 1.6 %collective-permute-done.13.refs_3_ = bf16[2,16,1024]{2,1,0:T(8,128)(2,1)S(1)} collective-permute-done((bf16[2,16,1024]{2,1,0:T(8,128)(2,1)S(1)}, bf16[2,16,1024]{2,1,0:T(8,128)(2,1)S(1)}, u32[]{:S(2)}, u32[]{:S(2)}) %collective-permute-start.13) | collective-permute-done | bytes 65568 | tf_op jit(solution)/shard_map/ppermute | solution.py:267
  71.2 1.6 %collective-permute-start.16 = (bf16[4,112,128]{2,1,0:T(8,128)(2,1)S(1)}, bf16[4,112,128]{2,1,0:T(8,128)(2,1)S(1)}, u32[]{:S(2)}, u32[]{:S(2)}) collective-permute-start(bf16[4,112,128]{2,1,0:T(8,128)(2,1)S(1)} %reduce_sum.12.refs_0_), channel_id=1, source_target_pairs={{192,0},{0,64},{64,128},{128,192},{193,1},{1,65},{65,129},{129,193... | collective-permute-start | bytes 344072 | tf_op jit(solution)/shard_map/ppermute | solution.py:261
  72.8 2.4 %collective-permute-start.15 = (bf16[4,112,128]{2,1,0:T(8,128)(2,1)S(1)}, bf16[4,112,128]{2,1,0:T(8,128)(2,1)S(1)}, u32[]{:S(2)}, u32[]{:S(2)}) collective-permute-start(bf16[4,112,128]{2,1,0:T(8,128)(2,1)S(1)} %reduce_sum.12.refs_0_), channel_id=1, source_target_pairs={{128,0},{192,64},{0,128},{64,192},{129,1},{193,65},{1,129},{65,193... | collective-permute-start | bytes 344072 | tf_op jit(solution)/shard_map/ppermute | solution.py:261
  75.2 0.0 collective-permute-done.17.refs_0_
  75.2 1.2 %collective-permute-start.14 = (bf16[4,112,128]{2,1,0:T(8,128)(2,1)S(1)}, bf16[4,112,128]{2,1,0:T(8,128)(2,1)S(1)}, u32[]{:S(2)}, u32[]{:S(2)}) collective-permute-start(bf16[4,112,128]{2,1,0:T(8,128)(2,1)S(1)} %reduce_sum.12.refs_0_), channel_id=1, source_target_pairs={{64,0},{128,64},{192,128},{0,192},{65,1},{129,65},{193,129},{1,193... | collective-permute-start | bytes 344072 | tf_op jit(solution)/shard_map/ppermute | solution.py:261
  76.3 0.0 collective-permute-done.18.refs_1_
  76.3 0.0 collective-permute-done.19.refs_2_
  76.3 0.3 collective-permute-done.16.refs_3_
  76.6 3.5 %collective-permute-done.15.refs_2_ = bf16[4,112,128]{2,1,0:T(8,128)(2,1)S(1)} collective-permute-done((bf16[4,112,128]{2,1,0:T(8,128)(2,1)S(1)}, bf16[4,112,128]{2,1,0:T(8,128)(2,1)S(1)}, u32[]{:S(2)}, u32[]{:S(2)}) %collective-permute-start.15) | collective-permute-done | bytes 114720 | tf_op jit(solution)/shard_map/ppermute | solution.py:261
  80.1 0.0 collective-permute-done.14.refs_1_
  80.1 0.1 pad_maximum_fusion
  80.2 1.7 %collective-permute-start.21 = (bf16[4,4,112,128]{3,2,1,0:T(8,128)(2,1)S(1)}, bf16[4,4,112,128]{3,2,1,0:T(8,128)(2,1)S(1)}, u32[]{:S(2)}, u32[]{:S(2)}) collective-permute-start(bf16[4,4,112,128]{3,2,1,0:T(8,128)(2,1)S(1)} %pad_maximum_fusion), channel_id=1, source_target_pairs={{0,1},{1,0},{2,3},{3,2},{4,5},{5,4},{6,7},{7,6},{8,9},{9,8},{10,11... | collective-permute-start | bytes 1376264 | tf_op jit(solution)/shard_map/ppermute | solution.py:256
  81.9 0.6 sum.1
  82.5 0.1 collective-permute-start.20
  82.6 1.2 %collective-permute-done.20 = bf16[2,16,1024]{2,1,0:T(8,128)(2,1)S(1)} collective-permute-done((bf16[2,16,1024]{2,1,0:T(8,128)(2,1)S(1)}, bf16[2,16,1024]{2,1,0:T(8,128)(2,1)S(1)}, u32[]{:S(2)}, u32[]{:S(2)}) %collective-permute-start.20) | collective-permute-done | bytes 65568 | tf_op jit(solution)/shard_map/ppermute | solution.py:256
  83.8 0.6 select_bitcast_fusion
  84.5 0.0 collective-permute-done.21.refs_4_
  84.5 2.6 %finish.1 = (f32[432,512]{1,0:T(8,128)}, f32[432,512]{1,0:T(8,128)}) custom-call(s32[4]{0:T(128)S(1)} %pad_add_fusion.at_ref, bf16[4,112,128]{2,1,0:T(8,128)(2,1)S(1)} %reduce_sum.12.refs_0_, bf16[4,112,128]{2,1,0:T(8,128)(2,1)S(1)} %collective-permute-done.14.refs_1_, bf16[4,112,128]{2,1,0:T(8,128)(2,1)S(1)} %collective-permute-done.15.refs_2_, ...), custom_call_target="tpu_custom_call" | custom-call | tf_op jit(solution)/shard_map/finish/pallas_call | solution.py:243
  (8 shorter events, 0.1 us)
Async XLA Ops:
  2.3 10.2 %copy-start = (bf16[27,16,512]{2,1,0:T(8,128)(2,1)S(1)}, bf16[27,16,512]{2,1,0:T(8,128)(2,1)}, u32[]{:S(2)}) copy-start(bf16[27,16,512]{2,1,0:T(8,128)(2,1)} %param.5) | copy-start | bytes 1327108
  2.3 10.2 %copy-start.1 = (bf16[27,16,512]{2,1,0:T(8,128)(2,1)S(1)}, bf16[27,16,512]{2,1,0:T(8,128)(2,1)}, u32[]{:S(2)}) copy-start(bf16[27,16,512]{2,1,0:T(8,128)(2,1)} %param.6) | copy-start | bytes 1327108
  2.3 27.4 %all-to-all-start = ((bf16[16,16,1024]{2,1,0:T(8,128)(2,1)}), bf16[16,16,1024]{2,1,0:T(8,128)(2,1)S(1)}, u32[]{:S(2)}, u32[]{:S(2)}) async-start(bf16[16,16,1024]{2,1,0:T(8,128)(2,1)} %bitcast.6), calls=%async_computation | async-start | bytes 1048576 | tf_op jit(solution)/shard_map/all_to_all | solution.py:284
  13.7 16.1 %collective-permute-start = (bf16[432,128]{1,0:T(8,128)(2,1)S(1)}, bf16[432,128]{1,0:T(8,128)(2,1)S(1)}, u32[]{:S(2)}, u32[]{:S(2)}) collective-permute-start(bf16[432,128]{1,0:T(8,128)(2,1)S(1)} %get-tuple-element.33), channel_id=1, source_target_pairs={{2,0},{4,2},{6,4},{0,6},{3,1},{5,3},{7,5},{1,7},{10,8},{12,10},{14... | collective-permute-start | bytes 331784 | tf_op jit(solution)/shard_map/ppermute | solution.py:261
  16.2 13.5 %collective-permute-start.1 = (bf16[432,128]{1,0:T(8,128)(2,1)S(1)}, bf16[432,128]{1,0:T(8,128)(2,1)S(1)}, u32[]{:S(2)}, u32[]{:S(2)}) collective-permute-start(bf16[432,128]{1,0:T(8,128)(2,1)S(1)} %get-tuple-element.34), channel_id=1, source_target_pairs={{4,0},{6,2},{0,4},{2,6},{5,1},{7,3},{1,5},{3,7},{12,8},{14,10},{8,... | collective-permute-start | bytes 331784 | tf_op jit(solution)/shard_map/ppermute | solution.py:261
  16.7 13.0 %collective-permute-start.2 = (bf16[432,128]{1,0:T(8,128)(2,1)S(1)}, bf16[432,128]{1,0:T(8,128)(2,1)S(1)}, u32[]{:S(2)}, u32[]{:S(2)}) collective-permute-start(bf16[432,128]{1,0:T(8,128)(2,1)S(1)} %get-tuple-element.35), channel_id=1, source_target_pairs={{6,0},{0,2},{2,4},{4,6},{7,1},{1,3},{3,5},{5,7},{14,8},{8,10},{10,... | collective-permute-start | bytes 331784 | tf_op jit(solution)/shard_map/ppermute | solution.py:261
  29.7 20.4 %collective-permute-start.11 = (bf16[8,2,16,1024]{3,2,1,0:T(8,128)(2,1)S(1)}, bf16[8,2,16,1024]{3,2,1,0:T(8,128)(2,1)S(1)}, u32[]{:S(2)}, u32[]{:S(2)}) collective-permute-start(bf16[8,2,16,1024]{3,2,1,0:T(8,128)(2,1)S(1)} %bitcast.29), channel_id=1, source_target_pairs={{0,1},{1,0},{2,3},{3,2},{4,5},{5,4},{6,7},{7,6},{8,9},{9,8},{10,11... | collective-permute-start | bytes 1572872 | tf_op jit(solution)/shard_map/ppermute | solution.py:256
  32.2 6.2 %collective-permute-start.3 = (bf16[2,16,1024]{2,1,0:T(8,128)(2,1)S(1)}, bf16[2,16,1024]{2,1,0:T(8,128)(2,1)S(1)}, u32[]{:S(2)}, u32[]{:S(2)}) collective-permute-start(bf16[2,16,1024]{2,1,0:T(8,128)(2,1)S(1)} %get-tuple-element.37), channel_id=1, source_target_pairs={{6,0},{0,2},{2,4},{4,6},{7,1},{1,3},{3,5},{5,7},{14,8},{8,10},{10,... | collective-permute-start | bytes 196616 | tf_op jit(solution)/shard_map/ppermute | solution.py:261
  33.5 5.3 %collective-permute-start.4 = (bf16[2,16,1024]{2,1,0:T(8,128)(2,1)S(1)}, bf16[2,16,1024]{2,1,0:T(8,128)(2,1)S(1)}, u32[]{:S(2)}, u32[]{:S(2)}) collective-permute-start(bf16[2,16,1024]{2,1,0:T(8,128)(2,1)S(1)} %get-tuple-element.38), channel_id=1, source_target_pairs={{4,0},{6,2},{0,4},{2,6},{5,1},{7,3},{1,5},{3,7},{12,8},{14,10},{8,... | collective-permute-start | bytes 196616 | tf_op jit(solution)/shard_map/ppermute | solution.py:261
  36.0 3.5 %collective-permute-start.5 = (bf16[2,16,1024]{2,1,0:T(8,128)(2,1)S(1)}, bf16[2,16,1024]{2,1,0:T(8,128)(2,1)S(1)}, u32[]{:S(2)}, u32[]{:S(2)}) collective-permute-start(bf16[2,16,1024]{2,1,0:T(8,128)(2,1)S(1)} %get-tuple-element.39), channel_id=1, source_target_pairs={{2,0},{4,2},{6,4},{0,6},{3,1},{5,3},{7,5},{1,7},{10,8},{12,10},{14... | collective-permute-start | bytes 196616 | tf_op jit(solution)/shard_map/ppermute | solution.py:261
  37.1 13.0 %collective-permute-start.10 = (bf16[4,432,128]{2,1,0:T(8,128)(2,1)S(1)}, bf16[4,432,128]{2,1,0:T(8,128)(2,1)S(1)}, u32[]{:S(2)}, u32[]{:S(2)}) collective-permute-start(bf16[4,432,128]{2,1,0:T(8,128)(2,1)S(1)} %get-tuple-element.40), channel_id=1, source_target_pairs={{0,1},{1,0},{2,3},{3,2},{4,5},{5,4},{6,7},{7,6},{8,9},{9,8},{10,11... | collective-permute-start | bytes 1327112 | tf_op jit(solution)/shard_map/ppermute | solution.py:256
  39.5 2.9 %collective-permute-start.6 = (f32[2,16,1024]{2,1,0:T(8,128)S(1)}, f32[2,16,1024]{2,1,0:T(8,128)S(1)}, u32[]{:S(2)}, u32[]{:S(2)}) collective-permute-start(f32[2,16,1024]{2,1,0:T(8,128)S(1)} %add_add_fusion.own_ref), channel_id=1, source_target_pairs={{0,1},{1,0},{2,3},{3,2},{4,5},{5,4},{6,7},{7,6},{8,9},{9,8},{10,11... | collective-permute-start | bytes 393224 | tf_op jit(solution)/shard_map/ppermute | solution.py:256
  43.0 4.4 %collective-permute-start.9 = (bf16[2,16,1024]{2,1,0:T(8,128)(2,1)S(1)}, bf16[2,16,1024]{2,1,0:T(8,128)(2,1)S(1)}, u32[]{:S(2)}, u32[]{:S(2)}) collective-permute-start(bf16[2,16,1024]{2,1,0:T(8,128)(2,1)S(1)} %act.1.refs_0_), channel_id=1, source_target_pairs={{6,0},{0,2},{2,4},{4,6},{7,1},{1,3},{3,5},{5,7},{14,8},{8,10},{10,... | collective-permute-start | bytes 196616 | tf_op jit(solution)/shard_map/ppermute | solution.py:261
  43.4 6.2 %collective-permute-start.8 = (bf16[2,16,1024]{2,1,0:T(8,128)(2,1)S(1)}, bf16[2,16,1024]{2,1,0:T(8,128)(2,1)S(1)}, u32[]{:S(2)}, u32[]{:S(2)}) collective-permute-start(bf16[2,16,1024]{2,1,0:T(8,128)(2,1)S(1)} %act.1.refs_0_), channel_id=1, source_target_pairs={{4,0},{6,2},{0,4},{2,6},{5,1},{7,3},{1,5},{3,7},{12,8},{14,10},{8,... | collective-permute-start | bytes 196616 | tf_op jit(solution)/shard_map/ppermute | solution.py:261
  46.6 3.5 %collective-permute-start.7 = (bf16[2,16,1024]{2,1,0:T(8,128)(2,1)S(1)}, bf16[2,16,1024]{2,1,0:T(8,128)(2,1)S(1)}, u32[]{:S(2)}, u32[]{:S(2)}) collective-permute-start(bf16[2,16,1024]{2,1,0:T(8,128)(2,1)S(1)} %act.1.refs_0_), channel_id=1, source_target_pairs={{2,0},{4,2},{6,4},{0,6},{3,1},{5,3},{7,5},{1,7},{10,8},{12,10},{14... | collective-permute-start | bytes 196616 | tf_op jit(solution)/shard_map/ppermute | solution.py:261
  53.8 15.7 %all-to-all-start.1 = ((bf16[16,112,128]{2,1,0:T(8,128)(2,1)}), bf16[16,112,128]{2,1,0:T(8,128)(2,1)S(1)}, u32[]{:S(2)}, u32[]{:S(2)}) async-start(bf16[16,112,128]{2,1,0:T(8,128)(2,1)} %get-tuple-element.41), calls=%async_computation.1 | async-start | bytes 917504 | tf_op jit(solution)/shard_map/all_to_all | solution.py:308
  59.9 2.4 %collective-permute-start.12 = (bf16[7,16,1024]{2,1,0:T(8,128)(2,1)S(1)}, bf16[7,16,1024]{2,1,0:T(8,128)(2,1)S(1)}, u32[]{:S(2)}, u32[]{:S(2)}) collective-permute-start(bf16[7,16,1024]{2,1,0:T(8,128)(2,1)S(1)} %get-tuple-element.43), channel_id=1, source_target_pairs={{0,1},{1,0},{2,3},{3,2},{4,5},{5,4},{6,7},{7,6},{8,9},{9,8},{10,11... | collective-permute-start | bytes 688136 | tf_op jit(solution)/shard_map/ppermute | solution.py:256
  62.3 8.9 %collective-permute-start.13 = (bf16[2,16,1024]{2,1,0:T(8,128)(2,1)S(1)}, bf16[2,16,1024]{2,1,0:T(8,128)(2,1)S(1)}, u32[]{:S(2)}, u32[]{:S(2)}) collective-permute-start(bf16[2,16,1024]{2,1,0:T(8,128)(2,1)S(1)} %pad_maximum_fusion.5), channel_id=1, source_target_pairs={{0,32},{8,40},{16,48},{24,56},{32,0},{40,8},{48,16},{56,24},{1,33}... | collective-permute-start | bytes 196616 | tf_op jit(solution)/shard_map/ppermute | solution.py:267
  63.6 11.5 %collective-permute-start.17 = (bf16[2,2,16,1024]{3,2,1,0:T(8,128)(2,1)S(1)}, bf16[2,2,16,1024]{3,2,1,0:T(8,128)(2,1)S(1)}, u32[]{:S(2)}, u32[]{:S(2)}) collective-permute-start(bf16[2,2,16,1024]{3,2,1,0:T(8,128)(2,1)S(1)} %pad_maximum_fusion.1), channel_id=1, source_target_pairs={{0,8},{8,16},{16,24},{24,32},{32,40},{40,48},{48,56},{56,0},{1,57}... | collective-permute-start | bytes 393224 | tf_op jit(solution)/shard_map/ppermute | solution.py:267
  66.0 10.3 %collective-permute-start.18 = (bf16[2,2,16,1024]{3,2,1,0:T(8,128)(2,1)S(1)}, bf16[2,2,16,1024]{3,2,1,0:T(8,128)(2,1)S(1)}, u32[]{:S(2)}, u32[]{:S(2)}) collective-permute-start(bf16[2,2,16,1024]{3,2,1,0:T(8,128)(2,1)S(1)} %pad_maximum_fusion.2), channel_id=1, source_target_pairs={{0,16},{8,24},{16,32},{24,40},{32,48},{40,56},{48,0},{56,8},{1,49}... | collective-permute-start | bytes 393224 | tf_op jit(solution)/shard_map/ppermute | solution.py:267
  66.1 10.2 %collective-permute-start.19 = (bf16[2,2,16,1024]{3,2,1,0:T(8,128)(2,1)S(1)}, bf16[2,2,16,1024]{3,2,1,0:T(8,128)(2,1)S(1)}, u32[]{:S(2)}, u32[]{:S(2)}) collective-permute-start(bf16[2,2,16,1024]{3,2,1,0:T(8,128)(2,1)S(1)} %pad_maximum_fusion.3), channel_id=1, source_target_pairs={{0,24},{8,32},{16,40},{24,48},{32,56},{40,0},{48,8},{56,16},{1,41}... | collective-permute-start | bytes 393224 | tf_op jit(solution)/shard_map/ppermute | solution.py:267
  71.2 5.4 %collective-permute-start.16 = (bf16[4,112,128]{2,1,0:T(8,128)(2,1)S(1)}, bf16[4,112,128]{2,1,0:T(8,128)(2,1)S(1)}, u32[]{:S(2)}, u32[]{:S(2)}) collective-permute-start(bf16[4,112,128]{2,1,0:T(8,128)(2,1)S(1)} %reduce_sum.12.refs_0_), channel_id=1, source_target_pairs={{192,0},{0,64},{64,128},{128,192},{193,1},{1,65},{65,129},{129,193... | collective-permute-start | bytes 344072 | tf_op jit(solution)/shard_map/ppermute | solution.py:261
  72.8 7.4 %collective-permute-start.15 = (bf16[4,112,128]{2,1,0:T(8,128)(2,1)S(1)}, bf16[4,112,128]{2,1,0:T(8,128)(2,1)S(1)}, u32[]{:S(2)}, u32[]{:S(2)}) collective-permute-start(bf16[4,112,128]{2,1,0:T(8,128)(2,1)S(1)} %reduce_sum.12.refs_0_), channel_id=1, source_target_pairs={{128,0},{192,64},{0,128},{64,192},{129,1},{193,65},{1,129},{65,193... | collective-permute-start | bytes 344072 | tf_op jit(solution)/shard_map/ppermute | solution.py:261
  75.2 5.0 %collective-permute-start.14 = (bf16[4,112,128]{2,1,0:T(8,128)(2,1)S(1)}, bf16[4,112,128]{2,1,0:T(8,128)(2,1)S(1)}, u32[]{:S(2)}, u32[]{:S(2)}) collective-permute-start(bf16[4,112,128]{2,1,0:T(8,128)(2,1)S(1)} %reduce_sum.12.refs_0_), channel_id=1, source_target_pairs={{64,0},{128,64},{192,128},{0,192},{65,1},{129,65},{193,129},{1,193... | collective-permute-start | bytes 344072 | tf_op jit(solution)/shard_map/ppermute | solution.py:261
  80.2 4.3 %collective-permute-start.21 = (bf16[4,4,112,128]{3,2,1,0:T(8,128)(2,1)S(1)}, bf16[4,4,112,128]{3,2,1,0:T(8,128)(2,1)S(1)}, u32[]{:S(2)}, u32[]{:S(2)}) collective-permute-start(bf16[4,4,112,128]{3,2,1,0:T(8,128)(2,1)S(1)} %pad_maximum_fusion), channel_id=1, source_target_pairs={{0,1},{1,0},{2,3},{3,2},{4,5},{5,4},{6,7},{7,6},{8,9},{9,8},{10,11... | collective-permute-start | bytes 1376264 | tf_op jit(solution)/shard_map/ppermute | solution.py:256
  82.5 1.3 %collective-permute-start.20 = (bf16[2,16,1024]{2,1,0:T(8,128)(2,1)S(1)}, bf16[2,16,1024]{2,1,0:T(8,128)(2,1)S(1)}, u32[]{:S(2)}, u32[]{:S(2)}) collective-permute-start(bf16[2,16,1024]{2,1,0:T(8,128)(2,1)S(1)} %get-tuple-element.53), channel_id=1, source_target_pairs={{0,1},{1,0},{2,3},{3,2},{4,5},{5,4},{6,7},{7,6},{8,9},{9,8},{10,11... | collective-permute-start | bytes 196616 | tf_op jit(solution)/shard_map/ppermute | solution.py:256

commit v9 on v8

--- a/solution.py
+++ b/solution.py
@@ -209,43 +209,58 @@
 
 
 def finish_kernel(at_ref, *refs):
-    own_refs, other_ref, (one_ref, two_ref, near, far) = refs[:4], refs[4], refs[5:]
+    own_refs, other_ref, keep_ref, got_ref = refs[:4], refs[4], refs[5], refs[6]
+    mixed_ref, input_ref, one_ref, two_ref, near, far, wide, cells, sems = refs[7:]
     taps, channels = one_ref.shape
     _, _, size, group = other_ref.shape
     width = group // NZ
+    third = taps // 3
     old = lax.broadcasted_iota(jnp.int32, (channels, channels), 0)
     new = lax.broadcasted_iota(jnp.int32, (channels, channels), 1)
     place = (new // width) % NX * group + new // (NX * width) * width + new % width
     order = (old == place).astype(F32).astype(BF16)
 
-    def put(piece, full, out_ref):
-        for k in range(4):
-            rows = pl.ds(pl.multiple_of(lax.rem(at_ref[2] + k, 4) * size, 16), size)
-            for x in range(NX):
-                full[rows, x * group : (x + 1) * group] = piece(k, x)
-        out_ref[...] = dot(full[0:taps, :], order, ((1,), (0,)))
-
-    def run(own_out, other_out):
-        put(lambda k, x: own_refs[k][x], near, own_out)
-        put(lambda k, x: other_ref[k, x], far, other_out)
-
-    @pl.when(at_ref[0] == 0)
-    def _():
-        run(two_ref, one_ref)
-
-    @pl.when(at_ref[0] == 1)
-    def _():
-        run(one_ref, two_ref)
-
-
-def call(kernel, outs, scratch, name, cost, *args):
+    def run(cell_outs, grad_outs):
+        copies = []
+
+        def send(source, target):
+            copy = pltpu.make_async_copy(source, target, sems.at[len(copies)])
+            copy.start()
+            copies.append(copy)
+
+        for array in range(2):
+            cells[array] = (keep_ref[array] + got_ref[1 - array].astype(F32)).astype(BF16)
+            send(cells.at[array], cell_outs[array])
+        pieces = (lambda k, x: own_refs[k][x]), (lambda k, x: other_ref[k, x])
+        for n, full in enumerate((near, far)):
+            for k in range(4):
+                rows = pl.ds(pl.multiple_of(lax.rem(at_ref[2] + k, 4) * size, 16), size)
+                for x in range(NX):
+                    full[rows, x * group : (x + 1) * group] = pieces[n](k, x)
+            for a in range(3):
+                rows = pl.ds(a * third, third)
+                wide[n, rows, :] = dot(full[a * third : (a + 1) * third, :], order, ((1,), (0,)))
+                send(wide.at[n, rows], grad_outs[n].at[rows])
+        for copy in copies:
+            copy.wait()
+
+    @pl.when(at_ref[0] == 0)
+    def _():
+        run((mixed_ref, input_ref), (two_ref, one_ref))
+
+    @pl.when(at_ref[0] == 1)
+    def _():
+        run((input_ref, mixed_ref), (one_ref, two_ref))
+
+
+def call(kernel, outs, scratch, name, cost, *args, out_space=pltpu.VMEM):
     vmem = pl.BlockSpec(memory_space=pltpu.VMEM)
     return pl.pallas_call(
         kernel,
         out_shape=tuple(jax.ShapeDtypeStruct(s, t) for s, t in outs),
         in_specs=[pl.BlockSpec(memory_space=pltpu.SMEM)] + [vmem] * (len(args) - 1),
-        out_specs=tuple([vmem] * len(outs)),
-        scratch_shapes=[pltpu.VMEM(s, t) for s, t in scratch],
+        out_specs=tuple([pl.BlockSpec(memory_space=out_space)] * len(outs)),
+        scratch_shapes=[pltpu.VMEM(*s) if isinstance(s, tuple) else s for s in scratch],
         compiler_params=PARAMS,
         cost_estimate=pl.CostEstimate(flops=cost, bytes_accessed=0, transcendentals=0),
         name=name,
@@ -315,22 +330,18 @@
     pieces, came = lax.optimization_barrier((pieces, came))
     others = swap(jnp.stack(pieces))
     keep, give = call(
-        sum_kernel, [(plane, F32), (plane, BF16)], [], "sum", 0,
-        at, *[came[j] for j in range(1, far)], came[far], zero,
-    )
-    got = swap(give)
-    first = lax.axis_index("spatial") == 0
-    ours = (keep[0] + got[1].astype(F32)).astype(BF16)
-    theirs = (keep[1] + got[0].astype(F32)).astype(BF16)
-
-    grad_one, grad_two = call(
-        finish_kernel, [((taps, channels), F32)] * 2, [((28 * width, channels), BF16)] * 2, "finish", 0, at, *pieces, others
+        sum_kernel, [(plane, F32), (plane, BF16)], [], "sum", 0, at, *[came[j] for j in range(1, far)], came[far], zero
+    )
+    mixed_out, input_grad, grad_one, grad_two = call(
+        finish_kernel,
+        [((width, PLANE), BF16)] * 2 + [((taps, channels), F32)] * 2,
+        [((28 * width, channels), BF16)] * 2
+        + [((2, taps, channels), F32), (plane, BF16), pltpu.SemaphoreType.DMA((8,))],
+        "finish", 0, at, *pieces, others, keep, swap(give), out_space=pl.ANY,
     )
     shape = (width, 1, 1, PLANE)
-    mixed_out = jnp.where(first, ours, theirs).reshape(shape)
-    input_grad = jnp.where(first, theirs, ours).reshape(shape)
     weights = (27, width, channels)
-    return mixed_out, input_grad, grad_one.reshape(weights), grad_two.reshape(weights)
+    return mixed_out.reshape(shape), input_grad.reshape(shape), grad_one.reshape(weights), grad_two.reshape(weights)
 
 
 def solution(mesh):

time: 87.4 us -> 86.7 us (level)
  transfers between devices with their start and end apart: 24 -> 24, of which waited for: 13 -> 13; matrix products, arithmetic and copies ran while one was open for 1% -> 0% of each run, Pallas kernels for 6% -> 6%
where the time goes in v9:
time: 86.7 us; the launch traced here: 86.3 us
  starting transfers between devices  46.1 us (53%)
  waiting for transfers between devices  26.4 us (30%)
  Pallas kernels  10.9 us (13%)
  other arithmetic  1.07 us (1%)
  between operations  0.91 us (1%)
  local copies, waits for them, and re-layouts  0.89 us (1%)
    ppermute x12, starting transfers between devices, around(): lax.ppermute(values, axis, [((i + step) % size, i) for i in range(size)])  17.4 us
    all_to_all x1, waiting for transfers between devices, body(): lax.all_to_all(pair, ('z', 'spatial'), 0, 0, tiled=True)  12.3 us
    pallas_call x6, Pallas kernels, call(): pl.pallas_call(kernel, out_shape=tuple((jax.ShapeDtypeStruct(s, t) for s,...  10.9 us
    all_to_all x1, starting transfers between devices, body(): lax.all_to_all(pair, ('z', 'spatial'), 0, 0, tiled=True)  10.1 us
    ppermute x12, waiting for transfers between devices, around(): lax.ppermute(values, axis, [((i + step) % size, i) for i in range(size)])  8.23 us
    ppermute x6, starting transfers between devices, swap(): return lax.ppermute(values, 'spatial', [(0, 1), (1, 0)])  6.31 us
    ppermute x4, starting transfers between devices, apart(): return lax.ppermute(values, ('z', 'spatial'), pairs)  6.25 us
    all_to_all x1, starting transfers between devices, body(): grads = lax.all_to_all(grads, ('samples', 'x'), 0, 0, tiled=True)  6.1 us
  transfers between devices with their start and end apart: 24, of which 13 were waited for; matrix products, arithmetic and copies ran while one was open for 0% of the time, Pallas kernels for 6%

profile of v9, /device:TPU:1, one launch (start us, length us, event | category | flops | bytes accessed | tf_op | source)
XLA Modules:
  0.0 86.3 jit_solution(14822525564489557364)
XLA Ops:
  0.6 0.8 pad_maximum_fusion.4
  1.4 0.9 broadcast_in_dim.3
  2.3 0.0 copy-start
  2.3 0.0 copy-start.1
  2.3 10.1 %all-to-all-start = ((bf16[16,16,1024]{2,1,0:T(8,128)(2,1)}), bf16[16,16,1024]{2,1,0:T(8,128)(2,1)S(1)}, u32[]{:S(2)}, u32[]{:S(2)}) async-start(bf16[16,16,1024]{2,1,0:T(8,128)(2,1)} %bitcast.6), calls=%async_computation | async-start | bytes 1048576 | tf_op jit(solution)/shard_map/all_to_all | solution.py:299
  12.4 0.1 pad_add_fusion.at_ref
  12.5 0.0 copy-done
  12.5 0.0 copy-done.1
  12.5 1.2 %regroup.1 = (bf16[432,128]{1,0:T(8,128)(2,1)S(1)}, bf16[432,128]{1,0:T(8,128)(2,1)S(1)}, bf16[432,128]{1,0:T(8,128)(2,1)S(1)}, bf16[432,128]{1,0:T(8,128)(2,1)S(1)}) custom-call(s32[4]{0:T(128)S(1)} %pad_add_fusion.at_ref, bf16[432,512]{1,0:T(8,128)(2,1)S(1)} %bitcast.32, bf16[432,512]{1,0:T(8,128)(2,1)S(1)} %bitcast.33), custom_call_target="tpu_custom_call" | custom-call | flops 226492416 | tf_op jit(solution)/shard_map/regroup/pallas_call | solution.py:258
  13.7 2.6 %collective-permute-start = (bf16[432,128]{1,0:T(8,128)(2,1)S(1)}, bf16[432,128]{1,0:T(8,128)(2,1)S(1)}, u32[]{:S(2)}, u32[]{:S(2)}) collective-permute-start(bf16[432,128]{1,0:T(8,128)(2,1)S(1)} %get-tuple-element.35), channel_id=1, source_target_pairs={{2,0},{4,2},{6,4},{0,6},{3,1},{5,3},{7,5},{1,7},{10,8},{12,10},{14... | collective-permute-start | bytes 331784 | tf_op jit(solution)/shard_map/ppermute | solution.py:276
  16.2 0.5 collective-permute-start.1
  16.7 0.6 collective-permute-start.2
  17.4 12.3 %all-to-all-done = bf16[16,16,1024]{2,1,0:T(8,128)(2,1)S(1)} async-done(((bf16[16,16,1024]{2,1,0:T(8,128)(2,1)}), bf16[16,16,1024]{2,1,0:T(8,128)(2,1)S(1)}, u32[]{:S(2)}, u32[]{:S(2)}) %all-to-all-start) | async-done | bytes 524320 | tf_op jit(solution)/shard_map/all_to_all | solution.py:299
  29.7 0.0 collective-permute-start.11
  29.7 0.0 collective-permute-done.refs_1_
  29.7 0.0 collective-permute-done.1.refs_2_
  29.7 0.0 collective-permute-done.2.refs_3_
  29.7 2.5 %conv_in.1 = (f32[2,16,1024]{2,1,0:T(8,128)S(1)}, bf16[2,16,1024]{2,1,0:T(8,128)(2,1)S(1)}, bf16[2,16,1024]{2,1,0:T(8,128)(2,1)S(1)}, bf16[2,16,1024]{2,1,0:T(8,128)(2,1)S(1)}, bf16[4,432,128]{2,1,0:T(8,128)(2,1)S(1)}) custom-call(s32[4]{0:T(128)S(1)} %pad_add_fusion.at_ref, bf16[8,2,16,1024]{3,2,1,0:T(8,128)(2,1)S(1)} %bitcast.28, ...), custom_call_target="tpu_custom_call" | custom-call | flops 603979776 | tf_op jit(solution)/shard_map/conv_in/pallas_call | solution.py:258
  32.2 1.3 %collective-permute-start.3 = (bf16[2,16,1024]{2,1,0:T(8,128)(2,1)S(1)}, bf16[2,16,1024]{2,1,0:T(8,128)(2,1)S(1)}, u32[]{:S(2)}, u32[]{:S(2)}) collective-permute-start(bf16[2,16,1024]{2,1,0:T(8,128)(2,1)S(1)} %get-tuple-element.39), channel_id=1, source_target_pairs={{6,0},{0,2},{2,4},{4,6},{7,1},{1,3},{3,5},{5,7},{14,8},{8,10},{10,... | collective-permute-start | bytes 196616 | tf_op jit(solution)/shard_map/ppermute | solution.py:276
  33.5 2.5 %collective-permute-start.4 = (bf16[2,16,1024]{2,1,0:T(8,128)(2,1)S(1)}, bf16[2,16,1024]{2,1,0:T(8,128)(2,1)S(1)}, u32[]{:S(2)}, u32[]{:S(2)}) collective-permute-start(bf16[2,16,1024]{2,1,0:T(8,128)(2,1)S(1)} %get-tuple-element.40), channel_id=1, source_target_pairs={{4,0},{6,2},{0,4},{2,6},{5,1},{7,3},{1,5},{3,7},{12,8},{14,10},{8,... | collective-permute-start | bytes 196616 | tf_op jit(solution)/shard_map/ppermute | solution.py:276
  36.0 1.1 %collective-permute-start.5 = (bf16[2,16,1024]{2,1,0:T(8,128)(2,1)S(1)}, bf16[2,16,1024]{2,1,0:T(8,128)(2,1)S(1)}, u32[]{:S(2)}, u32[]{:S(2)}) collective-permute-start(bf16[2,16,1024]{2,1,0:T(8,128)(2,1)S(1)} %get-tuple-element.41), channel_id=1, source_target_pairs={{2,0},{4,2},{6,4},{0,6},{3,1},{5,3},{7,5},{1,7},{10,8},{12,10},{14... | collective-permute-start | bytes 196616 | tf_op jit(solution)/shard_map/ppermute | solution.py:276
  37.1 1.3 %collective-permute-start.10 = (bf16[4,432,128]{2,1,0:T(8,128)(2,1)S(1)}, bf16[4,432,128]{2,1,0:T(8,128)(2,1)S(1)}, u32[]{:S(2)}, u32[]{:S(2)}) collective-permute-start(bf16[4,432,128]{2,1,0:T(8,128)(2,1)S(1)} %get-tuple-element.42), channel_id=1, source_target_pairs={{0,1},{1,0},{2,3},{3,2},{4,5},{5,4},{6,7},{7,6},{8,9},{9,8},{10,11... | collective-permute-start | bytes 1327112 | tf_op jit(solution)/shard_map/ppermute | solution.py:271
  38.4 0.0 collective-permute-done.3
  38.4 0.4 collective-permute-done.4
  38.8 0.6 collective-permute-done.5
  39.5 1.9 %collective-permute-start.6 = (f32[2,16,1024]{2,1,0:T(8,128)S(1)}, f32[2,16,1024]{2,1,0:T(8,128)S(1)}, u32[]{:S(2)}, u32[]{:S(2)}) collective-permute-start(f32[2,16,1024]{2,1,0:T(8,128)S(1)} %add_add_fusion.own_ref), channel_id=1, source_target_pairs={{0,1},{1,0},{2,3},{3,2},{4,5},{5,4},{6,7},{7,6},{8,9},{9,8},{10,11... | collective-permute-start | bytes 393224 | tf_op jit(solution)/shard_map/ppermute | solution.py:271
  41.4 1.0 %collective-permute-done.6.other_ref = f32[2,16,1024]{2,1,0:T(8,128)S(1)} collective-permute-done((f32[2,16,1024]{2,1,0:T(8,128)S(1)}, f32[2,16,1024]{2,1,0:T(8,128)S(1)}, u32[]{:S(2)}, u32[]{:S(2)}) %collective-permute-start.6) | collective-permute-done | bytes 131104 | tf_op jit(solution)/shard_map/ppermute | solution.py:271
  42.4 0.6 act.1.refs_0_
  43.0 0.4 collective-permute-start.9
  43.4 3.3 %collective-permute-start.8 = (bf16[2,16,1024]{2,1,0:T(8,128)(2,1)S(1)}, bf16[2,16,1024]{2,1,0:T(8,128)(2,1)S(1)}, u32[]{:S(2)}, u32[]{:S(2)}) collective-permute-start(bf16[2,16,1024]{2,1,0:T(8,128)(2,1)S(1)} %act.1.refs_0_), channel_id=1, source_target_pairs={{4,0},{6,2},{0,4},{2,6},{5,1},{7,3},{1,5},{3,7},{12,8},{14,10},{8,... | collective-permute-start | bytes 196616 | tf_op jit(solution)/shard_map/ppermute | solution.py:276
  46.6 0.0 collective-permute-start.7
  46.6 0.8 collective-permute-done.9.refs_3_
  47.4 2.2 %collective-permute-done.8.refs_2_ = bf16[2,16,1024]{2,1,0:T(8,128)(2,1)S(1)} collective-permute-done((bf16[2,16,1024]{2,1,0:T(8,128)(2,1)S(1)}, bf16[2,16,1024]{2,1,0:T(8,128)(2,1)S(1)}, u32[]{:S(2)}, u32[]{:S(2)}) %collective-permute-start.8) | collective-permute-done | bytes 65568 | tf_op jit(solution)/shard_map/ppermute | solution.py:276
  49.6 0.5 collective-permute-done.7.refs_1_
  50.1 0.0 collective-permute-done.10.refs_4_
  50.1 0.0 collective-permute-done.11.refs_5_
  50.1 3.7 %conv_out.1 = (bf16[2,16,1024]{2,1,0:T(8,128)(2,1)S(1)}, bf16[3,2,16,1024]{3,2,1,0:T(8,128)(2,1)S(1)}, bf16[16,1024]{1,0:T(8,128)(2,1)S(1)}, bf16[7,16,1024]{2,1,0:T(8,128)(2,1)S(1)}, bf16[16,112,128]{2,1,0:T(8,128)(2,1)}) custom-call(s32[4]{0:T(128)S(1)} %pad_add_fusion.at_ref, bf16[2,16,1024]{2,1,0:T(8,128)(2,1)S(1)} %act.1.refs_0_, ...), custom_call_target="tpu_custom_call" | custom-call | flops 1207959552 | tf_op jit(solution)/shard_map/conv_out/pallas_call | solution.py:258
  53.8 6.1 %all-to-all-start.1 = ((bf16[16,112,128]{2,1,0:T(8,128)(2,1)}), bf16[16,112,128]{2,1,0:T(8,128)(2,1)S(1)}, u32[]{:S(2)}, u32[]{:S(2)}) async-start(bf16[16,112,128]{2,1,0:T(8,128)(2,1)} %get-tuple-element.43), calls=%async_computation.1 | async-start | bytes 917504 | tf_op jit(solution)/shard_map/all_to_all | solution.py:323
  59.9 1.3 %collective-permute-start.12 = (bf16[7,16,1024]{2,1,0:T(8,128)(2,1)S(1)}, bf16[7,16,1024]{2,1,0:T(8,128)(2,1)S(1)}, u32[]{:S(2)}, u32[]{:S(2)}) collective-permute-start(bf16[7,16,1024]{2,1,0:T(8,128)(2,1)S(1)} %get-tuple-element.45), channel_id=1, source_target_pairs={{0,1},{1,0},{2,3},{3,2},{4,5},{5,4},{6,7},{7,6},{8,9},{9,8},{10,11... | collective-permute-start | bytes 688136 | tf_op jit(solution)/shard_map/ppermute | solution.py:271
  61.2 1.1 %collective-permute-done.12 = bf16[7,16,1024]{2,1,0:T(8,128)(2,1)S(1)} collective-permute-done((bf16[7,16,1024]{2,1,0:T(8,128)(2,1)S(1)}, bf16[7,16,1024]{2,1,0:T(8,128)(2,1)S(1)}, u32[]{:S(2)}, u32[]{:S(2)}) %collective-permute-start.12) | collective-permute-done | bytes 229408 | tf_op jit(solution)/shard_map/ppermute | solution.py:271
  62.3 1.3 %collective-permute-start.13 = (bf16[2,16,1024]{2,1,0:T(8,128)(2,1)S(1)}, bf16[2,16,1024]{2,1,0:T(8,128)(2,1)S(1)}, u32[]{:S(2)}, u32[]{:S(2)}) collective-permute-start(bf16[2,16,1024]{2,1,0:T(8,128)(2,1)S(1)} %pad_maximum_fusion.5), channel_id=1, source_target_pairs={{0,32},{8,40},{16,48},{24,56},{32,0},{40,8},{48,16},{56,24},{1,33}... | collective-permute-start | bytes 196616 | tf_op jit(solution)/shard_map/ppermute | solution.py:282
  63.6 2.4 %collective-permute-start.17 = (bf16[2,2,16,1024]{3,2,1,0:T(8,128)(2,1)S(1)}, bf16[2,2,16,1024]{3,2,1,0:T(8,128)(2,1)S(1)}, u32[]{:S(2)}, u32[]{:S(2)}) collective-permute-start(bf16[2,2,16,1024]{3,2,1,0:T(8,128)(2,1)S(1)} %pad_maximum_fusion.1), channel_id=1, source_target_pairs={{0,8},{8,16},{16,24},{24,32},{32,40},{40,48},{48,56},{56,0},{1,57}... | collective-permute-start | bytes 393224 | tf_op jit(solution)/shard_map/ppermute | solution.py:282
  66.0 0.1 collective-permute-start.18
  66.1 2.5 %collective-permute-start.19 = (bf16[2,2,16,1024]{3,2,1,0:T(8,128)(2,1)S(1)}, bf16[2,2,16,1024]{3,2,1,0:T(8,128)(2,1)S(1)}, u32[]{:S(2)}, u32[]{:S(2)}) collective-permute-start(bf16[2,2,16,1024]{3,2,1,0:T(8,128)(2,1)S(1)} %pad_maximum_fusion.3), channel_id=1, source_target_pairs={{0,24},{8,32},{16,40},{24,48},{32,56},{40,0},{48,8},{56,16},{1,41}... | collective-permute-start | bytes 393224 | tf_op jit(solution)/shard_map/ppermute | solution.py:282
  68.6 0.9 all-to-all-done.1
  69.5 0.1 reduce_sum.12.refs_0_
  69.6 1.6 %collective-permute-done.13.refs_3_ = bf16[2,16,1024]{2,1,0:T(8,128)(2,1)S(1)} collective-permute-done((bf16[2,16,1024]{2,1,0:T(8,128)(2,1)S(1)}, bf16[2,16,1024]{2,1,0:T(8,128)(2,1)S(1)}, u32[]{:S(2)}, u32[]{:S(2)}) %collective-permute-start.13) | collective-permute-done | bytes 65568 | tf_op jit(solution)/shard_map/ppermute | solution.py:282
  71.2 1.6 %collective-permute-start.16 = (bf16[4,112,128]{2,1,0:T(8,128)(2,1)S(1)}, bf16[4,112,128]{2,1,0:T(8,128)(2,1)S(1)}, u32[]{:S(2)}, u32[]{:S(2)}) collective-permute-start(bf16[4,112,128]{2,1,0:T(8,128)(2,1)S(1)} %reduce_sum.12.refs_0_), channel_id=1, source_target_pairs={{192,0},{0,64},{64,128},{128,192},{193,1},{1,65},{65,129},{129,193... | collective-permute-start | bytes 344072 | tf_op jit(solution)/shard_map/ppermute | solution.py:276
  72.8 2.4 %collective-permute-start.15 = (bf16[4,112,128]{2,1,0:T(8,128)(2,1)S(1)}, bf16[4,112,128]{2,1,0:T(8,128)(2,1)S(1)}, u32[]{:S(2)}, u32[]{:S(2)}) collective-permute-start(bf16[4,112,128]{2,1,0:T(8,128)(2,1)S(1)} %reduce_sum.12.refs_0_), channel_id=1, source_target_pairs={{128,0},{192,64},{0,128},{64,192},{129,1},{193,65},{1,129},{65,193... | collective-permute-start | bytes 344072 | tf_op jit(solution)/shard_map/ppermute | solution.py:276
  75.2 0.0 collective-permute-done.17.refs_0_
  75.2 1.2 %collective-permute-start.14 = (bf16[4,112,128]{2,1,0:T(8,128)(2,1)S(1)}, bf16[4,112,128]{2,1,0:T(8,128)(2,1)S(1)}, u32[]{:S(2)}, u32[]{:S(2)}) collective-permute-start(bf16[4,112,128]{2,1,0:T(8,128)(2,1)S(1)} %reduce_sum.12.refs_0_), channel_id=1, source_target_pairs={{64,0},{128,64},{192,128},{0,192},{65,1},{129,65},{193,129},{1,193... | collective-permute-start | bytes 344072 | tf_op jit(solution)/shard_map/ppermute | solution.py:276
  76.3 0.0 collective-permute-done.18.refs_1_
  76.3 0.0 collective-permute-done.19.refs_2_
  76.3 0.3 collective-permute-done.16.refs_3_
  76.6 3.5 %collective-permute-done.15.refs_2_ = bf16[4,112,128]{2,1,0:T(8,128)(2,1)S(1)} collective-permute-done((bf16[4,112,128]{2,1,0:T(8,128)(2,1)S(1)}, bf16[4,112,128]{2,1,0:T(8,128)(2,1)S(1)}, u32[]{:S(2)}, u32[]{:S(2)}) %collective-permute-start.15) | collective-permute-done | bytes 114720 | tf_op jit(solution)/shard_map/ppermute | solution.py:276
  80.1 0.0 collective-permute-done.14.refs_1_
  80.1 0.1 pad_maximum_fusion
  80.2 1.7 %collective-permute-start.20 = (bf16[4,4,112,128]{3,2,1,0:T(8,128)(2,1)S(1)}, bf16[4,4,112,128]{3,2,1,0:T(8,128)(2,1)S(1)}, u32[]{:S(2)}, u32[]{:S(2)}) collective-permute-start(bf16[4,4,112,128]{3,2,1,0:T(8,128)(2,1)S(1)} %pad_maximum_fusion), channel_id=1, source_target_pairs={{0,1},{1,0},{2,3},{3,2},{4,5},{5,4},{6,7},{7,6},{8,9},{9,8},{10,11... | collective-permute-start | bytes 1376264 | tf_op jit(solution)/shard_map/ppermute | solution.py:271
  81.9 0.6 sum.1
  82.5 0.1 collective-permute-start.21
  82.6 1.2 %collective-permute-done.21.refs_6_ = bf16[2,16,1024]{2,1,0:T(8,128)(2,1)S(1)} collective-permute-done((bf16[2,16,1024]{2,1,0:T(8,128)(2,1)S(1)}, bf16[2,16,1024]{2,1,0:T(8,128)(2,1)S(1)}, u32[]{:S(2)}, u32[]{:S(2)}) %collective-permute-start.21) | collective-permute-done | bytes 65568 | tf_op jit(solution)/shard_map/ppermute | solution.py:271
  83.8 0.0 collective-permute-done.20.refs_4_
  83.8 2.3 %finish.1 = (bf16[16,1024]{1,0:T(8,128)(2,1)}, bf16[16,1024]{1,0:T(8,128)(2,1)}, f32[432,512]{1,0:T(8,128)}, f32[432,512]{1,0:T(8,128)}) custom-call(s32[4]{0:T(128)S(1)} %pad_add_fusion.at_ref, bf16[4,112,128]{2,1,0:T(8,128)(2,1)S(1)} %reduce_sum.12.refs_0_, bf16[4,112,128]{2,1,0:T(8,128)(2,1)S(1)} %collective-permute-done.14.refs_1_, ...), custom_call_target="tpu_custom_call" | custom-call | tf_op jit(solution)/shard_map/finish/pallas_call | solution.py:258
  (8 shorter events, 0.1 us)
Async XLA Ops:
  2.3 10.2 %copy-start = (bf16[27,16,512]{2,1,0:T(8,128)(2,1)S(1)}, bf16[27,16,512]{2,1,0:T(8,128)(2,1)}, u32[]{:S(2)}) copy-start(bf16[27,16,512]{2,1,0:T(8,128)(2,1)} %param.5) | copy-start | bytes 1327108
  2.3 10.2 %copy-start.1 = (bf16[27,16,512]{2,1,0:T(8,128)(2,1)S(1)}, bf16[27,16,512]{2,1,0:T(8,128)(2,1)}, u32[]{:S(2)}) copy-start(bf16[27,16,512]{2,1,0:T(8,128)(2,1)} %param.6) | copy-start | bytes 1327108
  2.3 27.4 %all-to-all-start = ((bf16[16,16,1024]{2,1,0:T(8,128)(2,1)}), bf16[16,16,1024]{2,1,0:T(8,128)(2,1)S(1)}, u32[]{:S(2)}, u32[]{:S(2)}) async-start(bf16[16,16,1024]{2,1,0:T(8,128)(2,1)} %bitcast.6), calls=%async_computation | async-start | bytes 1048576 | tf_op jit(solution)/shard_map/all_to_all | solution.py:299
  13.7 16.1 %collective-permute-start = (bf16[432,128]{1,0:T(8,128)(2,1)S(1)}, bf16[432,128]{1,0:T(8,128)(2,1)S(1)}, u32[]{:S(2)}, u32[]{:S(2)}) collective-permute-start(bf16[432,128]{1,0:T(8,128)(2,1)S(1)} %get-tuple-element.35), channel_id=1, source_target_pairs={{2,0},{4,2},{6,4},{0,6},{3,1},{5,3},{7,5},{1,7},{10,8},{12,10},{14... | collective-permute-start | bytes 331784 | tf_op jit(solution)/shard_map/ppermute | solution.py:276
  16.2 13.5 %collective-permute-start.1 = (bf16[432,128]{1,0:T(8,128)(2,1)S(1)}, bf16[432,128]{1,0:T(8,128)(2,1)S(1)}, u32[]{:S(2)}, u32[]{:S(2)}) collective-permute-start(bf16[432,128]{1,0:T(8,128)(2,1)S(1)} %get-tuple-element.36), channel_id=1, source_target_pairs={{4,0},{6,2},{0,4},{2,6},{5,1},{7,3},{1,5},{3,7},{12,8},{14,10},{8,... | collective-permute-start | bytes 331784 | tf_op jit(solution)/shard_map/ppermute | solution.py:276
  16.7 13.0 %collective-permute-start.2 = (bf16[432,128]{1,0:T(8,128)(2,1)S(1)}, bf16[432,128]{1,0:T(8,128)(2,1)S(1)}, u32[]{:S(2)}, u32[]{:S(2)}) collective-permute-start(bf16[432,128]{1,0:T(8,128)(2,1)S(1)} %get-tuple-element.37), channel_id=1, source_target_pairs={{6,0},{0,2},{2,4},{4,6},{7,1},{1,3},{3,5},{5,7},{14,8},{8,10},{10,... | collective-permute-start | bytes 331784 | tf_op jit(solution)/shard_map/ppermute | solution.py:276
  29.7 20.4 %collective-permute-start.11 = (bf16[8,2,16,1024]{3,2,1,0:T(8,128)(2,1)S(1)}, bf16[8,2,16,1024]{3,2,1,0:T(8,128)(2,1)S(1)}, u32[]{:S(2)}, u32[]{:S(2)}) collective-permute-start(bf16[8,2,16,1024]{3,2,1,0:T(8,128)(2,1)S(1)} %bitcast.27), channel_id=1, source_target_pairs={{0,1},{1,0},{2,3},{3,2},{4,5},{5,4},{6,7},{7,6},{8,9},{9,8},{10,11... | collective-permute-start | bytes 1572872 | tf_op jit(solution)/shard_map/ppermute | solution.py:271
  32.2 6.2 %collective-permute-start.3 = (bf16[2,16,1024]{2,1,0:T(8,128)(2,1)S(1)}, bf16[2,16,1024]{2,1,0:T(8,128)(2,1)S(1)}, u32[]{:S(2)}, u32[]{:S(2)}) collective-permute-start(bf16[2,16,1024]{2,1,0:T(8,128)(2,1)S(1)} %get-tuple-element.39), channel_id=1, source_target_pairs={{6,0},{0,2},{2,4},{4,6},{7,1},{1,3},{3,5},{5,7},{14,8},{8,10},{10,... | collective-permute-start | bytes 196616 | tf_op jit(solution)/shard_map/ppermute | solution.py:276
  33.5 5.3 %collective-permute-start.4 = (bf16[2,16,1024]{2,1,0:T(8,128)(2,1)S(1)}, bf16[2,16,1024]{2,1,0:T(8,128)(2,1)S(1)}, u32[]{:S(2)}, u32[]{:S(2)}) collective-permute-start(bf16[2,16,1024]{2,1,0:T(8,128)(2,1)S(1)} %get-tuple-element.40), channel_id=1, source_target_pairs={{4,0},{6,2},{0,4},{2,6},{5,1},{7,3},{1,5},{3,7},{12,8},{14,10},{8,... | collective-permute-start | bytes 196616 | tf_op jit(solution)/shard_map/ppermute | solution.py:276
  36.0 3.5 %collective-permute-start.5 = (bf16[2,16,1024]{2,1,0:T(8,128)(2,1)S(1)}, bf16[2,16,1024]{2,1,0:T(8,128)(2,1)S(1)}, u32[]{:S(2)}, u32[]{:S(2)}) collective-permute-start(bf16[2,16,1024]{2,1,0:T(8,128)(2,1)S(1)} %get-tuple-element.41), channel_id=1, source_target_pairs={{2,0},{4,2},{6,4},{0,6},{3,1},{5,3},{7,5},{1,7},{10,8},{12,10},{14... | collective-permute-start | bytes 196616 | tf_op jit(solution)/shard_map/ppermute | solution.py:276
  37.1 13.0 %collective-permute-start.10 = (bf16[4,432,128]{2,1,0:T(8,128)(2,1)S(1)}, bf16[4,432,128]{2,1,0:T(8,128)(2,1)S(1)}, u32[]{:S(2)}, u32[]{:S(2)}) collective-permute-start(bf16[4,432,128]{2,1,0:T(8,128)(2,1)S(1)} %get-tuple-element.42), channel_id=1, source_target_pairs={{0,1},{1,0},{2,3},{3,2},{4,5},{5,4},{6,7},{7,6},{8,9},{9,8},{10,11... | collective-permute-start | bytes 1327112 | tf_op jit(solution)/shard_map/ppermute | solution.py:271
  39.5 2.9 %collective-permute-start.6 = (f32[2,16,1024]{2,1,0:T(8,128)S(1)}, f32[2,16,1024]{2,1,0:T(8,128)S(1)}, u32[]{:S(2)}, u32[]{:S(2)}) collective-permute-start(f32[2,16,1024]{2,1,0:T(8,128)S(1)} %add_add_fusion.own_ref), channel_id=1, source_target_pairs={{0,1},{1,0},{2,3},{3,2},{4,5},{5,4},{6,7},{7,6},{8,9},{9,8},{10,11... | collective-permute-start | bytes 393224 | tf_op jit(solution)/shard_map/ppermute | solution.py:271
  43.0 4.4 %collective-permute-start.9 = (bf16[2,16,1024]{2,1,0:T(8,128)(2,1)S(1)}, bf16[2,16,1024]{2,1,0:T(8,128)(2,1)S(1)}, u32[]{:S(2)}, u32[]{:S(2)}) collective-permute-start(bf16[2,16,1024]{2,1,0:T(8,128)(2,1)S(1)} %act.1.refs_0_), channel_id=1, source_target_pairs={{6,0},{0,2},{2,4},{4,6},{7,1},{1,3},{3,5},{5,7},{14,8},{8,10},{10,... | collective-permute-start | bytes 196616 | tf_op jit(solution)/shard_map/ppermute | solution.py:276
  43.4 6.2 %collective-permute-start.8 = (bf16[2,16,1024]{2,1,0:T(8,128)(2,1)S(1)}, bf16[2,16,1024]{2,1,0:T(8,128)(2,1)S(1)}, u32[]{:S(2)}, u32[]{:S(2)}) collective-permute-start(bf16[2,16,1024]{2,1,0:T(8,128)(2,1)S(1)} %act.1.refs_0_), channel_id=1, source_target_pairs={{4,0},{6,2},{0,4},{2,6},{5,1},{7,3},{1,5},{3,7},{12,8},{14,10},{8,... | collective-permute-start | bytes 196616 | tf_op jit(solution)/shard_map/ppermute | solution.py:276
  46.6 3.5 %collective-permute-start.7 = (bf16[2,16,1024]{2,1,0:T(8,128)(2,1)S(1)}, bf16[2,16,1024]{2,1,0:T(8,128)(2,1)S(1)}, u32[]{:S(2)}, u32[]{:S(2)}) collective-permute-start(bf16[2,16,1024]{2,1,0:T(8,128)(2,1)S(1)} %act.1.refs_0_), channel_id=1, source_target_pairs={{2,0},{4,2},{6,4},{0,6},{3,1},{5,3},{7,5},{1,7},{10,8},{12,10},{14... | collective-permute-start | bytes 196616 | tf_op jit(solution)/shard_map/ppermute | solution.py:276
  53.8 15.7 %all-to-all-start.1 = ((bf16[16,112,128]{2,1,0:T(8,128)(2,1)}), bf16[16,112,128]{2,1,0:T(8,128)(2,1)S(1)}, u32[]{:S(2)}, u32[]{:S(2)}) async-start(bf16[16,112,128]{2,1,0:T(8,128)(2,1)} %get-tuple-element.43), calls=%async_computation.1 | async-start | bytes 917504 | tf_op jit(solution)/shard_map/all_to_all | solution.py:323
  59.9 2.4 %collective-permute-start.12 = (bf16[7,16,1024]{2,1,0:T(8,128)(2,1)S(1)}, bf16[7,16,1024]{2,1,0:T(8,128)(2,1)S(1)}, u32[]{:S(2)}, u32[]{:S(2)}) collective-permute-start(bf16[7,16,1024]{2,1,0:T(8,128)(2,1)S(1)} %get-tuple-element.45), channel_id=1, source_target_pairs={{0,1},{1,0},{2,3},{3,2},{4,5},{5,4},{6,7},{7,6},{8,9},{9,8},{10,11... | collective-permute-start | bytes 688136 | tf_op jit(solution)/shard_map/ppermute | solution.py:271
  62.3 8.9 %collective-permute-start.13 = (bf16[2,16,1024]{2,1,0:T(8,128)(2,1)S(1)}, bf16[2,16,1024]{2,1,0:T(8,128)(2,1)S(1)}, u32[]{:S(2)}, u32[]{:S(2)}) collective-permute-start(bf16[2,16,1024]{2,1,0:T(8,128)(2,1)S(1)} %pad_maximum_fusion.5), channel_id=1, source_target_pairs={{0,32},{8,40},{16,48},{24,56},{32,0},{40,8},{48,16},{56,24},{1,33}... | collective-permute-start | bytes 196616 | tf_op jit(solution)/shard_map/ppermute | solution.py:282
  63.6 11.5 %collective-permute-start.17 = (bf16[2,2,16,1024]{3,2,1,0:T(8,128)(2,1)S(1)}, bf16[2,2,16,1024]{3,2,1,0:T(8,128)(2,1)S(1)}, u32[]{:S(2)}, u32[]{:S(2)}) collective-permute-start(bf16[2,2,16,1024]{3,2,1,0:T(8,128)(2,1)S(1)} %pad_maximum_fusion.1), channel_id=1, source_target_pairs={{0,8},{8,16},{16,24},{24,32},{32,40},{40,48},{48,56},{56,0},{1,57}... | collective-permute-start | bytes 393224 | tf_op jit(solution)/shard_map/ppermute | solution.py:282
  66.0 10.3 %collective-permute-start.18 = (bf16[2,2,16,1024]{3,2,1,0:T(8,128)(2,1)S(1)}, bf16[2,2,16,1024]{3,2,1,0:T(8,128)(2,1)S(1)}, u32[]{:S(2)}, u32[]{:S(2)}) collective-permute-start(bf16[2,2,16,1024]{3,2,1,0:T(8,128)(2,1)S(1)} %pad_maximum_fusion.2), channel_id=1, source_target_pairs={{0,16},{8,24},{16,32},{24,40},{32,48},{40,56},{48,0},{56,8},{1,49}... | collective-permute-start | bytes 393224 | tf_op jit(solution)/shard_map/ppermute | solution.py:282
  66.1 10.2 %collective-permute-start.19 = (bf16[2,2,16,1024]{3,2,1,0:T(8,128)(2,1)S(1)}, bf16[2,2,16,1024]{3,2,1,0:T(8,128)(2,1)S(1)}, u32[]{:S(2)}, u32[]{:S(2)}) collective-permute-start(bf16[2,2,16,1024]{3,2,1,0:T(8,128)(2,1)S(1)} %pad_maximum_fusion.3), channel_id=1, source_target_pairs={{0,24},{8,32},{16,40},{24,48},{32,56},{40,0},{48,8},{56,16},{1,41}... | collective-permute-start | bytes 393224 | tf_op jit(solution)/shard_map/ppermute | solution.py:282
  71.2 5.4 %collective-permute-start.16 = (bf16[4,112,128]{2,1,0:T(8,128)(2,1)S(1)}, bf16[4,112,128]{2,1,0:T(8,128)(2,1)S(1)}, u32[]{:S(2)}, u32[]{:S(2)}) collective-permute-start(bf16[4,112,128]{2,1,0:T(8,128)(2,1)S(1)} %reduce_sum.12.refs_0_), channel_id=1, source_target_pairs={{192,0},{0,64},{64,128},{128,192},{193,1},{1,65},{65,129},{129,193... | collective-permute-start | bytes 344072 | tf_op jit(solution)/shard_map/ppermute | solution.py:276
  72.8 7.4 %collective-permute-start.15 = (bf16[4,112,128]{2,1,0:T(8,128)(2,1)S(1)}, bf16[4,112,128]{2,1,0:T(8,128)(2,1)S(1)}, u32[]{:S(2)}, u32[]{:S(2)}) collective-permute-start(bf16[4,112,128]{2,1,0:T(8,128)(2,1)S(1)} %reduce_sum.12.refs_0_), channel_id=1, source_target_pairs={{128,0},{192,64},{0,128},{64,192},{129,1},{193,65},{1,129},{65,193... | collective-permute-start | bytes 344072 | tf_op jit(solution)/shard_map/ppermute | solution.py:276
  75.2 5.0 %collective-permute-start.14 = (bf16[4,112,128]{2,1,0:T(8,128)(2,1)S(1)}, bf16[4,112,128]{2,1,0:T(8,128)(2,1)S(1)}, u32[]{:S(2)}, u32[]{:S(2)}) collective-permute-start(bf16[4,112,128]{2,1,0:T(8,128)(2,1)S(1)} %reduce_sum.12.refs_0_), channel_id=1, source_target_pairs={{64,0},{128,64},{192,128},{0,192},{65,1},{129,65},{193,129},{1,193... | collective-permute-start | bytes 344072 | tf_op jit(solution)/shard_map/ppermute | solution.py:276
  80.2 3.6 %collective-permute-start.20 = (bf16[4,4,112,128]{3,2,1,0:T(8,128)(2,1)S(1)}, bf16[4,4,112,128]{3,2,1,0:T(8,128)(2,1)S(1)}, u32[]{:S(2)}, u32[]{:S(2)}) collective-permute-start(bf16[4,4,112,128]{3,2,1,0:T(8,128)(2,1)S(1)} %pad_maximum_fusion), channel_id=1, source_target_pairs={{0,1},{1,0},{2,3},{3,2},{4,5},{5,4},{6,7},{7,6},{8,9},{9,8},{10,11... | collective-permute-start | bytes 1376264 | tf_op jit(solution)/shard_map/ppermute | solution.py:271
  82.5 1.3 %collective-permute-start.21 = (bf16[2,16,1024]{2,1,0:T(8,128)(2,1)S(1)}, bf16[2,16,1024]{2,1,0:T(8,128)(2,1)S(1)}, u32[]{:S(2)}, u32[]{:S(2)}) collective-permute-start(bf16[2,16,1024]{2,1,0:T(8,128)(2,1)S(1)} %get-tuple-element.59), channel_id=1, source_target_pairs={{0,1},{1,0},{2,3},{3,2},{4,5},{5,4},{6,7},{7,6},{8,9},{9,8},{10,11... | collective-permute-start | bytes 196616 | tf_op jit(solution)/shard_map/ppermute | solution.py:271

commit v10 on v9

--- a/solution.py
+++ b/solution.py
@@ -66,13 +66,18 @@
     channels = one_ref.shape[1]
     width = channels // (NX * NZ)
     group = NZ * width
+    low = width.bit_length() - 1
     old = lax.broadcasted_iota(jnp.int32, (channels, group), 0)
     new = lax.broadcasted_iota(jnp.int32, (channels, group), 1)
+    for part in range(NX):
+        column = new + part * group
+        place = (column >> low & 3) * group + (column >> low + 2 << low) + (column & (width - 1))
+        out_refs[NX][:, part * group : (part + 1) * group] = (old == place).astype(F32).astype(BF16)
 
     def run(ref):
         for k in range(NX):
             x = lax.rem(at_ref[1] + k, NX)
-            home = (new // width) * (NX * width) + x * width + new % width
+            home = (new >> low << low + 2) + (x << low) + (new & (width - 1))
             order = (old == home).astype(F32).astype(BF16)
             out_refs[k][...] = dot(ref[...], order, ((1,), (0,))).astype(BF16)
 
@@ -133,7 +138,7 @@
 
 
 def second_kernel(at_ref, *refs):
-    acts, held, across, refs = refs[:NX], refs[NX], refs[NX + 1], refs[NX + 2 :]
+    acts, held, across, refs = (refs[0], refs[1], refs[3], refs[2]), refs[NX], refs[NX + 1], refs[NX + 2 :]
     zero_ref, hold_ref, half_ref, give_ref, grad_ref, col, tall, both, parts = refs
     width = held.shape[1] // 27
     third = 9 * width
@@ -209,16 +214,11 @@
 
 
 def finish_kernel(at_ref, *refs):
-    own_refs, other_ref, keep_ref, got_ref = refs[:4], refs[4], refs[5], refs[6]
-    mixed_ref, input_ref, one_ref, two_ref, near, far, wide, cells, sems = refs[7:]
+    own_refs, other_ref, keep_ref, got_ref, order_ref = refs[:4], *refs[4:8]
+    mixed_ref, input_ref, one_ref, two_ref, near, far, wide, cells, sems = refs[8:]
     taps, channels = one_ref.shape
     _, _, size, group = other_ref.shape
-    width = group // NZ
     third = taps // 3
-    old = lax.broadcasted_iota(jnp.int32, (channels, channels), 0)
-    new = lax.broadcasted_iota(jnp.int32, (channels, channels), 1)
-    place = (new // width) % NX * group + new // (NX * width) * width + new % width
-    order = (old == place).astype(F32).astype(BF16)
 
     def run(cell_outs, grad_outs):
         copies = []
@@ -234,12 +234,12 @@
         pieces = (lambda k, x: own_refs[k][x]), (lambda k, x: other_ref[k, x])
         for n, full in enumerate((near, far)):
             for k in range(4):
-                rows = pl.ds(pl.multiple_of(lax.rem(at_ref[2] + k, 4) * size, 16), size)
+                rows = pl.ds(pl.multiple_of(lax.rem(at_ref[2] + (0, 1, 3, 2)[k], 4) * size, 16), size)
                 for x in range(NX):
                     full[rows, x * group : (x + 1) * group] = pieces[n](k, x)
             for a in range(3):
                 rows = pl.ds(a * third, third)
-                wide[n, rows, :] = dot(full[a * third : (a + 1) * third, :], order, ((1,), (0,)))
+                wide[n, rows, :] = dot(full[a * third : (a + 1) * third, :], order_ref[...], ((1,), (0,)))
                 send(wide.at[n, rows], grad_outs[n].at[rows])
         for copy in copies:
             copy.wait()
@@ -298,7 +298,7 @@
     pair = jnp.broadcast_to(pair, (NZ,) + plane).reshape(everyone)
     mine = lax.all_to_all(pair, ("z", "spatial"), 0, 0, tiled=True).reshape((NZ,) + plane)
 
-    groups = call(regroup_kernel, [((taps, group), BF16)] * NX, [], "regroup", 2 * taps * channels * channels, at, one, two)
+    *groups, order = call(regroup_kernel, [((taps, group), BF16)] * NX + [((channels, channels), BF16)], [], "regroup", 2 * taps * channels * channels, at, one, two)
     kernels = [groups[0]] + [around(groups[NX - k], "x", k) for k in range(1, NX)]
 
     own, *sends, held = call(
@@ -307,18 +307,18 @@
         [((NX * 9 * width, 2 * group), BF16), ((2 * group, PLANE), BF16), ((NX * 9 * width, PLANE), F32)],
         "conv_in", work, at, mine, *kernels,
     )
-    sends = [around(part, "x", NX - k) for k, part in enumerate(sends, 1)]
+    sends = [around(sends[k - 1], "x", NX - k) for k in (2, 1, 3)]
     own = own + sum(part.astype(F32) for part in sends)
     held, across = swap(held), swap(mine)
 
     (send,) = call(act_kernel, [(plane, BF16)], [], "act", 0, at, own, swap(own))
-    acts = [send] + [around(send, "x", k) for k in range(1, NX)]
+    acts = {k: around(send, "x", k) for k in (1, 3, 2)}
     far = NZ // 2
     zero, hold, half, give, grads = call(
         second_kernel,
         [(plane, BF16), ((far - 1,) + plane, BF16), (plane[1:], BF16), ((NZ - 1,) + plane[1:], BF16), ((4 * NX,) + piece, BF16)],
         [((NX * 18 * width, PLANE), BF16), ((NX * 18 * width, group), BF16), ((2 * group, PLANE), BF16), ((NZ,) + plane, BF16)],
-        "conv_out", 2 * work, at, *acts, held, across,
+        "conv_out", 2 * work, at, send, acts[1], acts[3], acts[2], held, across,
     )
     grads = lax.all_to_all(grads, ("samples", "x"), 0, 0, tiled=True)
     got = swap(give)
@@ -326,7 +326,8 @@
     came = {j: apart(sends[j - 1], j) for j in range(far, 0, -1)}
     summed = jnp.sum(grads.reshape((4, NX) + piece).astype(F32), axis=0).astype(BF16)
     summed, came[far] = lax.optimization_barrier((summed, came[far]))
-    pieces = [summed] + [around(summed, "samples", k) for k in (1, 2, 3)]
+    pieces = {k: around(summed, "samples", k) for k in (1, 3, 2)}
+    pieces = [summed] + [pieces[k] for k in (1, 3, 2)]
     pieces, came = lax.optimization_barrier((pieces, came))
     others = swap(jnp.stack(pieces))
     keep, give = call(
@@ -337,7 +338,7 @@
         [((width, PLANE), BF16)] * 2 + [((taps, channels), F32)] * 2,
         [((28 * width, channels), BF16)] * 2
         + [((2, taps, channels), F32), (plane, BF16), pltpu.SemaphoreType.DMA((8,))],
-        "finish", 0, at, *pieces, others, keep, swap(give), out_space=pl.ANY,
+        "finish", 0, at, *pieces, others, keep, swap(give), order, out_space=pl.ANY,
     )
     shape = (width, 1, 1, PLANE)
     weights = (27, width, channels)

time: 86.7 us -> 86.2 us (level)
  waiting for transfers between devices: 26.4 us -> 24.1 us
  starting transfers between devices: 46.1 us -> 48 us
    ppermute x12, waiting for transfers between devices: 8.23 us -> 6.25 us  [around(): lax.ppermute(values, axis, [((i + step) % size, i) for i in range(size)])]
    ppermute x12, starting transfers between devices: 17.4 us -> 18.9 us  [around(): lax.ppermute(values, axis, [((i + step) % size, i) for i in range(size)])]
  transfers between devices with their start and end apart: 24 -> 24, of which waited for: 13 -> 12; matrix products, arithmetic and copies ran while one was open for 0% -> 0% of each run, Pallas kernels for 6% -> 6%
where the time goes in v10:
time: 86.2 us; the launch traced here: 85.8 us
  starting transfers between devices  48 us (56%)
  waiting for transfers between devices  24.1 us (28%)
  Pallas kernels  10.9 us (13%)
  other arithmetic  1.07 us (1%)
  between operations  0.92 us (1%)
  local copies, waits for them, and re-layouts  0.89 us (1%)
    ppermute x12, starting transfers between devices, around(): lax.ppermute(values, axis, [((i + step) % size, i) for i in range(size)])  18.9 us
    all_to_all x1, waiting for transfers between devices, body(): lax.all_to_all(pair, ('z', 'spatial'), 0, 0, tiled=True)  12.2 us
    pallas_call x6, Pallas kernels, call(): pl.pallas_call(kernel, out_shape=tuple((jax.ShapeDtypeStruct(s, t) for s,...  10.9 us
    all_to_all x1, starting transfers between devices, body(): lax.all_to_all(pair, ('z', 'spatial'), 0, 0, tiled=True)  10.1 us
    all_to_all x1, starting transfers between devices, body(): grads = lax.all_to_all(grads, ('samples', 'x'), 0, 0, tiled=True)  6.35 us
    ppermute x6, starting transfers between devices, swap(): return lax.ppermute(values, 'spatial', [(0, 1), (1, 0)])  6.33 us
    ppermute x4, starting transfers between devices, apart(): return lax.ppermute(values, ('z', 'spatial'), pairs)  6.26 us
    ppermute x12, waiting for transfers between devices, around(): lax.ppermute(values, axis, [((i + step) % size, i) for i in range(size)])  6.25 us
  transfers between devices with their start and end apart: 24, of which 12 were waited for; matrix products, arithmetic and copies ran while one was open for 0% of the time, Pallas kernels for 6%

profile of v10, /device:TPU:1, one launch (start us, length us, event | category | flops | bytes accessed | tf_op | source)
XLA Modules:
  0.0 85.8 jit_solution(14059666540375972580)
XLA Ops:
  0.6 0.8 pad_maximum_fusion.4
  1.4 0.9 broadcast_in_dim.3
  2.3 0.0 copy-start
  2.3 0.0 copy-start.1
  2.3 10.1 %all-to-all-start = ((bf16[16,16,1024]{2,1,0:T(8,128)(2,1)}), bf16[16,16,1024]{2,1,0:T(8,128)(2,1)S(1)}, u32[]{:S(2)}, u32[]{:S(2)}) async-start(bf16[16,16,1024]{2,1,0:T(8,128)(2,1)} %bitcast.6), calls=%async_computation | async-start | bytes 1048576 | tf_op jit(solution)/shard_map/all_to_all | solution.py:299
  12.4 0.1 pad_add_fusion.at_ref
  12.5 0.0 copy-done
  12.5 0.0 copy-done.1
  12.5 1.3 %regroup.1 = (bf16[432,128]{1,0:T(8,128)(2,1)S(1)}, bf16[432,128]{1,0:T(8,128)(2,1)S(1)}, bf16[432,128]{1,0:T(8,128)(2,1)S(1)}, bf16[432,128]{1,0:T(8,128)(2,1)S(1)}, bf16[512,512]{1,0:T(8,128)(2,1)S(1)}) custom-call(s32[4]{0:T(128)S(1)} %pad_add_fusion.at_ref, bf16[432,512]{1,0:T(8,128)(2,1)S(1)} %bitcast.32, bf16[432,512]{1,0:T(8,128)(2,1)S(1)} %bitcast.33), custom_call_target="tpu_custom_call" | custom-call | flops 226492416 | tf_op jit(solution)/shard_map/regroup/pallas_call | solution.py:258
  13.8 2.6 %collective-permute-start = (bf16[432,128]{1,0:T(8,128)(2,1)S(1)}, bf16[432,128]{1,0:T(8,128)(2,1)S(1)}, u32[]{:S(2)}, u32[]{:S(2)}) collective-permute-start(bf16[432,128]{1,0:T(8,128)(2,1)S(1)} %get-tuple-element.36), channel_id=1, source_target_pairs={{2,0},{4,2},{6,4},{0,6},{3,1},{5,3},{7,5},{1,7},{10,8},{12,10},{14... | collective-permute-start | bytes 331784 | tf_op jit(solution)/shard_map/ppermute | solution.py:276
  16.4 0.5 collective-permute-start.1
  16.9 0.6 collective-permute-start.2
  17.5 12.2 %all-to-all-done = bf16[16,16,1024]{2,1,0:T(8,128)(2,1)S(1)} async-done(((bf16[16,16,1024]{2,1,0:T(8,128)(2,1)}), bf16[16,16,1024]{2,1,0:T(8,128)(2,1)S(1)}, u32[]{:S(2)}, u32[]{:S(2)}) %all-to-all-start) | async-done | bytes 524320 | tf_op jit(solution)/shard_map/all_to_all | solution.py:299
  29.7 0.0 collective-permute-start.11
  29.7 0.0 collective-permute-done.refs_1_
  29.7 0.0 collective-permute-done.1.refs_2_
  29.7 0.0 collective-permute-done.2.refs_3_
  29.7 2.5 %conv_in.1 = (f32[2,16,1024]{2,1,0:T(8,128)S(1)}, bf16[2,16,1024]{2,1,0:T(8,128)(2,1)S(1)}, bf16[2,16,1024]{2,1,0:T(8,128)(2,1)S(1)}, bf16[2,16,1024]{2,1,0:T(8,128)(2,1)S(1)}, bf16[4,432,128]{2,1,0:T(8,128)(2,1)S(1)}) custom-call(s32[4]{0:T(128)S(1)} %pad_add_fusion.at_ref, bf16[8,2,16,1024]{3,2,1,0:T(8,128)(2,1)S(1)} %bitcast.28, ...), custom_call_target="tpu_custom_call" | custom-call | flops 603979776 | tf_op jit(solution)/shard_map/conv_in/pallas_call | solution.py:258
  32.2 2.8 %collective-permute-start.3 = (bf16[2,16,1024]{2,1,0:T(8,128)(2,1)S(1)}, bf16[2,16,1024]{2,1,0:T(8,128)(2,1)S(1)}, u32[]{:S(2)}, u32[]{:S(2)}) collective-permute-start(bf16[2,16,1024]{2,1,0:T(8,128)(2,1)S(1)} %get-tuple-element.40), channel_id=1, source_target_pairs={{4,0},{6,2},{0,4},{2,6},{5,1},{7,3},{1,5},{3,7},{12,8},{14,10},{8,... | collective-permute-start | bytes 196616 | tf_op jit(solution)/shard_map/ppermute | solution.py:276
  35.1 0.3 collective-permute-start.4
  35.4 2.4 %collective-permute-start.5 = (bf16[2,16,1024]{2,1,0:T(8,128)(2,1)S(1)}, bf16[2,16,1024]{2,1,0:T(8,128)(2,1)S(1)}, u32[]{:S(2)}, u32[]{:S(2)}) collective-permute-start(bf16[2,16,1024]{2,1,0:T(8,128)(2,1)S(1)} %get-tuple-element.42), channel_id=1, source_target_pairs={{2,0},{4,2},{6,4},{0,6},{3,1},{5,3},{7,5},{1,7},{10,8},{12,10},{14... | collective-permute-start | bytes 196616 | tf_op jit(solution)/shard_map/ppermute | solution.py:276
  37.7 1.3 %collective-permute-start.10 = (bf16[4,432,128]{2,1,0:T(8,128)(2,1)S(1)}, bf16[4,432,128]{2,1,0:T(8,128)(2,1)S(1)}, u32[]{:S(2)}, u32[]{:S(2)}) collective-permute-start(bf16[4,432,128]{2,1,0:T(8,128)(2,1)S(1)} %get-tuple-element.43), channel_id=1, source_target_pairs={{0,1},{1,0},{2,3},{3,2},{4,5},{5,4},{6,7},{7,6},{8,9},{9,8},{10,11... | collective-permute-start | bytes 1327112 | tf_op jit(solution)/shard_map/ppermute | solution.py:271
  39.0 0.0 collective-permute-done.3
  39.1 0.3 collective-permute-done.4
  39.4 0.0 collective-permute-done.5
  39.4 2.0 %collective-permute-start.6 = (f32[2,16,1024]{2,1,0:T(8,128)S(1)}, f32[2,16,1024]{2,1,0:T(8,128)S(1)}, u32[]{:S(2)}, u32[]{:S(2)}) collective-permute-start(f32[2,16,1024]{2,1,0:T(8,128)S(1)} %add_add_fusion.own_ref), channel_id=1, source_target_pairs={{0,1},{1,0},{2,3},{3,2},{4,5},{5,4},{6,7},{7,6},{8,9},{9,8},{10,11... | collective-permute-start | bytes 393224 | tf_op jit(solution)/shard_map/ppermute | solution.py:271
  41.4 1.0 %collective-permute-done.6.other_ref = f32[2,16,1024]{2,1,0:T(8,128)S(1)} collective-permute-done((f32[2,16,1024]{2,1,0:T(8,128)S(1)}, f32[2,16,1024]{2,1,0:T(8,128)S(1)}, u32[]{:S(2)}, u32[]{:S(2)}) %collective-permute-start.6) | collective-permute-done | bytes 131104 | tf_op jit(solution)/shard_map/ppermute | solution.py:271
  42.4 0.6 act.1.refs_0_
  43.0 1.3 %collective-permute-start.9 = (bf16[2,16,1024]{2,1,0:T(8,128)(2,1)S(1)}, bf16[2,16,1024]{2,1,0:T(8,128)(2,1)S(1)}, u32[]{:S(2)}, u32[]{:S(2)}) collective-permute-start(bf16[2,16,1024]{2,1,0:T(8,128)(2,1)S(1)} %act.1.refs_0_), channel_id=1, source_target_pairs={{4,0},{6,2},{0,4},{2,6},{5,1},{7,3},{1,5},{3,7},{12,8},{14,10},{8,... | collective-permute-start | bytes 196616 | tf_op jit(solution)/shard_map/ppermute | solution.py:276
  44.3 2.3 %collective-permute-start.8 = (bf16[2,16,1024]{2,1,0:T(8,128)(2,1)S(1)}, bf16[2,16,1024]{2,1,0:T(8,128)(2,1)S(1)}, u32[]{:S(2)}, u32[]{:S(2)}) collective-permute-start(bf16[2,16,1024]{2,1,0:T(8,128)(2,1)S(1)} %act.1.refs_0_), channel_id=1, source_target_pairs={{6,0},{0,2},{2,4},{4,6},{7,1},{1,3},{3,5},{5,7},{14,8},{8,10},{10,... | collective-permute-start | bytes 196616 | tf_op jit(solution)/shard_map/ppermute | solution.py:276
  46.6 0.3 collective-permute-start.7
  47.0 0.8 collective-permute-done.9.refs_3_
  47.7 2.0 %collective-permute-done.8.refs_2_ = bf16[2,16,1024]{2,1,0:T(8,128)(2,1)S(1)} collective-permute-done((bf16[2,16,1024]{2,1,0:T(8,128)(2,1)S(1)}, bf16[2,16,1024]{2,1,0:T(8,128)(2,1)S(1)}, u32[]{:S(2)}, u32[]{:S(2)}) %collective-permute-start.8) | collective-permute-done | bytes 65568 | tf_op jit(solution)/shard_map/ppermute | solution.py:276
  49.8 0.3 collective-permute-done.7.refs_1_
  50.1 0.0 collective-permute-done.10.refs_4_
  50.1 0.0 collective-permute-done.11.refs_5_
  50.1 3.7 %conv_out.1 = (bf16[2,16,1024]{2,1,0:T(8,128)(2,1)S(1)}, bf16[3,2,16,1024]{3,2,1,0:T(8,128)(2,1)S(1)}, bf16[16,1024]{1,0:T(8,128)(2,1)S(1)}, bf16[7,16,1024]{2,1,0:T(8,128)(2,1)S(1)}, bf16[16,112,128]{2,1,0:T(8,128)(2,1)}) custom-call(s32[4]{0:T(128)S(1)} %pad_add_fusion.at_ref, bf16[2,16,1024]{2,1,0:T(8,128)(2,1)S(1)} %act.1.refs_0_, ...), custom_call_target="tpu_custom_call" | custom-call | flops 1207959552 | tf_op jit(solution)/shard_map/conv_out/pallas_call | solution.py:258
  53.8 6.3 %all-to-all-start.1 = ((bf16[16,112,128]{2,1,0:T(8,128)(2,1)}), bf16[16,112,128]{2,1,0:T(8,128)(2,1)S(1)}, u32[]{:S(2)}, u32[]{:S(2)}) async-start(bf16[16,112,128]{2,1,0:T(8,128)(2,1)} %get-tuple-element.44), calls=%async_computation.1 | async-start | bytes 917504 | tf_op jit(solution)/shard_map/all_to_all | solution.py:323
  60.1 1.3 %collective-permute-start.12 = (bf16[7,16,1024]{2,1,0:T(8,128)(2,1)S(1)}, bf16[7,16,1024]{2,1,0:T(8,128)(2,1)S(1)}, u32[]{:S(2)}, u32[]{:S(2)}) collective-permute-start(bf16[7,16,1024]{2,1,0:T(8,128)(2,1)S(1)} %get-tuple-element.46), channel_id=1, source_target_pairs={{0,1},{1,0},{2,3},{3,2},{4,5},{5,4},{6,7},{7,6},{8,9},{9,8},{10,11... | collective-permute-start | bytes 688136 | tf_op jit(solution)/shard_map/ppermute | solution.py:271
  61.5 1.1 %collective-permute-done.12 = bf16[7,16,1024]{2,1,0:T(8,128)(2,1)S(1)} collective-permute-done((bf16[7,16,1024]{2,1,0:T(8,128)(2,1)S(1)}, bf16[7,16,1024]{2,1,0:T(8,128)(2,1)S(1)}, u32[]{:S(2)}, u32[]{:S(2)}) %collective-permute-start.12) | collective-permute-done | bytes 229408 | tf_op jit(solution)/shard_map/ppermute | solution.py:271
  62.6 1.0 %collective-permute-start.13 = (bf16[2,16,1024]{2,1,0:T(8,128)(2,1)S(1)}, bf16[2,16,1024]{2,1,0:T(8,128)(2,1)S(1)}, u32[]{:S(2)}, u32[]{:S(2)}) collective-permute-start(bf16[2,16,1024]{2,1,0:T(8,128)(2,1)S(1)} %pad_maximum_fusion.5), channel_id=1, source_target_pairs={{0,32},{8,40},{16,48},{24,56},{32,0},{40,8},{48,16},{56,24},{1,33}... | collective-permute-start | bytes 196616 | tf_op jit(solution)/shard_map/ppermute | solution.py:282
  63.7 2.4 %collective-permute-start.17 = (bf16[2,2,16,1024]{3,2,1,0:T(8,128)(2,1)S(1)}, bf16[2,2,16,1024]{3,2,1,0:T(8,128)(2,1)S(1)}, u32[]{:S(2)}, u32[]{:S(2)}) collective-permute-start(bf16[2,2,16,1024]{3,2,1,0:T(8,128)(2,1)S(1)} %pad_maximum_fusion.1), channel_id=1, source_target_pairs={{0,8},{8,16},{16,24},{24,32},{32,40},{40,48},{48,56},{56,0},{1,57}... | collective-permute-start | bytes 393224 | tf_op jit(solution)/shard_map/ppermute | solution.py:282
  66.0 0.1 collective-permute-start.18
  66.2 2.8 %collective-permute-start.19 = (bf16[2,2,16,1024]{3,2,1,0:T(8,128)(2,1)S(1)}, bf16[2,2,16,1024]{3,2,1,0:T(8,128)(2,1)S(1)}, u32[]{:S(2)}, u32[]{:S(2)}) collective-permute-start(bf16[2,2,16,1024]{3,2,1,0:T(8,128)(2,1)S(1)} %pad_maximum_fusion.3), channel_id=1, source_target_pairs={{0,24},{8,32},{16,40},{24,48},{32,56},{40,0},{48,8},{56,16},{1,41}... | collective-permute-start | bytes 393224 | tf_op jit(solution)/shard_map/ppermute | solution.py:282
  68.9 0.8 all-to-all-done.1
  69.7 0.1 reduce_sum.12.refs_0_
  69.8 1.5 %collective-permute-done.13.refs_3_ = bf16[2,16,1024]{2,1,0:T(8,128)(2,1)S(1)} collective-permute-done((bf16[2,16,1024]{2,1,0:T(8,128)(2,1)S(1)}, bf16[2,16,1024]{2,1,0:T(8,128)(2,1)S(1)}, u32[]{:S(2)}, u32[]{:S(2)}) %collective-permute-start.13) | collective-permute-done | bytes 65568 | tf_op jit(solution)/shard_map/ppermute | solution.py:282
  71.3 3.1 %collective-permute-start.16 = (bf16[4,112,128]{2,1,0:T(8,128)(2,1)S(1)}, bf16[4,112,128]{2,1,0:T(8,128)(2,1)S(1)}, u32[]{:S(2)}, u32[]{:S(2)}) collective-permute-start(bf16[4,112,128]{2,1,0:T(8,128)(2,1)S(1)} %reduce_sum.12.refs_0_), channel_id=1, source_target_pairs={{128,0},{192,64},{0,128},{64,192},{129,1},{193,65},{1,129},{65,193... | collective-permute-start | bytes 344072 | tf_op jit(solution)/shard_map/ppermute | solution.py:276
  74.4 0.3 collective-permute-start.15
  74.7 0.0 collective-permute-done.17.refs_0_
  74.7 2.4 %collective-permute-start.14 = (bf16[4,112,128]{2,1,0:T(8,128)(2,1)S(1)}, bf16[4,112,128]{2,1,0:T(8,128)(2,1)S(1)}, u32[]{:S(2)}, u32[]{:S(2)}) collective-permute-start(bf16[4,112,128]{2,1,0:T(8,128)(2,1)S(1)} %reduce_sum.12.refs_0_), channel_id=1, source_target_pairs={{64,0},{128,64},{192,128},{0,192},{65,1},{129,65},{193,129},{1,193... | collective-permute-start | bytes 344072 | tf_op jit(solution)/shard_map/ppermute | solution.py:276
  77.1 0.0 collective-permute-done.18.refs_1_
  77.1 0.0 collective-permute-done.19.refs_2_
  77.1 0.0 collective-permute-done.16.refs_3_
  77.1 2.5 %collective-permute-done.15.refs_2_ = bf16[4,112,128]{2,1,0:T(8,128)(2,1)S(1)} collective-permute-done((bf16[4,112,128]{2,1,0:T(8,128)(2,1)S(1)}, bf16[4,112,128]{2,1,0:T(8,128)(2,1)S(1)}, u32[]{:S(2)}, u32[]{:S(2)}) %collective-permute-start.15) | collective-permute-done | bytes 114720 | tf_op jit(solution)/shard_map/ppermute | solution.py:276
  79.7 0.2 collective-permute-done.14.refs_1_
  79.9 0.1 pad_maximum_fusion
  79.9 1.6 %collective-permute-start.20 = (bf16[4,4,112,128]{3,2,1,0:T(8,128)(2,1)S(1)}, bf16[4,4,112,128]{3,2,1,0:T(8,128)(2,1)S(1)}, u32[]{:S(2)}, u32[]{:S(2)}) collective-permute-start(bf16[4,4,112,128]{3,2,1,0:T(8,128)(2,1)S(1)} %pad_maximum_fusion), channel_id=1, source_target_pairs={{0,1},{1,0},{2,3},{3,2},{4,5},{5,4},{6,7},{7,6},{8,9},{9,8},{10,11... | collective-permute-start | bytes 1376264 | tf_op jit(solution)/shard_map/ppermute | solution.py:271
  81.5 0.6 sum.1
  82.2 0.1 collective-permute-start.21
  82.3 1.2 %collective-permute-done.21.refs_6_ = bf16[2,16,1024]{2,1,0:T(8,128)(2,1)S(1)} collective-permute-done((bf16[2,16,1024]{2,1,0:T(8,128)(2,1)S(1)}, bf16[2,16,1024]{2,1,0:T(8,128)(2,1)S(1)}, u32[]{:S(2)}, u32[]{:S(2)}) %collective-permute-start.21) | collective-permute-done | bytes 65568 | tf_op jit(solution)/shard_map/ppermute | solution.py:271
  83.5 0.0 collective-permute-done.20.refs_4_
  83.5 2.2 %finish.1 = (bf16[16,1024]{1,0:T(8,128)(2,1)}, bf16[16,1024]{1,0:T(8,128)(2,1)}, f32[432,512]{1,0:T(8,128)}, f32[432,512]{1,0:T(8,128)}) custom-call(s32[4]{0:T(128)S(1)} %pad_add_fusion.at_ref, bf16[4,112,128]{2,1,0:T(8,128)(2,1)S(1)} %reduce_sum.12.refs_0_, bf16[4,112,128]{2,1,0:T(8,128)(2,1)S(1)} %collective-permute-done.14.refs_1_, ...), custom_call_target="tpu_custom_call" | custom-call | tf_op jit(solution)/shard_map/finish/pallas_call | solution.py:258
  (8 shorter events, 0.1 us)
Async XLA Ops:
  2.3 10.2 %copy-start = (bf16[27,16,512]{2,1,0:T(8,128)(2,1)S(1)}, bf16[27,16,512]{2,1,0:T(8,128)(2,1)}, u32[]{:S(2)}) copy-start(bf16[27,16,512]{2,1,0:T(8,128)(2,1)} %param.5) | copy-start | bytes 1327108
  2.3 10.2 %copy-start.1 = (bf16[27,16,512]{2,1,0:T(8,128)(2,1)S(1)}, bf16[27,16,512]{2,1,0:T(8,128)(2,1)}, u32[]{:S(2)}) copy-start(bf16[27,16,512]{2,1,0:T(8,128)(2,1)} %param.6) | copy-start | bytes 1327108
  2.3 27.4 %all-to-all-start = ((bf16[16,16,1024]{2,1,0:T(8,128)(2,1)}), bf16[16,16,1024]{2,1,0:T(8,128)(2,1)S(1)}, u32[]{:S(2)}, u32[]{:S(2)}) async-start(bf16[16,16,1024]{2,1,0:T(8,128)(2,1)} %bitcast.6), calls=%async_computation | async-start | bytes 1048576 | tf_op jit(solution)/shard_map/all_to_all | solution.py:299
  13.8 15.9 %collective-permute-start = (bf16[432,128]{1,0:T(8,128)(2,1)S(1)}, bf16[432,128]{1,0:T(8,128)(2,1)S(1)}, u32[]{:S(2)}, u32[]{:S(2)}) collective-permute-start(bf16[432,128]{1,0:T(8,128)(2,1)S(1)} %get-tuple-element.36), channel_id=1, source_target_pairs={{2,0},{4,2},{6,4},{0,6},{3,1},{5,3},{7,5},{1,7},{10,8},{12,10},{14... | collective-permute-start | bytes 331784 | tf_op jit(solution)/shard_map/ppermute | solution.py:276
  16.4 13.3 %collective-permute-start.1 = (bf16[432,128]{1,0:T(8,128)(2,1)S(1)}, bf16[432,128]{1,0:T(8,128)(2,1)S(1)}, u32[]{:S(2)}, u32[]{:S(2)}) collective-permute-start(bf16[432,128]{1,0:T(8,128)(2,1)S(1)} %get-tuple-element.37), channel_id=1, source_target_pairs={{4,0},{6,2},{0,4},{2,6},{5,1},{7,3},{1,5},{3,7},{12,8},{14,10},{8,... | collective-permute-start | bytes 331784 | tf_op jit(solution)/shard_map/ppermute | solution.py:276
  16.9 12.9 %collective-permute-start.2 = (bf16[432,128]{1,0:T(8,128)(2,1)S(1)}, bf16[432,128]{1,0:T(8,128)(2,1)S(1)}, u32[]{:S(2)}, u32[]{:S(2)}) collective-permute-start(bf16[432,128]{1,0:T(8,128)(2,1)S(1)} %get-tuple-element.38), channel_id=1, source_target_pairs={{6,0},{0,2},{2,4},{4,6},{7,1},{1,3},{3,5},{5,7},{14,8},{8,10},{10,... | collective-permute-start | bytes 331784 | tf_op jit(solution)/shard_map/ppermute | solution.py:276
  29.7 20.4 %collective-permute-start.11 = (bf16[8,2,16,1024]{3,2,1,0:T(8,128)(2,1)S(1)}, bf16[8,2,16,1024]{3,2,1,0:T(8,128)(2,1)S(1)}, u32[]{:S(2)}, u32[]{:S(2)}) collective-permute-start(bf16[8,2,16,1024]{3,2,1,0:T(8,128)(2,1)S(1)} %bitcast.27), channel_id=1, source_target_pairs={{0,1},{1,0},{2,3},{3,2},{4,5},{5,4},{6,7},{7,6},{8,9},{9,8},{10,11... | collective-permute-start | bytes 1572872 | tf_op jit(solution)/shard_map/ppermute | solution.py:271
  32.2 6.8 %collective-permute-start.3 = (bf16[2,16,1024]{2,1,0:T(8,128)(2,1)S(1)}, bf16[2,16,1024]{2,1,0:T(8,128)(2,1)S(1)}, u32[]{:S(2)}, u32[]{:S(2)}) collective-permute-start(bf16[2,16,1024]{2,1,0:T(8,128)(2,1)S(1)} %get-tuple-element.40), channel_id=1, source_target_pairs={{4,0},{6,2},{0,4},{2,6},{5,1},{7,3},{1,5},{3,7},{12,8},{14,10},{8,... | collective-permute-start | bytes 196616 | tf_op jit(solution)/shard_map/ppermute | solution.py:276
  35.1 4.3 %collective-permute-start.4 = (bf16[2,16,1024]{2,1,0:T(8,128)(2,1)S(1)}, bf16[2,16,1024]{2,1,0:T(8,128)(2,1)S(1)}, u32[]{:S(2)}, u32[]{:S(2)}) collective-permute-start(bf16[2,16,1024]{2,1,0:T(8,128)(2,1)S(1)} %get-tuple-element.41), channel_id=1, source_target_pairs={{6,0},{0,2},{2,4},{4,6},{7,1},{1,3},{3,5},{5,7},{14,8},{8,10},{10,... | collective-permute-start | bytes 196616 | tf_op jit(solution)/shard_map/ppermute | solution.py:276
  35.4 4.0 %collective-permute-start.5 = (bf16[2,16,1024]{2,1,0:T(8,128)(2,1)S(1)}, bf16[2,16,1024]{2,1,0:T(8,128)(2,1)S(1)}, u32[]{:S(2)}, u32[]{:S(2)}) collective-permute-start(bf16[2,16,1024]{2,1,0:T(8,128)(2,1)S(1)} %get-tuple-element.42), channel_id=1, source_target_pairs={{2,0},{4,2},{6,4},{0,6},{3,1},{5,3},{7,5},{1,7},{10,8},{12,10},{14... | collective-permute-start | bytes 196616 | tf_op jit(solution)/shard_map/ppermute | solution.py:276
  37.7 12.4 %collective-permute-start.10 = (bf16[4,432,128]{2,1,0:T(8,128)(2,1)S(1)}, bf16[4,432,128]{2,1,0:T(8,128)(2,1)S(1)}, u32[]{:S(2)}, u32[]{:S(2)}) collective-permute-start(bf16[4,432,128]{2,1,0:T(8,128)(2,1)S(1)} %get-tuple-element.43), channel_id=1, source_target_pairs={{0,1},{1,0},{2,3},{3,2},{4,5},{5,4},{6,7},{7,6},{8,9},{9,8},{10,11... | collective-permute-start | bytes 1327112 | tf_op jit(solution)/shard_map/ppermute | solution.py:271
  39.4 3.0 %collective-permute-start.6 = (f32[2,16,1024]{2,1,0:T(8,128)S(1)}, f32[2,16,1024]{2,1,0:T(8,128)S(1)}, u32[]{:S(2)}, u32[]{:S(2)}) collective-permute-start(f32[2,16,1024]{2,1,0:T(8,128)S(1)} %add_add_fusion.own_ref), channel_id=1, source_target_pairs={{0,1},{1,0},{2,3},{3,2},{4,5},{5,4},{6,7},{7,6},{8,9},{9,8},{10,11... | collective-permute-start | bytes 393224 | tf_op jit(solution)/shard_map/ppermute | solution.py:271
  43.0 4.7 %collective-permute-start.9 = (bf16[2,16,1024]{2,1,0:T(8,128)(2,1)S(1)}, bf16[2,16,1024]{2,1,0:T(8,128)(2,1)S(1)}, u32[]{:S(2)}, u32[]{:S(2)}) collective-permute-start(bf16[2,16,1024]{2,1,0:T(8,128)(2,1)S(1)} %act.1.refs_0_), channel_id=1, source_target_pairs={{4,0},{6,2},{0,4},{2,6},{5,1},{7,3},{1,5},{3,7},{12,8},{14,10},{8,... | collective-permute-start | bytes 196616 | tf_op jit(solution)/shard_map/ppermute | solution.py:276
  44.3 5.5 %collective-permute-start.8 = (bf16[2,16,1024]{2,1,0:T(8,128)(2,1)S(1)}, bf16[2,16,1024]{2,1,0:T(8,128)(2,1)S(1)}, u32[]{:S(2)}, u32[]{:S(2)}) collective-permute-start(bf16[2,16,1024]{2,1,0:T(8,128)(2,1)S(1)} %act.1.refs_0_), channel_id=1, source_target_pairs={{6,0},{0,2},{2,4},{4,6},{7,1},{1,3},{3,5},{5,7},{14,8},{8,10},{10,... | collective-permute-start | bytes 196616 | tf_op jit(solution)/shard_map/ppermute | solution.py:276
  46.6 3.5 %collective-permute-start.7 = (bf16[2,16,1024]{2,1,0:T(8,128)(2,1)S(1)}, bf16[2,16,1024]{2,1,0:T(8,128)(2,1)S(1)}, u32[]{:S(2)}, u32[]{:S(2)}) collective-permute-start(bf16[2,16,1024]{2,1,0:T(8,128)(2,1)S(1)} %act.1.refs_0_), channel_id=1, source_target_pairs={{2,0},{4,2},{6,4},{0,6},{3,1},{5,3},{7,5},{1,7},{10,8},{12,10},{14... | collective-permute-start | bytes 196616 | tf_op jit(solution)/shard_map/ppermute | solution.py:276
  53.8 15.9 %all-to-all-start.1 = ((bf16[16,112,128]{2,1,0:T(8,128)(2,1)}), bf16[16,112,128]{2,1,0:T(8,128)(2,1)S(1)}, u32[]{:S(2)}, u32[]{:S(2)}) async-start(bf16[16,112,128]{2,1,0:T(8,128)(2,1)} %get-tuple-element.44), calls=%async_computation.1 | async-start | bytes 917504 | tf_op jit(solution)/shard_map/all_to_all | solution.py:323
  60.1 2.4 %collective-permute-start.12 = (bf16[7,16,1024]{2,1,0:T(8,128)(2,1)S(1)}, bf16[7,16,1024]{2,1,0:T(8,128)(2,1)S(1)}, u32[]{:S(2)}, u32[]{:S(2)}) collective-permute-start(bf16[7,16,1024]{2,1,0:T(8,128)(2,1)S(1)} %get-tuple-element.46), channel_id=1, source_target_pairs={{0,1},{1,0},{2,3},{3,2},{4,5},{5,4},{6,7},{7,6},{8,9},{9,8},{10,11... | collective-permute-start | bytes 688136 | tf_op jit(solution)/shard_map/ppermute | solution.py:271
  62.6 8.7 %collective-permute-start.13 = (bf16[2,16,1024]{2,1,0:T(8,128)(2,1)S(1)}, bf16[2,16,1024]{2,1,0:T(8,128)(2,1)S(1)}, u32[]{:S(2)}, u32[]{:S(2)}) collective-permute-start(bf16[2,16,1024]{2,1,0:T(8,128)(2,1)S(1)} %pad_maximum_fusion.5), channel_id=1, source_target_pairs={{0,32},{8,40},{16,48},{24,56},{32,0},{40,8},{48,16},{56,24},{1,33}... | collective-permute-start | bytes 196616 | tf_op jit(solution)/shard_map/ppermute | solution.py:282
  63.7 11.0 %collective-permute-start.17 = (bf16[2,2,16,1024]{3,2,1,0:T(8,128)(2,1)S(1)}, bf16[2,2,16,1024]{3,2,1,0:T(8,128)(2,1)S(1)}, u32[]{:S(2)}, u32[]{:S(2)}) collective-permute-start(bf16[2,2,16,1024]{3,2,1,0:T(8,128)(2,1)S(1)} %pad_maximum_fusion.1), channel_id=1, source_target_pairs={{0,8},{8,16},{16,24},{24,32},{32,40},{40,48},{48,56},{56,0},{1,57}... | collective-permute-start | bytes 393224 | tf_op jit(solution)/shard_map/ppermute | solution.py:282
  66.0 11.1 %collective-permute-start.18 = (bf16[2,2,16,1024]{3,2,1,0:T(8,128)(2,1)S(1)}, bf16[2,2,16,1024]{3,2,1,0:T(8,128)(2,1)S(1)}, u32[]{:S(2)}, u32[]{:S(2)}) collective-permute-start(bf16[2,2,16,1024]{3,2,1,0:T(8,128)(2,1)S(1)} %pad_maximum_fusion.2), channel_id=1, source_target_pairs={{0,16},{8,24},{16,32},{24,40},{32,48},{40,56},{48,0},{56,8},{1,49}... | collective-permute-start | bytes 393224 | tf_op jit(solution)/shard_map/ppermute | solution.py:282
  66.2 10.9 %collective-permute-start.19 = (bf16[2,2,16,1024]{3,2,1,0:T(8,128)(2,1)S(1)}, bf16[2,2,16,1024]{3,2,1,0:T(8,128)(2,1)S(1)}, u32[]{:S(2)}, u32[]{:S(2)}) collective-permute-start(bf16[2,2,16,1024]{3,2,1,0:T(8,128)(2,1)S(1)} %pad_maximum_fusion.3), channel_id=1, source_target_pairs={{0,24},{8,32},{16,40},{24,48},{32,56},{40,0},{48,8},{56,16},{1,41}... | collective-permute-start | bytes 393224 | tf_op jit(solution)/shard_map/ppermute | solution.py:282
  71.3 5.8 %collective-permute-start.16 = (bf16[4,112,128]{2,1,0:T(8,128)(2,1)S(1)}, bf16[4,112,128]{2,1,0:T(8,128)(2,1)S(1)}, u32[]{:S(2)}, u32[]{:S(2)}) collective-permute-start(bf16[4,112,128]{2,1,0:T(8,128)(2,1)S(1)} %reduce_sum.12.refs_0_), channel_id=1, source_target_pairs={{128,0},{192,64},{0,128},{64,192},{129,1},{193,65},{1,129},{65,193... | collective-permute-start | bytes 344072 | tf_op jit(solution)/shard_map/ppermute | solution.py:276
  74.4 5.2 %collective-permute-start.15 = (bf16[4,112,128]{2,1,0:T(8,128)(2,1)S(1)}, bf16[4,112,128]{2,1,0:T(8,128)(2,1)S(1)}, u32[]{:S(2)}, u32[]{:S(2)}) collective-permute-start(bf16[4,112,128]{2,1,0:T(8,128)(2,1)S(1)} %reduce_sum.12.refs_0_), channel_id=1, source_target_pairs={{192,0},{0,64},{64,128},{128,192},{193,1},{1,65},{65,129},{129,193... | collective-permute-start | bytes 344072 | tf_op jit(solution)/shard_map/ppermute | solution.py:276
  74.7 5.2 %collective-permute-start.14 = (bf16[4,112,128]{2,1,0:T(8,128)(2,1)S(1)}, bf16[4,112,128]{2,1,0:T(8,128)(2,1)S(1)}, u32[]{:S(2)}, u32[]{:S(2)}) collective-permute-start(bf16[4,112,128]{2,1,0:T(8,128)(2,1)S(1)} %reduce_sum.12.refs_0_), channel_id=1, source_target_pairs={{64,0},{128,64},{192,128},{0,192},{65,1},{129,65},{193,129},{1,193... | collective-permute-start | bytes 344072 | tf_op jit(solution)/shard_map/ppermute | solution.py:276
  79.9 3.6 %collective-permute-start.20 = (bf16[4,4,112,128]{3,2,1,0:T(8,128)(2,1)S(1)}, bf16[4,4,112,128]{3,2,1,0:T(8,128)(2,1)S(1)}, u32[]{:S(2)}, u32[]{:S(2)}) collective-permute-start(bf16[4,4,112,128]{3,2,1,0:T(8,128)(2,1)S(1)} %pad_maximum_fusion), channel_id=1, source_target_pairs={{0,1},{1,0},{2,3},{3,2},{4,5},{5,4},{6,7},{7,6},{8,9},{9,8},{10,11... | collective-permute-start | bytes 1376264 | tf_op jit(solution)/shard_map/ppermute | solution.py:271
  82.2 1.3 %collective-permute-start.21 = (bf16[2,16,1024]{2,1,0:T(8,128)(2,1)S(1)}, bf16[2,16,1024]{2,1,0:T(8,128)(2,1)S(1)}, u32[]{:S(2)}, u32[]{:S(2)}) collective-permute-start(bf16[2,16,1024]{2,1,0:T(8,128)(2,1)S(1)} %get-tuple-element.60), channel_id=1, source_target_pairs={{0,1},{1,0},{2,3},{3,2},{4,5},{5,4},{6,7},{7,6},{8,9},{9,8},{10,11... | collective-permute-start | bytes 196616 | tf_op jit(solution)/shard_map/ppermute | solution.py:271

commit v11 on v10

--- a/solution.py
+++ b/solution.py
@@ -90,15 +90,31 @@
         run(two_ref)
 
 
-def first_kernel(at_ref, mine_ref, *refs):
+def first_kernel(at_ref, pair_ref, other_ref, *refs):
+    near_refs, far_ref, got_ref, refs = refs[: NZ // 2 - 1], refs[NZ // 2 - 1], refs[NZ // 2], refs[NZ // 2 + 1 :]
     kernels, own_ref, out_refs = refs[:NX], refs[NX], refs[NX + 1 : 2 * NX]
-    all_ref, lhs, rhs, stack = refs[2 * NX :]
-    width = mine_ref.shape[2]
+    all_ref, mine_ref, lhs, rhs, stack = refs[2 * NX :]
+    width = pair_ref.shape[1]
     group = NZ * width
     third = 9 * width
     ok = masks(width)
-    for d in range(2):
-        rhs[d * group : (d + 1) * group, :] = mine_ref[:, d].reshape(group, PLANE)
+
+    def put(step, plane, values):
+        z = lax.rem(at_ref[3] + (step + NZ), NZ)
+        rhs[pl.ds(pl.multiple_of(plane * group + z * width, 16), width), :] = values
+        mine_ref[z, plane] = values
+
+    def place(core, ahead):
+        put(0, core, pair_ref[core])
+        put(0, 1 - core, other_ref[core])
+        for j in range(1, NZ // 2):
+            put(ahead * j, core, near_refs[j - 1][0, core])
+            put(ahead * j, 1 - core, near_refs[j - 1][1, core])
+            put(-ahead * j, 1 - core, got_ref[2 * j - 2])
+            put(-ahead * j, core, got_ref[2 * j - 1])
+        put(NZ // 2, core, far_ref[core])
+        put(NZ // 2, 1 - core, got_ref[NZ - 2])
+
     for k in range(NX):
         all_ref[k] = kernels[k][...]
 
@@ -118,10 +134,12 @@
 
     @pl.when(at_ref[0] == 0)
     def _():
+        place(0, -1)
         run(1)
 
     @pl.when(at_ref[0] == 1)
     def _():
+        place(1, 1)
         run(-1)
 
 
@@ -290,22 +308,29 @@
     taps = 27 * width
     group = NZ * width
     plane = (2, width, PLANE)
-    everyone = (2 * NZ, width, PLANE)
     piece = (7 * width, group)
     work = 4 * 18 * width * channels * PLANE
 
+    far = NZ // 2
+    first = lax.axis_index("spatial") == 0
     pair = jnp.stack([features.reshape(width, PLANE), cotangent.reshape(width, PLANE)])
-    pair = jnp.broadcast_to(pair, (NZ,) + plane).reshape(everyone)
-    mine = lax.all_to_all(pair, ("z", "spatial"), 0, 0, tiled=True).reshape((NZ,) + plane)
-
+    came = {far: apart(pair, far)}
+    other = swap(pair)
+    both = jnp.stack([pair, other])
+    came.update({j: apart(both, j) for j in range(far - 1, 0, -1)})
     *groups, order = call(regroup_kernel, [((taps, group), BF16)] * NX + [((channels, channels), BF16)], [], "regroup", 2 * taps * channels * channels, at, one, two)
     kernels = [groups[0]] + [around(groups[NX - k], "x", k) for k in range(1, NX)]
-
-    own, *sends, held = call(
+    came, kernels = lax.optimization_barrier((came, kernels))
+
+    give = [jnp.where(first, came[j][:, 1], came[j][:, 0]) for j in range(1, far)]
+    give.append(jnp.where(first, came[far][1], came[far][0])[None])
+    got = swap(jnp.concatenate(give))
+
+    own, *sends, held, mine = call(
         first_kernel,
-        [(plane, F32)] + [(plane, BF16)] * (NX - 1) + [((NX, taps, group), BF16)],
+        [(plane, F32)] + [(plane, BF16)] * (NX - 1) + [((NX, taps, group), BF16), ((NZ,) + plane, BF16)],
         [((NX * 9 * width, 2 * group), BF16), ((2 * group, PLANE), BF16), ((NX * 9 * width, PLANE), F32)],
-        "conv_in", work, at, mine, *kernels,
+        "conv_in", work, at, pair, other, *[came[j] for j in range(1, far)], came[far], got, *kernels,
     )
     sends = [around(sends[k - 1], "x", NX - k) for k in (2, 1, 3)]
     own = own + sum(part.astype(F32) for part in sends)
@@ -313,7 +338,6 @@
 
     (send,) = call(act_kernel, [(plane, BF16)], [], "act", 0, at, own, swap(own))
     acts = {k: around(send, "x", k) for k in (1, 3, 2)}
-    far = NZ // 2
     zero, hold, half, give, grads = call(
         second_kernel,
         [(plane, BF16), ((far - 1,) + plane, BF16), (plane[1:], BF16), ((NZ - 1,) + plane[1:], BF16), ((4 * NX,) + piece, BF16)],

time: 86.2 us -> 86.4 us (level)
  waiting for transfers between devices: 24.1 us -> 20.2 us
  starting transfers between devices: 48 us -> 50.7 us
  local copies, waits for them, and re-layouts: 0.89 us -> 2.06 us
    ppermute x4 -> x8, starting transfers between devices: 6.26 us -> 19.8 us  [apart(): return lax.ppermute(values, ('z', 'spatial'), pairs)]
    all_to_all x1 -> x0, waiting for transfers between devices: 12.2 us -> none  [body(): lax.all_to_all(pair, ('z', 'spatial'), 0, 0, tiled=True)]
    all_to_all x1 -> x0, starting transfers between devices: 10.1 us -> none  [body(): lax.all_to_all(pair, ('z', 'spatial'), 0, 0, tiled=True)]
    ppermute x12, waiting for transfers between devices: 6.25 us -> 15.6 us  [around(): lax.ppermute(values, axis, [((i + step) % size, i) for i in range(size)])]
    ppermute x6 -> x8, starting transfers between devices: 6.33 us -> 9.48 us  [swap(): return lax.ppermute(values, 'spatial', [(0, 1), (1, 0)])]
    ppermute x12, starting transfers between devices: 18.9 us -> 15.9 us  [around(): lax.ppermute(values, axis, [((i + step) % size, i) for i in range(size)])]
    unnamed x4, local copies, waits for them, and re-layouts: 0.01 us -> 2.03 us
    ppermute x4 -> x8, waiting for transfers between devices: 1.55 us -> 0.17 us  [apart(): return lax.ppermute(values, ('z', 'spatial'), pairs)]
  transfers between devices with their start and end apart: 24 -> 29, of which waited for: 12 -> 12; matrix products, arithmetic and copies ran while one was open for 0% -> 0% of each run, Pallas kernels for 6% -> 3%
where the time goes in v11:
time: 86.4 us; the launch traced here: 86 us
  starting transfers between devices  50.7 us (59%)
  waiting for transfers between devices  20.2 us (23%)
  Pallas kernels  11 us (13%)
  local copies, waits for them, and re-layouts  2.06 us (2%)
  other arithmetic  1.16 us (1%)
  between operations  0.97 us (1%)
    ppermute x8, starting transfers between devices, apart(): return lax.ppermute(values, ('z', 'spatial'), pairs)  19.8 us
    ppermute x12, starting transfers between devices, around(): lax.ppermute(values, axis, [((i + step) % size, i) for i in range(size)])  15.9 us
    ppermute x12, waiting for transfers between devices, around(): lax.ppermute(values, axis, [((i + step) % size, i) for i in range(size)])  15.6 us
    pallas_call x6, Pallas kernels, call(): pl.pallas_call(kernel, out_shape=tuple((jax.ShapeDtypeStruct(s, t) for s,...  11 us
    ppermute x8, starting transfers between devices, swap(): return lax.ppermute(values, 'spatial', [(0, 1), (1, 0)])  9.48 us
    all_to_all x1, starting transfers between devices, body(): grads = lax.all_to_all(grads, ('samples', 'x'), 0, 0, tiled=True)  5.52 us
    ppermute x8, waiting for transfers between devices, swap(): return lax.ppermute(values, 'spatial', [(0, 1), (1, 0)])  4.45 us
    unnamed x4, local copies, waits for them, and re-layouts  2.03 us
  transfers between devices with their start and end apart: 29, of which 12 were waited for; matrix products, arithmetic and copies ran while one was open for 0% of the time, Pallas kernels for 3%

profile of v11, /device:TPU:1, one launch (start us, length us, event | category | flops | bytes accessed | tf_op | source)
XLA Modules:
  0.0 86.0 jit_solution(15670763180366334177)
XLA Ops:
  0.6 0.8 fusion
  1.4 7.8 %collective-permute-start.4 = (bf16[2,16,1024]{2,1,0:T(8,128)(2,1)S(1)}, bf16[2,16,1024]{2,1,0:T(8,128)(2,1)S(1)}, u32[]{:S(2)}, u32[]{:S(2)}) collective-permute-start(bf16[2,16,1024]{2,1,0:T(8,128)(2,1)S(1)} %get-tuple-element.91.pair_ref), channel_id=1, source_target_pairs={{0,32},{8,40},{16,48},{24,56},{32,0},{40,8},{48,16},{56,24},{1,33}... | collective-permute-start | bytes 196616 | tf_op jit(solution)/shard_map/ppermute | solution.py:300
  9.2 1.0 %collective-permute-start = (bf16[2,16,1024]{2,1,0:T(8,128)(2,1)S(1)}, bf16[2,16,1024]{2,1,0:T(8,128)(2,1)S(1)}, u32[]{:S(2)}, u32[]{:S(2)}) collective-permute-start(bf16[2,16,1024]{2,1,0:T(8,128)(2,1)S(1)} %get-tuple-element.91.pair_ref), channel_id=1, source_target_pairs={{0,1},{1,0},{2,3},{3,2},{4,5},{5,4},{6,7},{7,6},{8,9},{9,8},{10,11... | collective-permute-start | bytes 196616 | tf_op jit(solution)/shard_map/ppermute | solution.py:289
  10.2 0.1 pad_add_fusion.at_ref
  10.3 1.0 %copy-done = bf16[27,16,512]{2,1,0:T(8,128)(2,1)S(1)} copy-done((bf16[27,16,512]{2,1,0:T(8,128)(2,1)S(1)}, bf16[27,16,512]{2,1,0:T(8,128)(2,1)}, u32[]{:S(2)}) %copy-start) | copy-done | bytes 442392
  11.3 1.0 %copy-done.1 = bf16[27,16,512]{2,1,0:T(8,128)(2,1)S(1)} copy-done((bf16[27,16,512]{2,1,0:T(8,128)(2,1)S(1)}, bf16[27,16,512]{2,1,0:T(8,128)(2,1)}, u32[]{:S(2)}) %copy-start.1) | copy-done | bytes 442392
  12.3 1.3 %regroup.1 = (bf16[432,128]{1,0:T(8,128)(2,1)S(1)}, bf16[432,128]{1,0:T(8,128)(2,1)S(1)}, bf16[432,128]{1,0:T(8,128)(2,1)S(1)}, bf16[432,128]{1,0:T(8,128)(2,1)S(1)}, bf16[512,512]{1,0:T(8,128)(2,1)S(1)}) custom-call(s32[4]{0:T(128)S(1)} %pad_add_fusion.at_ref, bf16[432,512]{1,0:T(8,128)(2,1)S(1)} %bitcast.37, bf16[432,512]{1,0:T(8,128)(2,1)S(1)} %bitcast.38), custom_call_target="tpu_custom_call" | custom-call | flops 226492416 | tf_op jit(solution)/shard_map/regroup/pallas_call | solution.py:276
  13.6 2.6 %collective-permute-start.5 = (bf16[432,128]{1,0:T(8,128)(2,1)S(1)}, bf16[432,128]{1,0:T(8,128)(2,1)S(1)}, u32[]{:S(2)}, u32[]{:S(2)}) collective-permute-start(bf16[432,128]{1,0:T(8,128)(2,1)S(1)} %get-tuple-element.45), channel_id=1, source_target_pairs={{2,0},{4,2},{6,4},{0,6},{3,1},{5,3},{7,5},{1,7},{10,8},{12,10},{14... | collective-permute-start | bytes 331784 | tf_op jit(solution)/shard_map/ppermute | solution.py:294
  16.2 0.0 collective-permute-done.other_ref
  16.2 0.1 collective-permute-start.3
  16.3 4.0 %collective-permute-start.2 = (bf16[2,2,16,1024]{3,2,1,0:T(8,128)(2,1)S(1)}, bf16[2,2,16,1024]{3,2,1,0:T(8,128)(2,1)S(1)}, u32[]{:S(2)}, u32[]{:S(2)}) collective-permute-start(bf16[2,2,16,1024]{3,2,1,0:T(8,128)(2,1)S(1)} %pad_maximum_fusion.2), channel_id=1, source_target_pairs={{0,16},{8,24},{16,32},{24,40},{32,48},{40,56},{48,0},{56,8},{1,49}... | collective-permute-start | bytes 393224 | tf_op jit(solution)/shard_map/ppermute | solution.py:300
  20.3 0.7 collective-permute-start.1
  21.0 0.0 collective-permute-done.4.refs_3_
  21.0 0.5 collective-permute-start.6
  21.6 0.0 collective-permute-done.5.refs_6_
  21.6 0.6 collective-permute-start.7
  22.2 5.0 %collective-permute-done.6.refs_7_ = bf16[432,128]{1,0:T(8,128)(2,1)S(1)} collective-permute-done((bf16[432,128]{1,0:T(8,128)(2,1)S(1)}, bf16[432,128]{1,0:T(8,128)(2,1)S(1)}, u32[]{:S(2)}, u32[]{:S(2)}) %collective-permute-start.6) | collective-permute-done | bytes 110624 | tf_op jit(solution)/shard_map/ppermute | solution.py:294
  27.2 1.1 %collective-permute-done.7.refs_8_ = bf16[432,128]{1,0:T(8,128)(2,1)S(1)} collective-permute-done((bf16[432,128]{1,0:T(8,128)(2,1)S(1)}, bf16[432,128]{1,0:T(8,128)(2,1)S(1)}, u32[]{:S(2)}, u32[]{:S(2)}) %collective-permute-start.7) | collective-permute-done | bytes 110624 | tf_op jit(solution)/shard_map/ppermute | solution.py:294
  28.3 0.0 collective-permute-done.3.refs_2_
  28.3 0.0 collective-permute-done.2.refs_1_
  28.3 0.0 collective-permute-done.1.refs_0_
  28.4 2.5 %collective-permute-start.8 = (bf16[7,16,1024]{2,1,0:T(8,128)(2,1)S(1)}, bf16[7,16,1024]{2,1,0:T(8,128)(2,1)S(1)}, u32[]{:S(2)}, u32[]{:S(2)}) collective-permute-start(bf16[7,16,1024]{2,1,0:T(8,128)(2,1)S(1)} %pad_maximum_fusion.1), channel_id=1, source_target_pairs={{0,1},{1,0},{2,3},{3,2},{4,5},{5,4},{6,7},{7,6},{8,9},{9,8},{10,11... | collective-permute-start | bytes 688136 | tf_op jit(solution)/shard_map/ppermute | solution.py:289
  30.9 1.1 %collective-permute-done.8.refs_4_ = bf16[7,16,1024]{2,1,0:T(8,128)(2,1)S(1)} collective-permute-done((bf16[7,16,1024]{2,1,0:T(8,128)(2,1)S(1)}, bf16[7,16,1024]{2,1,0:T(8,128)(2,1)S(1)}, u32[]{:S(2)}, u32[]{:S(2)}) %collective-permute-start.8) | collective-permute-done | bytes 229408 | tf_op jit(solution)/shard_map/ppermute | solution.py:289
  32.0 2.6 %conv_in.1 = (f32[2,16,1024]{2,1,0:T(8,128)S(1)}, bf16[2,16,1024]{2,1,0:T(8,128)(2,1)S(1)}, bf16[2,16,1024]{2,1,0:T(8,128)(2,1)S(1)}, bf16[2,16,1024]{2,1,0:T(8,...) custom-call(s32[4]{0:T(128)S(1)} %pad_add_fusion.at_ref, ...), custom_call_target="tpu_custom_call" | custom-call | flops 603979776 | tf_op jit(solution)/shard_map/conv_in/pallas_call | solution.py:276
  34.6 0.4 collective-permute-start.17
  35.0 0.5 collective-permute-start.9
  35.5 0.6 collective-permute-start.10
  36.1 2.1 %collective-permute-start.11 = (bf16[2,16,1024]{2,1,0:T(8,128)(2,1)S(1)}, bf16[2,16,1024]{2,1,0:T(8,128)(2,1)S(1)}, u32[]{:S(2)}, u32[]{:S(2)}) collective-permute-start(bf16[2,16,1024]{2,1,0:T(8,128)(2,1)S(1)} %get-tuple-element.59), channel_id=1, source_target_pairs={{2,0},{4,2},{6,4},{0,6},{3,1},{5,3},{7,5},{1,7},{10,8},{12,10},{14... | collective-permute-start | bytes 196616 | tf_op jit(solution)/shard_map/ppermute | solution.py:294
  38.2 1.0 %collective-permute-start.16 = (bf16[4,432,128]{2,1,0:T(8,128)(2,1)S(1)}, bf16[4,432,128]{2,1,0:T(8,128)(2,1)S(1)}, u32[]{:S(2)}, u32[]{:S(2)}) collective-permute-start(bf16[4,432,128]{2,1,0:T(8,128)(2,1)S(1)} %get-tuple-element.60), channel_id=1, source_target_pairs={{0,1},{1,0},{2,3},{3,2},{4,5},{5,4},{6,7},{7,6},{8,9},{9,8},{10,11... | collective-permute-start | bytes 1327112 | tf_op jit(solution)/shard_map/ppermute | solution.py:289
  39.2 0.8 collective-permute-done.9
  40.0 1.8 %collective-permute-done.10 = bf16[2,16,1024]{2,1,0:T(8,128)(2,1)S(1)} collective-permute-done((bf16[2,16,1024]{2,1,0:T(8,128)(2,1)S(1)}, bf16[2,16,1024]{2,1,0:T(8,128)(2,1)S(1)}, u32[]{:S(2)}, u32[]{:S(2)}) %collective-permute-start.10) | collective-permute-done | bytes 65568 | tf_op jit(solution)/shard_map/ppermute | solution.py:294
  41.9 0.6 collective-permute-start.12
  42.5 1.0 %collective-permute-done.12.other_ref = f32[2,16,1024]{2,1,0:T(8,128)S(1)} collective-permute-done((f32[2,16,1024]{2,1,0:T(8,128)S(1)}, f32[2,16,1024]{2,1,0:T(8,128)S(1)}, u32[]{:S(2)}, u32[]{:S(2)}) %collective-permute-start.12) | collective-permute-done | bytes 131104 | tf_op jit(solution)/shard_map/ppermute | solution.py:289
  43.5 0.6 act.1.refs_0_
  44.1 0.7 collective-permute-start.15
  44.8 2.0 %collective-permute-start.14 = (bf16[2,16,1024]{2,1,0:T(8,128)(2,1)S(1)}, bf16[2,16,1024]{2,1,0:T(8,128)(2,1)S(1)}, u32[]{:S(2)}, u32[]{:S(2)}) collective-permute-start(bf16[2,16,1024]{2,1,0:T(8,128)(2,1)S(1)} %act.1.refs_0_), channel_id=1, source_target_pairs={{6,0},{0,2},{2,4},{4,6},{7,1},{1,3},{3,5},{5,7},{14,8},{8,10},{10,... | collective-permute-start | bytes 196616 | tf_op jit(solution)/shard_map/ppermute | solution.py:294
  46.8 0.7 collective-permute-start.13
  47.5 1.4 %collective-permute-done.15.refs_3_ = bf16[2,16,1024]{2,1,0:T(8,128)(2,1)S(1)} collective-permute-done((bf16[2,16,1024]{2,1,0:T(8,128)(2,1)S(1)}, bf16[2,16,1024]{2,1,0:T(8,128)(2,1)S(1)}, u32[]{:S(2)}, u32[]{:S(2)}) %collective-permute-start.15) | collective-permute-done | bytes 65568 | tf_op jit(solution)/shard_map/ppermute | solution.py:294
  48.9 2.0 %collective-permute-done.14.refs_2_ = bf16[2,16,1024]{2,1,0:T(8,128)(2,1)S(1)} collective-permute-done((bf16[2,16,1024]{2,1,0:T(8,128)(2,1)S(1)}, bf16[2,16,1024]{2,1,0:T(8,128)(2,1)S(1)}, u32[]{:S(2)}, u32[]{:S(2)}) %collective-permute-start.14) | collective-permute-done | bytes 65568 | tf_op jit(solution)/shard_map/ppermute | solution.py:294
  50.8 0.0 collective-permute-done.13.refs_1_
  50.8 0.0 collective-permute-done.16.refs_4_
  50.8 0.0 collective-permute-done.17.refs_5_
  50.9 3.7 %conv_out.1 = (bf16[2,16,1024]{2,1,0:T(8,128)(2,1)S(1)}, bf16[3,2,16,1024]{3,2,1,0:T(8,128)(2,1)S(1)}, bf16[16,1024]{1,0:T(8,128)(2,1)S(1)}, bf16[7,16,1024]{2,1,0:T(8,128)(2,1)S(1)}, bf16[16,112,128]{2,1,0:T(8,128)(2,1)}) custom-call(s32[4]{0:T(128)S(1)} %pad_add_fusion.at_ref, bf16[2,16,1024]{2,1,0:T(8,128)(2,1)S(1)} %act.1.refs_0_, ...), custom_call_target="tpu_custom_call" | custom-call | flops 1207959552 | tf_op jit(solution)/shard_map/conv_out/pallas_call | solution.py:276
  54.5 5.5 %all-to-all-start = ((bf16[16,112,128]{2,1,0:T(8,128)(2,1)}), bf16[16,112,128]{2,1,0:T(8,128)(2,1)S(1)}, u32[]{:S(2)}, u32[]{:S(2)}) async-start(bf16[16,112,128]{2,1,0:T(8,128)(2,1)} %get-tuple-element.62), calls=%async_computation | async-start | bytes 917504 | tf_op jit(solution)/shard_map/all_to_all | solution.py:347
  60.1 1.8 %collective-permute-start.18 = (bf16[7,16,1024]{2,1,0:T(8,128)(2,1)S(1)}, bf16[7,16,1024]{2,1,0:T(8,128)(2,1)S(1)}, u32[]{:S(2)}, u32[]{:S(2)}) collective-permute-start(bf16[7,16,1024]{2,1,0:T(8,128)(2,1)S(1)} %get-tuple-element.64), channel_id=1, source_target_pairs={{0,1},{1,0},{2,3},{3,2},{4,5},{5,4},{6,7},{7,6},{8,9},{9,8},{10,11... | collective-permute-start | bytes 688136 | tf_op jit(solution)/shard_map/ppermute | solution.py:289
  61.9 1.1 %collective-permute-done.18 = bf16[7,16,1024]{2,1,0:T(8,128)(2,1)S(1)} collective-permute-done((bf16[7,16,1024]{2,1,0:T(8,128)(2,1)S(1)}, bf16[7,16,1024]{2,1,0:T(8,128)(2,1)S(1)}, u32[]{:S(2)}, u32[]{:S(2)}) %collective-permute-start.18) | collective-permute-done | bytes 229408 | tf_op jit(solution)/shard_map/ppermute | solution.py:289
  63.0 1.5 %collective-permute-start.19 = (bf16[2,16,1024]{2,1,0:T(8,128)(2,1)S(1)}, bf16[2,16,1024]{2,1,0:T(8,128)(2,1)S(1)}, u32[]{:S(2)}, u32[]{:S(2)}) collective-permute-start(bf16[2,16,1024]{2,1,0:T(8,128)(2,1)S(1)} %pad_maximum_fusion.7), channel_id=1, source_target_pairs={{0,32},{8,40},{16,48},{24,56},{32,0},{40,8},{48,16},{56,24},{1,33}... | collective-permute-start | bytes 196616 | tf_op jit(solution)/shard_map/ppermute | solution.py:300
  64.5 1.7 %collective-permute-start.23 = (bf16[2,2,16,1024]{3,2,1,0:T(8,128)(2,1)S(1)}, bf16[2,2,16,1024]{3,2,1,0:T(8,128)(2,1)S(1)}, u32[]{:S(2)}, u32[]{:S(2)}) collective-permute-start(bf16[2,2,16,1024]{3,2,1,0:T(8,128)(2,1)S(1)} %pad_maximum_fusion.3), channel_id=1, source_target_pairs={{0,8},{8,16},{16,24},{24,32},{32,40},{40,48},{48,56},{56,0},{1,57}... | collective-permute-start | bytes 393224 | tf_op jit(solution)/shard_map/ppermute | solution.py:300
  66.2 1.5 %collective-permute-start.24 = (bf16[2,2,16,1024]{3,2,1,0:T(8,128)(2,1)S(1)}, bf16[2,2,16,1024]{3,2,1,0:T(8,128)(2,1)S(1)}, u32[]{:S(2)}, u32[]{:S(2)}) collective-permute-start(bf16[2,2,16,1024]{3,2,1,0:T(8,128)(2,1)S(1)} %pad_maximum_fusion.4), channel_id=1, source_target_pairs={{0,16},{8,24},{16,32},{24,40},{32,48},{40,56},{48,0},{56,8},{1,49}... | collective-permute-start | bytes 393224 | tf_op jit(solution)/shard_map/ppermute | solution.py:300
  67.7 2.5 %collective-permute-start.25 = (bf16[2,2,16,1024]{3,2,1,0:T(8,128)(2,1)S(1)}, bf16[2,2,16,1024]{3,2,1,0:T(8,128)(2,1)S(1)}, u32[]{:S(2)}, u32[]{:S(2)}) collective-permute-start(bf16[2,2,16,1024]{3,2,1,0:T(8,128)(2,1)S(1)} %pad_maximum_fusion.5), channel_id=1, source_target_pairs={{0,24},{8,32},{16,40},{24,48},{32,56},{40,0},{48,8},{56,16},{1,41}... | collective-permute-start | bytes 393224 | tf_op jit(solution)/shard_map/ppermute | solution.py:300
  70.2 0.1 reduce_sum.12.refs_0_
  70.3 0.1 collective-permute-done.19.refs_3_
  70.4 3.0 %collective-permute-start.22 = (bf16[4,112,128]{2,1,0:T(8,128)(2,1)S(1)}, bf16[4,112,128]{2,1,0:T(8,128)(2,1)S(1)}, u32[]{:S(2)}, u32[]{:S(2)}) collective-permute-start(bf16[4,112,128]{2,1,0:T(8,128)(2,1)S(1)} %reduce_sum.12.refs_0_), channel_id=1, source_target_pairs={{128,0},{192,64},{0,128},{64,192},{129,1},{193,65},{1,129},{65,193... | collective-permute-start | bytes 344072 | tf_op jit(solution)/shard_map/ppermute | solution.py:294
  73.4 0.3 collective-permute-start.21
  73.7 0.0 collective-permute-done.23.refs_0_
  73.7 2.4 %collective-permute-start.20 = (bf16[4,112,128]{2,1,0:T(8,128)(2,1)S(1)}, bf16[4,112,128]{2,1,0:T(8,128)(2,1)S(1)}, u32[]{:S(2)}, u32[]{:S(2)}) collective-permute-start(bf16[4,112,128]{2,1,0:T(8,128)(2,1)S(1)} %reduce_sum.12.refs_0_), channel_id=1, source_target_pairs={{64,0},{128,64},{192,128},{0,192},{65,1},{129,65},{193,129},{1,193... | collective-permute-start | bytes 344072 | tf_op jit(solution)/shard_map/ppermute | solution.py:294
  76.1 0.0 collective-permute-done.24.refs_1_
  76.1 3.5 %collective-permute-done.21.refs_2_ = bf16[4,112,128]{2,1,0:T(8,128)(2,1)S(1)} collective-permute-done((bf16[4,112,128]{2,1,0:T(8,128)(2,1)S(1)}, bf16[4,112,128]{2,1,0:T(8,128)(2,1)S(1)}, u32[]{:S(2)}, u32[]{:S(2)}) %collective-permute-start.21) | collective-permute-done | bytes 114720 | tf_op jit(solution)/shard_map/ppermute | solution.py:294
  79.6 0.1 pad_maximum_fusion
  79.6 2.1 %collective-permute-start.26 = (bf16[4,4,112,128]{3,2,1,0:T(8,128)(2,1)S(1)}, bf16[4,4,112,128]{3,2,1,0:T(8,128)(2,1)S(1)}, u32[]{:S(2)}, u32[]{:S(2)}) collective-permute-start(bf16[4,4,112,128]{3,2,1,0:T(8,128)(2,1)S(1)} %pad_maximum_fusion), channel_id=1, source_target_pairs={{0,1},{1,0},{2,3},{3,2},{4,5},{5,4},{6,7},{7,6},{8,9},{9,8},{10,11... | collective-permute-start | bytes 1376264 | tf_op jit(solution)/shard_map/ppermute | solution.py:289
  81.7 0.6 sum.1
  82.4 0.1 collective-permute-start.27
  82.5 1.2 %collective-permute-done.27.refs_6_ = bf16[2,16,1024]{2,1,0:T(8,128)(2,1)S(1)} collective-permute-done((bf16[2,16,1024]{2,1,0:T(8,128)(2,1)S(1)}, bf16[2,16,1024]{2,1,0:T(8,128)(2,1)S(1)}, u32[]{:S(2)}, u32[]{:S(2)}) %collective-permute-start.27) | collective-permute-done | bytes 65568 | tf_op jit(solution)/shard_map/ppermute | solution.py:289
  83.7 2.2 %finish.1 = (bf16[16,1024]{1,0:T(8,128)(2,1)}, bf16[16,1024]{1,0:T(8,128)(2,1)}, f32[432,512]{1,0:T(8,128)}, f32[432,512]{1,0:T(8,128)}) custom-call(s32[4]{0:T(128)S(1)} %pad_add_fusion.at_ref, bf16[4,112,128]{2,1,0:T(8,128)(2,1)S(1)} %reduce_sum.12.refs_0_, bf16[4,112,128]{2,1,0:T(8,128)(2,1)S(1)} %collective-permute-done.20.refs_1_, ...), custom_call_target="tpu_custom_call" | custom-call | tf_op jit(solution)/shard_map/finish/pallas_call | solution.py:276
  (21 shorter events, 0.2 us)
Async XLA Ops:
  1.4 19.6 %collective-permute-start.4 = (bf16[2,16,1024]{2,1,0:T(8,128)(2,1)S(1)}, bf16[2,16,1024]{2,1,0:T(8,128)(2,1)S(1)}, u32[]{:S(2)}, u32[]{:S(2)}) collective-permute-start(bf16[2,16,1024]{2,1,0:T(8,128)(2,1)S(1)} %get-tuple-element.91.pair_ref), channel_id=1, source_target_pairs={{0,32},{8,40},{16,48},{24,56},{32,0},{40,8},{48,16},{56,24},{1,33}... | collective-permute-start | bytes 196616 | tf_op jit(solution)/shard_map/ppermute | solution.py:300
  9.2 6.9 %collective-permute-start = (bf16[2,16,1024]{2,1,0:T(8,128)(2,1)S(1)}, bf16[2,16,1024]{2,1,0:T(8,128)(2,1)S(1)}, u32[]{:S(2)}, u32[]{:S(2)}) collective-permute-start(bf16[2,16,1024]{2,1,0:T(8,128)(2,1)S(1)} %get-tuple-element.91.pair_ref), channel_id=1, source_target_pairs={{0,1},{1,0},{2,3},{3,2},{4,5},{5,4},{6,7},{7,6},{8,9},{9,8},{10,11... | collective-permute-start | bytes 196616 | tf_op jit(solution)/shard_map/ppermute | solution.py:289
  10.3 1.0 %copy-start = (bf16[27,16,512]{2,1,0:T(8,128)(2,1)S(1)}, bf16[27,16,512]{2,1,0:T(8,128)(2,1)}, u32[]{:S(2)}) copy-start(bf16[27,16,512]{2,1,0:T(8,128)(2,1)} %param.5) | copy-start | bytes 1327108
  11.3 1.0 %copy-start.1 = (bf16[27,16,512]{2,1,0:T(8,128)(2,1)S(1)}, bf16[27,16,512]{2,1,0:T(8,128)(2,1)}, u32[]{:S(2)}) copy-start(bf16[27,16,512]{2,1,0:T(8,128)(2,1)} %param.6) | copy-start | bytes 1327108
  13.6 7.9 %collective-permute-start.5 = (bf16[432,128]{1,0:T(8,128)(2,1)S(1)}, bf16[432,128]{1,0:T(8,128)(2,1)S(1)}, u32[]{:S(2)}, u32[]{:S(2)}) collective-permute-start(bf16[432,128]{1,0:T(8,128)(2,1)S(1)} %get-tuple-element.45), channel_id=1, source_target_pairs={{2,0},{4,2},{6,4},{0,6},{3,1},{5,3},{7,5},{1,7},{10,8},{12,10},{14... | collective-permute-start | bytes 331784 | tf_op jit(solution)/shard_map/ppermute | solution.py:294
  16.2 12.1 %collective-permute-start.3 = (bf16[2,2,16,1024]{3,2,1,0:T(8,128)(2,1)S(1)}, bf16[2,2,16,1024]{3,2,1,0:T(8,128)(2,1)S(1)}, u32[]{:S(2)}, u32[]{:S(2)}) collective-permute-start(bf16[2,2,16,1024]{3,2,1,0:T(8,128)(2,1)S(1)} %pad_maximum_fusion.2), channel_id=1, source_target_pairs={{0,24},{8,32},{16,40},{24,48},{32,56},{40,0},{48,8},{56,16},{1,41}... | collective-permute-start | bytes 393224 | tf_op jit(solution)/shard_map/ppermute | solution.py:300
  16.3 12.0 %collective-permute-start.2 = (bf16[2,2,16,1024]{3,2,1,0:T(8,128)(2,1)S(1)}, bf16[2,2,16,1024]{3,2,1,0:T(8,128)(2,1)S(1)}, u32[]{:S(2)}, u32[]{:S(2)}) collective-permute-start(bf16[2,2,16,1024]{3,2,1,0:T(8,128)(2,1)S(1)} %pad_maximum_fusion.2), channel_id=1, source_target_pairs={{0,16},{8,24},{16,32},{24,40},{32,48},{40,56},{48,0},{56,8},{1,49}... | collective-permute-start | bytes 393224 | tf_op jit(solution)/shard_map/ppermute | solution.py:300
  20.3 8.0 %collective-permute-start.1 = (bf16[2,2,16,1024]{3,2,1,0:T(8,128)(2,1)S(1)}, bf16[2,2,16,1024]{3,2,1,0:T(8,128)(2,1)S(1)}, u32[]{:S(2)}, u32[]{:S(2)}) collective-permute-start(bf16[2,2,16,1024]{3,2,1,0:T(8,128)(2,1)S(1)} %pad_maximum_fusion.2), channel_id=1, source_target_pairs={{0,8},{8,16},{16,24},{24,32},{32,40},{40,48},{48,56},{56,0},{1,57}... | collective-permute-start | bytes 393224 | tf_op jit(solution)/shard_map/ppermute | solution.py:300
  21.0 6.2 %collective-permute-start.6 = (bf16[432,128]{1,0:T(8,128)(2,1)S(1)}, bf16[432,128]{1,0:T(8,128)(2,1)S(1)}, u32[]{:S(2)}, u32[]{:S(2)}) collective-permute-start(bf16[432,128]{1,0:T(8,128)(2,1)S(1)} %get-tuple-element.46), channel_id=1, source_target_pairs={{4,0},{6,2},{0,4},{2,6},{5,1},{7,3},{1,5},{3,7},{12,8},{14,10},{8,... | collective-permute-start | bytes 331784 | tf_op jit(solution)/shard_map/ppermute | solution.py:294
  21.6 6.7 %collective-permute-start.7 = (bf16[432,128]{1,0:T(8,128)(2,1)S(1)}, bf16[432,128]{1,0:T(8,128)(2,1)S(1)}, u32[]{:S(2)}, u32[]{:S(2)}) collective-permute-start(bf16[432,128]{1,0:T(8,128)(2,1)S(1)} %get-tuple-element.47), channel_id=1, source_target_pairs={{6,0},{0,2},{2,4},{4,6},{7,1},{1,3},{3,5},{5,7},{14,8},{8,10},{10,... | collective-permute-start | bytes 331784 | tf_op jit(solution)/shard_map/ppermute | solution.py:294
  28.4 3.6 %collective-permute-start.8 = (bf16[7,16,1024]{2,1,0:T(8,128)(2,1)S(1)}, bf16[7,16,1024]{2,1,0:T(8,128)(2,1)S(1)}, u32[]{:S(2)}, u32[]{:S(2)}) collective-permute-start(bf16[7,16,1024]{2,1,0:T(8,128)(2,1)S(1)} %pad_maximum_fusion.1), channel_id=1, source_target_pairs={{0,1},{1,0},{2,3},{3,2},{4,5},{5,4},{6,7},{7,6},{8,9},{9,8},{10,11... | collective-permute-start | bytes 688136 | tf_op jit(solution)/shard_map/ppermute | solution.py:289
  34.6 16.3 %collective-permute-start.17 = (bf16[8,2,16,1024]{3,2,1,0:T(8,128)(2,1)S(1)}, bf16[8,2,16,1024]{3,2,1,0:T(8,128)(2,1)S(1)}, u32[]{:S(2)}, u32[]{:S(2)}) collective-permute-start(bf16[8,2,16,1024]{3,2,1,0:T(8,128)(2,1)S(1)} %get-tuple-element.61), channel_id=1, source_target_pairs={{0,1},{1,0},{2,3},{3,2},{4,5},{5,4},{6,7},{7,6},{8,9},{9,8},{10,11... | collective-permute-start | bytes 1572872 | tf_op jit(solution)/shard_map/ppermute | solution.py:289
  35.0 5.0 %collective-permute-start.9 = (bf16[2,16,1024]{2,1,0:T(8,128)(2,1)S(1)}, bf16[2,16,1024]{2,1,0:T(8,128)(2,1)S(1)}, u32[]{:S(2)}, u32[]{:S(2)}) collective-permute-start(bf16[2,16,1024]{2,1,0:T(8,128)(2,1)S(1)} %get-tuple-element.57), channel_id=1, source_target_pairs={{4,0},{6,2},{0,4},{2,6},{5,1},{7,3},{1,5},{3,7},{12,8},{14,10},{8,... | collective-permute-start | bytes 196616 | tf_op jit(solution)/shard_map/ppermute | solution.py:294
  35.5 6.3 %collective-permute-start.10 = (bf16[2,16,1024]{2,1,0:T(8,128)(2,1)S(1)}, bf16[2,16,1024]{2,1,0:T(8,128)(2,1)S(1)}, u32[]{:S(2)}, u32[]{:S(2)}) collective-permute-start(bf16[2,16,1024]{2,1,0:T(8,128)(2,1)S(1)} %get-tuple-element.58), channel_id=1, source_target_pairs={{6,0},{0,2},{2,4},{4,6},{7,1},{1,3},{3,5},{5,7},{14,8},{8,10},{10,... | collective-permute-start | bytes 196616 | tf_op jit(solution)/shard_map/ppermute | solution.py:294
  36.1 5.7 %collective-permute-start.11 = (bf16[2,16,1024]{2,1,0:T(8,128)(2,1)S(1)}, bf16[2,16,1024]{2,1,0:T(8,128)(2,1)S(1)}, u32[]{:S(2)}, u32[]{:S(2)}) collective-permute-start(bf16[2,16,1024]{2,1,0:T(8,128)(2,1)S(1)} %get-tuple-element.59), channel_id=1, source_target_pairs={{2,0},{4,2},{6,4},{0,6},{3,1},{5,3},{7,5},{1,7},{10,8},{12,10},{14... | collective-permute-start | bytes 196616 | tf_op jit(solution)/shard_map/ppermute | solution.py:294
  38.2 12.7 %collective-permute-start.16 = (bf16[4,432,128]{2,1,0:T(8,128)(2,1)S(1)}, bf16[4,432,128]{2,1,0:T(8,128)(2,1)S(1)}, u32[]{:S(2)}, u32[]{:S(2)}) collective-permute-start(bf16[4,432,128]{2,1,0:T(8,128)(2,1)S(1)} %get-tuple-element.60), channel_id=1, source_target_pairs={{0,1},{1,0},{2,3},{3,2},{4,5},{5,4},{6,7},{7,6},{8,9},{9,8},{10,11... | collective-permute-start | bytes 1327112 | tf_op jit(solution)/shard_map/ppermute | solution.py:289
  41.9 1.6 %collective-permute-start.12 = (f32[2,16,1024]{2,1,0:T(8,128)S(1)}, f32[2,16,1024]{2,1,0:T(8,128)S(1)}, u32[]{:S(2)}, u32[]{:S(2)}) collective-permute-start(f32[2,16,1024]{2,1,0:T(8,128)S(1)} %add_add_fusion.own_ref), channel_id=1, source_target_pairs={{0,1},{1,0},{2,3},{3,2},{4,5},{5,4},{6,7},{7,6},{8,9},{9,8},{10,11... | collective-permute-start | bytes 393224 | tf_op jit(solution)/shard_map/ppermute | solution.py:289
  44.1 4.8 %collective-permute-start.15 = (bf16[2,16,1024]{2,1,0:T(8,128)(2,1)S(1)}, bf16[2,16,1024]{2,1,0:T(8,128)(2,1)S(1)}, u32[]{:S(2)}, u32[]{:S(2)}) collective-permute-start(bf16[2,16,1024]{2,1,0:T(8,128)(2,1)S(1)} %act.1.refs_0_), channel_id=1, source_target_pairs={{4,0},{6,2},{0,4},{2,6},{5,1},{7,3},{1,5},{3,7},{12,8},{14,10},{8,... | collective-permute-start | bytes 196616 | tf_op jit(solution)/shard_map/ppermute | solution.py:294
  44.8 6.0 %collective-permute-start.14 = (bf16[2,16,1024]{2,1,0:T(8,128)(2,1)S(1)}, bf16[2,16,1024]{2,1,0:T(8,128)(2,1)S(1)}, u32[]{:S(2)}, u32[]{:S(2)}) collective-permute-start(bf16[2,16,1024]{2,1,0:T(8,128)(2,1)S(1)} %act.1.refs_0_), channel_id=1, source_target_pairs={{6,0},{0,2},{2,4},{4,6},{7,1},{1,3},{3,5},{5,7},{14,8},{8,10},{10,... | collective-permute-start | bytes 196616 | tf_op jit(solution)/shard_map/ppermute | solution.py:294
  46.8 4.1 %collective-permute-start.13 = (bf16[2,16,1024]{2,1,0:T(8,128)(2,1)S(1)}, bf16[2,16,1024]{2,1,0:T(8,128)(2,1)S(1)}, u32[]{:S(2)}, u32[]{:S(2)}) collective-permute-start(bf16[2,16,1024]{2,1,0:T(8,128)(2,1)S(1)} %act.1.refs_0_), channel_id=1, source_target_pairs={{2,0},{4,2},{6,4},{0,6},{3,1},{5,3},{7,5},{1,7},{10,8},{12,10},{14... | collective-permute-start | bytes 196616 | tf_op jit(solution)/shard_map/ppermute | solution.py:294
  54.5 15.7 %all-to-all-start = ((bf16[16,112,128]{2,1,0:T(8,128)(2,1)}), bf16[16,112,128]{2,1,0:T(8,128)(2,1)S(1)}, u32[]{:S(2)}, u32[]{:S(2)}) async-start(bf16[16,112,128]{2,1,0:T(8,128)(2,1)} %get-tuple-element.62), calls=%async_computation | async-start | bytes 917504 | tf_op jit(solution)/shard_map/all_to_all | solution.py:347
  60.1 2.9 %collective-permute-start.18 = (bf16[7,16,1024]{2,1,0:T(8,128)(2,1)S(1)}, bf16[7,16,1024]{2,1,0:T(8,128)(2,1)S(1)}, u32[]{:S(2)}, u32[]{:S(2)}) collective-permute-start(bf16[7,16,1024]{2,1,0:T(8,128)(2,1)S(1)} %get-tuple-element.64), channel_id=1, source_target_pairs={{0,1},{1,0},{2,3},{3,2},{4,5},{5,4},{6,7},{7,6},{8,9},{9,8},{10,11... | collective-permute-start | bytes 688136 | tf_op jit(solution)/shard_map/ppermute | solution.py:289
  63.0 7.4 %collective-permute-start.19 = (bf16[2,16,1024]{2,1,0:T(8,128)(2,1)S(1)}, bf16[2,16,1024]{2,1,0:T(8,128)(2,1)S(1)}, u32[]{:S(2)}, u32[]{:S(2)}) collective-permute-start(bf16[2,16,1024]{2,1,0:T(8,128)(2,1)S(1)} %pad_maximum_fusion.7), channel_id=1, source_target_pairs={{0,32},{8,40},{16,48},{24,56},{32,0},{40,8},{48,16},{56,24},{1,33}... | collective-permute-start | bytes 196616 | tf_op jit(solution)/shard_map/ppermute | solution.py:300
  64.5 9.2 %collective-permute-start.23 = (bf16[2,2,16,1024]{3,2,1,0:T(8,128)(2,1)S(1)}, bf16[2,2,16,1024]{3,2,1,0:T(8,128)(2,1)S(1)}, u32[]{:S(2)}, u32[]{:S(2)}) collective-permute-start(bf16[2,2,16,1024]{3,2,1,0:T(8,128)(2,1)S(1)} %pad_maximum_fusion.3), channel_id=1, source_target_pairs={{0,8},{8,16},{16,24},{24,32},{32,40},{40,48},{48,56},{56,0},{1,57}... | collective-permute-start | bytes 393224 | tf_op jit(solution)/shard_map/ppermute | solution.py:300
  66.2 9.9 %collective-permute-start.24 = (bf16[2,2,16,1024]{3,2,1,0:T(8,128)(2,1)S(1)}, bf16[2,2,16,1024]{3,2,1,0:T(8,128)(2,1)S(1)}, u32[]{:S(2)}, u32[]{:S(2)}) collective-permute-start(bf16[2,2,16,1024]{3,2,1,0:T(8,128)(2,1)S(1)} %pad_maximum_fusion.4), channel_id=1, source_target_pairs={{0,16},{8,24},{16,32},{24,40},{32,48},{40,56},{48,0},{56,8},{1,49}... | collective-permute-start | bytes 393224 | tf_op jit(solution)/shard_map/ppermute | solution.py:300
  67.7 8.4 %collective-permute-start.25 = (bf16[2,2,16,1024]{3,2,1,0:T(8,128)(2,1)S(1)}, bf16[2,2,16,1024]{3,2,1,0:T(8,128)(2,1)S(1)}, u32[]{:S(2)}, u32[]{:S(2)}) collective-permute-start(bf16[2,2,16,1024]{3,2,1,0:T(8,128)(2,1)S(1)} %pad_maximum_fusion.5), channel_id=1, source_target_pairs={{0,24},{8,32},{16,40},{24,48},{32,56},{40,0},{48,8},{56,16},{1,41}... | collective-permute-start | bytes 393224 | tf_op jit(solution)/shard_map/ppermute | solution.py:300
  70.4 5.7 %collective-permute-start.22 = (bf16[4,112,128]{2,1,0:T(8,128)(2,1)S(1)}, bf16[4,112,128]{2,1,0:T(8,128)(2,1)S(1)}, u32[]{:S(2)}, u32[]{:S(2)}) collective-permute-start(bf16[4,112,128]{2,1,0:T(8,128)(2,1)S(1)} %reduce_sum.12.refs_0_), channel_id=1, source_target_pairs={{128,0},{192,64},{0,128},{64,192},{129,1},{193,65},{1,129},{65,193... | collective-permute-start | bytes 344072 | tf_op jit(solution)/shard_map/ppermute | solution.py:294
  73.4 6.2 %collective-permute-start.21 = (bf16[4,112,128]{2,1,0:T(8,128)(2,1)S(1)}, bf16[4,112,128]{2,1,0:T(8,128)(2,1)S(1)}, u32[]{:S(2)}, u32[]{:S(2)}) collective-permute-start(bf16[4,112,128]{2,1,0:T(8,128)(2,1)S(1)} %reduce_sum.12.refs_0_), channel_id=1, source_target_pairs={{192,0},{0,64},{64,128},{128,192},{193,1},{1,65},{65,129},{129,193... | collective-permute-start | bytes 344072 | tf_op jit(solution)/shard_map/ppermute | solution.py:294
  73.7 5.9 %collective-permute-start.20 = (bf16[4,112,128]{2,1,0:T(8,128)(2,1)S(1)}, bf16[4,112,128]{2,1,0:T(8,128)(2,1)S(1)}, u32[]{:S(2)}, u32[]{:S(2)}) collective-permute-start(bf16[4,112,128]{2,1,0:T(8,128)(2,1)S(1)} %reduce_sum.12.refs_0_), channel_id=1, source_target_pairs={{64,0},{128,64},{192,128},{0,192},{65,1},{129,65},{193,129},{1,193... | collective-permute-start | bytes 344072 | tf_op jit(solution)/shard_map/ppermute | solution.py:294
  79.6 4.0 %collective-permute-start.26 = (bf16[4,4,112,128]{3,2,1,0:T(8,128)(2,1)S(1)}, bf16[4,4,112,128]{3,2,1,0:T(8,128)(2,1)S(1)}, u32[]{:S(2)}, u32[]{:S(2)}) collective-permute-start(bf16[4,4,112,128]{3,2,1,0:T(8,128)(2,1)S(1)} %pad_maximum_fusion), channel_id=1, source_target_pairs={{0,1},{1,0},{2,3},{3,2},{4,5},{5,4},{6,7},{7,6},{8,9},{9,8},{10,11... | collective-permute-start | bytes 1376264 | tf_op jit(solution)/shard_map/ppermute | solution.py:289
  82.4 1.3 %collective-permute-start.27 = (bf16[2,16,1024]{2,1,0:T(8,128)(2,1)S(1)}, bf16[2,16,1024]{2,1,0:T(8,128)(2,1)S(1)}, u32[]{:S(2)}, u32[]{:S(2)}) collective-permute-start(bf16[2,16,1024]{2,1,0:T(8,128)(2,1)S(1)} %get-tuple-element.78), channel_id=1, source_target_pairs={{0,1},{1,0},{2,3},{3,2},{4,5},{5,4},{6,7},{7,6},{8,9},{9,8},{10,11... | collective-permute-start | bytes 196616 | tf_op jit(solution)/shard_map/ppermute | solution.py:289

commit v12 on v11

--- a/solution.py
+++ b/solution.py
@@ -318,6 +318,7 @@
     other = swap(pair)
     both = jnp.stack([pair, other])
     came.update({j: apart(both, j) for j in range(far - 1, 0, -1)})
+    one, two, came[1] = lax.optimization_barrier((one, two, came[1]))
     *groups, order = call(regroup_kernel, [((taps, group), BF16)] * NX + [((channels, channels), BF16)], [], "regroup", 2 * taps * channels * channels, at, one, two)
     kernels = [groups[0]] + [around(groups[NX - k], "x", k) for k in range(1, NX)]
     came, kernels = lax.optimization_barrier((came, kernels))

time: 86.4 us -> 85.5 us (0.990)
  waiting for transfers between devices: 20.2 us -> 21.4 us
  starting transfers between devices: 50.7 us -> 49.6 us
  local copies, waits for them, and re-layouts: 2.06 us -> 1.05 us
    ppermute x8, waiting for transfers between devices: 0.17 us -> 2.35 us  [apart(): return lax.ppermute(values, ('z', 'spatial'), pairs)]
    ppermute x12, waiting for transfers between devices: 15.6 us -> 13.7 us  [around(): lax.ppermute(values, axis, [((i + step) % size, i) for i in range(size)])]
    ppermute x8, starting transfers between devices: 19.8 us -> 18.3 us  [apart(): return lax.ppermute(values, ('z', 'spatial'), pairs)]
    unnamed x4, local copies, waits for them, and re-layouts: 2.03 us -> 1.02 us
    ppermute x8, waiting for transfers between devices: 4.45 us -> 5.35 us  [swap(): return lax.ppermute(values, 'spatial', [(0, 1), (1, 0)])]
  transfers between devices with their start and end apart: 29 -> 29, of which waited for: 12 -> 14; matrix products, arithmetic and copies ran while one was open for 0% -> 0% of each run, Pallas kernels for 3% -> 3%
where the time goes in v12:
time: 85.5 us; the launch traced here: 85.2 us
  starting transfers between devices  49.6 us (58%)
  waiting for transfers between devices  21.4 us (25%)
  Pallas kernels  11 us (13%)
  other arithmetic  1.21 us (1%)
  local copies, waits for them, and re-layouts  1.05 us (1%)
  between operations  0.96 us (1%)
    ppermute x8, starting transfers between devices, apart(): return lax.ppermute(values, ('z', 'spatial'), pairs)  18.3 us
    ppermute x12, starting transfers between devices, around(): lax.ppermute(values, axis, [((i + step) % size, i) for i in range(size)])  16 us
    ppermute x12, waiting for transfers between devices, around(): lax.ppermute(values, axis, [((i + step) % size, i) for i in range(size)])  13.7 us
    pallas_call x6, Pallas kernels, call(): pl.pallas_call(kernel, out_shape=tuple((jax.ShapeDtypeStruct(s, t) for s,...  11 us
    ppermute x8, starting transfers between devices, swap(): return lax.ppermute(values, 'spatial', [(0, 1), (1, 0)])  9.81 us
    all_to_all x1, starting transfers between devices, body(): grads = lax.all_to_all(grads, ('samples', 'x'), 0, 0, tiled=True)  5.49 us
    ppermute x8, waiting for transfers between devices, swap(): return lax.ppermute(values, 'spatial', [(0, 1), (1, 0)])  5.35 us
    ppermute x8, waiting for transfers between devices, apart(): return lax.ppermute(values, ('z', 'spatial'), pairs)  2.35 us
  transfers between devices with their start and end apart: 29, of which 14 were waited for; matrix products, arithmetic and copies ran while one was open for 0% of the time, Pallas kernels for 3%

profile of v12, /device:TPU:1, one launch (start us, length us, event | category | flops | bytes accessed | tf_op | source)
XLA Modules:
  0.0 85.2 jit_solution(16956131378318478758)
XLA Ops:
  0.6 0.8 fusion
  1.5 3.3 %collective-permute-start = (bf16[2,16,1024]{2,1,0:T(8,128)(2,1)S(1)}, bf16[2,16,1024]{2,1,0:T(8,128)(2,1)S(1)}, u32[]{:S(2)}, u32[]{:S(2)}) collective-permute-start(bf16[2,16,1024]{2,1,0:T(8,128)(2,1)S(1)} %get-tuple-element.97.pair_ref), channel_id=1, source_target_pairs={{0,1},{1,0},{2,3},{3,2},{4,5},{5,4},{6,7},{7,6},{8,9},{9,8},{10,11... | collective-permute-start | bytes 196616 | tf_op jit(solution)/shard_map/ppermute | solution.py:289
  4.8 0.9 %collective-permute-done.other_ref = bf16[2,16,1024]{2,1,0:T(8,128)(2,1)S(1)} collective-permute-done((bf16[2,16,1024]{2,1,0:T(8,128)(2,1)S(1)}, bf16[2,16,1024]{2,1,0:T(8,128)(2,1)S(1)}, u32[]{:S(2)}, u32[]{:S(2)}) %collective-permute-start) | collective-permute-done | bytes 65568 | tf_op jit(solution)/shard_map/ppermute | solution.py:289
  5.7 3.9 %collective-permute-start.1 = (bf16[2,2,16,1024]{3,2,1,0:T(8,128)(2,1)S(1)}, bf16[2,2,16,1024]{3,2,1,0:T(8,128)(2,1)S(1)}, u32[]{:S(2)}, u32[]{:S(2)}) collective-permute-start(bf16[2,2,16,1024]{3,2,1,0:T(8,128)(2,1)S(1)} %pad_maximum_fusion.2), channel_id=1, source_target_pairs={{0,8},{8,16},{16,24},{24,32},{32,40},{40,48},{48,56},{56,0},{1,57}... | collective-permute-start | bytes 393224 | tf_op jit(solution)/shard_map/ppermute | solution.py:300
  9.6 1.4 %collective-permute-start.4 = (bf16[2,16,1024]{2,1,0:T(8,128)(2,1)S(1)}, bf16[2,16,1024]{2,1,0:T(8,128)(2,1)S(1)}, u32[]{:S(2)}, u32[]{:S(2)}) collective-permute-start(bf16[2,16,1024]{2,1,0:T(8,128)(2,1)S(1)} %get-tuple-element.97.pair_ref), channel_id=1, source_target_pairs={{0,32},{8,40},{16,48},{24,56},{32,0},{40,8},{48,16},{56,24},{1,33}... | collective-permute-start | bytes 196616 | tf_op jit(solution)/shard_map/ppermute | solution.py:300
  11.1 0.1 pad_add_fusion.at_ref
  11.2 0.4 collective-permute-start.3
  11.6 4.3 %collective-permute-start.2 = (bf16[2,2,16,1024]{3,2,1,0:T(8,128)(2,1)S(1)}, bf16[2,2,16,1024]{3,2,1,0:T(8,128)(2,1)S(1)}, u32[]{:S(2)}, u32[]{:S(2)}) collective-permute-start(bf16[2,2,16,1024]{3,2,1,0:T(8,128)(2,1)S(1)} %pad_maximum_fusion.2), channel_id=1, source_target_pairs={{0,16},{8,24},{16,32},{24,40},{32,48},{40,56},{48,0},{56,8},{1,49}... | collective-permute-start | bytes 393224 | tf_op jit(solution)/shard_map/ppermute | solution.py:300
  15.8 0.0 collective-permute-done.1.refs_0_
  15.8 1.0 %copy-done.1 = bf16[27,16,512]{2,1,0:T(8,128)(2,1)S(1)} copy-done((bf16[27,16,512]{2,1,0:T(8,128)(2,1)S(1)}, bf16[27,16,512]{2,1,0:T(8,128)(2,1)}, u32[]{:S(2)}) %copy-start.1) | copy-done | bytes 442392
  16.9 1.3 %regroup.1 = (bf16[432,128]{1,0:T(8,128)(2,1)S(1)}, bf16[432,128]{1,0:T(8,128)(2,1)S(1)}, bf16[432,128]{1,0:T(8,128)(2,1)S(1)}, bf16[432,128]{1,0:T(8,128)(2,1)S(1)}, bf16[512,512]{1,0:T(8,128)(2,1)S(1)}) custom-call(s32[4]{0:T(128)S(1)} %pad_add_fusion.at_ref, bf16[432,512]{1,0:T(8,128)(2,1)S(1)} %bitcast.37, bf16[432,512]{1,0:T(8,128)(2,1)S(1)} %bitcast.38), custom_call_target="tpu_custom_call" | custom-call | flops 226492416 | tf_op jit(solution)/shard_map/regroup/pallas_call | solution.py:276
  18.2 2.6 %collective-permute-start.5 = (bf16[432,128]{1,0:T(8,128)(2,1)S(1)}, bf16[432,128]{1,0:T(8,128)(2,1)S(1)}, u32[]{:S(2)}, u32[]{:S(2)}) collective-permute-start(bf16[432,128]{1,0:T(8,128)(2,1)S(1)} %get-tuple-element.51), channel_id=1, source_target_pairs={{2,0},{4,2},{6,4},{0,6},{3,1},{5,3},{7,5},{1,7},{10,8},{12,10},{14... | collective-permute-start | bytes 331784 | tf_op jit(solution)/shard_map/ppermute | solution.py:294
  20.7 0.5 collective-permute-start.6
  21.3 0.0 collective-permute-done.4.refs_3_
  21.3 0.6 collective-permute-start.7
  21.9 0.0 collective-permute-done.3.refs_2_
  21.9 2.3 %collective-permute-done.2.refs_1_ = bf16[2,2,16,1024]{3,2,1,0:T(8,128)(2,1)S(1)} collective-permute-done((bf16[2,2,16,1024]{3,2,1,0:T(8,128)(2,1)S(1)}, bf16[2,2,16,1024]{3,2,1,0:T(8,128)(2,1)S(1)}, u32[]{:S(2)}, u32[]{:S(2)}) %collective-permute-start.2) | collective-permute-done | bytes 131104 | tf_op jit(solution)/shard_map/ppermute | solution.py:300
  24.2 0.7 collective-permute-done.5.refs_6_
  24.9 2.1 %collective-permute-done.6.refs_7_ = bf16[432,128]{1,0:T(8,128)(2,1)S(1)} collective-permute-done((bf16[432,128]{1,0:T(8,128)(2,1)S(1)}, bf16[432,128]{1,0:T(8,128)(2,1)S(1)}, u32[]{:S(2)}, u32[]{:S(2)}) %collective-permute-start.6) | collective-permute-done | bytes 110624 | tf_op jit(solution)/shard_map/ppermute | solution.py:294
  27.0 1.8 %collective-permute-done.7.refs_8_ = bf16[432,128]{1,0:T(8,128)(2,1)S(1)} collective-permute-done((bf16[432,128]{1,0:T(8,128)(2,1)S(1)}, bf16[432,128]{1,0:T(8,128)(2,1)S(1)}, u32[]{:S(2)}, u32[]{:S(2)}) %collective-permute-start.7) | collective-permute-done | bytes 110624 | tf_op jit(solution)/shard_map/ppermute | solution.py:294
  28.9 0.5 collective-permute-start.8
  29.4 1.1 %collective-permute-done.8.refs_4_ = bf16[7,16,1024]{2,1,0:T(8,128)(2,1)S(1)} collective-permute-done((bf16[7,16,1024]{2,1,0:T(8,128)(2,1)S(1)}, bf16[7,16,1024]{2,1,0:T(8,128)(2,1)S(1)}, u32[]{:S(2)}, u32[]{:S(2)}) %collective-permute-start.8) | collective-permute-done | bytes 229408 | tf_op jit(solution)/shard_map/ppermute | solution.py:289
  30.5 2.6 %conv_in.1 = (f32[2,16,1024]{2,1,0:T(8,128)S(1)}, bf16[2,16,1024]{2,1,0:T(8,128)(2,1)S(1)}, bf16[2,16,1024]{2,1,0:T(8,128)(2,1)S(1)}, bf16[2,16,1024]{2,1,0:T(8,...) custom-call(s32[4]{0:T(128)S(1)} %pad_add_fusion.at_ref, ...), custom_call_target="tpu_custom_call" | custom-call | flops 603979776 | tf_op jit(solution)/shard_map/conv_in/pallas_call | solution.py:276
  33.1 0.4 collective-permute-start.17
  33.5 0.5 collective-permute-start.9
  34.0 0.0 collective-permute-start.10
  34.0 2.7 %collective-permute-start.11 = (bf16[2,16,1024]{2,1,0:T(8,128)(2,1)S(1)}, bf16[2,16,1024]{2,1,0:T(8,128)(2,1)S(1)}, u32[]{:S(2)}, u32[]{:S(2)}) collective-permute-start(bf16[2,16,1024]{2,1,0:T(8,128)(2,1)S(1)} %get-tuple-element.65), channel_id=1, source_target_pairs={{2,0},{4,2},{6,4},{0,6},{3,1},{5,3},{7,5},{1,7},{10,8},{12,10},{14... | collective-permute-start | bytes 196616 | tf_op jit(solution)/shard_map/ppermute | solution.py:294
  36.7 1.0 %collective-permute-start.16 = (bf16[4,432,128]{2,1,0:T(8,128)(2,1)S(1)}, bf16[4,432,128]{2,1,0:T(8,128)(2,1)S(1)}, u32[]{:S(2)}, u32[]{:S(2)}) collective-permute-start(bf16[4,432,128]{2,1,0:T(8,128)(2,1)S(1)} %get-tuple-element.66), channel_id=1, source_target_pairs={{0,1},{1,0},{2,3},{3,2},{4,5},{5,4},{6,7},{7,6},{8,9},{9,8},{10,11... | collective-permute-start | bytes 1327112 | tf_op jit(solution)/shard_map/ppermute | solution.py:289
  37.7 0.8 collective-permute-done.9
  38.6 1.8 %collective-permute-done.10 = bf16[2,16,1024]{2,1,0:T(8,128)(2,1)S(1)} collective-permute-done((bf16[2,16,1024]{2,1,0:T(8,128)(2,1)S(1)}, bf16[2,16,1024]{2,1,0:T(8,128)(2,1)S(1)}, u32[]{:S(2)}, u32[]{:S(2)}) %collective-permute-start.10) | collective-permute-done | bytes 65568 | tf_op jit(solution)/shard_map/ppermute | solution.py:294
  40.4 0.0 collective-permute-done.11
  40.4 0.6 collective-permute-start.12
  41.1 1.0 %collective-permute-done.12.other_ref = f32[2,16,1024]{2,1,0:T(8,128)S(1)} collective-permute-done((f32[2,16,1024]{2,1,0:T(8,128)S(1)}, f32[2,16,1024]{2,1,0:T(8,128)S(1)}, u32[]{:S(2)}, u32[]{:S(2)}) %collective-permute-start.12) | collective-permute-done | bytes 131104 | tf_op jit(solution)/shard_map/ppermute | solution.py:289
  42.1 0.6 act.1.refs_0_
  42.7 0.7 collective-permute-start.15
  43.3 2.0 %collective-permute-start.14 = (bf16[2,16,1024]{2,1,0:T(8,128)(2,1)S(1)}, bf16[2,16,1024]{2,1,0:T(8,128)(2,1)S(1)}, u32[]{:S(2)}, u32[]{:S(2)}) collective-permute-start(bf16[2,16,1024]{2,1,0:T(8,128)(2,1)S(1)} %act.1.refs_0_), channel_id=1, source_target_pairs={{6,0},{0,2},{2,4},{4,6},{7,1},{1,3},{3,5},{5,7},{14,8},{8,10},{10,... | collective-permute-start | bytes 196616 | tf_op jit(solution)/shard_map/ppermute | solution.py:294
  45.3 0.7 collective-permute-start.13
  46.0 1.4 %collective-permute-done.15.refs_3_ = bf16[2,16,1024]{2,1,0:T(8,128)(2,1)S(1)} collective-permute-done((bf16[2,16,1024]{2,1,0:T(8,128)(2,1)S(1)}, bf16[2,16,1024]{2,1,0:T(8,128)(2,1)S(1)}, u32[]{:S(2)}, u32[]{:S(2)}) %collective-permute-start.15) | collective-permute-done | bytes 65568 | tf_op jit(solution)/shard_map/ppermute | solution.py:294
  47.4 2.0 %collective-permute-done.14.refs_2_ = bf16[2,16,1024]{2,1,0:T(8,128)(2,1)S(1)} collective-permute-done((bf16[2,16,1024]{2,1,0:T(8,128)(2,1)S(1)}, bf16[2,16,1024]{2,1,0:T(8,128)(2,1)S(1)}, u32[]{:S(2)}, u32[]{:S(2)}) %collective-permute-start.14) | collective-permute-done | bytes 65568 | tf_op jit(solution)/shard_map/ppermute | solution.py:294
  49.4 0.0 collective-permute-done.17.refs_5_
  49.4 3.7 %conv_out.1 = (bf16[2,16,1024]{2,1,0:T(8,128)(2,1)S(1)}, bf16[3,2,16,1024]{3,2,1,0:T(8,128)(2,1)S(1)}, bf16[16,1024]{1,0:T(8,128)(2,1)S(1)}, bf16[7,16,1024]{2,1,0:T(8,128)(2,1)S(1)}, bf16[16,112,128]{2,1,0:T(8,128)(2,1)}) custom-call(s32[4]{0:T(128)S(1)} %pad_add_fusion.at_ref, bf16[2,16,1024]{2,1,0:T(8,128)(2,1)S(1)} %act.1.refs_0_, ...), custom_call_target="tpu_custom_call" | custom-call | flops 1207959552 | tf_op jit(solution)/shard_map/conv_out/pallas_call | solution.py:276
  53.1 5.5 %all-to-all-start = ((bf16[16,112,128]{2,1,0:T(8,128)(2,1)}), bf16[16,112,128]{2,1,0:T(8,128)(2,1)S(1)}, u32[]{:S(2)}, u32[]{:S(2)}) async-start(bf16[16,112,128]{2,1,0:T(8,128)(2,1)} %get-tuple-element.68), calls=%async_computation | async-start | bytes 917504 | tf_op jit(solution)/shard_map/all_to_all | solution.py:348
  58.6 1.8 %collective-permute-start.18 = (bf16[7,16,1024]{2,1,0:T(8,128)(2,1)S(1)}, bf16[7,16,1024]{2,1,0:T(8,128)(2,1)S(1)}, u32[]{:S(2)}, u32[]{:S(2)}) collective-permute-start(bf16[7,16,1024]{2,1,0:T(8,128)(2,1)S(1)} %get-tuple-element.70), channel_id=1, source_target_pairs={{0,1},{1,0},{2,3},{3,2},{4,5},{5,4},{6,7},{7,6},{8,9},{9,8},{10,11... | collective-permute-start | bytes 688136 | tf_op jit(solution)/shard_map/ppermute | solution.py:289
  60.4 1.1 %collective-permute-done.18 = bf16[7,16,1024]{2,1,0:T(8,128)(2,1)S(1)} collective-permute-done((bf16[7,16,1024]{2,1,0:T(8,128)(2,1)S(1)}, bf16[7,16,1024]{2,1,0:T(8,128)(2,1)S(1)}, u32[]{:S(2)}, u32[]{:S(2)}) %collective-permute-start.18) | collective-permute-done | bytes 229408 | tf_op jit(solution)/shard_map/ppermute | solution.py:289
  61.5 2.9 %collective-permute-start.19 = (bf16[2,16,1024]{2,1,0:T(8,128)(2,1)S(1)}, bf16[2,16,1024]{2,1,0:T(8,128)(2,1)S(1)}, u32[]{:S(2)}, u32[]{:S(2)}) collective-permute-start(bf16[2,16,1024]{2,1,0:T(8,128)(2,1)S(1)} %pad_maximum_fusion.7), channel_id=1, source_target_pairs={{0,32},{8,40},{16,48},{24,56},{32,0},{40,8},{48,16},{56,24},{1,33}... | collective-permute-start | bytes 196616 | tf_op jit(solution)/shard_map/ppermute | solution.py:300
  64.5 2.0 %collective-permute-start.23 = (bf16[2,2,16,1024]{3,2,1,0:T(8,128)(2,1)S(1)}, bf16[2,2,16,1024]{3,2,1,0:T(8,128)(2,1)S(1)}, u32[]{:S(2)}, u32[]{:S(2)}) collective-permute-start(bf16[2,2,16,1024]{3,2,1,0:T(8,128)(2,1)S(1)} %pad_maximum_fusion.3), channel_id=1, source_target_pairs={{0,8},{8,16},{16,24},{24,32},{32,40},{40,48},{48,56},{56,0},{1,57}... | collective-permute-start | bytes 393224 | tf_op jit(solution)/shard_map/ppermute | solution.py:300
  66.5 1.4 %collective-permute-start.24 = (bf16[2,2,16,1024]{3,2,1,0:T(8,128)(2,1)S(1)}, bf16[2,2,16,1024]{3,2,1,0:T(8,128)(2,1)S(1)}, u32[]{:S(2)}, u32[]{:S(2)}) collective-permute-start(bf16[2,2,16,1024]{3,2,1,0:T(8,128)(2,1)S(1)} %pad_maximum_fusion.4), channel_id=1, source_target_pairs={{0,16},{8,24},{16,32},{24,40},{32,48},{40,56},{48,0},{56,8},{1,49}... | collective-permute-start | bytes 393224 | tf_op jit(solution)/shard_map/ppermute | solution.py:300
  67.9 1.9 %collective-permute-start.25 = (bf16[2,2,16,1024]{3,2,1,0:T(8,128)(2,1)S(1)}, bf16[2,2,16,1024]{3,2,1,0:T(8,128)(2,1)S(1)}, u32[]{:S(2)}, u32[]{:S(2)}) collective-permute-start(bf16[2,2,16,1024]{3,2,1,0:T(8,128)(2,1)S(1)} %pad_maximum_fusion.5), channel_id=1, source_target_pairs={{0,24},{8,32},{16,40},{24,48},{32,56},{40,0},{48,8},{56,16},{1,41}... | collective-permute-start | bytes 393224 | tf_op jit(solution)/shard_map/ppermute | solution.py:300
  69.8 0.1 reduce_sum.12.refs_0_
  69.9 0.0 collective-permute-done.19.refs_3_
  69.9 3.2 %collective-permute-start.22 = (bf16[4,112,128]{2,1,0:T(8,128)(2,1)S(1)}, bf16[4,112,128]{2,1,0:T(8,128)(2,1)S(1)}, u32[]{:S(2)}, u32[]{:S(2)}) collective-permute-start(bf16[4,112,128]{2,1,0:T(8,128)(2,1)S(1)} %reduce_sum.12.refs_0_), channel_id=1, source_target_pairs={{128,0},{192,64},{0,128},{64,192},{129,1},{193,65},{1,129},{65,193... | collective-permute-start | bytes 344072 | tf_op jit(solution)/shard_map/ppermute | solution.py:294
  73.1 0.3 collective-permute-start.21
  73.4 0.0 collective-permute-done.23.refs_0_
  73.4 2.4 %collective-permute-start.20 = (bf16[4,112,128]{2,1,0:T(8,128)(2,1)S(1)}, bf16[4,112,128]{2,1,0:T(8,128)(2,1)S(1)}, u32[]{:S(2)}, u32[]{:S(2)}) collective-permute-start(bf16[4,112,128]{2,1,0:T(8,128)(2,1)S(1)} %reduce_sum.12.refs_0_), channel_id=1, source_target_pairs={{64,0},{128,64},{192,128},{0,192},{65,1},{129,65},{193,129},{1,193... | collective-permute-start | bytes 344072 | tf_op jit(solution)/shard_map/ppermute | solution.py:294
  75.8 0.0 collective-permute-done.24.refs_1_
  75.8 3.0 %collective-permute-done.21.refs_2_ = bf16[4,112,128]{2,1,0:T(8,128)(2,1)S(1)} collective-permute-done((bf16[4,112,128]{2,1,0:T(8,128)(2,1)S(1)}, bf16[4,112,128]{2,1,0:T(8,128)(2,1)S(1)}, u32[]{:S(2)}, u32[]{:S(2)}) %collective-permute-start.21) | collective-permute-done | bytes 114720 | tf_op jit(solution)/shard_map/ppermute | solution.py:294
  78.8 0.0 collective-permute-done.20.refs_1_
  78.8 0.1 pad_maximum_fusion
  78.9 2.0 %collective-permute-start.26 = (bf16[4,4,112,128]{3,2,1,0:T(8,128)(2,1)S(1)}, bf16[4,4,112,128]{3,2,1,0:T(8,128)(2,1)S(1)}, u32[]{:S(2)}, u32[]{:S(2)}) collective-permute-start(bf16[4,4,112,128]{3,2,1,0:T(8,128)(2,1)S(1)} %pad_maximum_fusion), channel_id=1, source_target_pairs={{0,1},{1,0},{2,3},{3,2},{4,5},{5,4},{6,7},{7,6},{8,9},{9,8},{10,11... | collective-permute-start | bytes 1376264 | tf_op jit(solution)/shard_map/ppermute | solution.py:289
  80.9 0.6 sum.1
  81.5 0.1 collective-permute-start.27
  81.6 1.2 %collective-permute-done.27.refs_6_ = bf16[2,16,1024]{2,1,0:T(8,128)(2,1)S(1)} collective-permute-done((bf16[2,16,1024]{2,1,0:T(8,128)(2,1)S(1)}, bf16[2,16,1024]{2,1,0:T(8,128)(2,1)S(1)}, u32[]{:S(2)}, u32[]{:S(2)}) %collective-permute-start.27) | collective-permute-done | bytes 65568 | tf_op jit(solution)/shard_map/ppermute | solution.py:289
  82.9 0.0 collective-permute-done.26.refs_4_
  82.9 2.2 %finish.1 = (bf16[16,1024]{1,0:T(8,128)(2,1)}, bf16[16,1024]{1,0:T(8,128)(2,1)}, f32[432,512]{1,0:T(8,128)}, f32[432,512]{1,0:T(8,128)}) custom-call(s32[4]{0:T(128)S(1)} %pad_add_fusion.at_ref, bf16[4,112,128]{2,1,0:T(8,128)(2,1)S(1)} %reduce_sum.12.refs_0_, bf16[4,112,128]{2,1,0:T(8,128)(2,1)S(1)} %collective-permute-done.20.refs_1_, ...), custom_call_target="tpu_custom_call" | custom-call | tf_op jit(solution)/shard_map/finish/pallas_call | solution.py:276
  (21 shorter events, 0.2 us)
Async XLA Ops:
  0.6 15.2 %copy-start = (bf16[27,16,512]{2,1,0:T(8,128)(2,1)S(1)}, bf16[27,16,512]{2,1,0:T(8,128)(2,1)}, u32[]{:S(2)}) copy-start(bf16[27,16,512]{2,1,0:T(8,128)(2,1)} %param.5) | copy-start | bytes 1327108
  1.5 4.2 %collective-permute-start = (bf16[2,16,1024]{2,1,0:T(8,128)(2,1)S(1)}, bf16[2,16,1024]{2,1,0:T(8,128)(2,1)S(1)}, u32[]{:S(2)}, u32[]{:S(2)}) collective-permute-start(bf16[2,16,1024]{2,1,0:T(8,128)(2,1)S(1)} %get-tuple-element.97.pair_ref), channel_id=1, source_target_pairs={{0,1},{1,0},{2,3},{3,2},{4,5},{5,4},{6,7},{7,6},{8,9},{9,8},{10,11... | collective-permute-start | bytes 196616 | tf_op jit(solution)/shard_map/ppermute | solution.py:289
  5.7 10.1 %collective-permute-start.1 = (bf16[2,2,16,1024]{3,2,1,0:T(8,128)(2,1)S(1)}, bf16[2,2,16,1024]{3,2,1,0:T(8,128)(2,1)S(1)}, u32[]{:S(2)}, u32[]{:S(2)}) collective-permute-start(bf16[2,2,16,1024]{3,2,1,0:T(8,128)(2,1)S(1)} %pad_maximum_fusion.2), channel_id=1, source_target_pairs={{0,8},{8,16},{16,24},{24,32},{32,40},{40,48},{48,56},{56,0},{1,57}... | collective-permute-start | bytes 393224 | tf_op jit(solution)/shard_map/ppermute | solution.py:300
  9.6 11.6 %collective-permute-start.4 = (bf16[2,16,1024]{2,1,0:T(8,128)(2,1)S(1)}, bf16[2,16,1024]{2,1,0:T(8,128)(2,1)S(1)}, u32[]{:S(2)}, u32[]{:S(2)}) collective-permute-start(bf16[2,16,1024]{2,1,0:T(8,128)(2,1)S(1)} %get-tuple-element.97.pair_ref), channel_id=1, source_target_pairs={{0,32},{8,40},{16,48},{24,56},{32,0},{40,8},{48,16},{56,24},{1,33}... | collective-permute-start | bytes 196616 | tf_op jit(solution)/shard_map/ppermute | solution.py:300
  11.2 10.7 %collective-permute-start.3 = (bf16[2,2,16,1024]{3,2,1,0:T(8,128)(2,1)S(1)}, bf16[2,2,16,1024]{3,2,1,0:T(8,128)(2,1)S(1)}, u32[]{:S(2)}, u32[]{:S(2)}) collective-permute-start(bf16[2,2,16,1024]{3,2,1,0:T(8,128)(2,1)S(1)} %pad_maximum_fusion.2), channel_id=1, source_target_pairs={{0,24},{8,32},{16,40},{24,48},{32,56},{40,0},{48,8},{56,16},{1,41}... | collective-permute-start | bytes 393224 | tf_op jit(solution)/shard_map/ppermute | solution.py:300
  11.6 12.6 %collective-permute-start.2 = (bf16[2,2,16,1024]{3,2,1,0:T(8,128)(2,1)S(1)}, bf16[2,2,16,1024]{3,2,1,0:T(8,128)(2,1)S(1)}, u32[]{:S(2)}, u32[]{:S(2)}) collective-permute-start(bf16[2,2,16,1024]{3,2,1,0:T(8,128)(2,1)S(1)} %pad_maximum_fusion.2), channel_id=1, source_target_pairs={{0,16},{8,24},{16,32},{24,40},{32,48},{40,56},{48,0},{56,8},{1,49}... | collective-permute-start | bytes 393224 | tf_op jit(solution)/shard_map/ppermute | solution.py:300
  15.8 1.0 %copy-start.1 = (bf16[27,16,512]{2,1,0:T(8,128)(2,1)S(1)}, bf16[27,16,512]{2,1,0:T(8,128)(2,1)}, u32[]{:S(2)}) copy-start(bf16[27,16,512]{2,1,0:T(8,128)(2,1)} %param.6) | copy-start | bytes 1327108
  18.2 6.7 %collective-permute-start.5 = (bf16[432,128]{1,0:T(8,128)(2,1)S(1)}, bf16[432,128]{1,0:T(8,128)(2,1)S(1)}, u32[]{:S(2)}, u32[]{:S(2)}) collective-permute-start(bf16[432,128]{1,0:T(8,128)(2,1)S(1)} %get-tuple-element.51), channel_id=1, source_target_pairs={{2,0},{4,2},{6,4},{0,6},{3,1},{5,3},{7,5},{1,7},{10,8},{12,10},{14... | collective-permute-start | bytes 331784 | tf_op jit(solution)/shard_map/ppermute | solution.py:294
  20.7 6.3 %collective-permute-start.6 = (bf16[432,128]{1,0:T(8,128)(2,1)S(1)}, bf16[432,128]{1,0:T(8,128)(2,1)S(1)}, u32[]{:S(2)}, u32[]{:S(2)}) collective-permute-start(bf16[432,128]{1,0:T(8,128)(2,1)S(1)} %get-tuple-element.52), channel_id=1, source_target_pairs={{4,0},{6,2},{0,4},{2,6},{5,1},{7,3},{1,5},{3,7},{12,8},{14,10},{8,... | collective-permute-start | bytes 331784 | tf_op jit(solution)/shard_map/ppermute | solution.py:294
  21.3 7.6 %collective-permute-start.7 = (bf16[432,128]{1,0:T(8,128)(2,1)S(1)}, bf16[432,128]{1,0:T(8,128)(2,1)S(1)}, u32[]{:S(2)}, u32[]{:S(2)}) collective-permute-start(bf16[432,128]{1,0:T(8,128)(2,1)S(1)} %get-tuple-element.53), channel_id=1, source_target_pairs={{6,0},{0,2},{2,4},{4,6},{7,1},{1,3},{3,5},{5,7},{14,8},{8,10},{10,... | collective-permute-start | bytes 331784 | tf_op jit(solution)/shard_map/ppermute | solution.py:294
  28.9 1.6 %collective-permute-start.8 = (bf16[7,16,1024]{2,1,0:T(8,128)(2,1)S(1)}, bf16[7,16,1024]{2,1,0:T(8,128)(2,1)S(1)}, u32[]{:S(2)}, u32[]{:S(2)}) collective-permute-start(bf16[7,16,1024]{2,1,0:T(8,128)(2,1)S(1)} %pad_maximum_fusion.1), channel_id=1, source_target_pairs={{0,1},{1,0},{2,3},{3,2},{4,5},{5,4},{6,7},{7,6},{8,9},{9,8},{10,11... | collective-permute-start | bytes 688136 | tf_op jit(solution)/shard_map/ppermute | solution.py:289
  33.1 16.3 %collective-permute-start.17 = (bf16[8,2,16,1024]{3,2,1,0:T(8,128)(2,1)S(1)}, bf16[8,2,16,1024]{3,2,1,0:T(8,128)(2,1)S(1)}, u32[]{:S(2)}, u32[]{:S(2)}) collective-permute-start(bf16[8,2,16,1024]{3,2,1,0:T(8,128)(2,1)S(1)} %get-tuple-element.67), channel_id=1, source_target_pairs={{0,1},{1,0},{2,3},{3,2},{4,5},{5,4},{6,7},{7,6},{8,9},{9,8},{10,11... | collective-permute-start | bytes 1572872 | tf_op jit(solution)/shard_map/ppermute | solution.py:289
  33.5 5.0 %collective-permute-start.9 = (bf16[2,16,1024]{2,1,0:T(8,128)(2,1)S(1)}, bf16[2,16,1024]{2,1,0:T(8,128)(2,1)S(1)}, u32[]{:S(2)}, u32[]{:S(2)}) collective-permute-start(bf16[2,16,1024]{2,1,0:T(8,128)(2,1)S(1)} %get-tuple-element.63), channel_id=1, source_target_pairs={{4,0},{6,2},{0,4},{2,6},{5,1},{7,3},{1,5},{3,7},{12,8},{14,10},{8,... | collective-permute-start | bytes 196616 | tf_op jit(solution)/shard_map/ppermute | solution.py:294
  34.0 6.4 %collective-permute-start.10 = (bf16[2,16,1024]{2,1,0:T(8,128)(2,1)S(1)}, bf16[2,16,1024]{2,1,0:T(8,128)(2,1)S(1)}, u32[]{:S(2)}, u32[]{:S(2)}) collective-permute-start(bf16[2,16,1024]{2,1,0:T(8,128)(2,1)S(1)} %get-tuple-element.64), channel_id=1, source_target_pairs={{6,0},{0,2},{2,4},{4,6},{7,1},{1,3},{3,5},{5,7},{14,8},{8,10},{10,... | collective-permute-start | bytes 196616 | tf_op jit(solution)/shard_map/ppermute | solution.py:294
  34.0 6.4 %collective-permute-start.11 = (bf16[2,16,1024]{2,1,0:T(8,128)(2,1)S(1)}, bf16[2,16,1024]{2,1,0:T(8,128)(2,1)S(1)}, u32[]{:S(2)}, u32[]{:S(2)}) collective-permute-start(bf16[2,16,1024]{2,1,0:T(8,128)(2,1)S(1)} %get-tuple-element.65), channel_id=1, source_target_pairs={{2,0},{4,2},{6,4},{0,6},{3,1},{5,3},{7,5},{1,7},{10,8},{12,10},{14... | collective-permute-start | bytes 196616 | tf_op jit(solution)/shard_map/ppermute | solution.py:294
  36.7 12.7 %collective-permute-start.16 = (bf16[4,432,128]{2,1,0:T(8,128)(2,1)S(1)}, bf16[4,432,128]{2,1,0:T(8,128)(2,1)S(1)}, u32[]{:S(2)}, u32[]{:S(2)}) collective-permute-start(bf16[4,432,128]{2,1,0:T(8,128)(2,1)S(1)} %get-tuple-element.66), channel_id=1, source_target_pairs={{0,1},{1,0},{2,3},{3,2},{4,5},{5,4},{6,7},{7,6},{8,9},{9,8},{10,11... | collective-permute-start | bytes 1327112 | tf_op jit(solution)/shard_map/ppermute | solution.py:289
  40.4 1.6 %collective-permute-start.12 = (f32[2,16,1024]{2,1,0:T(8,128)S(1)}, f32[2,16,1024]{2,1,0:T(8,128)S(1)}, u32[]{:S(2)}, u32[]{:S(2)}) collective-permute-start(f32[2,16,1024]{2,1,0:T(8,128)S(1)} %add_add_fusion.own_ref), channel_id=1, source_target_pairs={{0,1},{1,0},{2,3},{3,2},{4,5},{5,4},{6,7},{7,6},{8,9},{9,8},{10,11... | collective-permute-start | bytes 393224 | tf_op jit(solution)/shard_map/ppermute | solution.py:289
  42.7 4.8 %collective-permute-start.15 = (bf16[2,16,1024]{2,1,0:T(8,128)(2,1)S(1)}, bf16[2,16,1024]{2,1,0:T(8,128)(2,1)S(1)}, u32[]{:S(2)}, u32[]{:S(2)}) collective-permute-start(bf16[2,16,1024]{2,1,0:T(8,128)(2,1)S(1)} %act.1.refs_0_), channel_id=1, source_target_pairs={{4,0},{6,2},{0,4},{2,6},{5,1},{7,3},{1,5},{3,7},{12,8},{14,10},{8,... | collective-permute-start | bytes 196616 | tf_op jit(solution)/shard_map/ppermute | solution.py:294
  43.3 6.1 %collective-permute-start.14 = (bf16[2,16,1024]{2,1,0:T(8,128)(2,1)S(1)}, bf16[2,16,1024]{2,1,0:T(8,128)(2,1)S(1)}, u32[]{:S(2)}, u32[]{:S(2)}) collective-permute-start(bf16[2,16,1024]{2,1,0:T(8,128)(2,1)S(1)} %act.1.refs_0_), channel_id=1, source_target_pairs={{6,0},{0,2},{2,4},{4,6},{7,1},{1,3},{3,5},{5,7},{14,8},{8,10},{10,... | collective-permute-start | bytes 196616 | tf_op jit(solution)/shard_map/ppermute | solution.py:294
  45.3 4.1 %collective-permute-start.13 = (bf16[2,16,1024]{2,1,0:T(8,128)(2,1)S(1)}, bf16[2,16,1024]{2,1,0:T(8,128)(2,1)S(1)}, u32[]{:S(2)}, u32[]{:S(2)}) collective-permute-start(bf16[2,16,1024]{2,1,0:T(8,128)(2,1)S(1)} %act.1.refs_0_), channel_id=1, source_target_pairs={{2,0},{4,2},{6,4},{0,6},{3,1},{5,3},{7,5},{1,7},{10,8},{12,10},{14... | collective-permute-start | bytes 196616 | tf_op jit(solution)/shard_map/ppermute | solution.py:294
  53.1 16.8 %all-to-all-start = ((bf16[16,112,128]{2,1,0:T(8,128)(2,1)}), bf16[16,112,128]{2,1,0:T(8,128)(2,1)S(1)}, u32[]{:S(2)}, u32[]{:S(2)}) async-start(bf16[16,112,128]{2,1,0:T(8,128)(2,1)} %get-tuple-element.68), calls=%async_computation | async-start | bytes 917504 | tf_op jit(solution)/shard_map/all_to_all | solution.py:348
  58.6 2.9 %collective-permute-start.18 = (bf16[7,16,1024]{2,1,0:T(8,128)(2,1)S(1)}, bf16[7,16,1024]{2,1,0:T(8,128)(2,1)S(1)}, u32[]{:S(2)}, u32[]{:S(2)}) collective-permute-start(bf16[7,16,1024]{2,1,0:T(8,128)(2,1)S(1)} %get-tuple-element.70), channel_id=1, source_target_pairs={{0,1},{1,0},{2,3},{3,2},{4,5},{5,4},{6,7},{7,6},{8,9},{9,8},{10,11... | collective-permute-start | bytes 688136 | tf_op jit(solution)/shard_map/ppermute | solution.py:289
  61.5 8.4 %collective-permute-start.19 = (bf16[2,16,1024]{2,1,0:T(8,128)(2,1)S(1)}, bf16[2,16,1024]{2,1,0:T(8,128)(2,1)S(1)}, u32[]{:S(2)}, u32[]{:S(2)}) collective-permute-start(bf16[2,16,1024]{2,1,0:T(8,128)(2,1)S(1)} %pad_maximum_fusion.7), channel_id=1, source_target_pairs={{0,32},{8,40},{16,48},{24,56},{32,0},{40,8},{48,16},{56,24},{1,33}... | collective-permute-start | bytes 196616 | tf_op jit(solution)/shard_map/ppermute | solution.py:300
  64.5 8.9 %collective-permute-start.23 = (bf16[2,2,16,1024]{3,2,1,0:T(8,128)(2,1)S(1)}, bf16[2,2,16,1024]{3,2,1,0:T(8,128)(2,1)S(1)}, u32[]{:S(2)}, u32[]{:S(2)}) collective-permute-start(bf16[2,2,16,1024]{3,2,1,0:T(8,128)(2,1)S(1)} %pad_maximum_fusion.3), channel_id=1, source_target_pairs={{0,8},{8,16},{16,24},{24,32},{32,40},{40,48},{48,56},{56,0},{1,57}... | collective-permute-start | bytes 393224 | tf_op jit(solution)/shard_map/ppermute | solution.py:300
  66.5 9.3 %collective-permute-start.24 = (bf16[2,2,16,1024]{3,2,1,0:T(8,128)(2,1)S(1)}, bf16[2,2,16,1024]{3,2,1,0:T(8,128)(2,1)S(1)}, u32[]{:S(2)}, u32[]{:S(2)}) collective-permute-start(bf16[2,2,16,1024]{3,2,1,0:T(8,128)(2,1)S(1)} %pad_maximum_fusion.4), channel_id=1, source_target_pairs={{0,16},{8,24},{16,32},{24,40},{32,48},{40,56},{48,0},{56,8},{1,49}... | collective-permute-start | bytes 393224 | tf_op jit(solution)/shard_map/ppermute | solution.py:300
  67.9 7.8 %collective-permute-start.25 = (bf16[2,2,16,1024]{3,2,1,0:T(8,128)(2,1)S(1)}, bf16[2,2,16,1024]{3,2,1,0:T(8,128)(2,1)S(1)}, u32[]{:S(2)}, u32[]{:S(2)}) collective-permute-start(bf16[2,2,16,1024]{3,2,1,0:T(8,128)(2,1)S(1)} %pad_maximum_fusion.5), channel_id=1, source_target_pairs={{0,24},{8,32},{16,40},{24,48},{32,56},{40,0},{48,8},{56,16},{1,41}... | collective-permute-start | bytes 393224 | tf_op jit(solution)/shard_map/ppermute | solution.py:300
  69.9 5.8 %collective-permute-start.22 = (bf16[4,112,128]{2,1,0:T(8,128)(2,1)S(1)}, bf16[4,112,128]{2,1,0:T(8,128)(2,1)S(1)}, u32[]{:S(2)}, u32[]{:S(2)}) collective-permute-start(bf16[4,112,128]{2,1,0:T(8,128)(2,1)S(1)} %reduce_sum.12.refs_0_), channel_id=1, source_target_pairs={{128,0},{192,64},{0,128},{64,192},{129,1},{193,65},{1,129},{65,193... | collective-permute-start | bytes 344072 | tf_op jit(solution)/shard_map/ppermute | solution.py:294
  73.1 5.7 %collective-permute-start.21 = (bf16[4,112,128]{2,1,0:T(8,128)(2,1)S(1)}, bf16[4,112,128]{2,1,0:T(8,128)(2,1)S(1)}, u32[]{:S(2)}, u32[]{:S(2)}) collective-permute-start(bf16[4,112,128]{2,1,0:T(8,128)(2,1)S(1)} %reduce_sum.12.refs_0_), channel_id=1, source_target_pairs={{192,0},{0,64},{64,128},{128,192},{193,1},{1,65},{65,129},{129,193... | collective-permute-start | bytes 344072 | tf_op jit(solution)/shard_map/ppermute | solution.py:294
  73.4 5.4 %collective-permute-start.20 = (bf16[4,112,128]{2,1,0:T(8,128)(2,1)S(1)}, bf16[4,112,128]{2,1,0:T(8,128)(2,1)S(1)}, u32[]{:S(2)}, u32[]{:S(2)}) collective-permute-start(bf16[4,112,128]{2,1,0:T(8,128)(2,1)S(1)} %reduce_sum.12.refs_0_), channel_id=1, source_target_pairs={{64,0},{128,64},{192,128},{0,192},{65,1},{129,65},{193,129},{1,193... | collective-permute-start | bytes 344072 | tf_op jit(solution)/shard_map/ppermute | solution.py:294
  78.9 4.0 %collective-permute-start.26 = (bf16[4,4,112,128]{3,2,1,0:T(8,128)(2,1)S(1)}, bf16[4,4,112,128]{3,2,1,0:T(8,128)(2,1)S(1)}, u32[]{:S(2)}, u32[]{:S(2)}) collective-permute-start(bf16[4,4,112,128]{3,2,1,0:T(8,128)(2,1)S(1)} %pad_maximum_fusion), channel_id=1, source_target_pairs={{0,1},{1,0},{2,3},{3,2},{4,5},{5,4},{6,7},{7,6},{8,9},{9,8},{10,11... | collective-permute-start | bytes 1376264 | tf_op jit(solution)/shard_map/ppermute | solution.py:289
  81.5 1.3 %collective-permute-start.27 = (bf16[2,16,1024]{2,1,0:T(8,128)(2,1)S(1)}, bf16[2,16,1024]{2,1,0:T(8,128)(2,1)S(1)}, u32[]{:S(2)}, u32[]{:S(2)}) collective-permute-start(bf16[2,16,1024]{2,1,0:T(8,128)(2,1)S(1)} %get-tuple-element.84), channel_id=1, source_target_pairs={{0,1},{1,0},{2,3},{3,2},{4,5},{5,4},{6,7},{7,6},{8,9},{9,8},{10,11... | collective-permute-start | bytes 196616 | tf_op jit(solution)/shard_map/ppermute | solution.py:289

commit v13 on v12

--- a/solution.py
+++ b/solution.py
@@ -231,52 +231,73 @@
         run(1, 0)
 
 
-def finish_kernel(at_ref, *refs):
-    own_refs, other_ref, keep_ref, got_ref, order_ref = refs[:4], *refs[4:8]
-    mixed_ref, input_ref, one_ref, two_ref, near, far, wide, cells, sems = refs[8:]
-    taps, channels = one_ref.shape
-    _, _, size, group = other_ref.shape
-    third = taps // 3
-
-    def run(cell_outs, grad_outs):
+def put_grad(at_ref, piece, full, wide, order_ref, target, send):
+    taps, channels = wide.shape
+    size, third, group = full.shape[0] // 4, taps // 3, channels // NX
+    for k in range(4):
+        rows = pl.ds(pl.multiple_of(lax.rem(at_ref[2] + (0, 1, 3, 2)[k], 4) * size, 16), size)
+        for x in range(NX):
+            full[rows, x * group : (x + 1) * group] = piece(k, x)
+    for a in range(3):
+        rows = pl.ds(a * third, third)
+        wide[rows, :] = dot(full[a * third : (a + 1) * third, :], order_ref[...], ((1,), (0,)))
+        send(wide.at[rows], target.at[rows])
+
+
+def sender(sems, copies):
+    def send(source, target):
+        copy = pltpu.make_async_copy(source, target, sems.at[len(copies)])
+        copy.start()
+        copies.append(copy)
+
+    return send
+
+
+def own_kernel(at_ref, p0_ref, p1_ref, p2_ref, p3_ref, order_ref, one_ref, two_ref, full, wide, sems):
+    own_refs = (p0_ref, p1_ref, p2_ref, p3_ref)
+
+    def run(target):
         copies = []
-
-        def send(source, target):
-            copy = pltpu.make_async_copy(source, target, sems.at[len(copies)])
-            copy.start()
-            copies.append(copy)
-
+        put_grad(at_ref, lambda k, x: own_refs[k][x], full, wide, order_ref, target, sender(sems, copies))
+        for copy in copies:
+            copy.wait()
+
+    @pl.when(at_ref[0] == 0)
+    def _():
+        run(two_ref)
+
+    @pl.when(at_ref[0] == 1)
+    def _():
+        run(one_ref)
+
+
+def finish_kernel(at_ref, other_ref, keep_ref, got_ref, order_ref, _one, _two, mixed_ref, input_ref, one_ref, two_ref, full, wide, cells, sems):
+    def run(cell_outs, target):
+        copies = []
+        send = sender(sems, copies)
         for array in range(2):
             cells[array] = (keep_ref[array] + got_ref[1 - array].astype(F32)).astype(BF16)
             send(cells.at[array], cell_outs[array])
-        pieces = (lambda k, x: own_refs[k][x]), (lambda k, x: other_ref[k, x])
-        for n, full in enumerate((near, far)):
-            for k in range(4):
-                rows = pl.ds(pl.multiple_of(lax.rem(at_ref[2] + (0, 1, 3, 2)[k], 4) * size, 16), size)
-                for x in range(NX):
-                    full[rows, x * group : (x + 1) * group] = pieces[n](k, x)
-            for a in range(3):
-                rows = pl.ds(a * third, third)
-                wide[n, rows, :] = dot(full[a * third : (a + 1) * third, :], order_ref[...], ((1,), (0,)))
-                send(wide.at[n, rows], grad_outs[n].at[rows])
+        put_grad(at_ref, lambda k, x: other_ref[k, x], full, wide, order_ref, target, send)
         for copy in copies:
             copy.wait()
 
     @pl.when(at_ref[0] == 0)
     def _():
-        run((mixed_ref, input_ref), (two_ref, one_ref))
-
-    @pl.when(at_ref[0] == 1)
-    def _():
-        run((input_ref, mixed_ref), (one_ref, two_ref))
-
-
-def call(kernel, outs, scratch, name, cost, *args, out_space=pltpu.VMEM):
+        run((mixed_ref, input_ref), one_ref)
+
+    @pl.when(at_ref[0] == 1)
+    def _():
+        run((input_ref, mixed_ref), two_ref)
+
+
+def call(kernel, outs, scratch, name, cost, *args, out_space=pltpu.VMEM, within=0):
     vmem = pl.BlockSpec(memory_space=pltpu.VMEM)
     return pl.pallas_call(
         kernel,
         out_shape=tuple(jax.ShapeDtypeStruct(s, t) for s, t in outs),
-        in_specs=[pl.BlockSpec(memory_space=pltpu.SMEM)] + [vmem] * (len(args) - 1),
+        in_specs=[pl.BlockSpec(memory_space=pltpu.SMEM)] + [vmem] * (len(args) - 1 - within) + [pl.BlockSpec(memory_space=pl.ANY)] * within,
+        input_output_aliases={len(args) - i: len(outs) - i for i in range(1, within + 1)},
         out_specs=tuple([pl.BlockSpec(memory_space=out_space)] * len(outs)),
         scratch_shapes=[pltpu.VMEM(*s) if isinstance(s, tuple) else s for s in scratch],
         compiler_params=PARAMS,
@@ -358,12 +379,17 @@
     keep, give = call(
         sum_kernel, [(plane, F32), (plane, BF16)], [], "sum", 0, at, *[came[j] for j in range(1, far)], came[far], zero
     )
+    got = swap(give)
+    scratch = [((28 * width, channels), BF16), ((taps, channels), F32)]
+    weights = [((taps, channels), F32)] * 2
+    grads = call(
+        own_kernel, weights, scratch + [pltpu.SemaphoreType.DMA((3,))], "finish_own", 4 * taps * channels * channels,
+        at, *pieces, order, out_space=pl.ANY,
+    )
     mixed_out, input_grad, grad_one, grad_two = call(
-        finish_kernel,
-        [((width, PLANE), BF16)] * 2 + [((taps, channels), F32)] * 2,
-        [((28 * width, channels), BF16)] * 2
-        + [((2, taps, channels), F32), (plane, BF16), pltpu.SemaphoreType.DMA((8,))],
-        "finish", 0, at, *pieces, others, keep, swap(give), order, out_space=pl.ANY,
+        finish_kernel, [((width, PLANE), BF16)] * 2 + weights,
+        scratch + [(plane, BF16), pltpu.SemaphoreType.DMA((5,))],
+        "finish", 0, at, others, keep, got, order, *grads, out_space=pl.ANY, within=2,
     )
     shape = (width, 1, 1, PLANE)
     weights = (27, width, channels)

time: 85.5 us -> 85.8 us (level)
  Pallas kernels: 11 us -> 12.4 us
  waiting for transfers between devices: 21.4 us -> 20.2 us
    pallas_call x6 -> x7, Pallas kernels: 11 us -> 12.4 us  [call(): pl.pallas_call(kernel, out_shape=tuple((jax.ShapeDtypeStruct(s, t) for s,...]
    ppermute x8, waiting for transfers between devices: 5.35 us -> 4.11 us  [swap(): return lax.ppermute(values, 'spatial', [(0, 1), (1, 0)])]
  transfers between devices with their start and end apart: 29 -> 29, of which waited for: 14 -> 13; matrix products, arithmetic and copies ran while one was open for 0% -> 0% of each run, Pallas kernels for 3% -> 5%
where the time goes in v13:
time: 85.8 us; the launch traced here: 85.4 us
  starting transfers between devices  49.6 us (58%)
  waiting for transfers between devices  20.2 us (24%)
  Pallas kernels  12.4 us (14%)
  other arithmetic  1.21 us (1%)
  local copies, waits for them, and re-layouts  1.05 us (1%)
  between operations  0.99 us (1%)
    ppermute x8, starting transfers between devices, apart(): return lax.ppermute(values, ('z', 'spatial'), pairs)  18.3 us
    ppermute x12, starting transfers between devices, around(): lax.ppermute(values, axis, [((i + step) % size, i) for i in range(size)])  16 us
    ppermute x12, waiting for transfers between devices, around(): lax.ppermute(values, axis, [((i + step) % size, i) for i in range(size)])  13.7 us
    pallas_call x7, Pallas kernels, call(): pl.pallas_call(kernel, out_shape=tuple((jax.ShapeDtypeStruct(s, t) for s,...  12.4 us
    ppermute x8, starting transfers between devices, swap(): return lax.ppermute(values, 'spatial', [(0, 1), (1, 0)])  9.81 us
    all_to_all x1, starting transfers between devices, body(): grads = lax.all_to_all(grads, ('samples', 'x'), 0, 0, tiled=True)  5.49 us
    ppermute x8, waiting for transfers between devices, swap(): return lax.ppermute(values, 'spatial', [(0, 1), (1, 0)])  4.11 us
    ppermute x8, waiting for transfers between devices, apart(): return lax.ppermute(values, ('z', 'spatial'), pairs)  2.35 us
  transfers between devices with their start and end apart: 29, of which 13 were waited for; matrix products, arithmetic and copies ran while one was open for 0% of the time, Pallas kernels for 5%

profile of v13, /device:TPU:1, one launch (start us, length us, event | category | flops | bytes accessed | tf_op | source)
XLA Modules:
  0.0 85.4 jit_solution(3602936632511376354)
XLA Ops:
  0.6 0.8 fusion
  1.5 3.3 %collective-permute-start = (bf16[2,16,1024]{2,1,0:T(8,128)(2,1)S(1)}, bf16[2,16,1024]{2,1,0:T(8,128)(2,1)S(1)}, u32[]{:S(2)}, u32[]{:S(2)}) collective-permute-start(bf16[2,16,1024]{2,1,0:T(8,128)(2,1)S(1)} %get-tuple-element.101.pair_ref), channel_id=1, source_target_pairs={{0,1},{1,0},{2,3},{3,2},{4,5},{5,4},{6,7},{7,6},{8,9},{9,8},{10,11... | collective-permute-start | bytes 196616 | tf_op jit(solution)/shard_map/ppermute | solution.py:310
  4.8 0.9 %collective-permute-done.other_ref = bf16[2,16,1024]{2,1,0:T(8,128)(2,1)S(1)} collective-permute-done((bf16[2,16,1024]{2,1,0:T(8,128)(2,1)S(1)}, bf16[2,16,1024]{2,1,0:T(8,128)(2,1)S(1)}, u32[]{:S(2)}, u32[]{:S(2)}) %collective-permute-start) | collective-permute-done | bytes 65568 | tf_op jit(solution)/shard_map/ppermute | solution.py:310
  5.7 3.9 %collective-permute-start.1 = (bf16[2,2,16,1024]{3,2,1,0:T(8,128)(2,1)S(1)}, bf16[2,2,16,1024]{3,2,1,0:T(8,128)(2,1)S(1)}, u32[]{:S(2)}, u32[]{:S(2)}) collective-permute-start(bf16[2,2,16,1024]{3,2,1,0:T(8,128)(2,1)S(1)} %pad_maximum_fusion.2), channel_id=1, source_target_pairs={{0,8},{8,16},{16,24},{24,32},{32,40},{40,48},{48,56},{56,0},{1,57}... | collective-permute-start | bytes 393224 | tf_op jit(solution)/shard_map/ppermute | solution.py:321
  9.6 1.4 %collective-permute-start.4 = (bf16[2,16,1024]{2,1,0:T(8,128)(2,1)S(1)}, bf16[2,16,1024]{2,1,0:T(8,128)(2,1)S(1)}, u32[]{:S(2)}, u32[]{:S(2)}) collective-permute-start(bf16[2,16,1024]{2,1,0:T(8,128)(2,1)S(1)} %get-tuple-element.101.pair_ref), channel_id=1, source_target_pairs={{0,32},{8,40},{16,48},{24,56},{32,0},{40,8},{48,16},{56,24},{1,33}... | collective-permute-start | bytes 196616 | tf_op jit(solution)/shard_map/ppermute | solution.py:321
  11.1 0.1 pad_add_fusion.at_ref
  11.2 0.4 collective-permute-start.3
  11.6 4.3 %collective-permute-start.2 = (bf16[2,2,16,1024]{3,2,1,0:T(8,128)(2,1)S(1)}, bf16[2,2,16,1024]{3,2,1,0:T(8,128)(2,1)S(1)}, u32[]{:S(2)}, u32[]{:S(2)}) collective-permute-start(bf16[2,2,16,1024]{3,2,1,0:T(8,128)(2,1)S(1)} %pad_maximum_fusion.2), channel_id=1, source_target_pairs={{0,16},{8,24},{16,32},{24,40},{32,48},{40,56},{48,0},{56,8},{1,49}... | collective-permute-start | bytes 393224 | tf_op jit(solution)/shard_map/ppermute | solution.py:321
  15.8 0.0 collective-permute-done.1.refs_0_
  15.8 1.0 %copy-done.1 = bf16[27,16,512]{2,1,0:T(8,128)(2,1)S(1)} copy-done((bf16[27,16,512]{2,1,0:T(8,128)(2,1)S(1)}, bf16[27,16,512]{2,1,0:T(8,128)(2,1)}, u32[]{:S(2)}) %copy-start.1) | copy-done | bytes 442392
  16.9 1.3 %regroup.1 = (bf16[432,128]{1,0:T(8,128)(2,1)S(1)}, bf16[432,128]{1,0:T(8,128)(2,1)S(1)}, bf16[432,128]{1,0:T(8,128)(2,1)S(1)}, bf16[432,128]{1,0:T(8,128)(2,1)S(1)}, bf16[512,512]{1,0:T(8,128)(2,1)S(1)}) custom-call(s32[4]{0:T(128)S(1)} %pad_add_fusion.at_ref, bf16[432,512]{1,0:T(8,128)(2,1)S(1)} %bitcast.34, bf16[432,512]{1,0:T(8,128)(2,1)S(1)} %bitcast.35), custom_call_target="tpu_custom_call" | custom-call | flops 226492416 | tf_op jit(solution)/shard_map/regroup/pallas_call | solution.py:296
  18.2 2.6 %collective-permute-start.5 = (bf16[432,128]{1,0:T(8,128)(2,1)S(1)}, bf16[432,128]{1,0:T(8,128)(2,1)S(1)}, u32[]{:S(2)}, u32[]{:S(2)}) collective-permute-start(bf16[432,128]{1,0:T(8,128)(2,1)S(1)} %get-tuple-element.53), channel_id=1, source_target_pairs={{2,0},{4,2},{6,4},{0,6},{3,1},{5,3},{7,5},{1,7},{10,8},{12,10},{14... | collective-permute-start | bytes 331784 | tf_op jit(solution)/shard_map/ppermute | solution.py:315
  20.7 0.5 collective-permute-start.6
  21.3 0.0 collective-permute-done.4.refs_3_
  21.3 0.6 collective-permute-start.7
  21.9 0.0 collective-permute-done.3.refs_2_
  21.9 2.3 %collective-permute-done.2.refs_1_ = bf16[2,2,16,1024]{3,2,1,0:T(8,128)(2,1)S(1)} collective-permute-done((bf16[2,2,16,1024]{3,2,1,0:T(8,128)(2,1)S(1)}, bf16[2,2,16,1024]{3,2,1,0:T(8,128)(2,1)S(1)}, u32[]{:S(2)}, u32[]{:S(2)}) %collective-permute-start.2) | collective-permute-done | bytes 131104 | tf_op jit(solution)/shard_map/ppermute | solution.py:321
  24.2 0.7 collective-permute-done.5.refs_6_
  24.9 2.1 %collective-permute-done.6.refs_7_ = bf16[432,128]{1,0:T(8,128)(2,1)S(1)} collective-permute-done((bf16[432,128]{1,0:T(8,128)(2,1)S(1)}, bf16[432,128]{1,0:T(8,128)(2,1)S(1)}, u32[]{:S(2)}, u32[]{:S(2)}) %collective-permute-start.6) | collective-permute-done | bytes 110624 | tf_op jit(solution)/shard_map/ppermute | solution.py:315
  27.0 1.8 %collective-permute-done.7.refs_8_ = bf16[432,128]{1,0:T(8,128)(2,1)S(1)} collective-permute-done((bf16[432,128]{1,0:T(8,128)(2,1)S(1)}, bf16[432,128]{1,0:T(8,128)(2,1)S(1)}, u32[]{:S(2)}, u32[]{:S(2)}) %collective-permute-start.7) | collective-permute-done | bytes 110624 | tf_op jit(solution)/shard_map/ppermute | solution.py:315
  28.9 0.5 collective-permute-start.8
  29.4 1.1 %collective-permute-done.8.refs_4_ = bf16[7,16,1024]{2,1,0:T(8,128)(2,1)S(1)} collective-permute-done((bf16[7,16,1024]{2,1,0:T(8,128)(2,1)S(1)}, bf16[7,16,1024]{2,1,0:T(8,128)(2,1)S(1)}, u32[]{:S(2)}, u32[]{:S(2)}) %collective-permute-start.8) | collective-permute-done | bytes 229408 | tf_op jit(solution)/shard_map/ppermute | solution.py:310
  30.5 2.6 %conv_in.1 = (f32[2,16,1024]{2,1,0:T(8,128)S(1)}, bf16[2,16,1024]{2,1,0:T(8,128)(2,1)S(1)}, bf16[2,16,1024]{2,1,0:T(8,128)(2,1)S(1)}, bf16[2,16,1024]{2,1,0:T(8,...) custom-call(s32[4]{0:T(128)S(1)} %pad_add_fusion.at_ref, ...), custom_call_target="tpu_custom_call" | custom-call | flops 603979776 | tf_op jit(solution)/shard_map/conv_in/pallas_call | solution.py:296
  33.1 0.4 collective-permute-start.17
  33.5 0.5 collective-permute-start.9
  34.0 0.0 collective-permute-start.10
  34.0 2.7 %collective-permute-start.11 = (bf16[2,16,1024]{2,1,0:T(8,128)(2,1)S(1)}, bf16[2,16,1024]{2,1,0:T(8,128)(2,1)S(1)}, u32[]{:S(2)}, u32[]{:S(2)}) collective-permute-start(bf16[2,16,1024]{2,1,0:T(8,128)(2,1)S(1)} %get-tuple-element.67), channel_id=1, source_target_pairs={{2,0},{4,2},{6,4},{0,6},{3,1},{5,3},{7,5},{1,7},{10,8},{12,10},{14... | collective-permute-start | bytes 196616 | tf_op jit(solution)/shard_map/ppermute | solution.py:315
  36.7 1.0 %collective-permute-start.16 = (bf16[4,432,128]{2,1,0:T(8,128)(2,1)S(1)}, bf16[4,432,128]{2,1,0:T(8,128)(2,1)S(1)}, u32[]{:S(2)}, u32[]{:S(2)}) collective-permute-start(bf16[4,432,128]{2,1,0:T(8,128)(2,1)S(1)} %get-tuple-element.68), channel_id=1, source_target_pairs={{0,1},{1,0},{2,3},{3,2},{4,5},{5,4},{6,7},{7,6},{8,9},{9,8},{10,11... | collective-permute-start | bytes 1327112 | tf_op jit(solution)/shard_map/ppermute | solution.py:310
  37.7 0.8 collective-permute-done.9
  38.6 1.8 %collective-permute-done.10 = bf16[2,16,1024]{2,1,0:T(8,128)(2,1)S(1)} collective-permute-done((bf16[2,16,1024]{2,1,0:T(8,128)(2,1)S(1)}, bf16[2,16,1024]{2,1,0:T(8,128)(2,1)S(1)}, u32[]{:S(2)}, u32[]{:S(2)}) %collective-permute-start.10) | collective-permute-done | bytes 65568 | tf_op jit(solution)/shard_map/ppermute | solution.py:315
  40.4 0.0 collective-permute-done.11
  40.4 0.6 collective-permute-start.12
  41.1 1.0 %collective-permute-done.12.other_ref = f32[2,16,1024]{2,1,0:T(8,128)S(1)} collective-permute-done((f32[2,16,1024]{2,1,0:T(8,128)S(1)}, f32[2,16,1024]{2,1,0:T(8,128)S(1)}, u32[]{:S(2)}, u32[]{:S(2)}) %collective-permute-start.12) | collective-permute-done | bytes 131104 | tf_op jit(solution)/shard_map/ppermute | solution.py:310
  42.1 0.6 act.1.refs_0_
  42.7 0.7 collective-permute-start.15
  43.3 2.0 %collective-permute-start.14 = (bf16[2,16,1024]{2,1,0:T(8,128)(2,1)S(1)}, bf16[2,16,1024]{2,1,0:T(8,128)(2,1)S(1)}, u32[]{:S(2)}, u32[]{:S(2)}) collective-permute-start(bf16[2,16,1024]{2,1,0:T(8,128)(2,1)S(1)} %act.1.refs_0_), channel_id=1, source_target_pairs={{6,0},{0,2},{2,4},{4,6},{7,1},{1,3},{3,5},{5,7},{14,8},{8,10},{10,... | collective-permute-start | bytes 196616 | tf_op jit(solution)/shard_map/ppermute | solution.py:315
  45.3 0.7 collective-permute-start.13
  46.0 1.4 %collective-permute-done.15.refs_3_ = bf16[2,16,1024]{2,1,0:T(8,128)(2,1)S(1)} collective-permute-done((bf16[2,16,1024]{2,1,0:T(8,128)(2,1)S(1)}, bf16[2,16,1024]{2,1,0:T(8,128)(2,1)S(1)}, u32[]{:S(2)}, u32[]{:S(2)}) %collective-permute-start.15) | collective-permute-done | bytes 65568 | tf_op jit(solution)/shard_map/ppermute | solution.py:315
  47.4 2.0 %collective-permute-done.14.refs_2_ = bf16[2,16,1024]{2,1,0:T(8,128)(2,1)S(1)} collective-permute-done((bf16[2,16,1024]{2,1,0:T(8,128)(2,1)S(1)}, bf16[2,16,1024]{2,1,0:T(8,128)(2,1)S(1)}, u32[]{:S(2)}, u32[]{:S(2)}) %collective-permute-start.14) | collective-permute-done | bytes 65568 | tf_op jit(solution)/shard_map/ppermute | solution.py:315
  49.4 0.0 collective-permute-done.13.refs_1_
  49.4 0.0 collective-permute-done.16.refs_4_
  49.4 0.0 collective-permute-done.17.refs_5_
  49.4 3.7 %conv_out.1 = (bf16[2,16,1024]{2,1,0:T(8,128)(2,1)S(1)}, bf16[3,2,16,1024]{3,2,1,0:T(8,128)(2,1)S(1)}, bf16[16,1024]{1,0:T(8,128)(2,1)S(1)}, bf16[7,16,1024]{2,1,0:T(8,128)(2,1)S(1)}, bf16[16,112,128]{2,1,0:T(8,128)(2,1)}) custom-call(s32[4]{0:T(128)S(1)} %pad_add_fusion.at_ref, bf16[2,16,1024]{2,1,0:T(8,128)(2,1)S(1)} %act.1.refs_0_, ...), custom_call_target="tpu_custom_call" | custom-call | flops 1207959552 | tf_op jit(solution)/shard_map/conv_out/pallas_call | solution.py:296
  53.1 5.5 %all-to-all-start = ((bf16[16,112,128]{2,1,0:T(8,128)(2,1)}), bf16[16,112,128]{2,1,0:T(8,128)(2,1)S(1)}, u32[]{:S(2)}, u32[]{:S(2)}) async-start(bf16[16,112,128]{2,1,0:T(8,128)(2,1)} %get-tuple-element.70), calls=%async_computation | async-start | bytes 917504 | tf_op jit(solution)/shard_map/all_to_all | solution.py:369
  58.6 1.8 %collective-permute-start.18 = (bf16[7,16,1024]{2,1,0:T(8,128)(2,1)S(1)}, bf16[7,16,1024]{2,1,0:T(8,128)(2,1)S(1)}, u32[]{:S(2)}, u32[]{:S(2)}) collective-permute-start(bf16[7,16,1024]{2,1,0:T(8,128)(2,1)S(1)} %get-tuple-element.72), channel_id=1, source_target_pairs={{0,1},{1,0},{2,3},{3,2},{4,5},{5,4},{6,7},{7,6},{8,9},{9,8},{10,11... | collective-permute-start | bytes 688136 | tf_op jit(solution)/shard_map/ppermute | solution.py:310
  60.4 1.1 %collective-permute-done.18 = bf16[7,16,1024]{2,1,0:T(8,128)(2,1)S(1)} collective-permute-done((bf16[7,16,1024]{2,1,0:T(8,128)(2,1)S(1)}, bf16[7,16,1024]{2,1,0:T(8,128)(2,1)S(1)}, u32[]{:S(2)}, u32[]{:S(2)}) %collective-permute-start.18) | collective-permute-done | bytes 229408 | tf_op jit(solution)/shard_map/ppermute | solution.py:310
  61.5 2.9 %collective-permute-start.19 = (bf16[2,16,1024]{2,1,0:T(8,128)(2,1)S(1)}, bf16[2,16,1024]{2,1,0:T(8,128)(2,1)S(1)}, u32[]{:S(2)}, u32[]{:S(2)}) collective-permute-start(bf16[2,16,1024]{2,1,0:T(8,128)(2,1)S(1)} %pad_maximum_fusion.7), channel_id=1, source_target_pairs={{0,32},{8,40},{16,48},{24,56},{32,0},{40,8},{48,16},{56,24},{1,33}... | collective-permute-start | bytes 196616 | tf_op jit(solution)/shard_map/ppermute | solution.py:321
  64.5 2.0 %collective-permute-start.23 = (bf16[2,2,16,1024]{3,2,1,0:T(8,128)(2,1)S(1)}, bf16[2,2,16,1024]{3,2,1,0:T(8,128)(2,1)S(1)}, u32[]{:S(2)}, u32[]{:S(2)}) collective-permute-start(bf16[2,2,16,1024]{3,2,1,0:T(8,128)(2,1)S(1)} %pad_maximum_fusion.3), channel_id=1, source_target_pairs={{0,8},{8,16},{16,24},{24,32},{32,40},{40,48},{48,56},{56,0},{1,57}... | collective-permute-start | bytes 393224 | tf_op jit(solution)/shard_map/ppermute | solution.py:321
  66.5 1.4 %collective-permute-start.24 = (bf16[2,2,16,1024]{3,2,1,0:T(8,128)(2,1)S(1)}, bf16[2,2,16,1024]{3,2,1,0:T(8,128)(2,1)S(1)}, u32[]{:S(2)}, u32[]{:S(2)}) collective-permute-start(bf16[2,2,16,1024]{3,2,1,0:T(8,128)(2,1)S(1)} %pad_maximum_fusion.4), channel_id=1, source_target_pairs={{0,16},{8,24},{16,32},{24,40},{32,48},{40,56},{48,0},{56,8},{1,49}... | collective-permute-start | bytes 393224 | tf_op jit(solution)/shard_map/ppermute | solution.py:321
  67.9 1.9 %collective-permute-start.25 = (bf16[2,2,16,1024]{3,2,1,0:T(8,128)(2,1)S(1)}, bf16[2,2,16,1024]{3,2,1,0:T(8,128)(2,1)S(1)}, u32[]{:S(2)}, u32[]{:S(2)}) collective-permute-start(bf16[2,2,16,1024]{3,2,1,0:T(8,128)(2,1)S(1)} %pad_maximum_fusion.5), channel_id=1, source_target_pairs={{0,24},{8,32},{16,40},{24,48},{32,56},{40,0},{48,8},{56,16},{1,41}... | collective-permute-start | bytes 393224 | tf_op jit(solution)/shard_map/ppermute | solution.py:321
  69.8 0.0 all-to-all-done
  69.8 0.1 reduce_sum.12.p0_ref
  69.9 0.0 collective-permute-done.19.refs_3_
  69.9 3.2 %collective-permute-start.22 = (bf16[4,112,128]{2,1,0:T(8,128)(2,1)S(1)}, bf16[4,112,128]{2,1,0:T(8,128)(2,1)S(1)}, u32[]{:S(2)}, u32[]{:S(2)}) collective-permute-start(bf16[4,112,128]{2,1,0:T(8,128)(2,1)S(1)} %reduce_sum.12.p0_ref), channel_id=1, source_target_pairs={{128,0},{192,64},{0,128},{64,192},{129,1},{193,65},{1,129},{65,193... | collective-permute-start | bytes 344072 | tf_op jit(solution)/shard_map/ppermute | solution.py:315
  73.1 0.3 collective-permute-start.21
  73.4 0.0 collective-permute-done.23.refs_0_
  73.4 2.4 %collective-permute-start.20 = (bf16[4,112,128]{2,1,0:T(8,128)(2,1)S(1)}, bf16[4,112,128]{2,1,0:T(8,128)(2,1)S(1)}, u32[]{:S(2)}, u32[]{:S(2)}) collective-permute-start(bf16[4,112,128]{2,1,0:T(8,128)(2,1)S(1)} %reduce_sum.12.p0_ref), channel_id=1, source_target_pairs={{64,0},{128,64},{192,128},{0,192},{65,1},{129,65},{193,129},{1,193... | collective-permute-start | bytes 344072 | tf_op jit(solution)/shard_map/ppermute | solution.py:315
  75.8 3.0 %collective-permute-done.21.p2_ref = bf16[4,112,128]{2,1,0:T(8,128)(2,1)S(1)} collective-permute-done((bf16[4,112,128]{2,1,0:T(8,128)(2,1)S(1)}, bf16[4,112,128]{2,1,0:T(8,128)(2,1)S(1)}, u32[]{:S(2)}, u32[]{:S(2)}) %collective-permute-start.21) | collective-permute-done | bytes 114720 | tf_op jit(solution)/shard_map/ppermute | solution.py:315
  78.8 0.1 pad_maximum_fusion
  78.9 2.0 %collective-permute-start.26 = (bf16[4,4,112,128]{3,2,1,0:T(8,128)(2,1)S(1)}, bf16[4,4,112,128]{3,2,1,0:T(8,128)(2,1)S(1)}, u32[]{:S(2)}, u32[]{:S(2)}) collective-permute-start(bf16[4,4,112,128]{3,2,1,0:T(8,128)(2,1)S(1)} %pad_maximum_fusion), channel_id=1, source_target_pairs={{0,1},{1,0},{2,3},{3,2},{4,5},{5,4},{6,7},{7,6},{8,9},{9,8},{10,11... | collective-permute-start | bytes 1376264 | tf_op jit(solution)/shard_map/ppermute | solution.py:310
  80.9 0.6 sum.1
  81.5 0.1 collective-permute-start.27
  81.6 1.8 %finish_own.1 = (f32[432,512]{1,0:T(8,128)}, f32[432,512]{1,0:T(8,128)}) custom-call(s32[4]{0:T(128)S(1)} %pad_add_fusion.at_ref, bf16[4,112,128]{2,1,0:T(8,128)(2,1)S(1)} %reduce_sum.12.p0_ref, bf16[4,112,128]{2,1,0:T(8,128)(2,1)S(1)} %collective-permute-done.20.p1_ref, bf16[4,112,128]{2,1,0:T(8,128)(2,1)S(1)} %collective-permute-done.21.p2_ref, ...), custom_call_target="tpu_custom_call" | custom-call | flops 452984832 | tf_op jit(solution)/shard_map/finish_own/pallas_call | solution.py:296
  83.4 1.8 %finish.1 = (bf16[16,1024]{1,0:T(8,128)(2,1)}, bf16[16,1024]{1,0:T(8,128)(2,1)}, f32[432,512]{1,0:T(8,128)}, f32[432,512]{1,0:T(8,128)}) custom-call(s32[4]{0:T(128)S(1)} %pad_add_fusion.at_ref, bf16[4,4,112,128]{3,2,1,0:T(8,128)(2,1)S(1)} %collective-permute-done.26.other_ref, ...), custom_call_target="tpu_custom_call", output_to_operand_aliasing={{3}: (6, {}), {2}: (5, {})} | custom-call | tf_op jit(solution)/shard_map/finish/pallas_call | solution.py:296
  (22 shorter events, 0.2 us)
Async XLA Ops:
  0.6 15.2 %copy-start = (bf16[27,16,512]{2,1,0:T(8,128)(2,1)S(1)}, bf16[27,16,512]{2,1,0:T(8,128)(2,1)}, u32[]{:S(2)}) copy-start(bf16[27,16,512]{2,1,0:T(8,128)(2,1)} %param.5) | copy-start | bytes 1327108
  1.5 4.2 %collective-permute-start = (bf16[2,16,1024]{2,1,0:T(8,128)(2,1)S(1)}, bf16[2,16,1024]{2,1,0:T(8,128)(2,1)S(1)}, u32[]{:S(2)}, u32[]{:S(2)}) collective-permute-start(bf16[2,16,1024]{2,1,0:T(8,128)(2,1)S(1)} %get-tuple-element.101.pair_ref), channel_id=1, source_target_pairs={{0,1},{1,0},{2,3},{3,2},{4,5},{5,4},{6,7},{7,6},{8,9},{9,8},{10,11... | collective-permute-start | bytes 196616 | tf_op jit(solution)/shard_map/ppermute | solution.py:310
  5.7 10.1 %collective-permute-start.1 = (bf16[2,2,16,1024]{3,2,1,0:T(8,128)(2,1)S(1)}, bf16[2,2,16,1024]{3,2,1,0:T(8,128)(2,1)S(1)}, u32[]{:S(2)}, u32[]{:S(2)}) collective-permute-start(bf16[2,2,16,1024]{3,2,1,0:T(8,128)(2,1)S(1)} %pad_maximum_fusion.2), channel_id=1, source_target_pairs={{0,8},{8,16},{16,24},{24,32},{32,40},{40,48},{48,56},{56,0},{1,57}... | collective-permute-start | bytes 393224 | tf_op jit(solution)/shard_map/ppermute | solution.py:321
  9.6 11.6 %collective-permute-start.4 = (bf16[2,16,1024]{2,1,0:T(8,128)(2,1)S(1)}, bf16[2,16,1024]{2,1,0:T(8,128)(2,1)S(1)}, u32[]{:S(2)}, u32[]{:S(2)}) collective-permute-start(bf16[2,16,1024]{2,1,0:T(8,128)(2,1)S(1)} %get-tuple-element.101.pair_ref), channel_id=1, source_target_pairs={{0,32},{8,40},{16,48},{24,56},{32,0},{40,8},{48,16},{56,24},{1,33}... | collective-permute-start | bytes 196616 | tf_op jit(solution)/shard_map/ppermute | solution.py:321
  11.2 10.7 %collective-permute-start.3 = (bf16[2,2,16,1024]{3,2,1,0:T(8,128)(2,1)S(1)}, bf16[2,2,16,1024]{3,2,1,0:T(8,128)(2,1)S(1)}, u32[]{:S(2)}, u32[]{:S(2)}) collective-permute-start(bf16[2,2,16,1024]{3,2,1,0:T(8,128)(2,1)S(1)} %pad_maximum_fusion.2), channel_id=1, source_target_pairs={{0,24},{8,32},{16,40},{24,48},{32,56},{40,0},{48,8},{56,16},{1,41}... | collective-permute-start | bytes 393224 | tf_op jit(solution)/shard_map/ppermute | solution.py:321
  11.6 12.6 %collective-permute-start.2 = (bf16[2,2,16,1024]{3,2,1,0:T(8,128)(2,1)S(1)}, bf16[2,2,16,1024]{3,2,1,0:T(8,128)(2,1)S(1)}, u32[]{:S(2)}, u32[]{:S(2)}) collective-permute-start(bf16[2,2,16,1024]{3,2,1,0:T(8,128)(2,1)S(1)} %pad_maximum_fusion.2), channel_id=1, source_target_pairs={{0,16},{8,24},{16,32},{24,40},{32,48},{40,56},{48,0},{56,8},{1,49}... | collective-permute-start | bytes 393224 | tf_op jit(solution)/shard_map/ppermute | solution.py:321
  15.8 1.0 %copy-start.1 = (bf16[27,16,512]{2,1,0:T(8,128)(2,1)S(1)}, bf16[27,16,512]{2,1,0:T(8,128)(2,1)}, u32[]{:S(2)}) copy-start(bf16[27,16,512]{2,1,0:T(8,128)(2,1)} %param.6) | copy-start | bytes 1327108
  18.2 6.7 %collective-permute-start.5 = (bf16[432,128]{1,0:T(8,128)(2,1)S(1)}, bf16[432,128]{1,0:T(8,128)(2,1)S(1)}, u32[]{:S(2)}, u32[]{:S(2)}) collective-permute-start(bf16[432,128]{1,0:T(8,128)(2,1)S(1)} %get-tuple-element.53), channel_id=1, source_target_pairs={{2,0},{4,2},{6,4},{0,6},{3,1},{5,3},{7,5},{1,7},{10,8},{12,10},{14... | collective-permute-start | bytes 331784 | tf_op jit(solution)/shard_map/ppermute | solution.py:315
  20.7 6.3 %collective-permute-start.6 = (bf16[432,128]{1,0:T(8,128)(2,1)S(1)}, bf16[432,128]{1,0:T(8,128)(2,1)S(1)}, u32[]{:S(2)}, u32[]{:S(2)}) collective-permute-start(bf16[432,128]{1,0:T(8,128)(2,1)S(1)} %get-tuple-element.54), channel_id=1, source_target_pairs={{4,0},{6,2},{0,4},{2,6},{5,1},{7,3},{1,5},{3,7},{12,8},{14,10},{8,... | collective-permute-start | bytes 331784 | tf_op jit(solution)/shard_map/ppermute | solution.py:315
  21.3 7.6 %collective-permute-start.7 = (bf16[432,128]{1,0:T(8,128)(2,1)S(1)}, bf16[432,128]{1,0:T(8,128)(2,1)S(1)}, u32[]{:S(2)}, u32[]{:S(2)}) collective-permute-start(bf16[432,128]{1,0:T(8,128)(2,1)S(1)} %get-tuple-element.55), channel_id=1, source_target_pairs={{6,0},{0,2},{2,4},{4,6},{7,1},{1,3},{3,5},{5,7},{14,8},{8,10},{10,... | collective-permute-start | bytes 331784 | tf_op jit(solution)/shard_map/ppermute | solution.py:315
  28.9 1.6 %collective-permute-start.8 = (bf16[7,16,1024]{2,1,0:T(8,128)(2,1)S(1)}, bf16[7,16,1024]{2,1,0:T(8,128)(2,1)S(1)}, u32[]{:S(2)}, u32[]{:S(2)}) collective-permute-start(bf16[7,16,1024]{2,1,0:T(8,128)(2,1)S(1)} %pad_maximum_fusion.1), channel_id=1, source_target_pairs={{0,1},{1,0},{2,3},{3,2},{4,5},{5,4},{6,7},{7,6},{8,9},{9,8},{10,11... | collective-permute-start | bytes 688136 | tf_op jit(solution)/shard_map/ppermute | solution.py:310
  33.1 16.3 %collective-permute-start.17 = (bf16[8,2,16,1024]{3,2,1,0:T(8,128)(2,1)S(1)}, bf16[8,2,16,1024]{3,2,1,0:T(8,128)(2,1)S(1)}, u32[]{:S(2)}, u32[]{:S(2)}) collective-permute-start(bf16[8,2,16,1024]{3,2,1,0:T(8,128)(2,1)S(1)} %get-tuple-element.69), channel_id=1, source_target_pairs={{0,1},{1,0},{2,3},{3,2},{4,5},{5,4},{6,7},{7,6},{8,9},{9,8},{10,11... | collective-permute-start | bytes 1572872 | tf_op jit(solution)/shard_map/ppermute | solution.py:310
  33.5 5.0 %collective-permute-start.9 = (bf16[2,16,1024]{2,1,0:T(8,128)(2,1)S(1)}, bf16[2,16,1024]{2,1,0:T(8,128)(2,1)S(1)}, u32[]{:S(2)}, u32[]{:S(2)}) collective-permute-start(bf16[2,16,1024]{2,1,0:T(8,128)(2,1)S(1)} %get-tuple-element.65), channel_id=1, source_target_pairs={{4,0},{6,2},{0,4},{2,6},{5,1},{7,3},{1,5},{3,7},{12,8},{14,10},{8,... | collective-permute-start | bytes 196616 | tf_op jit(solution)/shard_map/ppermute | solution.py:315
  34.0 6.4 %collective-permute-start.10 = (bf16[2,16,1024]{2,1,0:T(8,128)(2,1)S(1)}, bf16[2,16,1024]{2,1,0:T(8,128)(2,1)S(1)}, u32[]{:S(2)}, u32[]{:S(2)}) collective-permute-start(bf16[2,16,1024]{2,1,0:T(8,128)(2,1)S(1)} %get-tuple-element.66), channel_id=1, source_target_pairs={{6,0},{0,2},{2,4},{4,6},{7,1},{1,3},{3,5},{5,7},{14,8},{8,10},{10,... | collective-permute-start | bytes 196616 | tf_op jit(solution)/shard_map/ppermute | solution.py:315
  34.0 6.4 %collective-permute-start.11 = (bf16[2,16,1024]{2,1,0:T(8,128)(2,1)S(1)}, bf16[2,16,1024]{2,1,0:T(8,128)(2,1)S(1)}, u32[]{:S(2)}, u32[]{:S(2)}) collective-permute-start(bf16[2,16,1024]{2,1,0:T(8,128)(2,1)S(1)} %get-tuple-element.67), channel_id=1, source_target_pairs={{2,0},{4,2},{6,4},{0,6},{3,1},{5,3},{7,5},{1,7},{10,8},{12,10},{14... | collective-permute-start | bytes 196616 | tf_op jit(solution)/shard_map/ppermute | solution.py:315
  36.7 12.7 %collective-permute-start.16 = (bf16[4,432,128]{2,1,0:T(8,128)(2,1)S(1)}, bf16[4,432,128]{2,1,0:T(8,128)(2,1)S(1)}, u32[]{:S(2)}, u32[]{:S(2)}) collective-permute-start(bf16[4,432,128]{2,1,0:T(8,128)(2,1)S(1)} %get-tuple-element.68), channel_id=1, source_target_pairs={{0,1},{1,0},{2,3},{3,2},{4,5},{5,4},{6,7},{7,6},{8,9},{9,8},{10,11... | collective-permute-start | bytes 1327112 | tf_op jit(solution)/shard_map/ppermute | solution.py:310
  40.4 1.6 %collective-permute-start.12 = (f32[2,16,1024]{2,1,0:T(8,128)S(1)}, f32[2,16,1024]{2,1,0:T(8,128)S(1)}, u32[]{:S(2)}, u32[]{:S(2)}) collective-permute-start(f32[2,16,1024]{2,1,0:T(8,128)S(1)} %add_add_fusion.own_ref), channel_id=1, source_target_pairs={{0,1},{1,0},{2,3},{3,2},{4,5},{5,4},{6,7},{7,6},{8,9},{9,8},{10,11... | collective-permute-start | bytes 393224 | tf_op jit(solution)/shard_map/ppermute | solution.py:310
  42.7 4.8 %collective-permute-start.15 = (bf16[2,16,1024]{2,1,0:T(8,128)(2,1)S(1)}, bf16[2,16,1024]{2,1,0:T(8,128)(2,1)S(1)}, u32[]{:S(2)}, u32[]{:S(2)}) collective-permute-start(bf16[2,16,1024]{2,1,0:T(8,128)(2,1)S(1)} %act.1.refs_0_), channel_id=1, source_target_pairs={{4,0},{6,2},{0,4},{2,6},{5,1},{7,3},{1,5},{3,7},{12,8},{14,10},{8,... | collective-permute-start | bytes 196616 | tf_op jit(solution)/shard_map/ppermute | solution.py:315
  43.3 6.1 %collective-permute-start.14 = (bf16[2,16,1024]{2,1,0:T(8,128)(2,1)S(1)}, bf16[2,16,1024]{2,1,0:T(8,128)(2,1)S(1)}, u32[]{:S(2)}, u32[]{:S(2)}) collective-permute-start(bf16[2,16,1024]{2,1,0:T(8,128)(2,1)S(1)} %act.1.refs_0_), channel_id=1, source_target_pairs={{6,0},{0,2},{2,4},{4,6},{7,1},{1,3},{3,5},{5,7},{14,8},{8,10},{10,... | collective-permute-start | bytes 196616 | tf_op jit(solution)/shard_map/ppermute | solution.py:315
  45.3 4.1 %collective-permute-start.13 = (bf16[2,16,1024]{2,1,0:T(8,128)(2,1)S(1)}, bf16[2,16,1024]{2,1,0:T(8,128)(2,1)S(1)}, u32[]{:S(2)}, u32[]{:S(2)}) collective-permute-start(bf16[2,16,1024]{2,1,0:T(8,128)(2,1)S(1)} %act.1.refs_0_), channel_id=1, source_target_pairs={{2,0},{4,2},{6,4},{0,6},{3,1},{5,3},{7,5},{1,7},{10,8},{12,10},{14... | collective-permute-start | bytes 196616 | tf_op jit(solution)/shard_map/ppermute | solution.py:315
  53.1 16.8 %all-to-all-start = ((bf16[16,112,128]{2,1,0:T(8,128)(2,1)}), bf16[16,112,128]{2,1,0:T(8,128)(2,1)S(1)}, u32[]{:S(2)}, u32[]{:S(2)}) async-start(bf16[16,112,128]{2,1,0:T(8,128)(2,1)} %get-tuple-element.70), calls=%async_computation | async-start | bytes 917504 | tf_op jit(solution)/shard_map/all_to_all | solution.py:369
  58.6 2.9 %collective-permute-start.18 = (bf16[7,16,1024]{2,1,0:T(8,128)(2,1)S(1)}, bf16[7,16,1024]{2,1,0:T(8,128)(2,1)S(1)}, u32[]{:S(2)}, u32[]{:S(2)}) collective-permute-start(bf16[7,16,1024]{2,1,0:T(8,128)(2,1)S(1)} %get-tuple-element.72), channel_id=1, source_target_pairs={{0,1},{1,0},{2,3},{3,2},{4,5},{5,4},{6,7},{7,6},{8,9},{9,8},{10,11... | collective-permute-start | bytes 688136 | tf_op jit(solution)/shard_map/ppermute | solution.py:310
  61.5 8.4 %collective-permute-start.19 = (bf16[2,16,1024]{2,1,0:T(8,128)(2,1)S(1)}, bf16[2,16,1024]{2,1,0:T(8,128)(2,1)S(1)}, u32[]{:S(2)}, u32[]{:S(2)}) collective-permute-start(bf16[2,16,1024]{2,1,0:T(8,128)(2,1)S(1)} %pad_maximum_fusion.7), channel_id=1, source_target_pairs={{0,32},{8,40},{16,48},{24,56},{32,0},{40,8},{48,16},{56,24},{1,33}... | collective-permute-start | bytes 196616 | tf_op jit(solution)/shard_map/ppermute | solution.py:321
  64.5 8.9 %collective-permute-start.23 = (bf16[2,2,16,1024]{3,2,1,0:T(8,128)(2,1)S(1)}, bf16[2,2,16,1024]{3,2,1,0:T(8,128)(2,1)S(1)}, u32[]{:S(2)}, u32[]{:S(2)}) collective-permute-start(bf16[2,2,16,1024]{3,2,1,0:T(8,128)(2,1)S(1)} %pad_maximum_fusion.3), channel_id=1, source_target_pairs={{0,8},{8,16},{16,24},{24,32},{32,40},{40,48},{48,56},{56,0},{1,57}... | collective-permute-start | bytes 393224 | tf_op jit(solution)/shard_map/ppermute | solution.py:321
  66.5 9.3 %collective-permute-start.24 = (bf16[2,2,16,1024]{3,2,1,0:T(8,128)(2,1)S(1)}, bf16[2,2,16,1024]{3,2,1,0:T(8,128)(2,1)S(1)}, u32[]{:S(2)}, u32[]{:S(2)}) collective-permute-start(bf16[2,2,16,1024]{3,2,1,0:T(8,128)(2,1)S(1)} %pad_maximum_fusion.4), channel_id=1, source_target_pairs={{0,16},{8,24},{16,32},{24,40},{32,48},{40,56},{48,0},{56,8},{1,49}... | collective-permute-start | bytes 393224 | tf_op jit(solution)/shard_map/ppermute | solution.py:321
  67.9 7.8 %collective-permute-start.25 = (bf16[2,2,16,1024]{3,2,1,0:T(8,128)(2,1)S(1)}, bf16[2,2,16,1024]{3,2,1,0:T(8,128)(2,1)S(1)}, u32[]{:S(2)}, u32[]{:S(2)}) collective-permute-start(bf16[2,2,16,1024]{3,2,1,0:T(8,128)(2,1)S(1)} %pad_maximum_fusion.5), channel_id=1, source_target_pairs={{0,24},{8,32},{16,40},{24,48},{32,56},{40,0},{48,8},{56,16},{1,41}... | collective-permute-start | bytes 393224 | tf_op jit(solution)/shard_map/ppermute | solution.py:321
  69.9 5.8 %collective-permute-start.22 = (bf16[4,112,128]{2,1,0:T(8,128)(2,1)S(1)}, bf16[4,112,128]{2,1,0:T(8,128)(2,1)S(1)}, u32[]{:S(2)}, u32[]{:S(2)}) collective-permute-start(bf16[4,112,128]{2,1,0:T(8,128)(2,1)S(1)} %reduce_sum.12.p0_ref), channel_id=1, source_target_pairs={{128,0},{192,64},{0,128},{64,192},{129,1},{193,65},{1,129},{65,193... | collective-permute-start | bytes 344072 | tf_op jit(solution)/shard_map/ppermute | solution.py:315
  73.1 5.7 %collective-permute-start.21 = (bf16[4,112,128]{2,1,0:T(8,128)(2,1)S(1)}, bf16[4,112,128]{2,1,0:T(8,128)(2,1)S(1)}, u32[]{:S(2)}, u32[]{:S(2)}) collective-permute-start(bf16[4,112,128]{2,1,0:T(8,128)(2,1)S(1)} %reduce_sum.12.p0_ref), channel_id=1, source_target_pairs={{192,0},{0,64},{64,128},{128,192},{193,1},{1,65},{65,129},{129,193... | collective-permute-start | bytes 344072 | tf_op jit(solution)/shard_map/ppermute | solution.py:315
  73.4 5.4 %collective-permute-start.20 = (bf16[4,112,128]{2,1,0:T(8,128)(2,1)S(1)}, bf16[4,112,128]{2,1,0:T(8,128)(2,1)S(1)}, u32[]{:S(2)}, u32[]{:S(2)}) collective-permute-start(bf16[4,112,128]{2,1,0:T(8,128)(2,1)S(1)} %reduce_sum.12.p0_ref), channel_id=1, source_target_pairs={{64,0},{128,64},{192,128},{0,192},{65,1},{129,65},{193,129},{1,193... | collective-permute-start | bytes 344072 | tf_op jit(solution)/shard_map/ppermute | solution.py:315
  78.9 4.5 %collective-permute-start.26 = (bf16[4,4,112,128]{3,2,1,0:T(8,128)(2,1)S(1)}, bf16[4,4,112,128]{3,2,1,0:T(8,128)(2,1)S(1)}, u32[]{:S(2)}, u32[]{:S(2)}) collective-permute-start(bf16[4,4,112,128]{3,2,1,0:T(8,128)(2,1)S(1)} %pad_maximum_fusion), channel_id=1, source_target_pairs={{0,1},{1,0},{2,3},{3,2},{4,5},{5,4},{6,7},{7,6},{8,9},{9,8},{10,11... | collective-permute-start | bytes 1376264 | tf_op jit(solution)/shard_map/ppermute | solution.py:310
  81.5 1.9 %collective-permute-start.27 = (bf16[2,16,1024]{2,1,0:T(8,128)(2,1)S(1)}, bf16[2,16,1024]{2,1,0:T(8,128)(2,1)S(1)}, u32[]{:S(2)}, u32[]{:S(2)}) collective-permute-start(bf16[2,16,1024]{2,1,0:T(8,128)(2,1)S(1)} %get-tuple-element.86), channel_id=1, source_target_pairs={{0,1},{1,0},{2,3},{3,2},{4,5},{5,4},{6,7},{7,6},{8,9},{9,8},{10,11... | collective-permute-start | bytes 196616 | tf_op jit(solution)/shard_map/ppermute | solution.py:310
